TPU v7x, 256 devices: a whole 4x4x8 slice. The times are simulated.
256 devices in a mesh: group: 16 (over z, core), head: 16 (over y, x).
Axes of the slice: x: 4, y: 4, z: 8, core: 2. Of those that a mesh axis runs over, the one named last changes fastest.
Arguments:
- hidden_in: bfloat16 [2, 1024, 7168], P(None, ('group', 'head')), may hold values from -6 to 6
- queries: bfloat16 [2, 1024, 64, 576], P(None, ('group', 'head')), may hold values from -6 to 6
- fresh: bfloat16 [2, 1024, 576], P(None, ('group', 'head')), may hold values from -6 to 6
- res_cache: bfloat16 [512, 1024, 576], P(('group', 'head')), may hold values from -8 to 8
- res_len: int32 [512], P(('group', 'head')), may hold values from 1 to 1024, as said below
- pre_cache: bfloat16 [16, 32, 128, 576], P('head', None, 'group'), may hold values from -8 to 8
- pre_len: int32 [16, 32], P('head'), may hold values from 1 to 128, as said below
- arrival: int32 [16, 32], P('head'), may hold values from 0 to 31, each once within a row
- w_uv: bfloat16 [64, 512, 128], P('head'), may hold values from -0.25 to 0.25
- w_o: bfloat16 [8192, 7168], P('head', 'group'), may hold values from -0.0625 to 0.0625
- norm_gain: float32 [7168], replicated, may hold values from 0.5 to 1.5
- expert_ids: int32 [2, 1024, 8], P(None, 'group'), may hold values from 0 to 255, all different within a row; in each aligned block of 64 rows (0 to 63, 64 to 127, ..., all dimensions but the last counted through in order) at most 4 rows name the same one
- route_weight: float32 [2, 1024, 8], P(None, 'group'), may hold values from 0.2 to 1
- w_gu: bfloat16 [16, 2, 7168, 2048], P('head', None, None, 'group'), may hold values from -0.0625 to 0.0625
- w_down: bfloat16 [16, 2048, 7168], P('head', None, 'group'), may hold values from -0.125 to 0.125
Outputs:
- layer_out: bfloat16 [2, 1024, 7168], P(None, ('group', 'head'))
Inputs may be any that keep to these rules, and one draw needn't show every extreme that they name: `res_len`: some resident row has length exactly 1024. `pre_len`: some new request has length exactly 128. Each row of arrival is a permutation of 0 to 31. `expert_ids`: each row names 8 different experts. Within the rows of one group in one step (aligned blocks of 64 rows) no expert is named by more than 4 rows.
All inputs are finite; a program needn't handle non-finite values.
Results may differ from a plain program's by a relative error of at most 0.0065.
Values may be sent and summed in bfloat16 or wider, within the bound.
No kernel may reach another device: no remote copies, remote signals or barrier semaphores. Data moves between devices by JAX's collectives and lax.ppermute only.
A program may use at most 64 MiB of HBM per device.

v0:
```python
import jax
import jax.numpy as jnp
from jax import lax
from jax.sharding import PartitionSpec as P

LAT = 512
ROPE = 64
VD = 128
CAP = 4
STEPS = 2


def attend(query_rows, key_rows, lengths, recent):
    scaling = (VD + ROPE) ** (-0.5)
    cache_scores = (
        jnp.einsum("nhk,npk->nhp", query_rows, key_rows, preferred_element_type=jnp.float32)
        * scaling
    )
    places = lax.broadcasted_iota(jnp.int32, (1, 1, key_rows.shape[1]), 2)
    cache_scores = jnp.where(places < lengths[:, None, None], cache_scores, -jnp.inf)
    fresh_scores = (
        jnp.einsum("nhk,nsk->nhs", query_rows, recent, preferred_element_type=jnp.float32) * scaling
    )
    highest = jnp.maximum(jnp.max(cache_scores, axis=2), jnp.max(fresh_scores, axis=2))[:, :, None]
    cache_weights = jnp.exp(cache_scores - highest)
    fresh_weights = jnp.exp(fresh_scores - highest)
    totals = jnp.sum(cache_weights, axis=2, keepdims=True) + jnp.sum(
        fresh_weights, axis=2, keepdims=True
    )
    cache_probs = (cache_weights / totals).astype(jnp.bfloat16)
    fresh_probs = (fresh_weights / totals).astype(jnp.bfloat16)
    context = jnp.einsum(
        "nhp,npl->nhl", cache_probs, key_rows[:, :, :LAT], preferred_element_type=jnp.float32
    )
    context = context + jnp.einsum(
        "nhs,nsl->nhl", fresh_probs, recent[:, :, :LAT], preferred_element_type=jnp.float32
    )
    return context.astype(jnp.bfloat16)


def routing(ids_rows, weights_rows, expert):
    matched = ids_rows == expert
    present = jnp.any(matched, axis=1).astype(jnp.int32)
    row_weight = jnp.sum(jnp.where(matched, weights_rows, jnp.zeros_like(weights_rows)), axis=1)
    slot_index = jnp.cumsum(present) - present
    chosen = (slot_index[None, :] == jnp.arange(CAP, dtype=jnp.int32)[:, None]) & (
        present[None, :] == 1
    )
    return (chosen.astype(jnp.float32), row_weight)


def per_device(
    hidden_in,
    queries,
    fresh,
    res_cache,
    res_len,
    pre_cache,
    pre_len,
    arrival,
    w_uv,
    w_o,
    norm_gain,
    expert_ids,
    route_weight,
    w_gu,
    w_down,
):
    groups = lax.axis_size("group")
    columns = lax.axis_size("head")
    group_index = lax.axis_index("group")
    head_index = lax.axis_index("head")
    rows_dev = hidden_in.shape[1]
    resident = res_cache.shape[0]
    newcomers = rows_dev - resident
    requests = arrival.shape[1]
    model_width = hidden_in.shape[2]
    arrival_row = arrival[0]
    wanted = group_index * newcomers + jnp.arange(newcomers, dtype=jnp.int32)
    claimed = arrival_row[None, :] == wanted[:, None]
    new_len = jnp.sum(jnp.where(claimed, pre_len[0][None, :], 0), axis=1)
    chosen = jnp.sum(jnp.where(claimed, jnp.arange(requests, dtype=jnp.int32)[None, :], 0), axis=1)
    select_picked = jnp.take(
        lax.all_gather(pre_cache, "group", axis=2, tiled=True)[0], chosen, axis=0
    )
    outputs = []
    for step_index in range(STEPS):
        recent = jnp.swapaxes(fresh[: step_index + 1], 0, 1)
        resident_part = attend(
            queries[step_index, :resident], res_cache, res_len, recent[:resident]
        )
        arrived_part = attend(
            queries[step_index, resident:], select_picked, new_len, recent[resident:]
        )
        context = jnp.concatenate([resident_part, arrived_part], axis=0)
        by_head = lax.all_to_all(context, "head", split_axis=1, concat_axis=0, tiled=True)
        values = jnp.einsum(
            "rhl,hlv->rhv", by_head, w_uv, preferred_element_type=jnp.float32
        ).astype(jnp.bfloat16)
        values = values.reshape(columns, 1, rows_dev, w_uv.shape[0] * w_uv.shape[2])
        spread = lax.all_gather(values, "group", axis=1, tiled=True)
        flattened = spread.reshape(columns * groups * rows_dev, spread.shape[3])
        own_rows = lax.psum_scatter(
            jnp.dot(flattened, w_o, preferred_element_type=jnp.float32),
            "head",
            scatter_dimension=0,
            tiled=True,
        )
        attention = lax.all_to_all(
            own_rows.reshape(groups, rows_dev, own_rows.shape[1]),
            "group",
            split_axis=0,
            concat_axis=2,
            tiled=True,
        ).reshape(rows_dev, model_width)
        summed = hidden_in[step_index].astype(jnp.float32) + attention
        normed = (
            summed * lax.rsqrt(jnp.mean(summed * summed, axis=1, keepdims=True) + 1e-06) * norm_gain
        ).astype(jnp.bfloat16)
        group_rows = lax.all_gather(normed, "head", axis=0, tiled=True)
        ids_now = expert_ids[step_index]
        weights_now = route_weight[step_index]
        chooser, row_weight = routing(ids_now, weights_now, head_index)
        packed_rows = jnp.dot(
            chooser.astype(jnp.bfloat16), group_rows, preferred_element_type=jnp.float32
        ).astype(jnp.bfloat16)
        portion = lax.all_gather(packed_rows, "group", axis=0, tiled=True)
        gate_part = jnp.dot(portion, w_gu[0, 0], preferred_element_type=jnp.float32)
        up_part = jnp.dot(portion, w_gu[0, 1], preferred_element_type=jnp.float32)
        active = (jax.nn.silu(gate_part) * up_part).astype(jnp.bfloat16)
        rows_down = w_down[0]
        outcome = jnp.dot(
            lax.all_gather(active, "group", axis=1, tiled=True),
            rows_down,
            preferred_element_type=jnp.float32,
        )
        slot_values = (
            lax.all_to_all(
                outcome.reshape(groups, CAP, outcome.shape[1]).astype(jnp.bfloat16),
                "group",
                split_axis=0,
                concat_axis=2,
                tiled=True,
            )
            .astype(jnp.float32)
            .reshape(CAP, model_width)
        )
        weighted = chooser.T * row_weight[:, None]
        expert_mix = lax.psum_scatter(
            jnp.dot(
                weighted,
                slot_values,
                precision=lax.Precision.HIGHEST,
                preferred_element_type=jnp.float32,
            ).astype(jnp.bfloat16),
            "head",
            scatter_dimension=0,
            tiled=True,
        ).astype(jnp.float32)
        outputs.append((summed + expert_mix).astype(jnp.bfloat16))
    return jnp.stack(outputs)


def solution(mesh):
    placed = (
        P(None, ("group", "head"), None),
        P(None, ("group", "head"), None, None),
        P(None, ("group", "head"), None),
        P(("group", "head"), None, None),
        P(("group", "head")),
        P("head", None, "group", None),
        P("head", None),
        P("head", None),
        P("head", None, None),
        P("head", "group"),
        P(),
        P(None, "group", None),
        P(None, "group", None),
        P("head", None, None, "group"),
        P("head", None, "group"),
    )
    return jax.shard_map(
        per_device,
        mesh=mesh,
        in_specs=placed,
        out_specs=P(None, ("group", "head"), None),
        check_vma=False,
    )
```

profile of v0, /device:TPU:24, one launch (start us, length us, event | category | flops | bytes accessed | tf_op | source)
XLA Modules:
  0.0 595.8 jit_solution(17340914266991475579)
XLA Ops:
  8.9 1.1 fusion.155
  10.0 2.4 fusion.154
  15.1 40.9 %all-gather.8.cloned.1.call-done = bf16[1,32,128,576]{3,2,1,0:T(8,128)(2,1)} async-done(((bf16[1,32,8,576]{3,2,1,0:T(8,128)(2,1)}), bf16[1,32,128,576]{3,2,1,0:T(8,128)(2,1)}) %all-gather.8.cloned.1.call-update) | async-done | bytes 4718608 | tf_op jit(solution)/shard_map/all_gather | solution.py:84
  56.0 3.1 gather_fusion
  59.2 1.2 fusion.152
  62.1 7.2 %all-to-all-start.3 = ((bf16[4,64,512]{2,0,1:T(4,128)(2,1)}), bf16[4,64,512]{2,0,1:T(4,128)(2,1)S(1)}, u32[]{:S(2)}, u32[]{:S(2)}) async-start(bf16[4,64,512]{2,0,1:T(4,128)(2,1)} %copy.126), calls=%async_computation.4 | async-start | bytes 524288 | tf_op jit(solution)/shard_map/all_to_all | solution.py:96
  69.6 1.1 fusion.77
  70.7 5.5 all-to-all-done.3
  76.9 1.0 all_to_all.83
  79.0 2.4 fusion.31
  81.4 1.2 fusion.150
  83.4 11.6 %all_to_all.96 = bf16[4,64,512]{2,0,1:T(4,128)(2,1)S(1)} all-to-all(bf16[4,64,512]{2,0,1:T(4,128)(2,1)S(1)} %copy.113), channel_id=1, replica_groups=mesh['group'=16,'head'=16] {'head'}, dimensions={1} | all-to-all | bytes 524288 | tf_op jit(solution)/shard_map/all_to_all | solution.py:96
  96.2 17.9 %all-gather.12.cloned.1.call-done = bf16[16,16,4,512]{3,0,2,1:T(8,128)(2,1)} async-done(((bf16[16,1,4,512]{3,0,2,1:T(8,128)(2,1)}), bf16[16,16,4,512]{3,0,2,1:T(8,128)(2,1)}) %all-gather.12.cloned.1.call-update) | async-done | bytes 1048592 | tf_op jit(solution)/shard_map/all_gather | solution.py:101
  114.1 3.1 copy.130
  117.2 1.3 reshape.330
  118.5 2.1 fusion.157
  120.7 32.6 %all-gather.10.cloned.1.call-done = bf16[16,16,4,512]{3,0,2,1:T(8,128)(2,1)} async-done(((bf16[16,1,4,512]{3,0,2,1:T(8,128)(2,1)}), bf16[16,16,4,512]{3,0,2,1:T(8,128)(2,1)}) %all-gather.10.cloned.1.call-update) | async-done | bytes 1048592 | tf_op jit(solution)/shard_map/all_gather | solution.py:101
  153.3 3.0 copy.117
  156.3 1.3 reshape.324
  157.7 2.0 fusion.156
  161.1 73.2 %reduce-scatter.5.cloned.1.call-done = f32[64,448]{1,0:T(8,128)} async-done(((f32[1024,448]{1,0:T(8,128)}), f32[64,448]{1,0:T(8,128)}) %reduce-scatter.5.cloned.1.call-update) | async-done | bytes 114704 | tf_op jit(solution)/shard_map/reduce_scatter | solution.py:103
  234.4 1.6 reshape.331
  235.9 7.1 %all-to-all-start.4 = ((f32[16,4,448]{2,1,0:T(4,128)}), f32[16,4,448]{2,1,0:T(4,128)S(1)}, u32[]{:S(2)}, u32[]{:S(2)}) async-start(f32[16,4,448]{2,1,0:T(4,128)} %reshape.331), calls=%async_computation.6 | async-start | bytes 262144 | tf_op jit(solution)/shard_map/all_to_all | solution.py:109
  243.1 73.8 %reduce-scatter.3.cloned.1.call-done = f32[64,448]{1,0:T(8,128)} async-done(((f32[1024,448]{1,0:T(8,128)}), f32[64,448]{1,0:T(8,128)}) %reduce-scatter.3.cloned.1.call-update) | async-done | bytes 114704 | tf_op jit(solution)/shard_map/reduce_scatter | solution.py:103
  316.9 1.6 reshape.325
  318.5 7.1 %all-to-all-start.1 = ((f32[16,4,448]{2,1,0:T(4,128)}), f32[16,4,448]{2,1,0:T(4,128)S(1)}, u32[]{:S(2)}, u32[]{:S(2)}) async-start(f32[16,4,448]{2,1,0:T(4,128)} %reshape.325), calls=%async_computation.2 | async-start | bytes 262144 | tf_op jit(solution)/shard_map/all_to_all | solution.py:109
  326.0 8.3 %all-to-all-done.1 = f32[16,4,448]{2,1,0:T(4,128)S(1)} async-done(((f32[16,4,448]{2,1,0:T(4,128)}), f32[16,4,448]{2,1,0:T(4,128)S(1)}, u32[]{:S(2)}, u32[]{:S(2)}) %all-to-all-start.1) | async-done | bytes 114720 | tf_op jit(solution)/shard_map/all_to_all | solution.py:109
  334.9 24.7 %all-gather = bf16[16,4,7168]{2,1,0:T(4,128)(2,1)} all-gather(bf16[1,4,7168]{2,1,0:T(4,128)(2,1)S(1)} %get-tuple-element.14), channel_id=1, replica_groups=mesh['group'=16,'head'=16] {'head'}, dimensions={0}, use_global_device_ids=true | all-gather | bytes 974848 | tf_op jit(solution)/shard_map/all_gather | solution.py:120
  359.6 1.7 reshape.352
  361.5 17.5 %all-gather.1 = bf16[16,4,7168]{2,1,0:T(4,128)(2,1)S(1)} all-gather(bf16[1,4,7168]{2,1,0:T(4,128)(2,1)S(1)} %fusion), channel_id=1, replica_groups=mesh['group'=16,'head'=16] {'group'}, dimensions={0}, use_global_device_ids=true | all-gather | bytes 974848 | tf_op jit(solution)/shard_map/all_gather | solution.py:127
  379.0 1.1 reshape.354
  380.1 2.3 fusion.16
  382.5 1.9 fusion.59
  384.4 16.2 %all_gather.31 = bf16[64,2048]{1,0:T(8,128)(2,1)S(1)} all-gather(bf16[64,128]{1,0:T(8,128)(2,1)S(1)} %fusion.59), channel_id=1, replica_groups=mesh['group'=16,'head'=16] {'group'}, dimensions={1}, use_global_device_ids=true | all-gather | bytes 278528 | tf_op jit(solution)/shard_map/all_gather | solution.py:133
  402.0 4.1 all-to-all-start.2
  406.1 25.3 %all-gather.2 = bf16[16,4,7168]{2,1,0:T(4,128)(2,1)} all-gather(bf16[1,4,7168]{2,1,0:T(4,128)(2,1)S(1)} %get-tuple-element.15), channel_id=1, replica_groups=mesh['group'=16,'head'=16] {'head'}, dimensions={0}, use_global_device_ids=true | all-gather | bytes 974848 | tf_op jit(solution)/shard_map/all_gather | solution.py:120
  431.4 1.7 reshape.356
  433.3 19.7 %all-gather.3 = bf16[16,4,7168]{2,1,0:T(4,128)(2,1)S(1)} all-gather(bf16[1,4,7168]{2,1,0:T(4,128)(2,1)S(1)} %fusion.1), channel_id=1, replica_groups=mesh['group'=16,'head'=16] {'group'}, dimensions={0}, use_global_device_ids=true | all-gather | bytes 974848 | tf_op jit(solution)/shard_map/all_gather | solution.py:127
  453.0 1.1 reshape.358
  454.1 2.3 fusion.14
  456.4 1.9 fusion.56
  458.4 16.0 %all_gather.35 = bf16[64,2048]{1,0:T(8,128)(2,1)S(1)} all-gather(bf16[64,128]{1,0:T(8,128)(2,1)S(1)} %fusion.56), channel_id=1, replica_groups=mesh['group'=16,'head'=16] {'group'}, dimensions={1}, use_global_device_ids=true | all-gather | bytes 278528 | tf_op jit(solution)/shard_map/all_gather | solution.py:133
  475.8 5.0 all-to-all-start.5
  481.0 7.7 %all-to-all-done.5 = bf16[16,4,448]{2,1,0:T(4,128)(2,1)S(1)} async-done(((bf16[16,4,448]{2,1,0:T(4,128)(2,1)}), bf16[16,4,448]{2,1,0:T(4,128)(2,1)S(1)}, u32[]{:S(2)}, u32[]{:S(2)}) %all-to-all-start.5) | async-done | bytes 57376 | tf_op jit(solution)/shard_map/all_to_all | solution.py:138
  488.8 1.9 convolution_convert_fusion.1
  490.7 1.9 convolution_convert_fusion
  493.9 93.3 %all-reduce.5.cloned.1.call-done = (bf16[64,7168]{1,0:T(8,128)(2,1)}, bf16[64,7168]{1,0:T(8,128)(2,1)}) async-done(((bf16[64,7168]{1,0:T(8,128)(2,1)}, bf16[64,7168]{1,0:T(8,128)(2,1)}), (bf16[64,7168]{1,0:T(8,128)(2,1)}, bf16[64,7168]{1,0:T(8,128)(2,1)})) %all-reduce.5.cloned.1.call-update) | async-done | bytes 1835024
  587.2 1.1 fusion.98
  (133 shorter events, 17.8 us)
Async XLA Ops:
  6.5 394.2 %copy-start = (bf16[1,2048,448]{1,2,0:T(8,128)(2,1)S(1)}, bf16[1,2048,448]{1,2,0:T(8,128)(2,1)}, u32[]{:S(2)}) copy-start(bf16[1,2048,448]{1,2,0:T(8,128)(2,1)} %param.29) | copy-start | bytes 5505028
  6.5 6.5 %copy-start.9 = (bf16[2,4,576]{2,1,0:T(4,128)(2,1)S(1)}, bf16[2,4,576]{2,1,0:T(4,128)(2,1)}, u32[]{:S(2)}) copy-start(bf16[2,4,576]{2,1,0:T(4,128)(2,1)} %param.17) | copy-start | bytes 27652
  6.5 6.5 %copy-start.7 = (bf16[2,4,64,576]{3,2,1,0:T(8,128)(2,1)S(1)}, bf16[2,4,64,576]{3,2,1,0:T(8,128)(2,1)}, u32[]{:S(2)}) copy-start(bf16[2,4,64,576]{3,2,1,0:T(8,128)(2,1)} %param.16) | copy-start | bytes 1769476
  6.5 6.2 %copy-start.13 = (s32[1,32]{1,0:T(1,128)S(1)}, s32[1,32]{1,0:T(1,128)}, u32[]{:S(2)}) copy-start(s32[1,32]{1,0:T(1,128)} %param.22) | copy-start | bytes 388
  6.5 6.2 %copy-start.12 = (s32[1,32]{1,0:T(1,128)S(1)}, s32[1,32]{1,0:T(1,128)}, u32[]{:S(2)}) copy-start(s32[1,32]{1,0:T(1,128)} %param.21) | copy-start | bytes 388
  6.5 49.5 %all-gather.8.cloned.1.call-start = ((), (), s32[]{:S(2)}) async-start(), calls=%async_computation.8 | async-start | bytes 5570560 | tf_op jit(solution)/shard_map/all_gather | solution.py:84
  8.0 5.2 copy-start.1
  60.7 17.3 %copy-start.2 = (bf16[4,512,128]{2,1,0:T(8,128)(2,1)S(1)}, bf16[4,512,128]{2,1,0:T(8,128)(2,1)}, u32[]{:S(2)}) copy-start(bf16[4,512,128]{2,1,0:T(8,128)(2,1)} %param.23) | copy-start | bytes 1572868
  62.1 14.0 %all-to-all-start.3 = ((bf16[4,64,512]{2,0,1:T(4,128)(2,1)}), bf16[4,64,512]{2,0,1:T(4,128)(2,1)S(1)}, u32[]{:S(2)}, u32[]{:S(2)}) async-start(bf16[4,64,512]{2,0,1:T(4,128)(2,1)} %copy.126), calls=%async_computation.4 | async-start | bytes 524288 | tf_op jit(solution)/shard_map/all_to_all | solution.py:96
  69.4 44.7 %all-gather.12.cloned.1.call-start = ((), (), s32[]{:S(2)}) async-start(), calls=%async_computation.11 | async-start | bytes 1114112 | tf_op jit(solution)/shard_map/all_gather | solution.py:101
  79.0 74.3 %all-gather.10.cloned.1.call-start = ((), (), s32[]{:S(2)}) async-start(), calls=%async_computation.9 | async-start | bytes 1114112 | tf_op jit(solution)/shard_map/all_gather | solution.py:101
  96.1 22.4 %copy-start.3 = (bf16[512,448]{0,1:T(8,128)(2,1)S(1)}, bf16[512,448]{0,1:T(8,128)(2,1)}, u32[]{:S(2)}) copy-start(bf16[512,448]{0,1:T(8,128)(2,1)} %param.24) | copy-start | bytes 1376260
  96.1 138.2 %reduce-scatter.5.cloned.1.call-start = ((), (), s32[]{:S(2)}) async-start(), calls=%async_computation.12 | async-start | bytes 2228224 | tf_op jit(solution)/shard_map/reduce_scatter | solution.py:103
  120.6 196.3 %reduce-scatter.3.cloned.1.call-start = ((), (), s32[]{:S(2)}) async-start(), calls=%async_computation.10 | async-start | bytes 2228224 | tf_op jit(solution)/shard_map/reduce_scatter | solution.py:103
  157.7 2.1 copy-start.4
  159.7 0.7 copy-start.11
  159.7 1.0 copy-start.10
  159.7 175.0 %copy-start.8 = (f32[7168]{0:T(1024)S(1)}, f32[7168]{0:T(1024)}, u32[]{:S(2)}) copy-start(f32[7168]{0:T(1024)} %param.25) | copy-start | bytes 86020
  235.9 82.5 %all-to-all-start.4 = ((f32[16,4,448]{2,1,0:T(4,128)}), f32[16,4,448]{2,1,0:T(4,128)S(1)}, u32[]{:S(2)}, u32[]{:S(2)}) async-start(f32[16,4,448]{2,1,0:T(4,128)} %reshape.331), calls=%async_computation.6 | async-start | bytes 262144 | tf_op jit(solution)/shard_map/all_to_all | solution.py:109
  318.5 15.9 %all-to-all-start.1 = ((f32[16,4,448]{2,1,0:T(4,128)}), f32[16,4,448]{2,1,0:T(4,128)S(1)}, u32[]{:S(2)}, u32[]{:S(2)}) async-start(f32[16,4,448]{2,1,0:T(4,128)} %reshape.325), calls=%async_computation.2 | async-start | bytes 262144 | tf_op jit(solution)/shard_map/all_to_all | solution.py:109
  380.1 2.3 copy-start.5
  402.0 73.8 %all-to-all-start.2 = ((bf16[16,4,448]{2,1,0:T(4,128)(2,1)}), bf16[16,4,448]{2,1,0:T(4,128)(2,1)S(1)}, u32[]{:S(2)}, u32[]{:S(2)}) async-start(bf16[16,4,448]{2,1,0:T(4,128)(2,1)} %copy.122), calls=%async_computation.3 | async-start | bytes 131072 | tf_op jit(solution)/shard_map/all_to_all | solution.py:138
  454.1 2.3 copy-start.6
  475.8 12.8 %all-to-all-start.5 = ((bf16[16,4,448]{2,1,0:T(4,128)(2,1)}), bf16[16,4,448]{2,1,0:T(4,128)(2,1)S(1)}, u32[]{:S(2)}, u32[]{:S(2)}) async-start(bf16[16,4,448]{2,1,0:T(4,128)(2,1)} %copy.135), calls=%async_computation.7 | async-start | bytes 131072 | tf_op jit(solution)/shard_map/all_to_all | solution.py:138
  480.8 106.4 %all-reduce.5.cloned.1.call-start = ((), (), s32[]{:S(2)}) async-start(), calls=%async_computation.13 | async-start | bytes 3670016
  480.9 11.7 %copy-start.15 = (u32[256]{0:T(256)S(1)}, u32[256]{0:T(256)}, u32[]{:S(2)}) copy-start(u32[256]{0:T(256)} %constant.69) | copy-start | bytes 3076
  588.3 0.6 copy-start.14
Sparse Core Ops, SparseCore 0:
  9.2 46.7 all-gather.7
  79.1 34.9 all-gather.11
  115.9 37.3 all-gather.9
  156.7 77.6 reduce-scatter.4
  238.2 78.6 reduce-scatter.2
  492.7 94.4 all-reduce.4
where the time goes:
time: 597 us; the launch traced here: 596 us
  waiting for transfers between devices  354 us (59%)
  blocking collectives  131 us (22%)
  matrix products  30.8 us (5%)
  starting transfers between devices  30.7 us (5%)
  local copies, waits for them, and re-layouts  30.2 us (5%)
  between operations  14.7 us (2%)
    reduce_scatter x2, waiting for transfers between devices, per_device(): lax.psum_scatter(jnp.dot(flattened, w_o, preferred_element_type=jnp.float...  147 us
    unnamed x7, waiting for transfers between devices  94.1 us
    all_gather x2, waiting for transfers between devices, per_device(): spread = lax.all_gather(values, 'group', axis=1, tiled=True)  50.5 us
    all_gather x2, blocking collectives, per_device(): group_rows = lax.all_gather(normed, 'head', axis=0, tiled=True)  50 us
    all_gather x1, waiting for transfers between devices, per_device(): lax.all_gather(pre_cache, 'group', axis=2, tiled=True)[0]  40.9 us
    all_gather x2, blocking collectives, per_device(): portion = lax.all_gather(packed_rows, 'group', axis=0, tiled=True)  37.2 us
    all_gather x2, blocking collectives, per_device(): lax.all_gather(active, 'group', axis=1, tiled=True)  32.2 us
    all_to_all x2, starting transfers between devices, per_device(): lax.all_to_all(own_rows.reshape(groups, rows_dev, own_rows.shape[1]), 'gr...  14.2 us
  transfers between devices with their start and end apart: 11, of which 9 were waited for; matrix products, arithmetic and copies ran while one was open for 7% of the time, Pallas kernels for 0%

commit v1 on v0

v1 whole, which is shorter than its diff:
```python
import jax
import jax.numpy as jnp
from jax import lax
from jax.experimental import pallas as pl
from jax.experimental.pallas import tpu as pltpu
from jax.sharding import PartitionSpec as P

LAT = 512
ROPE = 64
VD = 128
CAP = 4
STEPS = 2


def attend(query_rows, key_rows, lengths, recent):
    rows, steps, heads, width = query_rows.shape
    scaling = (VD + ROPE) ** (-0.5)
    flat = query_rows.reshape(rows, steps * heads, width)
    cache_scores = (
        jnp.einsum("nqk,npk->nqp", flat, key_rows, preferred_element_type=jnp.float32) * scaling
    )
    places = lax.broadcasted_iota(jnp.int32, (1, 1, key_rows.shape[1]), 2)
    cache_scores = jnp.where(places < lengths[:, None, None], cache_scores, -jnp.inf)
    fresh_scores = (
        jnp.einsum("nqk,nsk->nqs", flat, recent, preferred_element_type=jnp.float32) * scaling
    )
    step_of = jnp.arange(steps * heads, dtype=jnp.int32)[:, None] // heads
    seen = jnp.arange(steps, dtype=jnp.int32)[None, :] <= step_of
    fresh_scores = jnp.where(seen[None], fresh_scores, -jnp.inf)
    highest = jnp.maximum(jnp.max(cache_scores, axis=2), jnp.max(fresh_scores, axis=2))[:, :, None]
    cache_weights = jnp.exp(cache_scores - highest)
    fresh_weights = jnp.exp(fresh_scores - highest)
    totals = jnp.sum(cache_weights, axis=2, keepdims=True) + jnp.sum(
        fresh_weights, axis=2, keepdims=True
    )
    cache_probs = (cache_weights / totals).astype(jnp.bfloat16)
    fresh_probs = (fresh_weights / totals).astype(jnp.bfloat16)
    context = jnp.einsum(
        "nqp,npl->nql", cache_probs, key_rows[:, :, :LAT], preferred_element_type=jnp.float32
    )
    context = context + jnp.einsum(
        "nqs,nsl->nql", fresh_probs, recent[:, :, :LAT], preferred_element_type=jnp.float32
    )
    return context.astype(jnp.bfloat16).reshape(rows, steps, heads, LAT)


def routing(ids, weights, experts):
    matched = ids[None] == jnp.arange(experts, dtype=jnp.int32)[:, None, None, None]
    present = jnp.any(matched, axis=3)
    row_weight = jnp.sum(jnp.where(matched, weights[None], 0.0), axis=3)
    rows = ids.shape[1]
    before = (
        jnp.arange(rows, dtype=jnp.int32)[:, None] < jnp.arange(rows, dtype=jnp.int32)[None, :]
    )
    slot_index = jnp.einsum(
        "etr,rs->ets",
        present.astype(jnp.bfloat16),
        before.astype(jnp.bfloat16),
        preferred_element_type=jnp.float32,
    ).astype(jnp.int32)
    slots = jnp.arange(CAP, dtype=jnp.int32)[None, None, :, None]
    chosen = (slot_index[:, :, None, :] == slots) & present[:, :, None, :]
    return chosen, row_weight


def project_body(x_ref, w_ref, own_ref, hidden_ref, rows_ref, slots_ref):
    blocks, _, width = w_ref.shape
    half = x_ref.shape[0] // 2
    parts = [
        jnp.dot(x_ref[...], w_ref[b], preferred_element_type=jnp.float32) for b in range(blocks)
    ]
    whole = jnp.concatenate(parts, axis=1)
    rows_ref[...] = whole[:half].astype(jnp.bfloat16)
    carried = jnp.dot(own_ref[...], hidden_ref[...], preferred_element_type=jnp.float32)
    slots_ref[...] = (whole[half:] + carried).astype(jnp.bfloat16)


def project(x, w, own, hidden):
    blocks, depth, width = w.shape
    half = x.shape[0] // 2
    each = 4
    out = jax.ShapeDtypeStruct((half, blocks * width), jnp.bfloat16)
    return pl.pallas_call(
        project_body,
        grid=(blocks // each,),
        in_specs=[
            pl.BlockSpec(x.shape, lambda i: (0, 0)),
            pl.BlockSpec((each, depth, width), lambda i: (i, 0, 0)),
            pl.BlockSpec(own.shape, lambda i: (0, 0)),
            pl.BlockSpec((hidden.shape[0], each * width), lambda i: (0, i)),
        ],
        out_specs=[pl.BlockSpec((half, each * width), lambda i: (0, i))] * 2,
        out_shape=[out, out],
        compiler_params=pltpu.CompilerParams(vmem_limit_bytes=40 * 1024 * 1024),
        cost_estimate=pl.CostEstimate(
            flops=2 * x.shape[0] * blocks * depth * width,
            bytes_accessed=2 * blocks * depth * width + 4 * x.shape[0] * blocks * width,
            transcendentals=0,
        ),
        name="project",
    )(x, w, own, hidden)


def per_device(
    hidden_in,
    queries,
    fresh,
    res_cache,
    res_len,
    pre_cache,
    pre_len,
    arrival,
    w_uv,
    w_o,
    norm_gain,
    expert_ids,
    route_weight,
    w_gu,
    w_down,
):
    groups = lax.axis_size("group")
    columns = lax.axis_size("head")
    group_index = lax.axis_index("group")
    head_index = lax.axis_index("head")
    steps, rows_dev, width = hidden_in.shape
    resident = res_cache.shape[0]
    newcomers = rows_dev - resident
    requests = arrival.shape[1]
    own_rows = steps * rows_dev
    rows_group = columns * own_rows
    heads_dev = w_uv.shape[0]
    slots_dev = steps * CAP

    w_all = lax.all_gather(w_o, "group", axis=0, tiled=False)

    places = jnp.arange(requests, dtype=jnp.int32)
    arrival_row = arrival[0]
    claimed = arrival_row[None, :] == places[:, None]
    order = jnp.sum(jnp.where(claimed, places[None, :], 0), axis=1)
    len_sorted = jnp.sum(jnp.where(claimed, pre_len[0][None, :], 0), axis=1)
    new_len = lax.dynamic_slice(len_sorted, (group_index * newcomers,), (newcomers,))
    sorted_cache = jnp.take(pre_cache[0], order, axis=0)
    taken = lax.all_to_all(
        sorted_cache.reshape(groups, newcomers, *sorted_cache.shape[1:]),
        "group",
        split_axis=0,
        concat_axis=0,
        tiled=False,
    )
    taken = jnp.swapaxes(taken, 0, 1).reshape(newcomers, -1, sorted_cache.shape[2])

    chosen, row_weight = routing(expert_ids, route_weight, columns)
    by_row = chosen.reshape(columns, steps, CAP, columns, rows_dev)
    same = jnp.arange(steps)[:, None] == jnp.arange(steps)[None, :]
    chooser = by_row[:, :, :, :, None, :] & same[None, :, None, None, :, None]
    chooser = chooser.reshape(columns * slots_dev, rows_group).astype(jnp.bfloat16)
    own_chooser = lax.dynamic_slice(
        chooser, (0, head_index * own_rows), (columns * slots_dev, own_rows)
    )
    mine = lax.dynamic_slice(chooser, (head_index * slots_dev, 0), (slots_dev, rows_group))
    weight_mine = lax.dynamic_slice(
        row_weight, (head_index, 0, 0), (1, steps, columns * rows_dev)
    )[0]
    weight_mine = jnp.swapaxes(weight_mine.reshape(steps, columns, rows_dev), 0, 1).reshape(
        rows_group, 1
    )
    spread = mine.astype(jnp.float32).T * weight_mine

    by_row_queries = jnp.swapaxes(queries, 0, 1)
    recent = jnp.swapaxes(fresh, 0, 1)
    context = jnp.concatenate(
        [
            attend(by_row_queries[:resident], res_cache, res_len, recent[:resident]),
            attend(by_row_queries[resident:], taken, new_len, recent[resident:]),
        ],
        axis=0,
    )
    context = context.reshape(rows_dev, steps, columns, heads_dev, LAT).transpose(2, 3, 1, 0, 4)
    by_head = lax.all_to_all(context, "head", split_axis=0, concat_axis=0, tiled=False)
    by_head = jnp.swapaxes(by_head, 0, 1).reshape(heads_dev, rows_group, LAT)
    values = jnp.einsum("hrl,hlv->rhv", by_head, w_uv, preferred_element_type=jnp.float32).astype(
        jnp.bfloat16
    )
    values = values.reshape(rows_group, heads_dev * VD)
    values_slots = jnp.dot(chooser, values, preferred_element_type=jnp.float32).astype(jnp.bfloat16)
    hidden_own = hidden_in.reshape(own_rows, width)
    part_rows, part_slots = project(
        jnp.concatenate([values, values_slots], axis=0), w_all, own_chooser, hidden_own
    )

    slot_parts = lax.all_to_all(
        part_slots.reshape(columns, slots_dev, width), "head", 0, 0, tiled=False
    )
    slot_rows = jnp.sum(slot_parts.astype(jnp.float32), axis=0)
    normed = (
        slot_rows
        * lax.rsqrt(jnp.mean(slot_rows * slot_rows, axis=1, keepdims=True) + 1e-06)
        * norm_gain
    ).astype(jnp.bfloat16)
    portion = lax.all_gather(normed, "group", axis=0, tiled=True)

    row_parts = lax.all_to_all(
        part_rows.reshape(columns, own_rows, width), "head", 0, 0, tiled=False
    )
    summed = hidden_own.astype(jnp.float32) + jnp.sum(row_parts.astype(jnp.float32), axis=0)

    gate_part = jnp.dot(portion, w_gu[0, 0], preferred_element_type=jnp.float32)
    up_part = jnp.dot(portion, w_gu[0, 1], preferred_element_type=jnp.float32)
    active = (jax.nn.silu(gate_part) * up_part).astype(jnp.bfloat16)
    outcome = jnp.dot(
        lax.all_gather(active, "group", axis=1, tiled=True),
        w_down[0],
        preferred_element_type=jnp.float32,
    )
    slot_values = lax.all_to_all(
        outcome.reshape(groups, slots_dev, outcome.shape[1]).astype(jnp.bfloat16),
        "group",
        split_axis=0,
        concat_axis=2,
        tiled=True,
    ).reshape(slots_dev, width)
    mixed = jnp.dot(
        spread,
        slot_values.astype(jnp.float32),
        precision=lax.Precision.HIGHEST,
        preferred_element_type=jnp.float32,
    ).astype(jnp.bfloat16)
    mix_parts = lax.all_to_all(mixed.reshape(columns, own_rows, width), "head", 0, 0, tiled=False)
    out = summed + jnp.sum(mix_parts.astype(jnp.float32), axis=0)
    return out.astype(jnp.bfloat16).reshape(steps, rows_dev, width)


def solution(mesh):
    placed = (
        P(None, ("group", "head"), None),
        P(None, ("group", "head"), None, None),
        P(None, ("group", "head"), None),
        P(("group", "head"), None, None),
        P(("group", "head")),
        P("head", None, "group", None),
        P("head", None),
        P("head", None),
        P("head", None, None),
        P("head", "group"),
        P(),
        P(None, "group", None),
        P(None, "group", None),
        P("head", None, None, "group"),
        P("head", None, "group"),
    )
    return jax.shard_map(
        per_device,
        mesh=mesh,
        in_specs=placed,
        out_specs=P(None, ("group", "head"), None),
        check_vma=False,
    )
```

time: 597 us -> 273 us (0.46)
  waiting for transfers between devices: 354 us -> 111 us
  blocking collectives: 131 us -> 61.7 us
  matrix products: 30.8 us -> 16.2 us
  other arithmetic: 4.4 us -> 12.3 us
  local copies, waits for them, and re-layouts: 30.2 us -> 22.7 us
    reduce_scatter x2 -> x0, waiting for transfers between devices: 147 us -> none  [per_device(): lax.psum_scatter(jnp.dot(flattened, w_o, preferred_element_type=jnp.float...]
    unnamed x7 -> x2, waiting for transfers between devices: 94.1 us -> 0.73 us
    all_gather x4 -> x0, blocking collectives: 87.2 us -> none  [the longest x2 50 us: per_device(): group_rows = lax.all_gather(normed, 'head', axis=0, tiled=True)]
    all_gather x3 -> x2, waiting for transfers between devices: 91.4 us -> 47.9 us  [the longest x1 36.7 us: per_device(): portion = lax.all_gather(normed, 'group', axis=0, tiled=True)]
    all_to_all x5 -> x4, waiting for transfers between devices: 21.5 us -> 62.7 us  [the longest x1 25.7 us: per_device(): lax.all_to_all(part_rows.reshape(columns, own_rows, width), 'head', 0, 0,...]
    all_to_all x1 -> x2, blocking collectives: 11.6 us -> 44.8 us  [the longest x1 30.7 us: per_device(): lax.all_to_all(part_slots.reshape(columns, slots_dev, width), 'head', 0,...]
    all_gather x2 -> x1, blocking collectives: 32.2 us -> 16.8 us  [per_device(): lax.all_gather(active, 'group', axis=1, tiled=True)]
    dot_general x24 -> x13, matrix products: 22.2 us -> 11.2 us  [the longest x1 3.56 us: per_device(): jnp.dot(spread, slot_values.astype(jnp.float32), precision=lax.Precision....]
  transfers between devices with their start and end apart: 11 -> 6, of which waited for: 9 -> 6; matrix products, arithmetic and copies ran while one was open for 7% -> 10% of each run, Pallas kernels for 0% -> 0%
where the time goes in v1:
time: 273 us; the launch traced here: 271 us
  waiting for transfers between devices  111 us (41%)
  blocking collectives  61.7 us (23%)
  starting transfers between devices  29.1 us (11%)
  local copies, waits for them, and re-layouts  22.7 us (8%)
  matrix products  16.2 us (6%)
  between operations  13.8 us (5%)
  other arithmetic  12.3 us (5%)
  Pallas kernels  3.58 us (1%)
    all_gather x1, waiting for transfers between devices, per_device(): portion = lax.all_gather(normed, 'group', axis=0, tiled=True)  36.7 us
    all_to_all x1, blocking collectives, per_device(): lax.all_to_all(part_slots.reshape(columns, slots_dev, width), 'head', 0,...  30.7 us
    all_to_all x1, waiting for transfers between devices, per_device(): lax.all_to_all(part_rows.reshape(columns, own_rows, width), 'head', 0, 0,...  25.7 us
    all_to_all x1, waiting for transfers between devices, per_device(): lax.all_to_all(mixed.reshape(columns, own_rows, width), 'head', 0, 0, til...  25.5 us
    all_gather x1, blocking collectives, per_device(): lax.all_gather(active, 'group', axis=1, tiled=True)  16.8 us
    all_to_all x1, blocking collectives, per_device(): lax.all_to_all(outcome.reshape(groups, slots_dev, outcome.shape[1]).astyp...  14.2 us
    all_gather x1, local copies, waits for them, and re-layouts, per_device(): w_all = lax.all_gather(w_o, 'group', axis=0, tiled=False)  11.6 us
    all_gather x1, waiting for transfers between devices, per_device(): w_all = lax.all_gather(w_o, 'group', axis=0, tiled=False)  11.2 us
  transfers between devices with their start and end apart: 6, of which 6 were waited for; matrix products, arithmetic and copies ran while one was open for 10% of the time, Pallas kernels for 0%

profile of v1, /device:TPU:24, one launch (start us, length us, event | category | flops | bytes accessed | tf_op | source)
XLA Modules:
  0.0 270.8 jit_solution(4451089704749753140)
XLA Ops:
  6.5 0.7 all-gather.6.cloned.1.call-update
  7.3 0.8 select_reduce_fusion.2
  8.2 1.6 gather_fusion
  9.8 0.8 broadcast_select_fusion
  10.6 8.7 %all-to-all-start = ((bf16[16,2,8,576]{3,2,1,0:T(8,128)(2,1)}), bf16[16,2,8,576]{3,2,1,0:T(8,128)(2,1)S(1)}, u32[]{:S(2)}, u32[]{:S(2)}) async-start(bf16[16,2,8,576]{3,2,1,0:T(8,128)(2,1)} %broadcast_select_fusion), calls=%async_computation | async-start | bytes 655360 | tf_op jit(solution)/shard_map/all_to_all | solution.py:143
  19.8 0.3 copy.100
  20.1 0.4 copy.102
  20.5 1.1 fusion.56
  21.9 0.2 fusion.60
  22.1 2.8 %fusion.59 = (f32[2,128]{1,0:T(2,128)S(1)}, f32[2,128,1024]{2,1,0:T(8,128)S(1)}) fusion(bf16[2,128,576]{2,1,0:T(8,128)(2,1)S(1)} %bitcast.85, bf16[2,1024,576]{1,2,0:T(8,128)(2,1)} %param.18, pred[2,1024]{1,0:T(4,128)(4,1)S(1)} %iota_compare_fusion.4), kind=kOutput, calls=%fused_computation.106 | convolution fusion | flops 302776064 | bytes 3705856 | tf_op jit(solution)/shard_map/nqk,npk->nqp/dot_general | solution.py:20
  25.0 0.3 fusion.28
  25.3 0.8 fusion.1
  26.2 0.3 fusion.12
  26.9 0.9 fusion.27
  27.8 5.2 %all-to-all-done = bf16[16,2,8,576]{3,2,1,0:T(8,128)(2,1)S(1)} async-done(((bf16[16,2,8,576]{3,2,1,0:T(8,128)(2,1)}), bf16[16,2,8,576]{3,2,1,0:T(8,128)(2,1)S(1)}, u32[]{:S(2)}, u32[]{:S(2)}) %all-to-all-start) | async-done | bytes 294944 | tf_op jit(solution)/shard_map/all_to_all | solution.py:143
  33.0 0.3 fusion.57
  33.4 0.3 fusion.32
  33.7 0.3 fusion.13
  34.1 1.1 copy_bitcast_fusion
  35.2 7.3 %all-to-all-start.1 = ((bf16[16,4,2,4,512]{4,1,2,3,0:T(4,128)(2,1)}), bf16[16,4,2,4,512]{4,1,2,3,0:T(4,128)(2,1)S(1)}, u32[]{:S(2)}, u32[]{:S(2)}) async-start(bf16[16,4,2,4,512]{4,1,2,3,0:T(4,128)(2,1)} %copy_bitcast_fusion), calls=%async_computation.1 | async-start | bytes 1048576 | tf_op jit(solution)/shard_map/all_to_all | solution.py:179
  42.5 2.5 broadcast_and_fusion
  45.0 1.9 and.74
  47.1 6.3 %all-to-all-done.1 = bf16[16,4,2,4,512]{4,1,2,3,0:T(4,128)(2,1)S(1)} async-done(((bf16[16,4,2,4,512]{4,1,2,3,0:T(4,128)(2,1)}), bf16[16,4,2,4,512]{4,1,2,3,0:T(4,128)(2,1)S(1)}, u32[]{:S(2)}, u32[]{:S(2)}) %all-to-all-start.1) | async-done | bytes 524320 | tf_op jit(solution)/shard_map/all_to_all | solution.py:179
  53.4 0.3 copy.95
  53.8 1.4 convolution_convert_fusion.1
  55.6 11.2 %all-gather.6.cloned.1.call-done = bf16[8192,448]{0,1:T(8,128)(2,1)} async-done(((bf16[512,448]{0,1:T(8,128)(2,1)}), bf16[8192,448]{0,1:T(8,128)(2,1)}) %all-gather.6.cloned.1.call-update) | async-done | bytes 7340048 | tf_op jit(solution)/shard_map/all_gather | solution.py:134
  66.8 11.6 %copy.103 = bf16[8192,448]{1,0:T(8,128)(2,1)} copy(bf16[8192,448]{0,1:T(8,128)(2,1)} %all-gather.6.cloned.1.call-done) | data formatting | bytes 14680064 | tf_op jit(solution)/shard_map/all_gather | solution.py:134
  78.4 3.4 %copy-done.1 = bf16[8192,448]{1,0:T(8,128)(2,1)S(1)} copy-done((bf16[8192,448]{1,0:T(8,128)(2,1)S(1)}, bf16[8192,448]{1,0:T(8,128)(2,1)}, u32[]{:S(2)}) %copy-start.1) | copy-done | bytes 7340056
  81.7 3.6 %project.1 = (bf16[128,7168]{1,0:T(8,128)(2,1)S(1)}, bf16[128,7168]{1,0:T(8,128)(2,1)S(1)}) custom-call(bf16[256,512]{1,0:T(8,128)(2,1)S(1)} %pad_maximum_fusion.1.x_ref, bf16[16,512,448]{2,1,0:T(8,128)(2,1)S(1)} %bitcast.81, bf16[128,8]{1,0:T(8,128)(2,1)S(1)} %constant_dynamic-slice_fusion.own_ref, bf16[8,7168]{1,0:T(8,128)(2,1)S(1)} %reshape.246.hidden_ref), custom_call_target="tpu_custom_call" | custom-call | flops 1879048192 | bytes 14680064 | tf_op jit(solution)/shard_map/project/pallas_call | solution.py:83
  85.3 30.7 %all_to_all.40 = bf16[16,8,7168]{2,1,0:T(8,128)(2,1)S(1)} all-to-all(bf16[16,8,7168]{2,1,0:T(8,128)(2,1)S(1)} %bitcast.83), channel_id=1, replica_groups=mesh['group'=16,'head'=16] {'head'}, dimensions={0} | all-to-all | bytes 3670016 | tf_op jit(solution)/shard_map/all_to_all | solution.py:191
  116.0 0.3 convert_reduce_fusion.1
  116.5 0.3 copy-done.7
  116.8 0.7 multiply_convert_fusion
  117.5 36.7 %all-gather.4.cloned.1.call-done = bf16[128,7168]{1,0:T(8,128)(2,1)} async-done(((bf16[8,7168]{1,0:T(8,128)(2,1)}), bf16[128,7168]{1,0:T(8,128)(2,1)}) %all-gather.4.cloned.1.call-update) | async-done | bytes 1835024 | tf_op jit(solution)/shard_map/all_gather | solution.py:200
  154.2 2.8 %fusion.7 = f32[128,128]{1,0:T(8,128)S(1)} fusion(bf16[128,7168]{1,0:T(8,128)(2,1)} %all-gather.4.cloned.1.call-done, bf16[1,2,7168,128]{3,2,1,0:T(8,128)(2,1)} %param.28), kind=kOutput, calls=%fused_computation.13 | convolution fusion | flops 234881024 | bytes 3735552 | tf_op jit(solution)/shard_map/dot_general | solution.py:207
  157.1 0.3 copy-done.11
  157.4 2.1 fusion.22
  159.5 16.8 %all_gather.15 = bf16[128,2048]{1,0:T(8,128)(2,1)S(1)} all-gather(bf16[128,128]{1,0:T(8,128)(2,1)S(1)} %fusion.22), channel_id=1, replica_groups=mesh['group'=16,'head'=16] {'group'}, dimensions={1}, use_global_device_ids=true | all-gather | bytes 557056 | tf_op jit(solution)/shard_map/all_gather | solution.py:211
  176.3 0.7 fusion.14
  177.0 14.2 %all_to_all.41 = bf16[16,8,448]{2,1,0:T(8,128)(2,1)S(1)} all-to-all(bf16[16,8,448]{2,1,0:T(8,128)(2,1)S(1)} %fusion.14), channel_id=1, replica_groups=mesh['group'=16,'head'=16] {'group'}, dimensions={0} | all-to-all | bytes 229376 | tf_op jit(solution)/shard_map/all_to_all | solution.py:215
  191.2 7.3 %all-to-all-start.2 = ((bf16[16,8,7168]{2,1,0:T(8,128)(2,1)}), bf16[16,8,7168]{2,1,0:T(8,128)(2,1)}, u32[]{:S(2)}, u32[]{:S(2)}) async-start(bf16[16,8,7168]{2,1,0:T(8,128)(2,1)} %bitcast.82), calls=%async_computation.2 | async-start | bytes 3670016 | tf_op jit(solution)/shard_map/all_to_all | solution.py:202
  199.1 3.6 %fusion = bf16[16,8,7168]{2,1,0:T(8,128)(2,1)} fusion(bf16[8,7168]{1,0:T(8,128)(2,1)S(1)} %reshape.249, f32[128]{0:T(128)S(1)} %mul.71, bf16[128,128]{1,0:T(8,128)(2,1)} %copy-done.5, s32[]{:T(128)S(6)} %select_n.86), kind=kOutput, calls=%fused_computation.2 | convolution fusion | flops 88999936 | bytes 1952260 | tf_op jit(solution)/shard_map/dot_general | solution.py:222
  202.6 25.7 %all-to-all-done.2 = bf16[16,8,7168]{2,1,0:T(8,128)(2,1)} async-done(((bf16[16,8,7168]{2,1,0:T(8,128)(2,1)}), bf16[16,8,7168]{2,1,0:T(8,128)(2,1)}, u32[]{:S(2)}, u32[]{:S(2)}) %all-to-all-start.2) | async-done | bytes 1835040 | tf_op jit(solution)/shard_map/all_to_all | solution.py:202
  228.3 5.8 %all-to-all-start.5 = ((bf16[16,8,7168]{2,1,0:T(8,128)(2,1)}), bf16[16,8,7168]{2,1,0:T(8,128)(2,1)}, u32[]{:S(2)}, u32[]{:S(2)}) async-start(bf16[16,8,7168]{2,1,0:T(8,128)(2,1)} %fusion), calls=%async_computation.5 | async-start | bytes 3670016 | tf_op jit(solution)/shard_map/all_to_all | solution.py:228
  234.1 1.8 convert_reduce_fusion.2
  235.9 25.5 %all-to-all-done.5 = bf16[16,8,7168]{2,1,0:T(8,128)(2,1)} async-done(((bf16[16,8,7168]{2,1,0:T(8,128)(2,1)}), bf16[16,8,7168]{2,1,0:T(8,128)(2,1)}, u32[]{:S(2)}, u32[]{:S(2)}) %all-to-all-start.5) | async-done | bytes 1835040 | tf_op jit(solution)/shard_map/all_to_all | solution.py:228
  261.4 1.8 convert_reduce_fusion
  263.2 0.7 add_convert_fusion
  (70 shorter events, 2.8 us)
Async XLA Ops:
  6.5 169.8 %copy-start = (bf16[1,2048,448]{1,2,0:T(8,128)(2,1)S(1)}, bf16[1,2048,448]{1,2,0:T(8,128)(2,1)}, u32[]{:S(2)}) copy-start(bf16[1,2048,448]{1,2,0:T(8,128)(2,1)} %param.29) | copy-start | bytes 5505028
  6.5 12.8 %copy-start.6 = (s32[2,64,8]{1,2,0:T(8,128)S(1)}, s32[2,64,8]{1,2,0:T(8,128)}, u32[]{:S(2)}) copy-start(s32[2,64,8]{1,2,0:T(8,128)} %param.26) | copy-start | bytes 12292
  6.5 60.3 %all-gather.6.cloned.1.call-start = ((), (), s32[]{:S(2)}) async-start(), calls=%async_computation.7 | async-start | bytes 7798784 | tf_op jit(solution)/shard_map/all_gather | solution.py:134
  9.8 11.9 %copy-start.8 = (bf16[2,4,576]{2,1,0:T(4,128)(2,1)S(1)}, bf16[2,4,576]{2,1,0:T(4,128)(2,1)}, u32[]{:S(2)}) copy-start(bf16[2,4,576]{2,1,0:T(4,128)(2,1)} %param.17) | copy-start | bytes 27652
  10.6 11.2 %copy-start.10 = (s32[2]{0:T(128)S(1)}, s32[2]{0:T(128)}, u32[]{:S(2)}) copy-start(s32[2]{0:T(128)} %param.19) | copy-start | bytes 28
  10.6 22.4 %all-to-all-start = ((bf16[16,2,8,576]{3,2,1,0:T(8,128)(2,1)}), bf16[16,2,8,576]{3,2,1,0:T(8,128)(2,1)S(1)}, u32[]{:S(2)}, u32[]{:S(2)}) async-start(bf16[16,2,8,576]{3,2,1,0:T(8,128)(2,1)} %broadcast_select_fusion), calls=%async_computation | async-start | bytes 655360 | tf_op jit(solution)/shard_map/all_to_all | solution.py:143
  22.1 3.2 %copy-start.3 = (bf16[2,1024,576]{1,2,0:T(8,128)(2,1)S(1)}, bf16[2,1024,576]{1,2,0:T(8,128)(2,1)}, u32[]{:S(2)}) copy-start(bf16[2,1024,576]{1,2,0:T(8,128)(2,1)} %param.18) | copy-start | bytes 7077892
  35.2 11.8 %copy-start.4 = (bf16[2,4,7168]{2,1,0:T(4,128)(2,1)S(1)}, bf16[2,4,7168]{2,1,0:T(4,128)(2,1)}, u32[]{:S(2)}) copy-start(bf16[2,4,7168]{2,1,0:T(4,128)(2,1)} %param.15) | copy-start | bytes 344068
  35.2 18.2 %all-to-all-start.1 = ((bf16[16,4,2,4,512]{4,1,2,3,0:T(4,128)(2,1)}), bf16[16,4,2,4,512]{4,1,2,3,0:T(4,128)(2,1)S(1)}, u32[]{:S(2)}, u32[]{:S(2)}) async-start(bf16[16,4,2,4,512]{4,1,2,3,0:T(4,128)(2,1)} %copy_bitcast_fusion), calls=%async_computation.1 | async-start | bytes 1048576 | tf_op jit(solution)/shard_map/all_to_all | solution.py:179
  42.5 111.7 %all-gather.4.cloned.1.call-start = ((), (), s32[]{:S(2)}) async-start(), calls=%async_computation.6 | async-start | bytes 1949696 | tf_op jit(solution)/shard_map/all_gather | solution.py:200
  47.0 6.5 %copy-start.5 = (bf16[128,128]{1,0:T(8,128)(2,1)}, bf16[128,128]{1,0:T(8,128)(2,1)S(1)}, u32[]{:S(2)}) copy-start(bf16[128,128]{1,0:T(8,128)(2,1)S(1)} %convert_element_type.80) | copy-start | bytes 98308
  78.4 3.4 %copy-start.1 = (bf16[8192,448]{1,0:T(8,128)(2,1)S(1)}, bf16[8192,448]{1,0:T(8,128)(2,1)}, u32[]{:S(2)}) copy-start(bf16[8192,448]{1,0:T(8,128)(2,1)} %copy.103) | copy-start | bytes 22020100
  85.3 30.7 %copy-start.2 = (bf16[128,7168]{1,0:T(8,128)(2,1)}, bf16[128,7168]{1,0:T(8,128)(2,1)S(1)}, u32[]{:S(2)}) copy-start(bf16[128,7168]{1,0:T(8,128)(2,1)S(1)} %get-tuple-element.7) | copy-start | bytes 5505028
  116.0 0.7 copy-start.7
  154.2 3.1 %copy-start.11 = (bf16[1,2,7168,128]{3,2,1,0:T(8,128)(2,1)S(1)}, bf16[1,2,7168,128]{3,2,1,0:T(8,128)(2,1)}, u32[]{:S(2)}) copy-start(bf16[1,2,7168,128]{3,2,1,0:T(8,128)(2,1)} %param.28) | copy-start | bytes 11010052
  191.2 7.4 %copy-start.9 = (f32[2,64,8]{1,2,0:T(8,128)S(1)}, f32[2,64,8]{1,2,0:T(8,128)}, u32[]{:S(2)}) copy-start(f32[2,64,8]{1,2,0:T(8,128)} %param.27) | copy-start | bytes 12292
  191.2 37.1 %all-to-all-start.2 = ((bf16[16,8,7168]{2,1,0:T(8,128)(2,1)}), bf16[16,8,7168]{2,1,0:T(8,128)(2,1)}, u32[]{:S(2)}, u32[]{:S(2)}) async-start(bf16[16,8,7168]{2,1,0:T(8,128)(2,1)} %bitcast.82), calls=%async_computation.2 | async-start | bytes 3670016 | tf_op jit(solution)/shard_map/all_to_all | solution.py:202
  228.3 33.1 %all-to-all-start.5 = ((bf16[16,8,7168]{2,1,0:T(8,128)(2,1)}), bf16[16,8,7168]{2,1,0:T(8,128)(2,1)}, u32[]{:S(2)}, u32[]{:S(2)}) async-start(bf16[16,8,7168]{2,1,0:T(8,128)(2,1)} %fusion), calls=%async_computation.5 | async-start | bytes 3670016 | tf_op jit(solution)/shard_map/all_to_all | solution.py:228
Sparse Core Ops, SparseCore 0:
  9.2 57.5 all-gather.5
  117.7 36.5 all-gather.3

commit v2 on v1

v2 whole, which is shorter than its diff:
```python
import jax
import jax.numpy as jnp
from jax import lax
from jax.experimental import pallas as pl
from jax.experimental.pallas import tpu as pltpu
from jax.sharding import Mesh
from jax.sharding import PartitionSpec as P

LAT = 512
ROPE = 64
VD = 128
CAP = 4
STEPS = 2


def attend(query_rows, key_rows, lengths, recent):
    rows, steps, heads, width = query_rows.shape
    scaling = (VD + ROPE) ** (-0.5)
    flat = query_rows.reshape(rows, steps * heads, width)
    cache_scores = (
        jnp.einsum("nqk,npk->nqp", flat, key_rows, preferred_element_type=jnp.float32) * scaling
    )
    places = lax.broadcasted_iota(jnp.int32, (1, 1, key_rows.shape[1]), 2)
    cache_scores = jnp.where(places < lengths[:, None, None], cache_scores, -jnp.inf)
    fresh_scores = (
        jnp.einsum("nqk,nsk->nqs", flat, recent, preferred_element_type=jnp.float32) * scaling
    )
    step_of = jnp.arange(steps * heads, dtype=jnp.int32)[:, None] // heads
    seen = jnp.arange(steps, dtype=jnp.int32)[None, :] <= step_of
    fresh_scores = jnp.where(seen[None], fresh_scores, -jnp.inf)
    highest = jnp.maximum(jnp.max(cache_scores, axis=2), jnp.max(fresh_scores, axis=2))[:, :, None]
    cache_weights = jnp.exp(cache_scores - highest)
    fresh_weights = jnp.exp(fresh_scores - highest)
    totals = jnp.sum(cache_weights, axis=2, keepdims=True) + jnp.sum(
        fresh_weights, axis=2, keepdims=True
    )
    cache_probs = (cache_weights / totals).astype(jnp.bfloat16)
    fresh_probs = (fresh_weights / totals).astype(jnp.bfloat16)
    context = jnp.einsum(
        "nqp,npl->nql", cache_probs, key_rows[:, :, :LAT], preferred_element_type=jnp.float32
    )
    context = context + jnp.einsum(
        "nqs,nsl->nql", fresh_probs, recent[:, :, :LAT], preferred_element_type=jnp.float32
    )
    return context.astype(jnp.bfloat16).reshape(rows, steps, heads, LAT)


def routing(ids, weights, experts):
    matched = ids[None] == jnp.arange(experts, dtype=jnp.int32)[:, None, None, None]
    present = jnp.any(matched, axis=3)
    row_weight = jnp.sum(jnp.where(matched, weights[None], 0.0), axis=3)
    rows = ids.shape[1]
    before = (
        jnp.arange(rows, dtype=jnp.int32)[:, None] < jnp.arange(rows, dtype=jnp.int32)[None, :]
    )
    slot_index = jnp.einsum(
        "etr,rs->ets",
        present.astype(jnp.bfloat16),
        before.astype(jnp.bfloat16),
        preferred_element_type=jnp.float32,
    ).astype(jnp.int32)
    slots = jnp.arange(CAP, dtype=jnp.int32)[None, None, :, None]
    chosen = (slot_index[:, :, None, :] == slots) & present[:, :, None, :]
    return chosen, row_weight


def project_body(x_ref, w_ref, own_ref, hidden_ref, rows_ref, slots_ref):
    half = x_ref.shape[0] // 2
    whole = lax.dot_general(
        x_ref[...], w_ref[...], (((1,), (1,)), ((), ())), preferred_element_type=jnp.float32
    )
    rows_ref[...] = whole[:half].reshape(rows_ref.shape)
    carried = jnp.dot(own_ref[...], hidden_ref[...], preferred_element_type=jnp.float32)
    slots_ref[...] = (whole[half:] + carried).astype(jnp.bfloat16)


def project(x, w, own, hidden):
    width, depth = w.shape
    half = x.shape[0] // 2
    tile = width // 8
    each = hidden.shape[0]
    return pl.pallas_call(
        project_body,
        grid=(width // tile,),
        in_specs=[
            pl.BlockSpec(x.shape, lambda i: (0, 0)),
            pl.BlockSpec((tile, depth), lambda i: (i, 0)),
            pl.BlockSpec(own.shape, lambda i: (0, 0)),
            pl.BlockSpec((hidden.shape[0], tile), lambda i: (0, i)),
        ],
        out_specs=[
            pl.BlockSpec((half // each, 1, each, tile), lambda i: (0, i, 0, 0)),
            pl.BlockSpec((half, tile), lambda i: (0, i)),
        ],
        out_shape=[
            jax.ShapeDtypeStruct((half // each, width // tile, each, tile), jnp.float32),
            jax.ShapeDtypeStruct((half, width), jnp.bfloat16),
        ],
        compiler_params=pltpu.CompilerParams(vmem_limit_bytes=40 * 1024 * 1024),
        cost_estimate=pl.CostEstimate(
            flops=2 * x.shape[0] * depth * width,
            bytes_accessed=2 * depth * width + 4 * x.shape[0] * width,
            transcendentals=0,
        ),
        name="project",
    )(x, w, own, hidden)


def gate_up_body(x_ref, own_ref, other_ref, active_ref, gate, up):
    step = pl.program_id(0)

    @pl.when(step == 0)
    def _():
        gate[...] = jnp.zeros_like(gate)
        up[...] = jnp.zeros_like(up)

    x = x_ref[...]
    for part, total in ((0, gate), (1, up)):
        both = jnp.concatenate([own_ref[part], other_ref[part]], axis=1)
        total[...] += jnp.dot(x, both, preferred_element_type=jnp.float32)

    @pl.when(step == pl.num_programs(0) - 1)
    def _():
        g = gate[...]
        active_ref[...] = (g * jax.nn.sigmoid(g) * up[...]).astype(jnp.bfloat16)


def gate_up(x, own, other):
    rows, depth = x.shape
    units = own.shape[2]
    tile = depth // 7
    return pl.pallas_call(
        gate_up_body,
        grid=(depth // tile,),
        in_specs=[
            pl.BlockSpec((rows, tile), lambda i: (0, i)),
            pl.BlockSpec((2, tile, units), lambda i: (0, i, 0)),
            pl.BlockSpec((2, tile, units), lambda i: (0, i, 0)),
        ],
        out_specs=pl.BlockSpec((rows, 2 * units), lambda i: (0, 0)),
        out_shape=jax.ShapeDtypeStruct((rows, 2 * units), jnp.bfloat16),
        scratch_shapes=[pltpu.VMEM((rows, 2 * units), jnp.float32)] * 2,
        compiler_params=pltpu.CompilerParams(vmem_limit_bytes=24 * 1024 * 1024),
        cost_estimate=pl.CostEstimate(
            flops=8 * rows * depth * units,
            bytes_accessed=8 * depth * units + 2 * rows * depth,
            transcendentals=2 * rows * units,
        ),
        name="gate_up",
    )(x, own, other)


def swap_cores(x):
    return lax.ppermute(x, "core", [(0, 1), (1, 0)])


def per_device(
    hidden_in,
    queries,
    fresh,
    res_cache,
    res_len,
    pre_cache,
    pre_len,
    arrival,
    w_uv,
    w_o,
    norm_gain,
    expert_ids,
    route_weight,
    w_gu,
    w_down,
):
    group, head = ("z", "core"), ("y", "x")
    chips, cores, long, short = (lax.axis_size(a) for a in ("z", "core", "y", "x"))
    groups, columns = chips * cores, long * short
    core, at_y, at_x = (lax.axis_index(a) for a in ("core", "y", "x"))
    group_index = lax.axis_index(group)
    head_index = lax.axis_index(head)
    steps, rows_dev, width = hidden_in.shape
    resident = res_cache.shape[0]
    newcomers = rows_dev - resident
    requests = arrival.shape[1]
    own_rows = steps * rows_dev
    rows_group = columns * own_rows
    heads_dev = w_uv.shape[0]
    slots_dev = steps * CAP

    w_all = lax.all_gather(w_o.T, group, axis=0, tiled=True)
    gu_other = swap_cores(w_gu[0])
    down = w_down[0].T
    down_other = swap_cores(down)

    places = jnp.arange(requests, dtype=jnp.int32)
    arrival_row = arrival[0]
    claimed = arrival_row[None, :] == places[:, None]
    order = jnp.sum(jnp.where(claimed, places[None, :], 0), axis=1)
    len_sorted = jnp.sum(jnp.where(claimed, pre_len[0][None, :], 0), axis=1)
    new_len = lax.dynamic_slice(len_sorted, (group_index * newcomers,), (newcomers,))
    sorted_cache = jnp.take(pre_cache[0], order, axis=0, mode="clip")
    taken = lax.all_to_all(
        sorted_cache.reshape(groups, newcomers, *sorted_cache.shape[1:]),
        group,
        split_axis=0,
        concat_axis=0,
        tiled=False,
    )
    taken = jnp.swapaxes(taken, 0, 1).reshape(newcomers, -1, sorted_cache.shape[2])

    chosen, row_weight = routing(expert_ids, route_weight, columns)
    by_row = chosen.reshape(columns, steps, CAP, columns, rows_dev)
    same = jnp.arange(steps)[:, None] == jnp.arange(steps)[None, :]
    chooser = by_row[:, :, :, :, None, :] & same[None, :, None, None, :, None]
    chooser = chooser.reshape(columns * slots_dev, rows_group).astype(jnp.bfloat16)
    own_chooser = lax.dynamic_slice(
        chooser, (0, head_index * own_rows), (columns * slots_dev, own_rows)
    )
    near = jnp.where(chosen, row_weight[:, :, None, :], 0.0).reshape(
        long, short, steps, CAP, long, short, rows_dev
    )
    near = lax.dynamic_index_in_dim(near, at_y, 0, keepdims=False)
    near = lax.dynamic_index_in_dim(near, at_x, 4, keepdims=False)
    spread = jnp.where(
        same[None, :, None, None, :, None], near[:, :, :, :, None, :], 0.0
    ).reshape(short * slots_dev, long * own_rows)

    by_row_queries = jnp.swapaxes(queries, 0, 1)
    recent = jnp.swapaxes(fresh, 0, 1)
    context = jnp.concatenate(
        [
            attend(by_row_queries[:resident], res_cache, res_len, recent[:resident]),
            attend(by_row_queries[resident:], taken, new_len, recent[resident:]),
        ],
        axis=0,
    )
    context = context.reshape(rows_dev, steps, columns, heads_dev, LAT).transpose(2, 3, 1, 0, 4)
    by_head = lax.all_to_all(context, head, split_axis=0, concat_axis=0, tiled=False)
    by_head = jnp.swapaxes(by_head, 0, 1).reshape(heads_dev, rows_group, LAT)
    values = jnp.einsum("hrl,hlv->rhv", by_head, w_uv, preferred_element_type=jnp.float32).astype(
        jnp.bfloat16
    )
    values = values.reshape(rows_group, heads_dev * VD)
    values_slots = jnp.dot(chooser, values, preferred_element_type=jnp.float32).astype(jnp.bfloat16)
    hidden_own = hidden_in.reshape(own_rows, width)
    part_rows, part_slots = project(
        jnp.concatenate([values, values_slots], axis=0), w_all, own_chooser, hidden_own
    )
    blocks, tile = part_rows.shape[1], part_rows.shape[3]
    attention = lax.psum_scatter(
        part_rows.reshape(-1, tile), head, scatter_dimension=0, tiled=True
    ).reshape(blocks, own_rows, tile)
    summed = hidden_own.astype(jnp.float32) + jnp.swapaxes(attention, 0, 1).reshape(own_rows, width)

    slot_parts = lax.all_to_all(
        part_slots.reshape(columns, slots_dev, width), head, 0, 0, tiled=False
    )
    slot_rows = jnp.sum(slot_parts.astype(jnp.float32), axis=0)
    normed = (
        slot_rows
        * lax.rsqrt(jnp.mean(slot_rows * slot_rows, axis=1, keepdims=True) + 1e-06)
        * norm_gain
    ).astype(jnp.bfloat16)
    portion = lax.all_gather(normed, "z", axis=0, tiled=True)
    active = gate_up(portion, w_gu[0], gu_other)
    units = active.shape[1] // 2
    active = jnp.where(
        core == 0,
        active,
        jnp.concatenate([active[:, units:], active[:, :units]], axis=1),
    )
    copies = jnp.broadcast_to(active[None], (chips, *active.shape))
    copies = lax.all_to_all(copies, "z", 0, 0, tiled=False)
    everywhere = jnp.swapaxes(copies, 0, 1).reshape(active.shape[0], -1)
    second = (((1,), (1,)), ((), ()))
    mine = lax.dot_general(everywhere, down, second, preferred_element_type=jnp.float32)
    others = lax.dot_general(everywhere, down_other, second, preferred_element_type=jnp.float32)
    mine, others = mine.astype(jnp.bfloat16), others.astype(jnp.bfloat16)
    outcome = jnp.where(
        core == 0,
        jnp.concatenate([mine, others], axis=1),
        jnp.concatenate([others, mine], axis=1),
    )
    slot_values = lax.all_to_all(
        outcome.reshape(chips, slots_dev, outcome.shape[1]), "z", 0, 0, tiled=False
    )
    slot_values = jnp.swapaxes(slot_values, 0, 1).reshape(slots_dev, width)
    beside = lax.all_gather(slot_values, "x", axis=0, tiled=True)
    mixed = lax.dot_general(
        spread,
        beside.astype(jnp.float32),
        (((0,), (0,)), ((), ())),
        precision=lax.Precision.HIGHEST,
        preferred_element_type=jnp.float32,
    ).astype(jnp.bfloat16)
    mix_parts = lax.all_to_all(mixed.reshape(long, own_rows, width), "y", 0, 0, tiled=False)
    out = summed + jnp.sum(mix_parts.astype(jnp.float32), axis=0)
    return out.astype(jnp.bfloat16).reshape(steps, rows_dev, width)


def solution(mesh):
    wide = Mesh(mesh.devices.reshape(8, 2, 4, 4), ("z", "core", "y", "x"))
    group, head = ("z", "core"), ("y", "x")
    both = group + head
    placed = (
        P(None, both, None),
        P(None, both, None, None),
        P(None, both, None),
        P(both, None, None),
        P(both),
        P(head, None, group, None),
        P(head, None),
        P(head, None),
        P(head, None, None),
        P(head, group),
        P(),
        P(None, group, None),
        P(None, group, None),
        P(head, None, None, group),
        P(head, None, group),
    )
    return jax.shard_map(
        per_device,
        mesh=wide,
        in_specs=placed,
        out_specs=P(None, both, None),
        check_vma=False,
    )
```

time: 273 us -> 215 us (0.79)
  waiting for transfers between devices: 111 us -> 71.3 us
  blocking collectives: 61.7 us -> 49.4 us
  matrix products: 16.2 us -> 8.19 us
  Pallas kernels: 3.58 us -> 11.3 us
  local copies, waits for them, and re-layouts: 22.7 us -> 18.7 us
  other arithmetic: 12.3 us -> 8.34 us
  starting transfers between devices: 29.1 us -> 32.2 us
    all_gather x2 -> x1, waiting for transfers between devices: 47.9 us -> 12.5 us  [per_device(): w_all = lax.all_gather(w_o.T, group, axis=0, tiled=True)]
    all_to_all x2 -> x1, blocking collectives: 44.8 us -> 9.97 us  [per_device(): lax.all_to_all(mixed.reshape(long, own_rows, width), 'y', 0, 0, tiled=False)]
    all_gather x1 -> x2, blocking collectives: 16.8 us -> 39.4 us  [the longest x1 26.8 us: per_device(): portion = lax.all_gather(normed, 'z', axis=0, tiled=True)]
    all_gather x1 -> x0, local copies, waits for them, and re-layouts: 11.6 us -> none  [per_device(): w_all = lax.all_gather(w_o, 'group', axis=0, tiled=False)]
    pallas_call x1 -> x2, Pallas kernels: 3.58 us -> 11.3 us  [the longest x1 5.68 us: gate_up(): pl.pallas_call(gate_up_body, grid=(depth // tile,), in_specs=[pl.BlockSpe...]
    dot_general x4 -> x3, matrix products: 9.18 us -> 3.36 us  [the longest x1 2.14 us: per_device(): lax.dot_general(everywhere, down_other, second, preferred_element_type=jn...]
    all_to_all x1, waiting for transfers between devices: 5.22 us -> 1.8 us  [per_device(): lax.all_to_all(sorted_cache.reshape(groups, newcomers, *sorted_cache.shap...]
    all_to_all x3 -> x4, starting transfers between devices: 20.4 us -> 22.9 us  [the longest x1 7.2 us: per_device(): lax.all_to_all(part_slots.reshape(columns, slots_dev, width), head, 0, 0,...]
  transfers between devices with their start and end apart: 6 -> 9, of which waited for: 6 -> 6; matrix products, arithmetic and copies ran while one was open for 10% -> 13% of each run, Pallas kernels for 0% -> 3%
where the time goes in v2:
time: 215 us; the launch traced here: 213 us
  waiting for transfers between devices  71.3 us (33%)
  blocking collectives  49.4 us (23%)
  starting transfers between devices  32.2 us (15%)
  local copies, waits for them, and re-layouts  18.7 us (9%)
  between operations  13.9 us (6%)
  Pallas kernels  11.3 us (5%)
  other arithmetic  8.34 us (4%)
  matrix products  8.19 us (4%)
    all_to_all x1, waiting for transfers between devices, per_device(): lax.all_to_all(part_slots.reshape(columns, slots_dev, width), head, 0, 0,...  30.9 us
    all_gather x1, blocking collectives, per_device(): portion = lax.all_gather(normed, 'z', axis=0, tiled=True)  26.8 us
    all_gather x1, blocking collectives, per_device(): beside = lax.all_gather(slot_values, 'x', axis=0, tiled=True)  12.6 us
    all_gather x1, waiting for transfers between devices, per_device(): w_all = lax.all_gather(w_o.T, group, axis=0, tiled=True)  12.5 us
    all_to_all x1, blocking collectives, per_device(): lax.all_to_all(mixed.reshape(long, own_rows, width), 'y', 0, 0, tiled=False)  9.97 us
    all_to_all x1, waiting for transfers between devices, per_device(): copies = lax.all_to_all(copies, 'z', 0, 0, tiled=False)  9.55 us
    all_to_all x1, starting transfers between devices, per_device(): lax.all_to_all(sorted_cache.reshape(groups, newcomers, *sorted_cache.shap...  8.7 us
    all_to_all x1, waiting for transfers between devices, per_device(): lax.all_to_all(outcome.reshape(chips, slots_dev, outcome.shape[1]), 'z',...  8.51 us
  transfers between devices with their start and end apart: 9, of which 6 were waited for; matrix products, arithmetic and copies ran while one was open for 13% of the time, Pallas kernels for 3%

profile of v2, /device:TPU:24, one launch (start us, length us, event | category | flops | bytes accessed | tf_op | source)
XLA Modules:
  0.0 213.5 jit_solution(7372080894171413008)
XLA Ops:
  6.5 0.7 all-gather.2.cloned.1.call-update
  7.3 0.8 select_reduce_fusion.2
  8.1 2.3 %gather_fusion = bf16[32,8,576]{2,1,0:T(8,128)(2,1)} fusion(bf16[32,8,576]{2,1,0:T(8,128)(2,1)} %bitcast.101, s32[1024]{0:T(1024)S(1)} %pad_clamp_fusion), kind=kCustom, calls=%fused_computation | custom fusion | bytes 589952 | tf_op jit(solution)/shard_map/jit(_take)/gather | solution.py:200
  10.4 8.7 %all-to-all-start = ((bf16[16,2,8,576]{3,2,1,0:T(8,128)(2,1)}), bf16[16,2,8,576]{3,2,1,0:T(8,128)(2,1)S(1)}, u32[]{:S(2)}, u32[]{:S(2)}) async-start(bf16[16,2,8,576]{3,2,1,0:T(8,128)(2,1)} %bitcast.91), calls=%async_computation | async-start | bytes 655360 | tf_op jit(solution)/shard_map/all_to_all | solution.py:201
  19.1 0.7 copy.161
  19.8 0.8 fusion.25
  20.8 0.7 copy.127
  21.6 0.4 copy.130
  22.0 1.9 copy.128
  23.8 1.1 fusion.42
  25.0 0.7 copy.116
  26.1 0.7 fusion.46
  26.8 0.3 fusion.20
  27.2 0.9 fusion.1
  28.0 0.3 fusion.6
  28.6 1.2 fusion.45
  29.8 1.1 fusion.19
  30.9 1.8 all-to-all-done
  33.8 1.1 copy_bitcast_fusion
  34.8 7.1 %all-to-all-start.1 = ((bf16[16,4,2,4,512]{4,1,2,3,0:T(4,128)(2,1)}), bf16[16,4,2,4,512]{4,1,2,3,0:T(4,128)(2,1)S(1)}, u32[]{:S(2)}, u32[]{:S(2)}) async-start(bf16[16,4,2,4,512]{4,1,2,3,0:T(4,128)(2,1)} %copy_bitcast_fusion), calls=%async_computation.1 | async-start | bytes 1048576 | tf_op jit(solution)/shard_map/all_to_all | solution.py:237
  42.0 1.6 broadcast_and_fusion
  43.6 1.9 and.74
  45.6 7.3 %all-to-all-done.1 = bf16[16,4,2,4,512]{4,1,2,3,0:T(4,128)(2,1)S(1)} async-done(((bf16[16,4,2,4,512]{4,1,2,3,0:T(4,128)(2,1)}), bf16[16,4,2,4,512]{4,1,2,3,0:T(4,128)(2,1)S(1)}, u32[]{:S(2)}, u32[]{:S(2)}) %all-to-all-start.1) | async-done | bytes 524320 | tf_op jit(solution)/shard_map/all_to_all | solution.py:237
  53.4 0.3 convolution_convert_fusion.1
  54.1 12.5 %all-gather.2.cloned.1.call-done.w_ref = bf16[7168,512]{1,0:T(8,128)(2,1)} async-done(((bf16[448,512]{1,0:T(8,128)(2,1)}), bf16[7168,512]{1,0:T(8,128)(2,1)}) %all-gather.2.cloned.1.call-update) | async-done | bytes 7340048 | tf_op jit(solution)/shard_map/all_gather | solution.py:189
  66.5 3.1 %copy-done.1 = bf16[7168,512]{1,0:T(8,128)(2,1)S(1)} copy-done((bf16[7168,512]{1,0:T(8,128)(2,1)S(1)}, bf16[7168,512]{1,0:T(8,128)(2,1)}, u32[]{:S(2)}) %copy-start.1) | copy-done | bytes 7340056
  69.6 5.7 %project.1 = (f32[16,8,8,896]{3,2,1,0:T(8,128)S(1)}, bf16[128,7168]{1,0:T(8,128)(2,1)}) custom-call(bf16[256,512]{1,0:T(8,128)(2,1)S(1)} %pad_maximum_fusion.1.x_ref, bf16[7168,512]{1,0:T(8,128)(2,1)S(1)} %copy-done.1, bf16[128,8]{1,0:T(8,128)(2,1)S(1)} %dynamic-slice_convert_fusion.own_ref, bf16[8,7168]{1,0:T(8,128)(2,1)S(1)} %reshape.251.hidden_ref), custom_call_target="tpu_custom_call" | custom-call | flops 1879048192 | bytes 14680064 | tf_op jit(solution)/shard_map/project/pallas_call | solution.py:82
  75.3 1.8 copy-done.2
  77.1 7.2 %all-to-all-start.2 = ((bf16[16,8,7168]{2,1,0:T(8,128)(2,1)}), bf16[16,8,7168]{2,1,0:T(8,128)(2,1)S(1)}, u32[]{:S(2)}, u32[]{:S(2)}) async-start(bf16[16,8,7168]{2,1,0:T(8,128)(2,1)} %bitcast.24), calls=%async_computation.3 | async-start | bytes 3670016 | tf_op jit(solution)/shard_map/all_to_all | solution.py:254
  84.4 0.5 collective-permute-start.1
  85.3 30.9 %all-to-all-done.2 = bf16[16,8,7168]{2,1,0:T(8,128)(2,1)S(1)} async-done(((bf16[16,8,7168]{2,1,0:T(8,128)(2,1)}), bf16[16,8,7168]{2,1,0:T(8,128)(2,1)S(1)}, u32[]{:S(2)}, u32[]{:S(2)}) %all-to-all-start.2) | async-done | bytes 1835040 | tf_op jit(solution)/shard_map/all_to_all | solution.py:254
  116.7 26.8 %all_gather.10.x_ref = bf16[64,7168]{1,0:T(8,128)(2,1)S(1)} all-gather(bf16[8,7168]{1,0:T(8,128)(2,1)S(1)} %multiply_convert_fusion), channel_id=1, replica_groups=mesh['z'=8,'core'=2,'y'=4,'x'=4] {'z'}, dimensions={0}, use_global_device_ids=true | all-gather | bytes 1032192 | tf_op jit(solution)/shard_map/all_gather | solution.py:263
  143.5 5.7 %gate_up.1 = bf16[64,256]{1,0:T(8,128)(2,1)S(1)} custom-call(bf16[64,7168]{1,0:T(8,128)(2,1)S(1)} %all_gather.10.x_ref, bf16[2,7168,128]{2,1,0:T(8,128)(2,1)S(1)} %bitcast.84, bf16[2,7168,128]{2,1,0:T(8,128)(2,1)} %collective-permute-done.other_ref), custom_call_target="tpu_custom_call" | custom-call | flops 469762048 | bytes 8257536 | tf_op jit(solution)/shard_map/gate_up/pallas_call | solution.py:132
  149.3 0.7 broadcast_in_dim.172
  150.0 5.2 %all-to-all-start.3 = ((bf16[8,64,256]{2,1,0:T(8,128)(2,1)}), bf16[8,64,256]{2,1,0:T(8,128)(2,1)S(1)}, u32[]{:S(2)}, u32[]{:S(2)}) async-start(bf16[8,64,256]{2,1,0:T(8,128)(2,1)} %broadcast_in_dim.172), calls=%async_computation.4 | async-start | bytes 524288 | tf_op jit(solution)/shard_map/all_to_all | solution.py:272
  155.2 0.3 eq.97
  155.6 0.3 reshape.270
  156.1 9.5 %all-to-all-done.3 = bf16[8,64,256]{2,1,0:T(8,128)(2,1)S(1)} async-done(((bf16[8,64,256]{2,1,0:T(8,128)(2,1)}), bf16[8,64,256]{2,1,0:T(8,128)(2,1)S(1)}, u32[]{:S(2)}, u32[]{:S(2)}) %all-to-all-start.3) | async-done | bytes 262176 | tf_op jit(solution)/shard_map/all_to_all | solution.py:272
  165.7 0.6 fusion.14
  166.4 2.1 %fusion.13 = bf16[8,8,448]{2,1,0:T(8,128)(2,1)S(1)} fusion(bf16[64,2048]{1,0:T(8,128)(2,1)S(1)} %bitcast.88, bf16[448,2048]{1,0:T(8,128)(2,1)} %collective-permute-done.1), kind=kOutput, calls=%fused_computation.22 | convolution fusion | flops 117469184 | bytes 2154496 | tf_op jit(solution)/shard_map/dot_general | solution.py:276
  168.5 0.8 maximum_select_fusion
  169.3 3.4 %all-to-all-start.4 = ((bf16[8,8,896]{2,1,0:T(8,128)(2,1)}), bf16[8,8,896]{2,1,0:T(8,128)(2,1)S(1)}, u32[]{:S(2)}, u32[]{:S(2)}) async-start(bf16[8,8,896]{2,1,0:T(8,128)(2,1)} %maximum_select_fusion), calls=%async_computation.5 | async-start | bytes 229376 | tf_op jit(solution)/shard_map/all_to_all | solution.py:283
  173.0 8.5 %all-to-all-done.4 = bf16[8,8,896]{2,1,0:T(8,128)(2,1)S(1)} async-done(((bf16[8,8,896]{2,1,0:T(8,128)(2,1)}), bf16[8,8,896]{2,1,0:T(8,128)(2,1)S(1)}, u32[]{:S(2)}, u32[]{:S(2)}) %all-to-all-start.4) | async-done | bytes 114720 | tf_op jit(solution)/shard_map/all_to_all | solution.py:283
  181.5 12.6 %all_gather.11 = bf16[32,7168]{1,0:T(8,128)(2,1)S(1)} all-gather(bf16[8,7168]{1,0:T(8,128)(2,1)S(1)} %bitcast.100), channel_id=1, replica_groups=mesh['z'=8,'core'=2,'y'=4,'x'=4] {'x'}, dimensions={0}, use_global_device_ids=true | all-gather | bytes 573440 | tf_op jit(solution)/shard_map/all_gather | solution.py:287
  194.1 0.6 fusion
  194.7 10.0 %all_to_all.30 = bf16[4,8,7168]{2,1,0:T(8,128)(2,1)S(1)} all-to-all(bf16[4,8,7168]{2,1,0:T(8,128)(2,1)S(1)} %fusion), channel_id=1, replica_groups=mesh['z'=8,'core'=2,'y'=4,'x'=4] {'y'}, dimensions={0} | all-to-all | bytes 917504 | tf_op jit(solution)/shard_map/all_to_all | solution.py:295
  204.8 1.0 copy.160
  205.9 0.7 add_convert_fusion
  (81 shorter events, 4.6 us)
Async XLA Ops:
  6.5 46.8 %copy-start = (bf16[4,512,128]{2,1,0:T(8,128)(2,1)S(1)}, bf16[4,512,128]{2,1,0:T(8,128)(2,1)}, u32[]{:S(2)}) copy-start(bf16[4,512,128]{2,1,0:T(8,128)(2,1)} %param.23) | copy-start | bytes 1572868
  6.5 15.4 %copy-start.7 = (bf16[2,4,7168]{2,1,0:T(4,128)(2,1)S(1)}, bf16[2,4,7168]{2,1,0:T(4,128)(2,1)}, u32[]{:S(2)}) copy-start(bf16[2,4,7168]{2,1,0:T(4,128)(2,1)} %param.15) | copy-start | bytes 344068
  6.5 60.0 %all-gather.2.cloned.1.call-start = ((), (), s32[]{:S(2)}) async-start(), calls=%async_computation.7 | async-start | bytes 7798784 | tf_op jit(solution)/shard_map/all_gather | solution.py:189
  10.3 15.4 %copy-start.11 = (s32[2]{0:T(128)S(1)}, s32[2]{0:T(128)}, u32[]{:S(2)}) copy-start(s32[2]{0:T(128)} %param.19) | copy-start | bytes 28
  10.3 15.7 %copy-start.4 = (bf16[2,1024,576]{1,2,0:T(8,128)(2,1)S(1)}, bf16[2,1024,576]{1,2,0:T(8,128)(2,1)}, u32[]{:S(2)}) copy-start(bf16[2,1024,576]{1,2,0:T(8,128)(2,1)} %param.18) | copy-start | bytes 7077892
  10.4 22.3 %all-to-all-start = ((bf16[16,2,8,576]{3,2,1,0:T(8,128)(2,1)}), bf16[16,2,8,576]{3,2,1,0:T(8,128)(2,1)S(1)}, u32[]{:S(2)}, u32[]{:S(2)}) async-start(bf16[16,2,8,576]{3,2,1,0:T(8,128)(2,1)} %bitcast.91), calls=%async_computation | async-start | bytes 655360 | tf_op jit(solution)/shard_map/all_to_all | solution.py:201
  28.0 4.7 %copy-start.6 = (bf16[2,2,64,576]{3,2,1,0:T(8,128)(2,1)S(1)}, bf16[2,2,64,576]{3,2,1,0:T(8,128)(2,1)}, u32[]{:S(2)}) copy-start(bf16[2,2,64,576]{3,2,1,0:T(8,128)(2,1)} %copy.116) | copy-start | bytes 884740
  34.8 18.1 %all-to-all-start.1 = ((bf16[16,4,2,4,512]{4,1,2,3,0:T(4,128)(2,1)}), bf16[16,4,2,4,512]{4,1,2,3,0:T(4,128)(2,1)S(1)}, u32[]{:S(2)}, u32[]{:S(2)}) async-start(bf16[16,4,2,4,512]{4,1,2,3,0:T(4,128)(2,1)} %copy_bitcast_fusion), calls=%async_computation.1 | async-start | bytes 1048576 | tf_op jit(solution)/shard_map/all_to_all | solution.py:237
  42.0 162.8 %reduce-scatter.2.cloned.1.call-start = ((), (), s32[]{:S(2)}) async-start(), calls=%async_computation.8 | async-start | bytes 3899392 | tf_op jit(solution)/shard_map/reduce_scatter | solution.py:249
  66.5 3.1 %copy-start.1 = (bf16[7168,512]{1,0:T(8,128)(2,1)S(1)}, bf16[7168,512]{1,0:T(8,128)(2,1)}, u32[]{:S(2)}) copy-start(bf16[7168,512]{1,0:T(8,128)(2,1)} %all-gather.2.cloned.1.call-done.w_ref) | copy-start | bytes 22020100
  75.3 1.8 copy-start.2
  77.1 8.1 %copy-start.8 = (s32[2,64,8]{1,2,0:T(8,128)S(1)}, s32[2,64,8]{1,2,0:T(8,128)}, u32[]{:S(2)}) copy-start(s32[2,64,8]{1,2,0:T(8,128)} %param.26) | copy-start | bytes 12292
  77.1 8.1 %copy-start.10 = (f32[2,64,8]{1,2,0:T(8,128)S(1)}, f32[2,64,8]{1,2,0:T(8,128)}, u32[]{:S(2)}) copy-start(f32[2,64,8]{1,2,0:T(8,128)} %param.27) | copy-start | bytes 12292
  77.1 39.1 %all-to-all-start.2 = ((bf16[16,8,7168]{2,1,0:T(8,128)(2,1)}), bf16[16,8,7168]{2,1,0:T(8,128)(2,1)S(1)}, u32[]{:S(2)}, u32[]{:S(2)}) async-start(bf16[16,8,7168]{2,1,0:T(8,128)(2,1)} %bitcast.24), calls=%async_computation.3 | async-start | bytes 3670016 | tf_op jit(solution)/shard_map/all_to_all | solution.py:254
  84.3 32.3 %copy-start.9 = (f32[7168]{0:T(1024)S(1)}, f32[7168]{0:T(1024)}, u32[]{:S(2)}) copy-start(f32[7168]{0:T(1024)} %param.25) | copy-start | bytes 86020
  84.3 59.2 %collective-permute-start = (bf16[2,7168,128]{2,1,0:T(8,128)(2,1)}, bf16[2,7168,128]{2,1,0:T(8,128)(2,1)}, u32[]{:S(2)}, u32[]{:S(2)}) collective-permute-start(bf16[2,7168,128]{2,1,0:T(8,128)(2,1)} %bitcast.83), channel_id=1, source_target_pairs={{0,16},{16,0},{1,17},{17,1},{2,18},{18,2},{3,19},{19,3},{4,20},{20... | collective-permute-start | bytes 11010056 | tf_op jit(solution)/shard_map/ppermute | solution.py:154
  84.4 81.9 %collective-permute-start.1 = (bf16[448,2048]{1,0:T(8,128)(2,1)}, bf16[448,2048]{1,0:T(8,128)(2,1)}, u32[]{:S(2)}, u32[]{:S(2)}) collective-permute-start(bf16[448,2048]{1,0:T(8,128)(2,1)} %bitcast.90), channel_id=1, source_target_pairs={{0,16},{16,0},{1,17},{17,1},{2,18},{18,2},{3,19},{19,3},{4,20},{20... | collective-permute-start | bytes 5505032 | tf_op jit(solution)/shard_map/ppermute | solution.py:154
  116.2 27.4 %copy-start.3 = (bf16[1,2,7168,128]{3,2,1,0:T(8,128)(2,1)S(1)}, bf16[1,2,7168,128]{3,2,1,0:T(8,128)(2,1)}, u32[]{:S(2)}) copy-start(bf16[1,2,7168,128]{3,2,1,0:T(8,128)(2,1)} %param.28) | copy-start | bytes 11010052
  149.2 16.5 %copy-start.5 = (bf16[1,2048,448]{1,2,0:T(8,128)(2,1)S(1)}, bf16[1,2048,448]{1,2,0:T(8,128)(2,1)}, u32[]{:S(2)}) copy-start(bf16[1,2048,448]{1,2,0:T(8,128)(2,1)} %param.29) | copy-start | bytes 5505028
  150.0 15.7 %all-to-all-start.3 = ((bf16[8,64,256]{2,1,0:T(8,128)(2,1)}), bf16[8,64,256]{2,1,0:T(8,128)(2,1)S(1)}, u32[]{:S(2)}, u32[]{:S(2)}) async-start(bf16[8,64,256]{2,1,0:T(8,128)(2,1)} %broadcast_in_dim.172), calls=%async_computation.4 | async-start | bytes 524288 | tf_op jit(solution)/shard_map/all_to_all | solution.py:272
  169.3 12.2 %all-to-all-start.4 = ((bf16[8,8,896]{2,1,0:T(8,128)(2,1)}), bf16[8,8,896]{2,1,0:T(8,128)(2,1)S(1)}, u32[]{:S(2)}, u32[]{:S(2)}) async-start(bf16[8,8,896]{2,1,0:T(8,128)(2,1)} %maximum_select_fusion), calls=%async_computation.5 | async-start | bytes 229376 | tf_op jit(solution)/shard_map/all_to_all | solution.py:283
Sparse Core Ops, SparseCore 0:
  9.2 57.2 all-gather.1
  77.2 91.9 reduce-scatter.1

commit v3 on v2

--- a/solution.py
+++ b/solution.py
@@ -1,3 +1,5 @@
+import functools
+
 import jax
 import jax.numpy as jnp
 from jax import lax
@@ -64,23 +66,21 @@
     return chosen, row_weight
 
 
-def project_body(x_ref, w_ref, own_ref, hidden_ref, rows_ref, slots_ref):
-    half = x_ref.shape[0] // 2
-    whole = lax.dot_general(
-        x_ref[...], w_ref[...], (((1,), (1,)), ((), ())), preferred_element_type=jnp.float32
-    )
-    rows_ref[...] = whole[:half].reshape(rows_ref.shape)
+NT = (((1,), (1,)), ((), ()))
+
+
+def project_slots_body(x_ref, w_ref, own_ref, hidden_ref, out_ref):
+    whole = lax.dot_general(x_ref[...], w_ref[...], NT, preferred_element_type=jnp.float32)
     carried = jnp.dot(own_ref[...], hidden_ref[...], preferred_element_type=jnp.float32)
-    slots_ref[...] = (whole[half:] + carried).astype(jnp.bfloat16)
-
-
-def project(x, w, own, hidden):
+    out_ref[...] = (whole + carried).astype(jnp.bfloat16)
+
+
+def project_slots(x, w, own, hidden):
     width, depth = w.shape
-    half = x.shape[0] // 2
-    tile = width // 8
-    each = hidden.shape[0]
-    return pl.pallas_call(
-        project_body,
+    rows = x.shape[0]
+    tile = width // 4
+    return pl.pallas_call(
+        project_slots_body,
         grid=(width // tile,),
         in_specs=[
             pl.BlockSpec(x.shape, lambda i: (0, 0)),
@@ -88,25 +88,65 @@
             pl.BlockSpec(own.shape, lambda i: (0, 0)),
             pl.BlockSpec((hidden.shape[0], tile), lambda i: (0, i)),
         ],
-        out_specs=[
-            pl.BlockSpec((half // each, 1, each, tile), lambda i: (0, i, 0, 0)),
-            pl.BlockSpec((half, tile), lambda i: (0, i)),
-        ],
-        out_shape=[
-            jax.ShapeDtypeStruct((half // each, width // tile, each, tile), jnp.float32),
-            jax.ShapeDtypeStruct((half, width), jnp.bfloat16),
-        ],
-        compiler_params=pltpu.CompilerParams(vmem_limit_bytes=40 * 1024 * 1024),
+        out_specs=pl.BlockSpec((rows, tile), lambda i: (0, i)),
+        out_shape=jax.ShapeDtypeStruct((rows, width), jnp.bfloat16),
+        compiler_params=pltpu.CompilerParams(vmem_limit_bytes=56 * 1024 * 1024),
         cost_estimate=pl.CostEstimate(
-            flops=2 * x.shape[0] * depth * width,
-            bytes_accessed=2 * depth * width + 4 * x.shape[0] * width,
+            flops=2 * rows * depth * width,
+            bytes_accessed=2 * depth * width + 2 * rows * width,
             transcendentals=0,
         ),
-        name="project",
+        name="project_slots",
     )(x, w, own, hidden)
 
 
-def gate_up_body(x_ref, own_ref, other_ref, active_ref, gate, up):
+def project_rows_body(outer, x_ref, w_ref, out_ref):
+    whole = lax.dot_general(x_ref[...], w_ref[...], NT, preferred_element_type=jnp.float32)
+    blocks, _, each, _ = out_ref.shape
+    inner = blocks // outer
+    for k in range(blocks):
+        out_ref[k % inner * outer + k // inner, 0] = whole[k * each : (k + 1) * each]
+
+
+def project_rows(x, w, each, outer):
+    width, depth = w.shape
+    rows = x.shape[0]
+    tile = width // 8
+    return pl.pallas_call(
+        functools.partial(project_rows_body, outer),
+        grid=(width // tile,),
+        in_specs=[
+            pl.BlockSpec(x.shape, lambda i: (0, 0)),
+            pl.BlockSpec((tile, depth), lambda i: (i, 0)),
+        ],
+        out_specs=pl.BlockSpec((rows // each, 1, each, tile), lambda i: (0, i, 0, 0)),
+        out_shape=jax.ShapeDtypeStruct((rows // each, width // tile, each, tile), jnp.float32),
+        compiler_params=pltpu.CompilerParams(vmem_limit_bytes=56 * 1024 * 1024),
+        cost_estimate=pl.CostEstimate(
+            flops=2 * rows * depth * width,
+            bytes_accessed=2 * depth * width + 4 * rows * width,
+            transcendentals=0,
+        ),
+        name="project_rows",
+    )(x, w)
+
+
+def after_body(x_ref, other_ref, out_ref):
+    del x_ref, other_ref, out_ref
+
+
+def after(x, other):
+    return pl.pallas_call(
+        after_body,
+        in_specs=[pl.BlockSpec(memory_space=pl.ANY)] * 2,
+        out_specs=pl.BlockSpec(memory_space=pl.ANY),
+        out_shape=jax.ShapeDtypeStruct(x.shape, x.dtype),
+        input_output_aliases={0: 0},
+        name="after",
+    )(x, other)
+
+
+def gate_up_body(core_ref, x_ref, own_ref, other_ref, active_ref, gate, up):
     step = pl.program_id(0)
 
     @pl.when(step == 0)
@@ -122,23 +162,38 @@
     @pl.when(step == pl.num_programs(0) - 1)
     def _():
         g = gate[...]
-        active_ref[...] = (g * jax.nn.sigmoid(g) * up[...]).astype(jnp.bfloat16)
-
-
-def gate_up(x, own, other):
+        active = (g * jax.nn.sigmoid(g) * up[...]).astype(jnp.bfloat16)
+        units = active.shape[1] // 2
+        first, second = active[:, :units], active[:, units:]
+
+        @pl.when(core_ref[0] == 0)
+        def _():
+            for k in range(active_ref.shape[0]):
+                active_ref[k, :, :units] = first
+                active_ref[k, :, units:] = second
+
+        @pl.when(core_ref[0] != 0)
+        def _():
+            for k in range(active_ref.shape[0]):
+                active_ref[k, :, :units] = second
+                active_ref[k, :, units:] = first
+
+
+def gate_up(core, x, own, other, copies):
     rows, depth = x.shape
     units = own.shape[2]
-    tile = depth // 7
+    tile = depth // 4
     return pl.pallas_call(
         gate_up_body,
         grid=(depth // tile,),
         in_specs=[
+            pl.BlockSpec(memory_space=pltpu.SMEM),
             pl.BlockSpec((rows, tile), lambda i: (0, i)),
             pl.BlockSpec((2, tile, units), lambda i: (0, i, 0)),
             pl.BlockSpec((2, tile, units), lambda i: (0, i, 0)),
         ],
-        out_specs=pl.BlockSpec((rows, 2 * units), lambda i: (0, 0)),
-        out_shape=jax.ShapeDtypeStruct((rows, 2 * units), jnp.bfloat16),
+        out_specs=pl.BlockSpec((copies, rows, 2 * units), lambda i: (0, 0, 0)),
+        out_shape=jax.ShapeDtypeStruct((copies, rows, 2 * units), jnp.bfloat16),
         scratch_shapes=[pltpu.VMEM((rows, 2 * units), jnp.float32)] * 2,
         compiler_params=pltpu.CompilerParams(vmem_limit_bytes=24 * 1024 * 1024),
         cost_estimate=pl.CostEstimate(
@@ -147,7 +202,86 @@
             transcendentals=2 * rows * units,
         ),
         name="gate_up",
-    )(x, own, other)
+    )(core, x, own, other)
+
+
+def down_body(core_ref, x_ref, own_ref, other_ref, out_ref):
+    x = jnp.concatenate([x_ref[k] for k in range(x_ref.shape[0])], axis=1)
+    half = own_ref.shape[0]
+    parts, each = out_ref.shape[0], out_ref.shape[1]
+    mine = lax.dot_general(x, own_ref[...], NT, preferred_element_type=jnp.float32)
+    others = lax.dot_general(x, other_ref[...], NT, preferred_element_type=jnp.float32)
+
+    def write(first, second):
+        both = jnp.concatenate([first, second], axis=1).reshape(parts, each, 2 * half)
+        out_ref[...] = both.astype(jnp.bfloat16)
+
+    @pl.when(core_ref[0] == 0)
+    def _():
+        write(mine, others)
+
+    @pl.when(core_ref[0] != 0)
+    def _():
+        write(others, mine)
+
+
+def down_project(core, x, own, other):
+    parts, rows, _ = x.shape
+    columns = 2 * own.shape[0]
+    vmem = pl.BlockSpec(memory_space=pltpu.VMEM)
+    return pl.pallas_call(
+        down_body,
+        in_specs=[pl.BlockSpec(memory_space=pltpu.SMEM), vmem, vmem, vmem],
+        out_specs=vmem,
+        out_shape=jax.ShapeDtypeStruct((parts, rows // parts, columns), jnp.bfloat16),
+        compiler_params=pltpu.CompilerParams(vmem_limit_bytes=24 * 1024 * 1024),
+        cost_estimate=pl.CostEstimate(
+            flops=2 * rows * own.shape[1] * columns,
+            bytes_accessed=2 * own.shape[1] * columns,
+            transcendentals=0,
+        ),
+        name="down_project",
+    )(core, x, own, other)
+
+
+def combine_body(spread_ref, *refs):
+    blocks, out_ref = refs[:-1], refs[-1]
+    weight = spread_ref[...]
+    high = weight.astype(jnp.bfloat16)
+    low = (weight - high.astype(jnp.float32)).astype(jnp.bfloat16)
+    parts, _, width = blocks[0].shape
+    for k in range(parts):
+        slots = jnp.concatenate([b[k].astype(jnp.float32) for b in blocks], axis=0)
+        slots = slots.astype(jnp.bfloat16)
+        mixed = jnp.dot(high, slots, preferred_element_type=jnp.float32) + jnp.dot(
+            low, slots, preferred_element_type=jnp.float32
+        )
+        mixed = mixed.astype(jnp.bfloat16).reshape(*out_ref.shape[:2], width)
+        out_ref[:, :, k * width : (k + 1) * width] = mixed
+
+
+def combine(spread, blocks, each):
+    rows = spread.shape[0]
+    width = blocks[0].shape[0] * blocks[0].shape[2]
+    vmem = pl.BlockSpec(memory_space=pltpu.VMEM)
+    return pl.pallas_call(
+        combine_body,
+        in_specs=[vmem] * (1 + len(blocks)),
+        out_specs=vmem,
+        out_shape=jax.ShapeDtypeStruct((rows // each, each, width), jnp.bfloat16),
+        compiler_params=pltpu.CompilerParams(vmem_limit_bytes=16 * 1024 * 1024),
+        cost_estimate=pl.CostEstimate(
+            flops=4 * rows * spread.shape[1] * width,
+            bytes_accessed=2 * (rows + spread.shape[1]) * width,
+            transcendentals=0,
+        ),
+        name="combine",
+    )(spread, *blocks)
+
+
+def shifted(x, axis, by):
+    size = lax.axis_size(axis)
+    return lax.ppermute(x, axis, [(i, (i + by) % size) for i in range(size)])
 
 
 def swap_cores(x):
@@ -215,14 +349,18 @@
     own_chooser = lax.dynamic_slice(
         chooser, (0, head_index * own_rows), (columns * slots_dev, own_rows)
     )
-    near = jnp.where(chosen, row_weight[:, :, None, :], 0.0).reshape(
-        long, short, steps, CAP, long, short, rows_dev
-    )
-    near = lax.dynamic_index_in_dim(near, at_y, 0, keepdims=False)
-    near = lax.dynamic_index_in_dim(near, at_x, 4, keepdims=False)
-    spread = jnp.where(
-        same[None, :, None, None, :, None], near[:, :, :, :, None, :], 0.0
-    ).reshape(short * slots_dev, long * own_rows)
+    near = jnp.where(chosen, row_weight[:, :, None, :], 0.0)
+    expert_of = at_y * short + (at_x - jnp.arange(short, dtype=jnp.int32)) % short
+    row_of = ((at_y + jnp.arange(long, dtype=jnp.int32)) % long * short + at_x) * rows_dev
+    row_of = (row_of[:, None] + jnp.arange(rows_dev, dtype=jnp.int32)[None, :]).reshape(-1)
+    pick_expert = expert_of[:, None] == jnp.arange(columns, dtype=jnp.int32)[None, :]
+    pick_row = row_of[:, None] == jnp.arange(columns * rows_dev, dtype=jnp.int32)[None, :]
+    exact = dict(precision=lax.Precision.HIGHEST, preferred_element_type=jnp.float32)
+    near = jnp.einsum("je,etcr->jtcr", pick_expert.astype(jnp.float32), near, **exact)
+    near = jnp.einsum("jtcr,qr->jtcq", near, pick_row.astype(jnp.float32), **exact)
+    near = near.reshape(short, steps, CAP, long, rows_dev).transpose(3, 4, 0, 1, 2)
+    spread = jnp.where(same[None, :, None, None, :, None], near[:, None], 0.0)
+    spread = spread.reshape(long * own_rows, short * slots_dev)
 
     by_row_queries = jnp.swapaxes(queries, 0, 1)
     recent = jnp.swapaxes(fresh, 0, 1)
@@ -242,58 +380,36 @@
     values = values.reshape(rows_group, heads_dev * VD)
     values_slots = jnp.dot(chooser, values, preferred_element_type=jnp.float32).astype(jnp.bfloat16)
     hidden_own = hidden_in.reshape(own_rows, width)
-    part_rows, part_slots = project(
-        jnp.concatenate([values, values_slots], axis=0), w_all, own_chooser, hidden_own
-    )
-    blocks, tile = part_rows.shape[1], part_rows.shape[3]
-    attention = lax.psum_scatter(
-        part_rows.reshape(-1, tile), head, scatter_dimension=0, tiled=True
-    ).reshape(blocks, own_rows, tile)
-    summed = hidden_own.astype(jnp.float32) + jnp.swapaxes(attention, 0, 1).reshape(own_rows, width)
-
+    part_slots = project_slots(values_slots, w_all, own_chooser, hidden_own)
     slot_parts = lax.all_to_all(
         part_slots.reshape(columns, slots_dev, width), head, 0, 0, tiled=False
     )
+    part_rows = project_rows(values, w_all, own_rows, long)
     slot_rows = jnp.sum(slot_parts.astype(jnp.float32), axis=0)
     normed = (
         slot_rows
         * lax.rsqrt(jnp.mean(slot_rows * slot_rows, axis=1, keepdims=True) + 1e-06)
         * norm_gain
     ).astype(jnp.bfloat16)
+
+    blocks, tile = part_rows.shape[1], part_rows.shape[3]
+    part_rows = after(part_rows.reshape(-1, tile), normed)
+    part_rows = lax.psum_scatter(part_rows, "x", scatter_dimension=0, tiled=True)
+    attention = lax.psum_scatter(part_rows, "y", scatter_dimension=0, tiled=True)
+    attention = jnp.swapaxes(attention.reshape(blocks, own_rows, tile), 0, 1)
+    summed = hidden_own.astype(jnp.float32) + attention.reshape(own_rows, width)
+
+    core_now = jnp.reshape(core, (1,)).astype(jnp.int32)
     portion = lax.all_gather(normed, "z", axis=0, tiled=True)
-    active = gate_up(portion, w_gu[0], gu_other)
-    units = active.shape[1] // 2
-    active = jnp.where(
-        core == 0,
-        active,
-        jnp.concatenate([active[:, units:], active[:, :units]], axis=1),
-    )
-    copies = jnp.broadcast_to(active[None], (chips, *active.shape))
-    copies = lax.all_to_all(copies, "z", 0, 0, tiled=False)
-    everywhere = jnp.swapaxes(copies, 0, 1).reshape(active.shape[0], -1)
-    second = (((1,), (1,)), ((), ()))
-    mine = lax.dot_general(everywhere, down, second, preferred_element_type=jnp.float32)
-    others = lax.dot_general(everywhere, down_other, second, preferred_element_type=jnp.float32)
-    mine, others = mine.astype(jnp.bfloat16), others.astype(jnp.bfloat16)
-    outcome = jnp.where(
-        core == 0,
-        jnp.concatenate([mine, others], axis=1),
-        jnp.concatenate([others, mine], axis=1),
-    )
-    slot_values = lax.all_to_all(
-        outcome.reshape(chips, slots_dev, outcome.shape[1]), "z", 0, 0, tiled=False
-    )
-    slot_values = jnp.swapaxes(slot_values, 0, 1).reshape(slots_dev, width)
-    beside = lax.all_gather(slot_values, "x", axis=0, tiled=True)
-    mixed = lax.dot_general(
-        spread,
-        beside.astype(jnp.float32),
-        (((0,), (0,)), ((), ())),
-        precision=lax.Precision.HIGHEST,
-        preferred_element_type=jnp.float32,
-    ).astype(jnp.bfloat16)
-    mix_parts = lax.all_to_all(mixed.reshape(long, own_rows, width), "y", 0, 0, tiled=False)
-    out = summed + jnp.sum(mix_parts.astype(jnp.float32), axis=0)
+    active = gate_up(core_now, portion, w_gu[0], gu_other, chips)
+    everywhere = lax.all_to_all(active, "z", 0, 0, tiled=False)
+    outcome = down_project(core_now, everywhere, down, down_other)
+    slot_values = lax.all_to_all(outcome, "z", 0, 0, tiled=False)
+    beside = [slot_values] + [shifted(slot_values, "x", k) for k in range(1, short)]
+    mixed = combine(spread, beside, own_rows)
+    out = summed + mixed[0].astype(jnp.float32)
+    for k in range(1, long):
+        out = out + shifted(mixed[k], "y", k).astype(jnp.float32)
     return out.astype(jnp.bfloat16).reshape(steps, rows_dev, width)
 
 

time: 215 us -> 210 us (0.977)
  blocking collectives: 49.4 us -> 26.6 us
  Pallas kernels: 11.3 us -> 22.2 us
  starting transfers between devices: 32.2 us -> 38.6 us
  matrix products: 8.19 us -> 5.49 us
  waiting for transfers between devices: 71.3 us -> 73.6 us
    pallas_call x1 -> x5, Pallas kernels: 5.65 us -> 19 us  [the longest x1 8.67 us: project_rows(): pl.pallas_call(functools.partial(project_rows_body, outer), grid=(width /...]
    all_gather x1 -> x0, blocking collectives: 12.6 us -> none  [per_device(): beside = lax.all_gather(slot_values, 'x', axis=0, tiled=True)]
    all_to_all x1, waiting for transfers between devices: 30.9 us -> 18.4 us  [per_device(): lax.all_to_all(part_slots.reshape(columns, slots_dev, width), head, 0, 0,...]
    ppermute x0 -> x6, waiting for transfers between devices: none -> 11.6 us  [shifted(): return lax.ppermute(x, axis, [(i, (i + by) % size) for i in range(size)])]
    all_to_all x1 -> x0, blocking collectives: 9.97 us -> none  [per_device(): lax.all_to_all(mixed.reshape(long, own_rows, width), 'y', 0, 0, tiled=False)]
    ppermute x0 -> x6, starting transfers between devices: none -> 7.49 us  [shifted(): return lax.ppermute(x, axis, [(i, (i + by) % size) for i in range(size)])]
    reduce_scatter x1 -> x2, waiting for transfers between devices: 0.02 us -> 4.93 us  [the longest x1 4.93 us: per_device(): lax.psum_scatter(part_rows, 'y', scatter_dimension=0, tiled=True)]
    dot_general x3 -> x2, matrix products: 3.36 us -> 0.41 us  [the longest x1 0.21 us: per_device(): jnp.einsum('jtcr,qr->jtcq', near, pick_row.astype(jnp.float32), **exact)]
  transfers between devices with their start and end apart: 9 -> 16, of which waited for: 6 -> 12; matrix products, arithmetic and copies ran while one was open for 13% -> 13% of each run, Pallas kernels for 3% -> 8%
where the time goes in v3:
time: 210 us; the launch traced here: 207 us
  waiting for transfers between devices  73.6 us (35%)
  starting transfers between devices  38.6 us (18%)
  blocking collectives  26.6 us (13%)
  Pallas kernels  22.2 us (11%)
  local copies, waits for them, and re-layouts  16.9 us (8%)
  between operations  13.5 us (6%)
  other arithmetic  10.3 us (5%)
  matrix products  5.49 us (3%)
    all_gather x1, blocking collectives, per_device(): portion = lax.all_gather(normed, 'z', axis=0, tiled=True)  26.6 us
    all_to_all x1, waiting for transfers between devices, per_device(): lax.all_to_all(part_slots.reshape(columns, slots_dev, width), head, 0, 0,...  18.4 us
    ppermute x6, waiting for transfers between devices, shifted(): return lax.ppermute(x, axis, [(i, (i + by) % size) for i in range(size)])  11.6 us
    all_gather x1, waiting for transfers between devices, per_device(): w_all = lax.all_gather(w_o.T, group, axis=0, tiled=True)  11.4 us
    all_to_all x1, waiting for transfers between devices, per_device(): everywhere = lax.all_to_all(active, 'z', 0, 0, tiled=False)  10.1 us
    pallas_call x1, Pallas kernels, project_rows(): pl.pallas_call(functools.partial(project_rows_body, outer), grid=(width /...  8.67 us
    all_to_all x1, starting transfers between devices, per_device(): lax.all_to_all(sorted_cache.reshape(groups, newcomers, *sorted_cache.shap...  8.57 us
    all_to_all x1, waiting for transfers between devices, per_device(): slot_values = lax.all_to_all(outcome, 'z', 0, 0, tiled=False)  8.13 us
  transfers between devices with their start and end apart: 16, of which 12 were waited for; matrix products, arithmetic and copies ran while one was open for 13% of the time, Pallas kernels for 8%

profile of v3, /device:TPU:24, one launch (start us, length us, event | category | flops | bytes accessed | tf_op | source)
XLA Modules:
  0.0 207.1 jit_solution(4682159475717516202)
XLA Ops:
  6.5 0.7 all-gather.2.cloned.1.call-update
  7.3 1.4 select_reduce_fusion.2
  8.6 2.4 %gather_fusion = bf16[32,8,576]{2,1,0:T(8,128)(2,1)} fusion(bf16[32,8,576]{2,1,0:T(8,128)(2,1)} %bitcast.94, s32[1024]{0:T(1024)S(1)} %pad_clamp_fusion), kind=kCustom, calls=%fused_computation | custom fusion | bytes 589952 | tf_op jit(solution)/shard_map/jit(_take)/gather | solution.py:334
  11.1 8.6 %all-to-all-start = ((bf16[16,2,8,576]{3,2,1,0:T(8,128)(2,1)}), bf16[16,2,8,576]{3,2,1,0:T(8,128)(2,1)S(1)}, u32[]{:S(2)}, u32[]{:S(2)}) async-start(bf16[16,2,8,576]{3,2,1,0:T(8,128)(2,1)} %bitcast.6), calls=%async_computation | async-start | bytes 655360 | tf_op jit(solution)/shard_map/all_to_all | solution.py:335
  19.6 0.8 fusion.19
  20.7 1.0 copy.100
  21.8 1.0 copy.102
  22.8 1.2 fusion.58
  24.0 0.8 copy.88
  25.5 0.7 iota_compare_fusion.6
  27.5 0.9 fusion
  28.8 0.7 dynamic_slice.6
  29.6 0.8 fusion.60
  30.4 1.1 fusion.9
  31.6 2.2 %all-to-all-done = bf16[16,2,8,576]{3,2,1,0:T(8,128)(2,1)S(1)} async-done(((bf16[16,2,8,576]{3,2,1,0:T(8,128)(2,1)}), bf16[16,2,8,576]{3,2,1,0:T(8,128)(2,1)S(1)}, u32[]{:S(2)}, u32[]{:S(2)}) %all-to-all-start) | async-done | bytes 294944 | tf_op jit(solution)/shard_map/all_to_all | solution.py:335
  34.8 1.1 copy_bitcast_fusion
  35.9 7.1 %all-to-all-start.1 = ((bf16[16,4,2,4,512]{4,1,2,3,0:T(4,128)(2,1)}), bf16[16,4,2,4,512]{4,1,2,3,0:T(4,128)(2,1)S(1)}, u32[]{:S(2)}, u32[]{:S(2)}) async-start(bf16[16,4,2,4,512]{4,1,2,3,0:T(4,128)(2,1)} %copy_bitcast_fusion), calls=%async_computation.1 | async-start | bytes 1048576 | tf_op jit(solution)/shard_map/all_to_all | solution.py:375
  43.1 1.5 broadcast_and_fusion
  44.6 1.9 and.94
  47.9 6.2 %all-to-all-done.1 = bf16[16,4,2,4,512]{4,1,2,3,0:T(4,128)(2,1)S(1)} async-done(((bf16[16,4,2,4,512]{4,1,2,3,0:T(4,128)(2,1)}), bf16[16,4,2,4,512]{4,1,2,3,0:T(4,128)(2,1)S(1)}, u32[]{:S(2)}, u32[]{:S(2)}) %all-to-all-start.1) | async-done | bytes 524320 | tf_op jit(solution)/shard_map/all_to_all | solution.py:375
  54.8 0.8 convolution_convert_fusion.1.x_ref
  55.7 11.4 %all-gather.2.cloned.1.call-done.w_ref = bf16[7168,512]{1,0:T(8,128)(2,1)} async-done(((bf16[448,512]{1,0:T(8,128)(2,1)}), bf16[7168,512]{1,0:T(8,128)(2,1)}) %all-gather.2.cloned.1.call-update) | async-done | bytes 7340048 | tf_op jit(solution)/shard_map/all_gather | solution.py:323
  67.1 6.6 %project_slots.1 = bf16[128,7168]{1,0:T(8,128)(2,1)} custom-call(bf16[128,512]{1,0:T(8,128)(2,1)} %convolution_convert_fusion.1.x_ref, bf16[7168,512]{1,0:T(8,128)(2,1)} %all-gather.2.cloned.1.call-done.w_ref, bf16[128,8]{1,0:T(8,128)(2,1)} %dynamic-slice_convert_fusion.own_ref, bf16[8,7168]{1,0:T(8,128)(2,1)} %reshape.280.hidden_ref), custom_call_target="tpu_custom_call" | custom-call | flops 939524096 | bytes 9175040 | tf_op jit(solution)/shard_map/project_slots/pallas_call | solution.py:82
  73.7 7.2 %all-to-all-start.2 = ((bf16[16,8,7168]{2,1,0:T(8,128)(2,1)}), bf16[16,8,7168]{2,1,0:T(8,128)(2,1)S(1)}, u32[]{:S(2)}, u32[]{:S(2)}) async-start(bf16[16,8,7168]{2,1,0:T(8,128)(2,1)} %bitcast.84), calls=%async_computation.2 | async-start | bytes 3670016 | tf_op jit(solution)/shard_map/all_to_all | solution.py:384
  80.9 0.8 copy.117.x_ref
  81.7 8.7 %project_rows.1 = f32[16,8,8,896]{3,2,1,0:T(8,128)} custom-call(bf16[128,512]{1,0:T(8,128)(2,1)} %copy.117.x_ref, bf16[7168,512]{1,0:T(8,128)(2,1)} %all-gather.2.cloned.1.call-done.w_ref), custom_call_target="tpu_custom_call" | custom-call | flops 939524096 | bytes 11010048 | tf_op jit(solution)/shard_map/project_rows/pallas_call | solution.py:115
  90.3 18.4 %all-to-all-done.2 = bf16[16,8,7168]{2,1,0:T(8,128)(2,1)S(1)} async-done(((bf16[16,8,7168]{2,1,0:T(8,128)(2,1)}), bf16[16,8,7168]{2,1,0:T(8,128)(2,1)S(1)}, u32[]{:S(2)}, u32[]{:S(2)}) %all-to-all-start.2) | async-done | bytes 1835040 | tf_op jit(solution)/shard_map/all_to_all | solution.py:384
  109.2 0.7 multiply_convert_fusion.other_ref
  110.0 1.4 copy-done.2
  111.5 26.6 %all_gather.7.x_ref = bf16[64,7168]{1,0:T(8,128)(2,1)S(1)} all-gather(bf16[8,7168]{1,0:T(8,128)(2,1)S(1)} %copy-done.6), channel_id=1, replica_groups=mesh['z'=8,'core'=2,'y'=4,'x'=4] {'z'}, dimensions={0}, use_global_device_ids=true | all-gather | bytes 1032192 | tf_op jit(solution)/shard_map/all_gather | solution.py:403
  138.0 2.1 %copy-done.1 = bf16[1,2,7168,128]{3,2,1,0:T(8,128)(2,1)S(1)} copy-done((bf16[1,2,7168,128]{3,2,1,0:T(8,128)(2,1)S(1)}, bf16[1,2,7168,128]{3,2,1,0:T(8,128)(2,1)}, u32[]{:S(2)}) %copy-start.1) | copy-done | bytes 3670040
  140.1 3.1 %gate_up.1 = bf16[8,64,256]{2,1,0:T(8,128)(2,1)} custom-call(s32[1]{0:T(128)} %bitcast.30.core_ref, bf16[64,7168]{1,0:T(8,128)(2,1)S(1)} %all_gather.7.x_ref, bf16[2,7168,128]{2,1,0:T(8,128)(2,1)S(1)} %bitcast.80, bf16[2,7168,128]{2,1,0:T(8,128)(2,1)S(1)} %collective-permute-done.other_ref), custom_call_target="tpu_custom_call" | custom-call | flops 469762048 | bytes 8257536 | tf_op jit(solution)/shard_map/gate_up/pallas_call | solution.py:186
  143.3 4.5 %all-to-all-start.3 = ((bf16[8,64,256]{2,1,0:T(8,128)(2,1)}), bf16[8,64,256]{2,1,0:T(8,128)(2,1)S(1)}, u32[]{:S(2)}, u32[]{:S(2)}) async-start(bf16[8,64,256]{2,1,0:T(8,128)(2,1)} %gate_up.1), calls=%async_computation.5 | async-start | bytes 524288 | tf_op jit(solution)/shard_map/all_to_all | solution.py:405
  148.2 10.1 %all-to-all-done.3.x_ref = bf16[8,64,256]{2,1,0:T(8,128)(2,1)S(1)} async-done(((bf16[8,64,256]{2,1,0:T(8,128)(2,1)}), bf16[8,64,256]{2,1,0:T(8,128)(2,1)S(1)}, u32[]{:S(2)}, u32[]{:S(2)}) %all-to-all-start.3) | async-done | bytes 262176 | tf_op jit(solution)/shard_map/all_to_all | solution.py:405
  158.3 3.4 %down_project.1 = bf16[8,8,896]{2,1,0:T(8,128)(2,1)} custom-call(s32[1]{0:T(128)} %bitcast.30.core_ref, bf16[8,64,256]{2,1,0:T(8,128)(2,1)S(1)} %all-to-all-done.3.x_ref, bf16[448,2048]{1,0:T(8,128)(2,1)S(1)} %bitcast.82, bf16[448,2048]{1,0:T(8,128)(2,1)} %collective-permute-done.1.other_ref), custom_call_target="tpu_custom_call" | custom-call | flops 234881024 | bytes 3670016 | tf_op jit(solution)/shard_map/down_project/pallas_call | solution.py:232
  161.7 3.5 %all-to-all-start.4 = ((bf16[8,8,896]{2,1,0:T(8,128)(2,1)}), bf16[8,8,896]{2,1,0:T(8,128)(2,1)S(1)}, u32[]{:S(2)}, u32[]{:S(2)}) async-start(bf16[8,8,896]{2,1,0:T(8,128)(2,1)} %down_project.1), calls=%async_computation.6 | async-start | bytes 229376 | tf_op jit(solution)/shard_map/all_to_all | solution.py:407
  165.9 8.1 %all-to-all-done.4.refs_0_ = bf16[8,8,896]{2,1,0:T(8,128)(2,1)S(1)} async-done(((bf16[8,8,896]{2,1,0:T(8,128)(2,1)}), bf16[8,8,896]{2,1,0:T(8,128)(2,1)S(1)}, u32[]{:S(2)}, u32[]{:S(2)}) %all-to-all-start.4) | async-done | bytes 114720 | tf_op jit(solution)/shard_map/all_to_all | solution.py:407
  174.0 0.9 collective-permute-start.3
  175.0 2.3 %collective-permute-start.4 = (bf16[8,8,896]{2,1,0:T(8,128)(2,1)S(1)}, bf16[8,8,896]{2,1,0:T(8,128)(2,1)S(1)}, u32[]{:S(2)}, u32[]{:S(2)}) collective-permute-start(bf16[8,8,896]{2,1,0:T(8,128)(2,1)S(1)} %all-to-all-done.4.refs_0_), channel_id=1, source_target_pairs={{0,3},{1,0},{2,1},{3,2},{4,7},{5,4},{6,5},{7,6},{8,11},{9,8},{10,9... | collective-permute-start | bytes 344072 | tf_op jit(solution)/shard_map/ppermute | solution.py:284
  177.6 3.7 %collective-permute-done.2.refs_1_ = bf16[8,8,896]{2,1,0:T(8,128)(2,1)S(1)} collective-permute-done((bf16[8,8,896]{2,1,0:T(8,128)(2,1)S(1)}, bf16[8,8,896]{2,1,0:T(8,128)(2,1)S(1)}, u32[]{:S(2)}, u32[]{:S(2)}) %collective-permute-start.2) | collective-permute-done | bytes 114720 | tf_op jit(solution)/shard_map/ppermute | solution.py:284
  181.3 0.9 collective-permute-done.4.refs_3_
  182.7 2.8 %collective-permute-start.6 = (bf16[8,7168]{1,0:T(8,128)(2,1)S(1)}, bf16[8,7168]{1,0:T(8,128)(2,1)S(1)}, u32[]{:S(2)}, u32[]{:S(2)}) collective-permute-start(bf16[8,7168]{1,0:T(8,128)(2,1)S(1)} %get-tuple-element.11), channel_id=1, source_target_pairs={{0,8},{4,12},{8,0},{12,4},{1,9},{5,13},{9,1},{13,5},{2,10},{6,14},... | collective-permute-start | bytes 344072 | tf_op jit(solution)/shard_map/ppermute | solution.py:284
  185.5 1.3 collective-permute-start.5
  186.8 1.9 collective-permute-done.7
  188.8 4.3 %collective-permute-done.6 = bf16[8,7168]{1,0:T(8,128)(2,1)S(1)} collective-permute-done((bf16[8,7168]{1,0:T(8,128)(2,1)S(1)}, bf16[8,7168]{1,0:T(8,128)(2,1)S(1)}, u32[]{:S(2)}, u32[]{:S(2)}) %collective-permute-start.6) | collective-permute-done | bytes 114720 | tf_op jit(solution)/shard_map/ppermute | solution.py:284
  193.1 0.8 collective-permute-done.5
  193.9 4.9 %reduce-scatter.5.cloned.1.call-done = f32[64,896]{1,0:T(8,128)} async-done(((f32[256,896]{1,0:T(8,128)}), f32[64,896]{1,0:T(8,128)}) %reduce-scatter.5.cloned.1.call-update) | async-done | bytes 229392 | tf_op jit(solution)/shard_map/reduce_scatter | solution.py:398
  198.8 1.0 fusion.18
  (90 shorter events, 9.2 us)
Async XLA Ops:
  6.5 47.9 %copy-start = (bf16[4,512,128]{2,1,0:T(8,128)(2,1)S(1)}, bf16[4,512,128]{2,1,0:T(8,128)(2,1)}, u32[]{:S(2)}) copy-start(bf16[4,512,128]{2,1,0:T(8,128)(2,1)} %param.23) | copy-start | bytes 1572868
  6.5 60.6 %all-gather.2.cloned.1.call-start = ((), (), s32[]{:S(2)}) async-start(), calls=%async_computation.7 | async-start | bytes 7798784 | tf_op jit(solution)/shard_map/all_gather | solution.py:323
  8.6 17.8 %copy-start.3 = (bf16[2,1024,576]{1,2,0:T(8,128)(2,1)S(1)}, bf16[2,1024,576]{1,2,0:T(8,128)(2,1)}, u32[]{:S(2)}) copy-start(bf16[2,1024,576]{1,2,0:T(8,128)(2,1)} %param.18) | copy-start | bytes 7077892
  11.1 22.7 %all-to-all-start = ((bf16[16,2,8,576]{3,2,1,0:T(8,128)(2,1)}), bf16[16,2,8,576]{3,2,1,0:T(8,128)(2,1)S(1)}, u32[]{:S(2)}, u32[]{:S(2)}) async-start(bf16[16,2,8,576]{3,2,1,0:T(8,128)(2,1)} %bitcast.6), calls=%async_computation | async-start | bytes 655360 | tf_op jit(solution)/shard_map/all_to_all | solution.py:335
  20.7 2.1 %copy-start.8 = (s32[16,2,64]{2,0,1:T(8,128)}, s32[16,2,64]{2,0,1:T(8,128)S(1)}, u32[]{:S(2)}) copy-start(s32[16,2,64]{2,0,1:T(8,128)S(1)} %convolution_convert_fusion.2) | copy-start | bytes 24580
  25.5 0.7 copy-start.13
  27.5 2.1 copy-start.4
  34.8 11.7 %copy-start.7 = (bf16[2,4,7168]{2,1,0:T(4,128)(2,1)S(1)}, bf16[2,4,7168]{2,1,0:T(4,128)(2,1)}, u32[]{:S(2)}) copy-start(bf16[2,4,7168]{2,1,0:T(4,128)(2,1)} %param.15) | copy-start | bytes 344068
  35.9 18.2 %all-to-all-start.1 = ((bf16[16,4,2,4,512]{4,1,2,3,0:T(4,128)(2,1)}), bf16[16,4,2,4,512]{4,1,2,3,0:T(4,128)(2,1)S(1)}, u32[]{:S(2)}, u32[]{:S(2)}) async-start(bf16[16,4,2,4,512]{4,1,2,3,0:T(4,128)(2,1)} %copy_bitcast_fusion), calls=%async_computation.1 | async-start | bytes 1048576 | tf_op jit(solution)/shard_map/all_to_all | solution.py:375
  73.7 35.0 %all-to-all-start.2 = ((bf16[16,8,7168]{2,1,0:T(8,128)(2,1)}), bf16[16,8,7168]{2,1,0:T(8,128)(2,1)S(1)}, u32[]{:S(2)}, u32[]{:S(2)}) async-start(bf16[16,8,7168]{2,1,0:T(8,128)(2,1)} %bitcast.84), calls=%async_computation.2 | async-start | bytes 3670016 | tf_op jit(solution)/shard_map/all_to_all | solution.py:384
  80.9 96.4 %reduce-scatter.3.cloned.1.call-start = ((), (), s32[]{:S(2)}) async-start(), calls=%async_computation.8 | async-start | bytes 4587520 | tf_op jit(solution)/shard_map/reduce_scatter | solution.py:397
  81.7 27.5 %copy-start.11 = (f32[7168]{0:T(1024)S(1)}, f32[7168]{0:T(1024)}, u32[]{:S(2)}) copy-start(f32[7168]{0:T(1024)} %param.25) | copy-start | bytes 86020
  109.9 1.5 copy-start.2
  109.9 1.5 copy-start.10
  109.9 1.5 copy-start.12
  109.9 1.6 copy-start.6
  109.9 28.1 %collective-permute-start = (bf16[2,7168,128]{2,1,0:T(8,128)(2,1)}, bf16[2,7168,128]{2,1,0:T(8,128)(2,1)S(1)}, u32[]{:S(2)}, u32[]{:S(2)}) collective-permute-start(bf16[2,7168,128]{2,1,0:T(8,128)(2,1)} %bitcast.79), channel_id=1, source_target_pairs={{0,16},{16,0},{1,17},{17,1},{2,18},{18,2},{3,19},{19,3},{4,20},{20... | collective-permute-start | bytes 11010056 | tf_op jit(solution)/shard_map/ppermute | solution.py:288
  111.4 36.8 %collective-permute-start.1 = (bf16[448,2048]{1,0:T(8,128)(2,1)S(1)}, bf16[448,2048]{1,0:T(8,128)(2,1)}, u32[]{:S(2)}, u32[]{:S(2)}) collective-permute-start(bf16[448,2048]{1,0:T(8,128)(2,1)S(1)} %bitcast.81), channel_id=1, source_target_pairs={{0,16},{16,0},{1,17},{17,1},{2,18},{18,2},{3,19},{19,3},{4,20},{20... | collective-permute-start | bytes 5505032 | tf_op jit(solution)/shard_map/ppermute | solution.py:288
  138.0 2.1 %copy-start.1 = (bf16[1,2,7168,128]{3,2,1,0:T(8,128)(2,1)S(1)}, bf16[1,2,7168,128]{3,2,1,0:T(8,128)(2,1)}, u32[]{:S(2)}) copy-start(bf16[1,2,7168,128]{3,2,1,0:T(8,128)(2,1)} %param.28) | copy-start | bytes 11010052
  140.1 7.9 %copy-start.9 = (s32[16,2,64]{2,0,1:T(8,128)S(1)}, s32[16,2,64]{2,0,1:T(8,128)}, u32[]{:S(2)}) copy-start(s32[16,2,64]{2,0,1:T(8,128)} %copy-done.8) | copy-start | bytes 24580
  143.3 15.0 %all-to-all-start.3 = ((bf16[8,64,256]{2,1,0:T(8,128)(2,1)}), bf16[8,64,256]{2,1,0:T(8,128)(2,1)S(1)}, u32[]{:S(2)}, u32[]{:S(2)}) async-start(bf16[8,64,256]{2,1,0:T(8,128)(2,1)} %gate_up.1), calls=%async_computation.5 | async-start | bytes 524288 | tf_op jit(solution)/shard_map/all_to_all | solution.py:405
  161.7 37.1 %copy-start.5 = (bf16[8,7168]{1,0:T(8,128)(2,1)S(1)}, bf16[8,7168]{1,0:T(8,128)(2,1)}, u32[]{:S(2)}) copy-start(bf16[8,7168]{1,0:T(8,128)(2,1)} %reshape.280.hidden_ref) | copy-start | bytes 344068
  161.7 12.3 %all-to-all-start.4 = ((bf16[8,8,896]{2,1,0:T(8,128)(2,1)}), bf16[8,8,896]{2,1,0:T(8,128)(2,1)S(1)}, u32[]{:S(2)}, u32[]{:S(2)}) async-start(bf16[8,8,896]{2,1,0:T(8,128)(2,1)} %down_project.1), calls=%async_computation.6 | async-start | bytes 229376 | tf_op jit(solution)/shard_map/all_to_all | solution.py:407
  165.2 33.6 %reduce-scatter.5.cloned.1.call-start = ((), (), s32[]{:S(2)}) async-start(), calls=%async_computation.9 | async-start | bytes 1146880 | tf_op jit(solution)/shard_map/reduce_scatter | solution.py:398
  174.0 7.2 %collective-permute-start.2 = (bf16[8,8,896]{2,1,0:T(8,128)(2,1)S(1)}, bf16[8,8,896]{2,1,0:T(8,128)(2,1)S(1)}, u32[]{:S(2)}, u32[]{:S(2)}) collective-permute-start(bf16[8,8,896]{2,1,0:T(8,128)(2,1)S(1)} %all-to-all-done.4.refs_0_), channel_id=1, source_target_pairs={{0,1},{1,2},{2,3},{3,0},{4,5},{5,6},{6,7},{7,4},{8,9},{9,10},{10,1... | collective-permute-start | bytes 344072 | tf_op jit(solution)/shard_map/ppermute | solution.py:284
  174.0 7.2 %collective-permute-start.3 = (bf16[8,8,896]{2,1,0:T(8,128)(2,1)S(1)}, bf16[8,8,896]{2,1,0:T(8,128)(2,1)S(1)}, u32[]{:S(2)}, u32[]{:S(2)}) collective-permute-start(bf16[8,8,896]{2,1,0:T(8,128)(2,1)S(1)} %all-to-all-done.4.refs_0_), channel_id=1, source_target_pairs={{0,2},{1,3},{2,0},{3,1},{4,6},{5,7},{6,4},{7,5},{8,10},{9,11},{10,... | collective-permute-start | bytes 344072 | tf_op jit(solution)/shard_map/ppermute | solution.py:284
  175.0 7.2 %collective-permute-start.4 = (bf16[8,8,896]{2,1,0:T(8,128)(2,1)S(1)}, bf16[8,8,896]{2,1,0:T(8,128)(2,1)S(1)}, u32[]{:S(2)}, u32[]{:S(2)}) collective-permute-start(bf16[8,8,896]{2,1,0:T(8,128)(2,1)S(1)} %all-to-all-done.4.refs_0_), channel_id=1, source_target_pairs={{0,3},{1,0},{2,1},{3,2},{4,7},{5,4},{6,5},{7,6},{8,11},{9,8},{10,9... | collective-permute-start | bytes 344072 | tf_op jit(solution)/shard_map/ppermute | solution.py:284
  182.6 6.2 %collective-permute-start.7 = (bf16[8,7168]{1,0:T(8,128)(2,1)S(1)}, bf16[8,7168]{1,0:T(8,128)(2,1)S(1)}, u32[]{:S(2)}, u32[]{:S(2)}) collective-permute-start(bf16[8,7168]{1,0:T(8,128)(2,1)S(1)} %get-tuple-element.10), channel_id=1, source_target_pairs={{0,12},{4,0},{8,4},{12,8},{1,13},{5,1},{9,5},{13,9},{2,14},{6,2},{... | collective-permute-start | bytes 344072 | tf_op jit(solution)/shard_map/ppermute | solution.py:284
  182.7 10.4 %collective-permute-start.6 = (bf16[8,7168]{1,0:T(8,128)(2,1)S(1)}, bf16[8,7168]{1,0:T(8,128)(2,1)S(1)}, u32[]{:S(2)}, u32[]{:S(2)}) collective-permute-start(bf16[8,7168]{1,0:T(8,128)(2,1)S(1)} %get-tuple-element.11), channel_id=1, source_target_pairs={{0,8},{4,12},{8,0},{12,4},{1,9},{5,13},{9,1},{13,5},{2,10},{6,14},... | collective-permute-start | bytes 344072 | tf_op jit(solution)/shard_map/ppermute | solution.py:284
  185.5 8.4 %collective-permute-start.5 = (bf16[8,7168]{1,0:T(8,128)(2,1)S(1)}, bf16[8,7168]{1,0:T(8,128)(2,1)S(1)}, u32[]{:S(2)}, u32[]{:S(2)}) collective-permute-start(bf16[8,7168]{1,0:T(8,128)(2,1)S(1)} %get-tuple-element.9), channel_id=1, source_target_pairs={{0,4},{4,8},{8,12},{12,0},{1,5},{5,9},{9,13},{13,1},{2,6},{6,10},{... | collective-permute-start | bytes 344072 | tf_op jit(solution)/shard_map/ppermute | solution.py:284
Sparse Core Ops, SparseCore 0:
  9.2 57.8 all-gather.1
  110.1 41.5 reduce-scatter.2
  177.4 21.3 reduce-scatter.4

commit v4 on v3

--- a/solution.py
+++ b/solution.py
@@ -69,66 +69,70 @@
 NT = (((1,), (1,)), ((), ()))
 
 
-def project_slots_body(x_ref, w_ref, own_ref, hidden_ref, out_ref):
-    whole = lax.dot_general(x_ref[...], w_ref[...], NT, preferred_element_type=jnp.float32)
-    carried = jnp.dot(own_ref[...], hidden_ref[...], preferred_element_type=jnp.float32)
-    out_ref[...] = (whole + carried).astype(jnp.bfloat16)
-
-
-def project_slots(x, w, own, hidden):
-    width, depth = w.shape
-    rows = x.shape[0]
-    tile = width // 4
+def spread_blocks(block):
+    chips = lax.axis_size("z")
+    far = chips // 2
+    half = block.shape[0] // 2
+    own = [None] * chips
+    own[0] = [block]
+    up = down = block
+    for k in range(1, far):
+        up, down = shifted(up, "z", 1), shifted(down, "z", -1)
+        own[k], own[chips - k] = [up], [down]
+    own[far] = [shifted(up[:half], "z", 1), shifted(down[half:], "z", -1)]
+    other = [[swap_cores(part) for part in parts] for parts in own]
+    return own, other
+
+
+def project_body(layout, place_ref, x_ref, *refs):
+    blocks = refs[: sum(map(sum, layout))]
+    *carry, out_ref = refs[len(blocks) :]
+    chips = len(layout)
+    x = x_ref[...]
+    first = place_ref[1] == 0
+    at = 0
+    for k, counts in enumerate(layout):
+        pair = []
+        for count in counts:
+            parts = [
+                lax.dot_general(x, r[...], NT, preferred_element_type=jnp.float32)
+                for r in blocks[at : at + count]
+            ]
+            pair.append(parts[0] if count == 1 else jnp.concatenate(parts, axis=1))
+            at += count
+        whole = jnp.concatenate(
+            [jnp.where(first, pair[0], pair[1]), jnp.where(first, pair[1], pair[0])], axis=1
+        )
+        width = whole.shape[1]
+        chip = lax.rem(place_ref[0] + (chips - k), chips)
+        columns = pl.ds(pl.multiple_of(chip * width, 128), width)
+        if carry:
+            own_ref, hidden_ref = carry
+            whole += jnp.dot(
+                own_ref[...], hidden_ref[:, columns], preferred_element_type=jnp.float32
+            )
+        out_ref[:, columns] = whole.astype(jnp.bfloat16)
+
+
+def project(place, x, own, other, carry=()):
+    layout = [(len(a), len(b)) for a, b in zip(own, other)]
+    blocks = [part for pair in zip(own, other) for parts in pair for part in parts]
+    rows, depth = x.shape
+    width = sum(part.shape[0] for part in blocks)
+    vmem = pl.BlockSpec(memory_space=pltpu.VMEM)
     return pl.pallas_call(
-        project_slots_body,
-        grid=(width // tile,),
-        in_specs=[
-            pl.BlockSpec(x.shape, lambda i: (0, 0)),
-            pl.BlockSpec((tile, depth), lambda i: (i, 0)),
-            pl.BlockSpec(own.shape, lambda i: (0, 0)),
-            pl.BlockSpec((hidden.shape[0], tile), lambda i: (0, i)),
-        ],
-        out_specs=pl.BlockSpec((rows, tile), lambda i: (0, i)),
+        functools.partial(project_body, layout),
+        in_specs=[pl.BlockSpec(memory_space=pltpu.SMEM)] + [vmem] * (1 + len(blocks) + len(carry)),
+        out_specs=vmem,
         out_shape=jax.ShapeDtypeStruct((rows, width), jnp.bfloat16),
-        compiler_params=pltpu.CompilerParams(vmem_limit_bytes=56 * 1024 * 1024),
+        compiler_params=pltpu.CompilerParams(vmem_limit_bytes=24 * 1024 * 1024),
         cost_estimate=pl.CostEstimate(
             flops=2 * rows * depth * width,
             bytes_accessed=2 * depth * width + 2 * rows * width,
             transcendentals=0,
         ),
-        name="project_slots",
-    )(x, w, own, hidden)
-
-
-def project_rows_body(outer, x_ref, w_ref, out_ref):
-    whole = lax.dot_general(x_ref[...], w_ref[...], NT, preferred_element_type=jnp.float32)
-    blocks, _, each, _ = out_ref.shape
-    inner = blocks // outer
-    for k in range(blocks):
-        out_ref[k % inner * outer + k // inner, 0] = whole[k * each : (k + 1) * each]
-
-
-def project_rows(x, w, each, outer):
-    width, depth = w.shape
-    rows = x.shape[0]
-    tile = width // 8
-    return pl.pallas_call(
-        functools.partial(project_rows_body, outer),
-        grid=(width // tile,),
-        in_specs=[
-            pl.BlockSpec(x.shape, lambda i: (0, 0)),
-            pl.BlockSpec((tile, depth), lambda i: (i, 0)),
-        ],
-        out_specs=pl.BlockSpec((rows // each, 1, each, tile), lambda i: (0, i, 0, 0)),
-        out_shape=jax.ShapeDtypeStruct((rows // each, width // tile, each, tile), jnp.float32),
-        compiler_params=pltpu.CompilerParams(vmem_limit_bytes=56 * 1024 * 1024),
-        cost_estimate=pl.CostEstimate(
-            flops=2 * rows * depth * width,
-            bytes_accessed=2 * depth * width + 4 * rows * width,
-            transcendentals=0,
-        ),
-        name="project_rows",
-    )(x, w)
+        name="project_slots" if carry else "project_rows",
+    )(place, x, *blocks, *carry)
 
 
 def after_body(x_ref, other_ref, out_ref):
@@ -205,7 +209,8 @@
     )(core, x, own, other)
 
 
-def down_body(core_ref, x_ref, own_ref, other_ref, out_ref):
+def down_body(core_ref, x_ref, own_ref, other_ref, ready_ref, out_ref):
+    del ready_ref
     x = jnp.concatenate([x_ref[k] for k in range(x_ref.shape[0])], axis=1)
     half = own_ref.shape[0]
     parts, each = out_ref.shape[0], out_ref.shape[1]
@@ -225,13 +230,19 @@
         write(others, mine)
 
 
-def down_project(core, x, own, other):
+def down_project(core, x, own, other, ready):
     parts, rows, _ = x.shape
     columns = 2 * own.shape[0]
     vmem = pl.BlockSpec(memory_space=pltpu.VMEM)
     return pl.pallas_call(
         down_body,
-        in_specs=[pl.BlockSpec(memory_space=pltpu.SMEM), vmem, vmem, vmem],
+        in_specs=[
+            pl.BlockSpec(memory_space=pltpu.SMEM),
+            vmem,
+            vmem,
+            vmem,
+            pl.BlockSpec(memory_space=pl.ANY),
+        ],
         out_specs=vmem,
         out_shape=jax.ShapeDtypeStruct((parts, rows // parts, columns), jnp.bfloat16),
         compiler_params=pltpu.CompilerParams(vmem_limit_bytes=24 * 1024 * 1024),
@@ -241,7 +252,7 @@
             transcendentals=0,
         ),
         name="down_project",
-    )(core, x, own, other)
+    )(core, x, own, other, ready)
 
 
 def combine_body(spread_ref, *refs):
@@ -320,7 +331,8 @@
     heads_dev = w_uv.shape[0]
     slots_dev = steps * CAP
 
-    w_all = lax.all_gather(w_o.T, group, axis=0, tiled=True)
+    place = jnp.stack([lax.axis_index("z"), core]).astype(jnp.int32)
+    w_own, w_other = spread_blocks(w_o.T)
     gu_other = swap_cores(w_gu[0])
     down = w_down[0].T
     down_other = swap_cores(down)
@@ -380,11 +392,11 @@
     values = values.reshape(rows_group, heads_dev * VD)
     values_slots = jnp.dot(chooser, values, preferred_element_type=jnp.float32).astype(jnp.bfloat16)
     hidden_own = hidden_in.reshape(own_rows, width)
-    part_slots = project_slots(values_slots, w_all, own_chooser, hidden_own)
+    part_slots = project(place, values_slots, w_own, w_other, (own_chooser, hidden_own))
     slot_parts = lax.all_to_all(
         part_slots.reshape(columns, slots_dev, width), head, 0, 0, tiled=False
     )
-    part_rows = project_rows(values, w_all, own_rows, long)
+    part_rows = project(place, values, w_own, w_other)
     slot_rows = jnp.sum(slot_parts.astype(jnp.float32), axis=0)
     normed = (
         slot_rows
@@ -392,18 +404,16 @@
         * norm_gain
     ).astype(jnp.bfloat16)
 
-    blocks, tile = part_rows.shape[1], part_rows.shape[3]
-    part_rows = after(part_rows.reshape(-1, tile), normed)
-    part_rows = lax.psum_scatter(part_rows, "x", scatter_dimension=0, tiled=True)
-    attention = lax.psum_scatter(part_rows, "y", scatter_dimension=0, tiled=True)
-    attention = jnp.swapaxes(attention.reshape(blocks, own_rows, tile), 0, 1)
-    summed = hidden_own.astype(jnp.float32) + attention.reshape(own_rows, width)
+    row_parts = lax.all_to_all(
+        after(part_rows.reshape(columns, own_rows, width), normed), head, 0, 0, tiled=False
+    )
+    summed = hidden_own.astype(jnp.float32) + jnp.sum(row_parts.astype(jnp.float32), axis=0)
 
     core_now = jnp.reshape(core, (1,)).astype(jnp.int32)
     portion = lax.all_gather(normed, "z", axis=0, tiled=True)
     active = gate_up(core_now, portion, w_gu[0], gu_other, chips)
     everywhere = lax.all_to_all(active, "z", 0, 0, tiled=False)
-    outcome = down_project(core_now, everywhere, down, down_other)
+    outcome = down_project(core_now, everywhere, down, down_other, row_parts)
     slot_values = lax.all_to_all(outcome, "z", 0, 0, tiled=False)
     beside = [slot_values] + [shifted(slot_values, "x", k) for k in range(1, short)]
     mixed = combine(spread, beside, own_rows)

time: 210 us -> 244 us (1.16)
  waiting for transfers between devices: 73.6 us -> 96.3 us
  starting transfers between devices: 38.6 us -> 57.4 us
  between operations: 13.5 us -> 0.6 us
  local copies, waits for them, and re-layouts: 16.9 us -> 26.6 us
  Pallas kernels: 22.2 us -> 18.4 us
    all_to_all x0 -> x1, waiting for transfers between devices: none -> 29.1 us  [per_device(): lax.all_to_all(after(part_rows.reshape(columns, own_rows, width), normed)...]
    ppermute x6 -> x14, waiting for transfers between devices: 11.6 us -> 27.4 us  [shifted(): return lax.ppermute(x, axis, [(i, (i + by) % size) for i in range(size)])]
    ppermute x6 -> x14, starting transfers between devices: 7.49 us -> 20.4 us  [shifted(): return lax.ppermute(x, axis, [(i, (i + by) % size) for i in range(size)])]
    all_gather x1 -> x0, waiting for transfers between devices: 11.4 us -> none  [per_device(): w_all = lax.all_gather(w_o.T, group, axis=0, tiled=True)]
    all_to_all x1, waiting for transfers between devices: 10.1 us -> 0.01 us  [per_device(): everywhere = lax.all_to_all(active, 'z', 0, 0, tiled=False)]
    all_to_all x1, waiting for transfers between devices: 18.4 us -> 27.6 us  [per_device(): lax.all_to_all(part_slots.reshape(columns, slots_dev, width), head, 0, 0,...]
    unnamed x29 -> x63, local copies, waits for them, and re-layouts: 4.21 us -> 10.4 us
    pallas_call x2, Pallas kernels: 15.3 us -> 10 us  [project(): pl.pallas_call(functools.partial(project_body, layout), in_specs=[pl.Bloc...]
  transfers between devices with their start and end apart: 16 -> 31, of which waited for: 12 -> 15; matrix products, arithmetic and copies ran while one was open for 13% -> 13% of each run, Pallas kernels for 8% -> 2%
where the time goes in v4:
time: 244 us; the launch traced here: 241 us
  waiting for transfers between devices  96.3 us (39%)
  starting transfers between devices  57.4 us (24%)
  local copies, waits for them, and re-layouts  26.6 us (11%)
  blocking collectives  26.6 us (11%)
  Pallas kernels  18.4 us (8%)
  other arithmetic  10.3 us (4%)
  matrix products  5.24 us (2%)
    all_to_all x1, waiting for transfers between devices, per_device(): lax.all_to_all(after(part_rows.reshape(columns, own_rows, width), normed)...  29.1 us
    all_to_all x1, waiting for transfers between devices, per_device(): lax.all_to_all(part_slots.reshape(columns, slots_dev, width), head, 0, 0,...  27.6 us
    ppermute x14, waiting for transfers between devices, shifted(): return lax.ppermute(x, axis, [(i, (i + by) % size) for i in range(size)])  27.4 us
    all_gather x1, blocking collectives, per_device(): portion = lax.all_gather(normed, 'z', axis=0, tiled=True)  26.6 us
    ppermute x14, starting transfers between devices, shifted(): return lax.ppermute(x, axis, [(i, (i + by) % size) for i in range(size)])  20.4 us
    unnamed x63, local copies, waits for them, and re-layouts  10.4 us
    pallas_call x2, Pallas kernels, project(): pl.pallas_call(functools.partial(project_body, layout), in_specs=[pl.Bloc...  10 us
    all_to_all x1, waiting for transfers between devices, per_device(): slot_values = lax.all_to_all(outcome, 'z', 0, 0, tiled=False)  8.25 us
  transfers between devices with their start and end apart: 31, of which 15 were waited for; matrix products, arithmetic and copies ran while one was open for 13% of the time, Pallas kernels for 2%

profile of v4, /device:TPU:24, one launch (start us, length us, event | category | flops | bytes accessed | tf_op | source)
XLA Modules:
  0.0 241.5 jit_solution(6355082785259179921)
XLA Ops:
  0.0 5.9 %collective-permute-start.8 = (bf16[448,512]{1,0:T(8,128)(2,1)}, bf16[448,512]{1,0:T(8,128)(2,1)S(1)}, u32[]{:S(2)}, u32[]{:S(2)}) collective-permute-start(bf16[448,512]{1,0:T(8,128)(2,1)} %bitcast.78), channel_id=1, source_target_pairs={{0,224},{32,0},{64,32},{96,64},{128,96},{160,128},{192,160},{224,1... | collective-permute-start | bytes 1376264 | tf_op jit(solution)/shard_map/ppermute | solution.py:295
  6.7 2.3 gather_fusion
  9.0 4.8 %all-to-all-start = ((bf16[16,2,8,576]{3,2,1,0:T(8,128)(2,1)}), bf16[16,2,8,576]{3,2,1,0:T(8,128)(2,1)S(1)}, u32[]{:S(2)}, u32[]{:S(2)}) async-start(bf16[16,2,8,576]{3,2,1,0:T(8,128)(2,1)} %bitcast.8), calls=%async_computation | async-start | bytes 655360 | tf_op jit(solution)/shard_map/all_to_all | solution.py:347
  17.1 1.3 fusion.58
  22.8 2.9 %collective-permute-start.9 = (bf16[448,512]{1,0:T(8,128)(2,1)S(1)}, bf16[448,512]{1,0:T(8,128)(2,1)}, u32[]{:S(2)}, u32[]{:S(2)}) collective-permute-start(bf16[448,512]{1,0:T(8,128)(2,1)S(1)} %collective-permute-done.8.refs_16_), channel_id=1, source_target_pairs={{0,224},{32,0},{64,32},{96,64},{128,96},{160,128},{192,160},{224,1... | collective-permute-start | bytes 1376264 | tf_op jit(solution)/shard_map/ppermute | solution.py:295
  26.5 9.5 %collective-permute-done.9.refs_14_ = bf16[448,512]{1,0:T(8,128)(2,1)} collective-permute-done((bf16[448,512]{1,0:T(8,128)(2,1)S(1)}, bf16[448,512]{1,0:T(8,128)(2,1)}, u32[]{:S(2)}, u32[]{:S(2)}) %collective-permute-start.9) | collective-permute-done | bytes 458784 | tf_op jit(solution)/shard_map/ppermute | solution.py:295
  36.0 3.8 %collective-permute-start.10 = (bf16[448,512]{1,0:T(8,128)(2,1)}, bf16[448,512]{1,0:T(8,128)(2,1)S(1)}, u32[]{:S(2)}, u32[]{:S(2)}) collective-permute-start(bf16[448,512]{1,0:T(8,128)(2,1)} %collective-permute-done.9.refs_14_), channel_id=1, source_target_pairs={{0,224},{32,0},{64,32},{96,64},{128,96},{160,128},{192,160},{224,1... | collective-permute-start | bytes 1376264 | tf_op jit(solution)/shard_map/ppermute | solution.py:295
  40.5 2.0 copy_bitcast_fusion
  42.5 7.2 %all-to-all-start.1 = ((bf16[16,4,2,4,512]{4,1,2,3,0:T(4,128)(2,1)}), bf16[16,4,2,4,512]{4,1,2,3,0:T(4,128)(2,1)}, u32[]{:S(2)}, u32[]{:S(2)}) async-start(bf16[16,4,2,4,512]{4,1,2,3,0:T(4,128)(2,1)} %copy_bitcast_fusion), calls=%async_computation.1 | async-start | bytes 1048576 | tf_op jit(solution)/shard_map/all_to_all | solution.py:387
  50.1 2.4 broadcast_and_fusion
  52.5 3.4 %and.94 = pred[128,128]{1,0:T(32,128)(4,1)S(1)} reshape(pred[16,2,4,16,2,4]{5,4,3,2,1,0:T(4,128)(4,1)} %broadcast_and_fusion) | data formatting | bytes 32768 | tf_op jit(solution)/shard_map/and | solution.py:359
  56.0 2.4 all-to-all-done.1
  58.4 2.2 copy.95
  60.6 2.0 reshape.277
  62.6 1.5 collective-permute-done.5.refs_6_
  64.7 1.6 collective-permute-start.7
  66.8 1.4 convolution_convert_fusion
  68.2 4.1 %collective-permute-done.11.refs_9_ = bf16[224,512]{1,0:T(8,128)(2,1)S(1)} collective-permute-done((bf16[224,512]{1,0:T(8,128)(2,1)S(1)}, bf16[224,512]{1,0:T(8,128)(2,1)S(1)}, u32[]{:S(2)}, u32[]{:S(2)}) %collective-permute-start.11) | collective-permute-done | bytes 229408 | tf_op jit(solution)/shard_map/ppermute | solution.py:295
  72.3 1.4 collective-permute-done.7.refs_8_
  73.9 1.2 collective-permute-done.12.refs_10_
  75.1 6.0 %project_slots.1 = bf16[128,7168]{1,0:T(8,128)(2,1)} custom-call(s32[2]{0:T(128)S(1)} %pad_add_fusion.place_ref, bf16[128,512]{1,0:T(8,128)(2,1)S(1)} %convolution_convert_fusion.1.x_ref, bf16[448,512]{1,0:T(8,128)(2,1)S(1)} %bitcast.81, bf16[448,512]{1,0:T(8,128)(2,1)S(1)} %collective-permute-done.refs_1_, ...), custom_call_target="tpu_custom_call" | custom-call | flops 939524096 | bytes 9175040 | tf_op jit(solution)/shard_map/project_slots/pallas_call | solution.py:123
  81.3 7.2 %all-to-all-start.2 = ((bf16[16,8,7168]{2,1,0:T(8,128)(2,1)}), bf16[16,8,7168]{2,1,0:T(8,128)(2,1)}, u32[]{:S(2)}, u32[]{:S(2)}) async-start(bf16[16,8,7168]{2,1,0:T(8,128)(2,1)} %bitcast.23), calls=%async_computation.2 | async-start | bytes 3670016 | tf_op jit(solution)/shard_map/all_to_all | solution.py:396
  88.5 27.6 %all-to-all-done.2 = bf16[16,8,7168]{2,1,0:T(8,128)(2,1)} async-done(((bf16[16,8,7168]{2,1,0:T(8,128)(2,1)}), bf16[16,8,7168]{2,1,0:T(8,128)(2,1)}, u32[]{:S(2)}, u32[]{:S(2)}) %all-to-all-start.2) | async-done | bytes 1835040 | tf_op jit(solution)/shard_map/all_to_all | solution.py:396
  116.1 1.9 convert_reduce_fusion.1
  118.3 26.6 %all_gather.3.x_ref = bf16[64,7168]{1,0:T(8,128)(2,1)S(1)} all-gather(bf16[8,7168]{1,0:T(8,128)(2,1)S(1)} %multiply_convert_fusion.other_ref), channel_id=1, replica_groups=mesh['z'=8,'core'=2,'y'=4,'x'=4] {'z'}, dimensions={0}, use_global_device_ids=true | all-gather | bytes 1032192 | tf_op jit(solution)/shard_map/all_gather | solution.py:413
  144.9 4.1 %gate_up.1 = bf16[8,64,256]{2,1,0:T(8,128)(2,1)S(1)} custom-call(s32[1]{0:T(128)} %bitcast.1.core_ref, bf16[64,7168]{1,0:T(8,128)(2,1)S(1)} %all_gather.3.x_ref, bf16[2,7168,128]{2,1,0:T(8,128)(2,1)S(1)} %bitcast.77, bf16[2,7168,128]{2,1,0:T(8,128)(2,1)} %collective-permute-done.17.other_ref), custom_call_target="tpu_custom_call" | custom-call | flops 469762048 | bytes 8257536 | tf_op jit(solution)/shard_map/gate_up/pallas_call | solution.py:190
  149.7 4.2 %all-to-all-start.4 = ((bf16[8,64,256]{2,1,0:T(8,128)(2,1)}), bf16[8,64,256]{2,1,0:T(8,128)(2,1)S(1)}, u32[]{:S(2)}, u32[]{:S(2)}) async-start(bf16[8,64,256]{2,1,0:T(8,128)(2,1)} %copy-done.10), calls=%async_computation.4 | async-start | bytes 524288 | tf_op jit(solution)/shard_map/all_to_all | solution.py:415
  153.9 1.7 copy.117.x_ref
  155.6 1.0 copy-done.5
  156.6 1.0 copy-done.7
  157.6 1.0 copy-done.9
  158.7 0.9 copy-done.14
  163.3 4.0 %project_rows.1 = bf16[128,7168]{1,0:T(8,128)(2,1)S(1)} custom-call(s32[2]{0:T(128)S(1)} %pad_add_fusion.place_ref, bf16[128,512]{1,0:T(8,128)(2,1)S(1)} %copy-done.21, bf16[448,512]{1,0:T(8,128)(2,1)S(1)} %bitcast.82, bf16[448,512]{1,0:T(8,128)(2,1)S(1)} %collective-permute-done.refs_1_, bf16[448,512]{1,0:T(8,128)(2,1)S(1)} %collective-permute-done.1.refs_2_, ...), custom_call_target="tpu_custom_call" | custom-call | flops 939524096 | bytes 9175040 | tf_op jit(solution)/shard_map/project_rows/pallas_call | solution.py:123
  167.3 1.2 copy-done.1
  168.5 5.2 %all-to-all-start.3 = ((bf16[16,8,7168]{2,1,0:T(8,128)(2,1)}), bf16[16,8,7168]{2,1,0:T(8,128)(2,1)S(1)}, u32[]{:S(2)}, u32[]{:S(2)}) async-start(bf16[16,8,7168]{2,1,0:T(8,128)(2,1)} %after.1), calls=%async_computation.3 | async-start | bytes 3670016 | tf_op jit(solution)/shard_map/all_to_all | solution.py:407
  174.1 29.1 %all-to-all-done.3.ready_ref = bf16[16,8,7168]{2,1,0:T(8,128)(2,1)S(1)} async-done(((bf16[16,8,7168]{2,1,0:T(8,128)(2,1)}), bf16[16,8,7168]{2,1,0:T(8,128)(2,1)S(1)}, u32[]{:S(2)}, u32[]{:S(2)}) %all-to-all-start.3) | async-done | bytes 1835040 | tf_op jit(solution)/shard_map/all_to_all | solution.py:407
  203.2 3.9 %down_project.1 = bf16[8,8,896]{2,1,0:T(8,128)(2,1)} custom-call(s32[1]{0:T(128)} %bitcast.1.core_ref, bf16[8,64,256]{2,1,0:T(8,128)(2,1)S(1)} %all-to-all-done.4.x_ref, bf16[448,2048]{1,0:T(8,128)(2,1)} %bitcast.31.own_ref, bf16[448,2048]{1,0:T(8,128)(2,1)} %collective-permute-done.18.other_ref, bf16[16,8,7168]{2,1,0:T(8,128)(2,1)S(1)} %all-to-all-done.3.ready_ref), custom_call_target="tpu_custom_call" | custom-call | flops 234881024 | bytes 3670016 | tf_op jit(solution)/shard_map/down_project/pallas_call | solution.py:237
  207.1 7.2 %all-to-all-start.5 = ((bf16[8,8,896]{2,1,0:T(8,128)(2,1)}), bf16[8,8,896]{2,1,0:T(8,128)(2,1)S(1)}, u32[]{:S(2)}, u32[]{:S(2)}) async-start(bf16[8,8,896]{2,1,0:T(8,128)(2,1)} %down_project.1), calls=%async_computation.5 | async-start | bytes 229376 | tf_op jit(solution)/shard_map/all_to_all | solution.py:417
  215.0 8.3 %all-to-all-done.5.refs_0_ = bf16[8,8,896]{2,1,0:T(8,128)(2,1)S(1)} async-done(((bf16[8,8,896]{2,1,0:T(8,128)(2,1)}), bf16[8,8,896]{2,1,0:T(8,128)(2,1)S(1)}, u32[]{:S(2)}, u32[]{:S(2)}) %all-to-all-start.5) | async-done | bytes 114720 | tf_op jit(solution)/shard_map/all_to_all | solution.py:417
  223.3 1.0 collective-permute-start.20
  224.3 1.0 collective-permute-start.19
  225.6 2.5 %collective-permute-done.21.refs_3_ = bf16[8,8,896]{2,1,0:T(8,128)(2,1)S(1)} collective-permute-done((bf16[8,8,896]{2,1,0:T(8,128)(2,1)S(1)}, bf16[8,8,896]{2,1,0:T(8,128)(2,1)S(1)}, u32[]{:S(2)}, u32[]{:S(2)}) %collective-permute-start.21) | collective-permute-done | bytes 114720 | tf_op jit(solution)/shard_map/ppermute | solution.py:295
  228.1 2.2 collective-permute-done.20.refs_2_
  230.3 1.1 collective-permute-done.19.refs_1_
  231.8 1.7 collective-permute-start.22
  233.9 1.3 collective-permute-start.23
  235.5 1.2 collective-permute-done.22
  236.6 4.0 %collective-permute-done.24 = bf16[8,7168]{1,0:T(8,128)(2,1)S(1)} collective-permute-done((bf16[8,7168]{1,0:T(8,128)(2,1)S(1)}, bf16[8,7168]{1,0:T(8,128)(2,1)S(1)}, u32[]{:S(2)}, u32[]{:S(2)}) %collective-permute-start.24) | collective-permute-done | bytes 114720 | tf_op jit(solution)/shard_map/ppermute | solution.py:295
  (155 shorter events, 19.6 us)
Async XLA Ops:
  0.0 66.8 %copy-start = (bf16[4,512,128]{2,1,0:T(8,128)(2,1)S(1)}, bf16[4,512,128]{2,1,0:T(8,128)(2,1)}, u32[]{:S(2)}) copy-start(bf16[4,512,128]{2,1,0:T(8,128)(2,1)} %param.23) | copy-start | bytes 1572868
  0.0 22.3 %collective-permute-start.8 = (bf16[448,512]{1,0:T(8,128)(2,1)}, bf16[448,512]{1,0:T(8,128)(2,1)S(1)}, u32[]{:S(2)}, u32[]{:S(2)}) collective-permute-start(bf16[448,512]{1,0:T(8,128)(2,1)} %bitcast.78), channel_id=1, source_target_pairs={{0,224},{32,0},{64,32},{96,64},{128,96},{160,128},{192,160},{224,1... | collective-permute-start | bytes 1376264 | tf_op jit(solution)/shard_map/ppermute | solution.py:295
  5.9 19.9 %collective-permute-start.1 = (bf16[448,512]{1,0:T(8,128)(2,1)}, bf16[448,512]{1,0:T(8,128)(2,1)S(1)}, u32[]{:S(2)}, u32[]{:S(2)}) collective-permute-start(bf16[448,512]{1,0:T(8,128)(2,1)} %bitcast.79), channel_id=1, source_target_pairs={{0,32},{32,64},{64,96},{96,128},{128,160},{160,192},{192,224},{224... | collective-permute-start | bytes 1376264 | tf_op jit(solution)/shard_map/ppermute | solution.py:295
  5.9 58.3 %collective-permute-start = (bf16[448,512]{1,0:T(8,128)(2,1)}, bf16[448,512]{1,0:T(8,128)(2,1)S(1)}, u32[]{:S(2)}, u32[]{:S(2)}) collective-permute-start(bf16[448,512]{1,0:T(8,128)(2,1)} %bitcast.80), channel_id=1, source_target_pairs={{0,16},{16,0},{1,17},{17,1},{2,18},{18,2},{3,19},{19,3},{4,20},{20... | collective-permute-start | bytes 1376264 | tf_op jit(solution)/shard_map/ppermute | solution.py:299
  9.0 17.2 %all-to-all-start = ((bf16[16,2,8,576]{3,2,1,0:T(8,128)(2,1)}), bf16[16,2,8,576]{3,2,1,0:T(8,128)(2,1)S(1)}, u32[]{:S(2)}, u32[]{:S(2)}) async-start(bf16[16,2,8,576]{3,2,1,0:T(8,128)(2,1)} %bitcast.8), calls=%async_computation | async-start | bytes 655360 | tf_op jit(solution)/shard_map/all_to_all | solution.py:347
  22.3 42.3 %collective-permute-start.16 = (bf16[448,512]{1,0:T(8,128)(2,1)S(1)}, bf16[448,512]{1,0:T(8,128)(2,1)}, u32[]{:S(2)}, u32[]{:S(2)}) collective-permute-start(bf16[448,512]{1,0:T(8,128)(2,1)S(1)} %collective-permute-done.8.refs_16_), channel_id=1, source_target_pairs={{0,16},{16,0},{1,17},{17,1},{2,18},{18,2},{3,19},{19,3},{4,20},{20... | collective-permute-start | bytes 1376264 | tf_op jit(solution)/shard_map/ppermute | solution.py:299
  22.8 13.2 %collective-permute-start.9 = (bf16[448,512]{1,0:T(8,128)(2,1)S(1)}, bf16[448,512]{1,0:T(8,128)(2,1)}, u32[]{:S(2)}, u32[]{:S(2)}) collective-permute-start(bf16[448,512]{1,0:T(8,128)(2,1)S(1)} %collective-permute-done.8.refs_16_), channel_id=1, source_target_pairs={{0,224},{32,0},{64,32},{96,64},{128,96},{160,128},{192,160},{224,1... | collective-permute-start | bytes 1376264 | tf_op jit(solution)/shard_map/ppermute | solution.py:295
  25.7 23.9 %collective-permute-start.3 = (bf16[448,512]{1,0:T(8,128)(2,1)S(1)}, bf16[448,512]{1,0:T(8,128)(2,1)}, u32[]{:S(2)}, u32[]{:S(2)}) collective-permute-start(bf16[448,512]{1,0:T(8,128)(2,1)S(1)} %collective-permute-done.1.refs_2_), channel_id=1, source_target_pairs={{0,32},{32,64},{64,96},{96,128},{128,160},{160,192},{192,224},{224... | collective-permute-start | bytes 1376264 | tf_op jit(solution)/shard_map/ppermute | solution.py:295
  25.7 40.5 %collective-permute-start.2 = (bf16[448,512]{1,0:T(8,128)(2,1)S(1)}, bf16[448,512]{1,0:T(8,128)(2,1)}, u32[]{:S(2)}, u32[]{:S(2)}) collective-permute-start(bf16[448,512]{1,0:T(8,128)(2,1)S(1)} %collective-permute-done.1.refs_2_), channel_id=1, source_target_pairs={{0,16},{16,0},{1,17},{17,1},{2,18},{18,2},{3,19},{19,3},{4,20},{20... | collective-permute-start | bytes 1376264 | tf_op jit(solution)/shard_map/ppermute | solution.py:299
  36.0 13.8 %collective-permute-start.10 = (bf16[448,512]{1,0:T(8,128)(2,1)}, bf16[448,512]{1,0:T(8,128)(2,1)S(1)}, u32[]{:S(2)}, u32[]{:S(2)}) collective-permute-start(bf16[448,512]{1,0:T(8,128)(2,1)} %collective-permute-done.9.refs_14_), channel_id=1, source_target_pairs={{0,224},{32,0},{64,32},{96,64},{128,96},{160,128},{192,160},{224,1... | collective-permute-start | bytes 1376264 | tf_op jit(solution)/shard_map/ppermute | solution.py:295
  40.4 12.1 %copy-start.25 = (bf16[2,4,7168]{2,1,0:T(4,128)(2,1)S(1)}, bf16[2,4,7168]{2,1,0:T(4,128)(2,1)}, u32[]{:S(2)}) copy-start(bf16[2,4,7168]{2,1,0:T(4,128)(2,1)} %param.15) | copy-start | bytes 344068
  42.5 16.0 %all-to-all-start.1 = ((bf16[16,4,2,4,512]{4,1,2,3,0:T(4,128)(2,1)}), bf16[16,4,2,4,512]{4,1,2,3,0:T(4,128)(2,1)}, u32[]{:S(2)}, u32[]{:S(2)}) async-start(bf16[16,4,2,4,512]{4,1,2,3,0:T(4,128)(2,1)} %copy_bitcast_fusion), calls=%async_computation.1 | async-start | bytes 1048576 | tf_op jit(solution)/shard_map/all_to_all | solution.py:387
  49.7 16.6 %collective-permute-start.15 = (bf16[448,512]{1,0:T(8,128)(2,1)}, bf16[448,512]{1,0:T(8,128)(2,1)}, u32[]{:S(2)}, u32[]{:S(2)}) collective-permute-start(bf16[448,512]{1,0:T(8,128)(2,1)} %collective-permute-done.9.refs_14_), channel_id=1, source_target_pairs={{0,16},{16,0},{1,17},{17,1},{2,18},{18,2},{3,19},{19,3},{4,20},{20... | collective-permute-start | bytes 1376264 | tf_op jit(solution)/shard_map/ppermute | solution.py:299
  49.8 14.3 %collective-permute-start.5 = (bf16[448,512]{1,0:T(8,128)(2,1)}, bf16[448,512]{1,0:T(8,128)(2,1)S(1)}, u32[]{:S(2)}, u32[]{:S(2)}) collective-permute-start(bf16[448,512]{1,0:T(8,128)(2,1)} %collective-permute-done.3.refs_4_), channel_id=1, source_target_pairs={{0,32},{32,64},{64,96},{96,128},{128,160},{160,192},{192,224},{224... | collective-permute-start | bytes 1376264 | tf_op jit(solution)/shard_map/ppermute | solution.py:295
  52.5 22.6 %copy-start.11 = (bf16[8,7168]{1,0:T(8,128)(2,1)}, bf16[8,7168]{1,0:T(8,128)(2,1)S(1)}, u32[]{:S(2)}) copy-start(bf16[8,7168]{1,0:T(8,128)(2,1)S(1)} %reshape.272.refs_19_) | copy-start | bytes 344068
  58.4 16.7 %copy-start.3 = (bf16[512,448]{0,1:T(8,128)(2,1)S(1)}, bf16[512,448]{0,1:T(8,128)(2,1)}, u32[]{:S(2)}) copy-start(bf16[512,448]{0,1:T(8,128)(2,1)} %param.24) | copy-start | bytes 1376260
  64.1 9.7 %collective-permute-start.4 = (bf16[448,512]{1,0:T(8,128)(2,1)}, bf16[448,512]{1,0:T(8,128)(2,1)S(1)}, u32[]{:S(2)}, u32[]{:S(2)}) collective-permute-start(bf16[448,512]{1,0:T(8,128)(2,1)} %collective-permute-done.3.refs_4_), channel_id=1, source_target_pairs={{0,16},{16,0},{1,17},{17,1},{2,18},{18,2},{3,19},{19,3},{4,20},{20... | collective-permute-start | bytes 1376264 | tf_op jit(solution)/shard_map/ppermute | solution.py:299
  64.2 8.1 %collective-permute-start.11 = (bf16[224,512]{1,0:T(8,128)(2,1)S(1)}, bf16[224,512]{1,0:T(8,128)(2,1)S(1)}, u32[]{:S(2)}, u32[]{:S(2)}) collective-permute-start(bf16[224,512]{1,0:T(8,128)(2,1)S(1)} %slice.68), channel_id=1, source_target_pairs={{0,224},{32,0},{64,32},{96,64},{128,96},{160,128},{192,160},{224,1... | collective-permute-start | bytes 688136 | tf_op jit(solution)/shard_map/ppermute | solution.py:295
  64.7 8.9 %collective-permute-start.7 = (bf16[224,512]{1,0:T(8,128)(2,1)S(1)}, bf16[224,512]{1,0:T(8,128)(2,1)S(1)}, u32[]{:S(2)}, u32[]{:S(2)}) collective-permute-start(bf16[224,512]{1,0:T(8,128)(2,1)S(1)} %slice.67), channel_id=1, source_target_pairs={{0,32},{32,64},{64,96},{96,128},{128,160},{160,192},{192,224},{224... | collective-permute-start | bytes 688136 | tf_op jit(solution)/shard_map/ppermute | solution.py:295
  66.3 7.6 %collective-permute-start.14 = (bf16[448,512]{1,0:T(8,128)(2,1)S(1)}, bf16[448,512]{1,0:T(8,128)(2,1)S(1)}, u32[]{:S(2)}, u32[]{:S(2)}) collective-permute-start(bf16[448,512]{1,0:T(8,128)(2,1)S(1)} %collective-permute-done.10.refs_12_), channel_id=1, source_target_pairs={{0,16},{16,0},{1,17},{17,1},{2,18},{18,2},{3,19},{19,3},{4,20},{20... | collective-permute-start | bytes 1376264 | tf_op jit(solution)/shard_map/ppermute | solution.py:299
  66.3 8.8 %collective-permute-start.6 = (bf16[448,512]{1,0:T(8,128)(2,1)S(1)}, bf16[448,512]{1,0:T(8,128)(2,1)S(1)}, u32[]{:S(2)}, u32[]{:S(2)}) collective-permute-start(bf16[448,512]{1,0:T(8,128)(2,1)S(1)} %collective-permute-done.5.refs_6_), channel_id=1, source_target_pairs={{0,16},{16,0},{1,17},{17,1},{2,18},{18,2},{3,19},{19,3},{4,20},{20... | collective-permute-start | bytes 1376264 | tf_op jit(solution)/shard_map/ppermute | solution.py:299
  68.2 6.9 %copy-start.23 = (bf16[4,128,128]{1,2,0:T(8,128)(2,1)}, bf16[4,128,128]{1,2,0:T(8,128)(2,1)S(1)}, u32[]{:S(2)}) copy-start(bf16[4,128,128]{1,2,0:T(8,128)(2,1)S(1)} %convolution_convert_fusion) | copy-start | bytes 393220
  72.2 8.9 %copy-start.13 = (bf16[224,512]{1,0:T(8,128)(2,1)}, bf16[224,512]{1,0:T(8,128)(2,1)S(1)}, u32[]{:S(2)}) copy-start(bf16[224,512]{1,0:T(8,128)(2,1)S(1)} %collective-permute-done.11.refs_9_) | copy-start | bytes 688132
  72.2 1.6 collective-permute-start.13
  73.6 7.6 %copy-start.15 = (bf16[224,512]{1,0:T(8,128)(2,1)}, bf16[224,512]{1,0:T(8,128)(2,1)S(1)}, u32[]{:S(2)}) copy-start(bf16[224,512]{1,0:T(8,128)(2,1)S(1)} %collective-permute-done.7.refs_8_) | copy-start | bytes 688132
  73.6 1.5 collective-permute-start.12
  73.8 7.4 %copy-start.4 = (bf16[448,512]{1,0:T(8,128)(2,1)}, bf16[448,512]{1,0:T(8,128)(2,1)S(1)}, u32[]{:S(2)}) copy-start(bf16[448,512]{1,0:T(8,128)(2,1)S(1)} %collective-permute-done.4.refs_5_) | copy-start | bytes 1376260
  73.8 7.4 %copy-start.17 = (bf16[224,512]{1,0:T(8,128)(2,1)}, bf16[224,512]{1,0:T(8,128)(2,1)S(1)}, u32[]{:S(2)}) copy-start(bf16[224,512]{1,0:T(8,128)(2,1)S(1)} %collective-permute-done.13.refs_11_) | copy-start | bytes 688132
  73.9 7.3 %copy-start.6 = (bf16[448,512]{1,0:T(8,128)(2,1)}, bf16[448,512]{1,0:T(8,128)(2,1)S(1)}, u32[]{:S(2)}) copy-start(bf16[448,512]{1,0:T(8,128)(2,1)S(1)} %collective-permute-done.14.refs_13_) | copy-start | bytes 1376260
  75.1 6.1 %copy-start.19 = (bf16[224,512]{1,0:T(8,128)(2,1)}, bf16[224,512]{1,0:T(8,128)(2,1)S(1)}, u32[]{:S(2)}) copy-start(bf16[224,512]{1,0:T(8,128)(2,1)S(1)} %collective-permute-done.12.refs_10_) | copy-start | bytes 688132
  75.1 6.1 %copy-start.8 = (bf16[448,512]{1,0:T(8,128)(2,1)}, bf16[448,512]{1,0:T(8,128)(2,1)S(1)}, u32[]{:S(2)}) copy-start(bf16[448,512]{1,0:T(8,128)(2,1)S(1)} %collective-permute-done.6.refs_7_) | copy-start | bytes 1376260
  81.2 36.9 %copy-start.29 = (f32[7168]{0:T(1024)S(1)}, f32[7168]{0:T(1024)}, u32[]{:S(2)}) copy-start(f32[7168]{0:T(1024)} %param.25) | copy-start | bytes 86020
  81.3 34.8 %all-to-all-start.2 = ((bf16[16,8,7168]{2,1,0:T(8,128)(2,1)}), bf16[16,8,7168]{2,1,0:T(8,128)(2,1)}, u32[]{:S(2)}, u32[]{:S(2)}) async-start(bf16[16,8,7168]{2,1,0:T(8,128)(2,1)} %bitcast.23), calls=%async_computation.2 | async-start | bytes 3670016 | tf_op jit(solution)/shard_map/all_to_all | solution.py:396
  88.4 56.4 %collective-permute-start.17 = (bf16[2,7168,128]{2,1,0:T(8,128)(2,1)}, bf16[2,7168,128]{2,1,0:T(8,128)(2,1)}, u32[]{:S(2)}, u32[]{:S(2)}) collective-permute-start(bf16[2,7168,128]{2,1,0:T(8,128)(2,1)} %bitcast.76), channel_id=1, source_target_pairs={{0,16},{16,0},{1,17},{17,1},{2,18},{18,2},{3,19},{19,3},{4,20},{20... | collective-permute-start | bytes 11010056 | tf_op jit(solution)/shard_map/ppermute | solution.py:299
  116.1 28.8 %copy-start.2 = (bf16[1,2,7168,128]{3,2,1,0:T(8,128)(2,1)S(1)}, bf16[1,2,7168,128]{3,2,1,0:T(8,128)(2,1)}, u32[]{:S(2)}) copy-start(bf16[1,2,7168,128]{3,2,1,0:T(8,128)(2,1)} %param.28) | copy-start | bytes 11010052
  118.3 26.6 %copy-start.24 = (bf16[8,7168]{1,0:T(8,128)(2,1)}, bf16[8,7168]{1,0:T(8,128)(2,1)S(1)}, u32[]{:S(2)}) copy-start(bf16[8,7168]{1,0:T(8,128)(2,1)S(1)} %multiply_convert_fusion.other_ref) | copy-start | bytes 344068
  149.7 18.8 %all-to-all-start.4 = ((bf16[8,64,256]{2,1,0:T(8,128)(2,1)}), bf16[8,64,256]{2,1,0:T(8,128)(2,1)S(1)}, u32[]{:S(2)}, u32[]{:S(2)}) async-start(bf16[8,64,256]{2,1,0:T(8,128)(2,1)} %copy-done.10), calls=%async_computation.4 | async-start | bytes 524288 | tf_op jit(solution)/shard_map/all_to_all | solution.py:415
  153.9 20.2 %collective-permute-start.18 = (bf16[448,2048]{1,0:T(8,128)(2,1)}, bf16[448,2048]{1,0:T(8,128)(2,1)}, u32[]{:S(2)}, u32[]{:S(2)}) collective-permute-start(bf16[448,2048]{1,0:T(8,128)(2,1)} %bitcast.31.own_ref), channel_id=1, source_target_pairs={{0,16},{16,0},{1,17},{17,1},{2,18},{18,2},{3,19},{19,3},{4,20},{20... | collective-permute-start | bytes 5505032 | tf_op jit(solution)/shard_map/ppermute | solution.py:299
  168.5 5.4 %copy-start.27 = (s32[16,2,64]{2,0,1:T(8,128)S(1)}, s32[16,2,64]{2,0,1:T(8,128)}, u32[]{:S(2)}) copy-start(s32[16,2,64]{2,0,1:T(8,128)} %copy-done.26) | copy-start | bytes 24580
  168.5 34.7 %all-to-all-start.3 = ((bf16[16,8,7168]{2,1,0:T(8,128)(2,1)}), bf16[16,8,7168]{2,1,0:T(8,128)(2,1)S(1)}, u32[]{:S(2)}, u32[]{:S(2)}) async-start(bf16[16,8,7168]{2,1,0:T(8,128)(2,1)} %after.1), calls=%async_computation.3 | async-start | bytes 3670016 | tf_op jit(solution)/shard_map/all_to_all | solution.py:407
  207.1 16.1 %all-to-all-start.5 = ((bf16[8,8,896]{2,1,0:T(8,128)(2,1)}), bf16[8,8,896]{2,1,0:T(8,128)(2,1)S(1)}, u32[]{:S(2)}, u32[]{:S(2)}) async-start(bf16[8,8,896]{2,1,0:T(8,128)(2,1)} %down_project.1), calls=%async_computation.5 | async-start | bytes 229376 | tf_op jit(solution)/shard_map/all_to_all | solution.py:417
  214.7 26.0 %copy-start.12 = (bf16[8,7168]{1,0:T(8,128)(2,1)S(1)}, bf16[8,7168]{1,0:T(8,128)(2,1)}, u32[]{:S(2)}) copy-start(bf16[8,7168]{1,0:T(8,128)(2,1)} %copy-done.11) | copy-start | bytes 344068
  223.3 4.8 %collective-permute-start.21 = (bf16[8,8,896]{2,1,0:T(8,128)(2,1)S(1)}, bf16[8,8,896]{2,1,0:T(8,128)(2,1)S(1)}, u32[]{:S(2)}, u32[]{:S(2)}) collective-permute-start(bf16[8,8,896]{2,1,0:T(8,128)(2,1)S(1)} %all-to-all-done.5.refs_0_), channel_id=1, source_target_pairs={{0,3},{1,0},{2,1},{3,2},{4,7},{5,4},{6,5},{7,6},{8,11},{9,8},{10,9... | collective-permute-start | bytes 344072 | tf_op jit(solution)/shard_map/ppermute | solution.py:295
  223.3 7.0 %collective-permute-start.20 = (bf16[8,8,896]{2,1,0:T(8,128)(2,1)S(1)}, bf16[8,8,896]{2,1,0:T(8,128)(2,1)S(1)}, u32[]{:S(2)}, u32[]{:S(2)}) collective-permute-start(bf16[8,8,896]{2,1,0:T(8,128)(2,1)S(1)} %all-to-all-done.5.refs_0_), channel_id=1, source_target_pairs={{0,2},{1,3},{2,0},{3,1},{4,6},{5,7},{6,4},{7,5},{8,10},{9,11},{10,... | collective-permute-start | bytes 344072 | tf_op jit(solution)/shard_map/ppermute | solution.py:295
  224.3 7.1 %collective-permute-start.19 = (bf16[8,8,896]{2,1,0:T(8,128)(2,1)S(1)}, bf16[8,8,896]{2,1,0:T(8,128)(2,1)S(1)}, u32[]{:S(2)}, u32[]{:S(2)}) collective-permute-start(bf16[8,8,896]{2,1,0:T(8,128)(2,1)S(1)} %all-to-all-done.5.refs_0_), channel_id=1, source_target_pairs={{0,1},{1,2},{2,3},{3,0},{4,5},{5,6},{6,7},{7,4},{8,9},{9,10},{10,1... | collective-permute-start | bytes 344072 | tf_op jit(solution)/shard_map/ppermute | solution.py:295
  231.8 4.9 %collective-permute-start.22 = (bf16[8,7168]{1,0:T(8,128)(2,1)S(1)}, bf16[8,7168]{1,0:T(8,128)(2,1)S(1)}, u32[]{:S(2)}, u32[]{:S(2)}) collective-permute-start(bf16[8,7168]{1,0:T(8,128)(2,1)S(1)} %get-tuple-element.9), channel_id=1, source_target_pairs={{0,4},{4,8},{8,12},{12,0},{1,5},{5,9},{9,13},{13,1},{2,6},{6,10},{... | collective-permute-start | bytes 344072 | tf_op jit(solution)/shard_map/ppermute | solution.py:295
  233.4 7.2 %collective-permute-start.24 = (bf16[8,7168]{1,0:T(8,128)(2,1)S(1)}, bf16[8,7168]{1,0:T(8,128)(2,1)S(1)}, u32[]{:S(2)}, u32[]{:S(2)}) collective-permute-start(bf16[8,7168]{1,0:T(8,128)(2,1)S(1)} %get-tuple-element.10), channel_id=1, source_target_pairs={{0,12},{4,0},{8,4},{12,8},{1,13},{5,1},{9,5},{13,9},{2,14},{6,2},{... | collective-permute-start | bytes 344072 | tf_op jit(solution)/shard_map/ppermute | solution.py:295
  233.9 6.8 %collective-permute-start.23 = (bf16[8,7168]{1,0:T(8,128)(2,1)S(1)}, bf16[8,7168]{1,0:T(8,128)(2,1)S(1)}, u32[]{:S(2)}, u32[]{:S(2)}) collective-permute-start(bf16[8,7168]{1,0:T(8,128)(2,1)S(1)} %get-tuple-element.11), channel_id=1, source_target_pairs={{0,8},{4,12},{8,0},{12,4},{1,9},{5,13},{9,1},{13,5},{2,10},{6,14},... | collective-permute-start | bytes 344072 | tf_op jit(solution)/shard_map/ppermute | solution.py:295
  (14 other events, 25.6 us)

commit v5 on v4

--- a/solution.py
+++ b/solution.py
@@ -48,7 +48,7 @@
 
 
 def routing(ids, weights, experts):
-    matched = ids[None] == jnp.arange(experts, dtype=jnp.int32)[:, None, None, None]
+    matched = ids[None] == experts[:, None, None, None]
     present = jnp.any(matched, axis=3)
     row_weight = jnp.sum(jnp.where(matched, weights[None], 0.0), axis=3)
     rows = ids.shape[1]
@@ -69,85 +69,193 @@
 NT = (((1,), (1,)), ((), ()))
 
 
+def part_body(start, block_ref, ready_ref, out_ref, sem):
+    del ready_ref
+    copy = pltpu.make_async_copy(block_ref.at[pl.ds(start, out_ref.shape[0])], out_ref, sem)
+    copy.start()
+    copy.wait()
+
+
+def part_after(block, start, size, ready):
+    anywhere = pl.BlockSpec(memory_space=pltpu.HBM)
+    return pl.pallas_call(
+        functools.partial(part_body, start),
+        in_specs=[anywhere, anywhere],
+        out_specs=anywhere,
+        out_shape=jax.ShapeDtypeStruct((size, block.shape[1]), block.dtype),
+        scratch_shapes=[pltpu.SemaphoreType.DMA(())],
+        name="part_after",
+    )(block, ready)
+
+
 def spread_blocks(block):
-    chips = lax.axis_size("z")
-    far = chips // 2
+    up = down = block
+    steps = []
+    for _ in range(1, lax.axis_size("z") // 2):
+        up, down = shifted(up, "z", 1), shifted(down, "z", -1)
+        steps.append((up, down))
+    return steps
+
+
+def all_blocks(block, steps, ready):
     half = block.shape[0] // 2
-    own = [None] * chips
-    own[0] = [block]
-    up = down = block
-    for k in range(1, far):
-        up, down = shifted(up, "z", 1), shifted(down, "z", -1)
-        own[k], own[chips - k] = [up], [down]
-    own[far] = [shifted(up[:half], "z", 1), shifted(down[half:], "z", -1)]
-    other = [[swap_cores(part) for part in parts] for parts in own]
-    return own, other
-
-
-def project_body(layout, place_ref, x_ref, *refs):
-    blocks = refs[: sum(map(sum, layout))]
-    *carry, out_ref = refs[len(blocks) :]
+    (up, down), far = steps[-1], lax.axis_size("z") // 2
+    last = [
+        shifted(part_after(up, 0, half, ready), "z", 1),
+        shifted(part_after(down, half, half, ready), "z", -1),
+    ]
+    own = [[block]] + [[u] for u, _ in steps] + [last] + [[d] for _, d in steps[::-1]]
+    assert len(own) == 2 * far
+    return own, [[swap_cores(part) for part in parts] for parts in own]
+
+
+def project_body(layout, place_ref, by_ref, uv_ref, select_ref, own_ref, hidden_ref, *refs):
+    total = sum(map(sum, layout))
+    blocks, outs = refs[:total], refs[total:-5]
+    held, slots_ref, rows_ref, sems, out_sems = refs[-5:]
     chips = len(layout)
-    x = x_ref[...]
+    copies, at, start = [], 0, 0
+    for counts in layout:
+        for count in counts:
+            for r in blocks[at : at + count]:
+                size = r.shape[0]
+                copies.append(pltpu.make_async_copy(r, held.at[pl.ds(start, size)], sems.at[at]))
+                copies[-1].start()
+                at, start = at + 1, start + size
+    values = []
+    for k in range(uv_ref.shape[0]):
+        context = by_ref[:, k].astype(jnp.float32).reshape(-1, by_ref.shape[3])
+        values.append(
+            jnp.dot(context.astype(jnp.bfloat16), uv_ref[k], preferred_element_type=jnp.float32)
+        )
+    values = jnp.concatenate(values, axis=1).astype(jnp.bfloat16)
+    x = jnp.dot(select_ref[...], values, preferred_element_type=jnp.float32).astype(jnp.bfloat16)
+    half = slots_ref.shape[0]
+    each = rows_ref.shape[1]
     first = place_ref[1] == 0
-    at = 0
+    at, start = 0, 0
+    width = held.shape[0] // chips
+    core_width = width // 2
+    leaving = []
     for k, counts in enumerate(layout):
-        pair = []
-        for count in counts:
-            parts = [
-                lax.dot_general(x, r[...], NT, preferred_element_type=jnp.float32)
-                for r in blocks[at : at + count]
-            ]
-            pair.append(parts[0] if count == 1 else jnp.concatenate(parts, axis=1))
-            at += count
+        for _ in range(sum(counts)):
+            copies[at].wait()
+            at += 1
+        pair = [
+            lax.dot_general(
+                x,
+                held[start + c * core_width : start + (c + 1) * core_width],
+                NT,
+                preferred_element_type=jnp.float32,
+            )
+            for c in range(2)
+        ]
+        start += width
         whole = jnp.concatenate(
             [jnp.where(first, pair[0], pair[1]), jnp.where(first, pair[1], pair[0])], axis=1
         )
-        width = whole.shape[1]
         chip = lax.rem(place_ref[0] + (chips - k), chips)
         columns = pl.ds(pl.multiple_of(chip * width, 128), width)
-        if carry:
-            own_ref, hidden_ref = carry
-            whole += jnp.dot(
-                own_ref[...], hidden_ref[:, columns], preferred_element_type=jnp.float32
+        carried = jnp.dot(own_ref[...], hidden_ref[:, columns], preferred_element_type=jnp.float32)
+        slots_ref[:, columns] = (whole[:half] + carried).astype(jnp.bfloat16)
+        for j in range(rows_ref.shape[0]):
+            row = half + j * each
+            rows_ref[j, :, columns] = whole[row : row + each].astype(jnp.bfloat16)
+        for j, out_ref in enumerate(outs):
+            source = slots_ref if j == 0 else rows_ref.at[j - 1]
+            leaving.append(
+                pltpu.make_async_copy(
+                    source.at[:, columns], out_ref.at[:, columns], out_sems.at[j, k]
+                )
             )
-        out_ref[:, columns] = whole.astype(jnp.bfloat16)
-
-
-def project(place, x, own, other, carry=()):
+            leaving[-1].start()
+    for copy in leaving:
+        copy.wait()
+
+
+def project(place, by_head, w_uv, select, own, other, chooser, hidden, outer, inner):
     layout = [(len(a), len(b)) for a, b in zip(own, other)]
     blocks = [part for pair in zip(own, other) for parts in pair for part in parts]
-    rows, depth = x.shape
+    rows, depth = select.shape[0], blocks[0].shape[1]
+    half = rows // 2
     width = sum(part.shape[0] for part in blocks)
+    each = half // inner
     vmem = pl.BlockSpec(memory_space=pltpu.VMEM)
+    anywhere = pl.BlockSpec(memory_space=pltpu.HBM)
     return pl.pallas_call(
         functools.partial(project_body, layout),
-        in_specs=[pl.BlockSpec(memory_space=pltpu.SMEM)] + [vmem] * (1 + len(blocks) + len(carry)),
-        out_specs=vmem,
-        out_shape=jax.ShapeDtypeStruct((rows, width), jnp.bfloat16),
-        compiler_params=pltpu.CompilerParams(vmem_limit_bytes=24 * 1024 * 1024),
+        in_specs=[pl.BlockSpec(memory_space=pltpu.SMEM)] + [vmem] * 5 + [anywhere] * len(blocks),
+        out_specs=[anywhere] * (1 + inner),
+        out_shape=[jax.ShapeDtypeStruct((half, width), jnp.bfloat16)]
+        + [jax.ShapeDtypeStruct((each, width), jnp.bfloat16)] * inner,
+        scratch_shapes=[
+            pltpu.VMEM((width, depth), jnp.bfloat16),
+            pltpu.VMEM((half, width), jnp.bfloat16),
+            pltpu.VMEM((inner, each, width), jnp.bfloat16),
+            pltpu.SemaphoreType.DMA((len(blocks),)),
+            pltpu.SemaphoreType.DMA((1 + inner, len(layout))),
+        ],
+        compiler_params=pltpu.CompilerParams(vmem_limit_bytes=58 * 1024 * 1024),
         cost_estimate=pl.CostEstimate(
             flops=2 * rows * depth * width,
             bytes_accessed=2 * depth * width + 2 * rows * width,
             transcendentals=0,
         ),
-        name="project_slots" if carry else "project_rows",
-    )(place, x, *blocks, *carry)
-
-
-def after_body(x_ref, other_ref, out_ref):
-    del x_ref, other_ref, out_ref
-
-
-def after(x, other):
+        name="project",
+    )(place, by_head, w_uv, select, chooser, hidden, *blocks)
+
+
+def after_body(*refs):
+    del refs
+
+
+def after(x, *others):
     return pl.pallas_call(
         after_body,
-        in_specs=[pl.BlockSpec(memory_space=pl.ANY)] * 2,
-        out_specs=pl.BlockSpec(memory_space=pl.ANY),
+        in_specs=[pl.BlockSpec(memory_space=pltpu.HBM)] * (1 + len(others)),
+        out_specs=pl.BlockSpec(memory_space=pltpu.HBM),
         out_shape=jax.ShapeDtypeStruct(x.shape, x.dtype),
         input_output_aliases={0: 0},
         name="after",
-    )(x, other)
+    )(x, *others)
+
+
+def norm_body(parts_ref, gain_ref, *refs):
+    total, out_ref = refs[-1], refs[(len(refs) - 2) // 2]
+    parts, _, width = parts_ref.shape
+    tile = width // 8
+    squares = 0.0
+    for k in range(8):
+        at = slice(k * tile, (k + 1) * tile)
+        here = parts_ref[0, :, at].astype(jnp.float32)
+        for j in range(1, parts):
+            here += parts_ref[j, :, at].astype(jnp.float32)
+        total[:, at] = here
+        squares += jnp.sum(here * here, axis=1, keepdims=True)
+    scale = lax.rsqrt(squares * (1.0 / width) + 1e-06)
+    for k in range(8):
+        at = slice(k * tile, (k + 1) * tile)
+        out_ref[:, at] = (total[:, at] * scale * gain_ref[:, at]).astype(jnp.bfloat16)
+
+
+def norm(parts, gain, held):
+    _, rows, width = parts.shape
+    vmem = pl.BlockSpec(memory_space=pltpu.VMEM)
+    anywhere = pl.BlockSpec(memory_space=pltpu.HBM)
+    return pl.pallas_call(
+        norm_body,
+        in_specs=[vmem, vmem] + [anywhere] * len(held),
+        out_specs=[vmem] + [anywhere] * len(held),
+        out_shape=[jax.ShapeDtypeStruct((rows, width), jnp.bfloat16)]
+        + [jax.ShapeDtypeStruct(h.shape, h.dtype) for h in held],
+        scratch_shapes=[pltpu.VMEM((rows, width), jnp.float32)],
+        input_output_aliases={2 + k: 1 + k for k in range(len(held))},
+        compiler_params=pltpu.CompilerParams(vmem_limit_bytes=16 * 1024 * 1024),
+        cost_estimate=pl.CostEstimate(
+            flops=2 * parts.size, bytes_accessed=2 * parts.size, transcendentals=0
+        ),
+        name="norm",
+    )(parts, gain, *held)
 
 
 def gate_up_body(core_ref, x_ref, own_ref, other_ref, active_ref, gate, up):
@@ -209,8 +317,8 @@
     )(core, x, own, other)
 
 
-def down_body(core_ref, x_ref, own_ref, other_ref, ready_ref, out_ref):
-    del ready_ref
+def down_body(core_ref, x_ref, own_ref, other_ref, *refs):
+    out_ref = refs[-1]
     x = jnp.concatenate([x_ref[k] for k in range(x_ref.shape[0])], axis=1)
     half = own_ref.shape[0]
     parts, each = out_ref.shape[0], out_ref.shape[1]
@@ -230,7 +338,7 @@
         write(others, mine)
 
 
-def down_project(core, x, own, other, ready):
+def down_project(core, x, own, other, *ready):
     parts, rows, _ = x.shape
     columns = 2 * own.shape[0]
     vmem = pl.BlockSpec(memory_space=pltpu.VMEM)
@@ -241,7 +349,7 @@
             vmem,
             vmem,
             vmem,
-            pl.BlockSpec(memory_space=pl.ANY),
+            *[pl.BlockSpec(memory_space=pltpu.HBM)] * len(ready),
         ],
         out_specs=vmem,
         out_shape=jax.ShapeDtypeStruct((parts, rows // parts, columns), jnp.bfloat16),
@@ -252,42 +360,51 @@
             transcendentals=0,
         ),
         name="down_project",
-    )(core, x, own, other, ready)
-
-
-def combine_body(spread_ref, *refs):
-    blocks, out_ref = refs[:-1], refs[-1]
+    )(core, x, own, other, *ready)
+
+
+def combine_body(count, spread_ref, hidden_ref, *refs):
+    blocks, sums, (here_ref, *away) = refs[:count], refs[count : 2 * count], refs[2 * count :]
     weight = spread_ref[...]
     high = weight.astype(jnp.bfloat16)
     low = (weight - high.astype(jnp.float32)).astype(jnp.bfloat16)
     parts, _, width = blocks[0].shape
+    each = here_ref.shape[0]
     for k in range(parts):
         slots = jnp.concatenate([b[k].astype(jnp.float32) for b in blocks], axis=0)
         slots = slots.astype(jnp.bfloat16)
         mixed = jnp.dot(high, slots, preferred_element_type=jnp.float32) + jnp.dot(
             low, slots, preferred_element_type=jnp.float32
         )
-        mixed = mixed.astype(jnp.bfloat16).reshape(*out_ref.shape[:2], width)
-        out_ref[:, :, k * width : (k + 1) * width] = mixed
-
-
-def combine(spread, blocks, each):
-    rows = spread.shape[0]
-    width = blocks[0].shape[0] * blocks[0].shape[2]
+        at = slice(k * width, (k + 1) * width)
+        for r in sums:
+            mixed += r[:, at].astype(jnp.float32)
+        for y in range(1 + len(away)):
+            row = mixed[y * each : (y + 1) * each]
+            if y == 0:
+                here_ref[:, at] = row + hidden_ref[:, at].astype(jnp.float32)
+            else:
+                away[y - 1][:, at] = row.astype(jnp.bfloat16)
+
+
+def combine(spread, hidden, blocks, sums):
+    each, width = hidden.shape
+    outer = spread.shape[0] // each
     vmem = pl.BlockSpec(memory_space=pltpu.VMEM)
-    return pl.pallas_call(
-        combine_body,
-        in_specs=[vmem] * (1 + len(blocks)),
-        out_specs=vmem,
-        out_shape=jax.ShapeDtypeStruct((rows // each, each, width), jnp.bfloat16),
+    away = jax.ShapeDtypeStruct((each, width), jnp.bfloat16)
+    return pl.pallas_call(
+        functools.partial(combine_body, len(blocks)),
+        in_specs=[vmem] * (2 + len(blocks) + len(sums)),
+        out_specs=[vmem] * outer,
+        out_shape=[jax.ShapeDtypeStruct((each, width), jnp.float32)] + [away] * (outer - 1),
         compiler_params=pltpu.CompilerParams(vmem_limit_bytes=16 * 1024 * 1024),
         cost_estimate=pl.CostEstimate(
-            flops=4 * rows * spread.shape[1] * width,
-            bytes_accessed=2 * (rows + spread.shape[1]) * width,
+            flops=4 * spread.shape[0] * spread.shape[1] * width,
+            bytes_accessed=10 * spread.shape[0] * width,
             transcendentals=0,
         ),
         name="combine",
-    )(spread, *blocks)
+    )(spread, hidden, *blocks, *sums)
 
 
 def shifted(x, axis, by):
@@ -332,7 +449,10 @@
     slots_dev = steps * CAP
 
     place = jnp.stack([lax.axis_index("z"), core]).astype(jnp.int32)
-    w_own, w_other = spread_blocks(w_o.T)
+    ring = spread_blocks(w_o.T)
+    came = [[part[:8, :128] for part in parts] for parts in ring]
+    experts = after(jnp.arange(columns, dtype=jnp.int32), *came[0])
+    res_len = after(res_len, *came[0])
     gu_other = swap_cores(w_gu[0])
     down = w_down[0].T
     down_other = swap_cores(down)
@@ -343,6 +463,7 @@
     order = jnp.sum(jnp.where(claimed, places[None, :], 0), axis=1)
     len_sorted = jnp.sum(jnp.where(claimed, pre_len[0][None, :], 0), axis=1)
     new_len = lax.dynamic_slice(len_sorted, (group_index * newcomers,), (newcomers,))
+    new_len = after(new_len, *came[1])
     sorted_cache = jnp.take(pre_cache[0], order, axis=0, mode="clip")
     taken = lax.all_to_all(
         sorted_cache.reshape(groups, newcomers, *sorted_cache.shape[1:]),
@@ -353,7 +474,7 @@
     )
     taken = jnp.swapaxes(taken, 0, 1).reshape(newcomers, -1, sorted_cache.shape[2])
 
-    chosen, row_weight = routing(expert_ids, route_weight, columns)
+    chosen, row_weight = routing(expert_ids, route_weight, experts)
     by_row = chosen.reshape(columns, steps, CAP, columns, rows_dev)
     same = jnp.arange(steps)[:, None] == jnp.arange(steps)[None, :]
     chooser = by_row[:, :, :, :, None, :] & same[None, :, None, None, :, None]
@@ -384,42 +505,35 @@
         axis=0,
     )
     context = context.reshape(rows_dev, steps, columns, heads_dev, LAT).transpose(2, 3, 1, 0, 4)
+    context = context.reshape(columns, heads_dev, own_rows, LAT)
+    w_own, w_other = all_blocks(w_o.T, ring, context[0, 0, :, :128])
     by_head = lax.all_to_all(context, head, split_axis=0, concat_axis=0, tiled=False)
-    by_head = jnp.swapaxes(by_head, 0, 1).reshape(heads_dev, rows_group, LAT)
-    values = jnp.einsum("hrl,hlv->rhv", by_head, w_uv, preferred_element_type=jnp.float32).astype(
-        jnp.bfloat16
-    )
-    values = values.reshape(rows_group, heads_dev * VD)
-    values_slots = jnp.dot(chooser, values, preferred_element_type=jnp.float32).astype(jnp.bfloat16)
     hidden_own = hidden_in.reshape(own_rows, width)
-    part_slots = project(place, values_slots, w_own, w_other, (own_chooser, hidden_own))
+    from_x = (at_x + jnp.arange(short, dtype=jnp.int32)) % short
+    from_y = (at_y + jnp.arange(long, dtype=jnp.int32)) % long
+    row_from = (from_y[None, :, None] * short + from_x[:, None, None]) * own_rows
+    row_from = (row_from + jnp.arange(own_rows, dtype=jnp.int32)).reshape(-1)
+    turned = row_from[:, None] == jnp.arange(rows_group, dtype=jnp.int32)[None, :]
+    select = jnp.concatenate([chooser, turned.astype(jnp.bfloat16)], axis=0)
+    part_slots, row_here, *row_away = project(
+        place, by_head, w_uv, select, w_own, w_other, own_chooser, hidden_own, long, short
+    )
     slot_parts = lax.all_to_all(
         part_slots.reshape(columns, slots_dev, width), head, 0, 0, tiled=False
     )
-    part_rows = project(place, values, w_own, w_other)
-    slot_rows = jnp.sum(slot_parts.astype(jnp.float32), axis=0)
-    normed = (
-        slot_rows
-        * lax.rsqrt(jnp.mean(slot_rows * slot_rows, axis=1, keepdims=True) + 1e-06)
-        * norm_gain
-    ).astype(jnp.bfloat16)
-
-    row_parts = lax.all_to_all(
-        after(part_rows.reshape(columns, own_rows, width), normed), head, 0, 0, tiled=False
-    )
-    summed = hidden_own.astype(jnp.float32) + jnp.sum(row_parts.astype(jnp.float32), axis=0)
+    normed, *row_away = norm(slot_parts, norm_gain[None], row_away)
+    row_parts = [row_here] + [shifted(r, "x", k + 1) for k, r in enumerate(row_away)]
 
     core_now = jnp.reshape(core, (1,)).astype(jnp.int32)
     portion = lax.all_gather(normed, "z", axis=0, tiled=True)
     active = gate_up(core_now, portion, w_gu[0], gu_other, chips)
     everywhere = lax.all_to_all(active, "z", 0, 0, tiled=False)
-    outcome = down_project(core_now, everywhere, down, down_other, row_parts)
+    outcome = down_project(core_now, everywhere, down, down_other, *row_parts[1:])
     slot_values = lax.all_to_all(outcome, "z", 0, 0, tiled=False)
     beside = [slot_values] + [shifted(slot_values, "x", k) for k in range(1, short)]
-    mixed = combine(spread, beside, own_rows)
-    out = summed + mixed[0].astype(jnp.float32)
-    for k in range(1, long):
-        out = out + shifted(mixed[k], "y", k).astype(jnp.float32)
+    out, *mixed = combine(spread, hidden_own, beside, row_parts)
+    for k, part in enumerate(mixed):
+        out = out + shifted(part, "y", k + 1).astype(jnp.float32)
     return out.astype(jnp.bfloat16).reshape(steps, rows_dev, width)
 
 

time: 244 us -> 230 us (0.943)
  waiting for transfers between devices: 96.3 us -> 68.5 us
  Pallas kernels: 18.4 us -> 32.3 us
    all_to_all x1 -> x0, waiting for transfers between devices: 29.1 us -> none  [per_device(): lax.all_to_all(after(part_rows.reshape(columns, own_rows, width), normed)...]
    pallas_call x2 -> x7, Pallas kernels: 0.38 us -> 17 us  [the longest x2 16.1 us: part_after(): pl.pallas_call(functools.partial(part_body, start), in_specs=[anywhere, a...]
    all_to_all x1, waiting for transfers between devices: 0.01 us -> 5.68 us  [per_device(): everywhere = lax.all_to_all(active, 'z', 0, 0, tiled=False)]
    all_to_all x1 -> x0, starting transfers between devices: 5.17 us -> none  [per_device(): lax.all_to_all(after(part_rows.reshape(columns, own_rows, width), normed)...]
    slice x2 -> x4, local copies, waits for them, and re-layouts: 0.03 us -> 5 us  [per_device(): came = [[part[:8, :128] for part in parts] for parts in ring]]
    ppermute x14 -> x17, starting transfers between devices: 20.4 us -> 24.9 us  [shifted(): return lax.ppermute(x, axis, [(i, (i + by) % size) for i in range(size)])]
    all_to_all x1, starting transfers between devices: 7.22 us -> 3.37 us  [per_device(): slot_values = lax.all_to_all(outcome, 'z', 0, 0, tiled=False)]
    and x1 -> x0, local copies, waits for them, and re-layouts: 3.38 us -> none  [per_device(): chooser = by_row[:, :, :, :, None, :] & same[None, :, None, None, :, None]]
  transfers between devices with their start and end apart: 31 -> 33, of which waited for: 15 -> 13; matrix products, arithmetic and copies ran while one was open for 13% -> 17% of each run, Pallas kernels for 2% -> 13%
where the time goes in v5:
time: 230 us; the launch traced here: 229 us
  waiting for transfers between devices  68.5 us (30%)
  starting transfers between devices  55.1 us (24%)
  Pallas kernels  32.3 us (14%)
  local copies, waits for them, and re-layouts  27.2 us (12%)
  blocking collectives  27.2 us (12%)
  other arithmetic  10.5 us (5%)
  matrix products  7.68 us (3%)
    ppermute x17, waiting for transfers between devices, shifted(): return lax.ppermute(x, axis, [(i, (i + by) % size) for i in range(size)])  28.4 us
    all_gather x1, blocking collectives, per_device(): portion = lax.all_gather(normed, 'z', axis=0, tiled=True)  27.2 us
    all_to_all x1, waiting for transfers between devices, per_device(): lax.all_to_all(part_slots.reshape(columns, slots_dev, width), head, 0, 0,...  27 us
    ppermute x17, starting transfers between devices, shifted(): return lax.ppermute(x, axis, [(i, (i + by) % size) for i in range(size)])  24.9 us
    pallas_call x2, Pallas kernels, part_after(): pl.pallas_call(functools.partial(part_body, start), in_specs=[anywhere, a...  16.1 us
    pallas_call x1, Pallas kernels, project(): pl.pallas_call(functools.partial(project_body, layout), in_specs=[pl.Bloc...  8.25 us
    all_to_all x1, waiting for transfers between devices, per_device(): slot_values = lax.all_to_all(outcome, 'z', 0, 0, tiled=False)  7.46 us
    all_to_all x1, starting transfers between devices, per_device(): lax.all_to_all(context, head, split_axis=0, concat_axis=0, tiled=False)  7.35 us
  transfers between devices with their start and end apart: 33, of which 13 were waited for; matrix products, arithmetic and copies ran while one was open for 17% of the time, Pallas kernels for 13%

profile of v5, /device:TPU:24, one launch (start us, length us, event | category | flops | bytes accessed | tf_op | source)
XLA Modules:
  0.0 229.2 jit_solution(12408193486741753709)
XLA Ops:
  0.0 1.3 copy.128.refs_0_
  1.3 5.9 %collective-permute-start.1 = (bf16[448,512]{1,0:T(8,128)(2,1)}, bf16[448,512]{1,0:T(8,128)(2,1)}, u32[]{:S(2)}, u32[]{:S(2)}) collective-permute-start(bf16[448,512]{1,0:T(8,128)(2,1)} %bitcast.79), channel_id=1, source_target_pairs={{0,224},{32,0},{64,32},{96,64},{128,96},{160,128},{192,160},{224,1... | collective-permute-start | bytes 1376264 | tf_op jit(solution)/shard_map/ppermute | solution.py:412
  8.0 1.3 gather_fusion
  9.3 4.9 %all-to-all-start = ((bf16[16,2,8,576]{3,2,1,0:T(8,128)(2,1)}), bf16[16,2,8,576]{3,2,1,0:T(8,128)(2,1)}, u32[]{:S(2)}, u32[]{:S(2)}) async-start(bf16[16,2,8,576]{3,2,1,0:T(8,128)(2,1)} %bitcast.15), calls=%async_computation | async-start | bytes 655360 | tf_op jit(solution)/shard_map/all_to_all | solution.py:468
  16.5 1.1 fusion.58
  20.7 1.2 fusion.59
  21.9 1.3 slice.57.refs_2_
  23.2 1.4 collective-permute-done.refs_2_
  24.6 1.3 slice.56.refs_1_
  30.1 2.5 %collective-permute-start.3 = (bf16[448,512]{1,0:T(8,128)(2,1)}, bf16[448,512]{1,0:T(8,128)(2,1)}, u32[]{:S(2)}, u32[]{:S(2)}) collective-permute-start(bf16[448,512]{1,0:T(8,128)(2,1)} %collective-permute-done.1.refs_16_), channel_id=1, source_target_pairs={{0,224},{32,0},{64,32},{96,64},{128,96},{160,128},{192,160},{224,1... | collective-permute-start | bytes 1376264 | tf_op jit(solution)/shard_map/ppermute | solution.py:412
  35.2 7.1 %collective-permute-done.3.refs_14_ = bf16[448,512]{1,0:T(8,128)(2,1)} collective-permute-done((bf16[448,512]{1,0:T(8,128)(2,1)}, bf16[448,512]{1,0:T(8,128)(2,1)}, u32[]{:S(2)}, u32[]{:S(2)}) %collective-permute-start.3) | collective-permute-done | bytes 458784 | tf_op jit(solution)/shard_map/ppermute | solution.py:412
  42.2 1.2 slice.62.refs_2_
  43.5 2.2 collective-permute-done.2.refs_4_
  45.6 1.3 slice.61.refs_1_
  47.6 1.2 bitcast_reduce_fusion
  49.0 1.6 collective-permute-start.10
  53.7 7.3 %all-to-all-start.1 = ((bf16[16,4,8,512]{3,2,1,0:T(8,128)(2,1)}), bf16[16,4,8,512]{3,2,1,0:T(8,128)(2,1)S(1)}, u32[]{:S(2)}, u32[]{:S(2)}) async-start(bf16[16,4,8,512]{3,2,1,0:T(8,128)(2,1)} %reshape.333), calls=%async_computation.1 | async-start | bytes 1048576 | tf_op jit(solution)/shard_map/all_to_all | solution.py:510
  61.2 1.5 collective-permute-done.7.block_ref.refs_6_
  62.7 1.2 slice_bitcast_fusion.ready_ref
  63.9 8.1 %part_after.3 = bf16[224,512]{1,0:T(8,128)(2,1)} custom-call(bf16[448,512]{1,0:T(8,128)(2,1)} %copy-done.10, bf16[8,128]{1,0:T(8,128)(2,1)} %slice_bitcast_fusion.ready_ref), custom_call_target="tpu_custom_call" | custom-call | tf_op jit(solution)/shard_map/part_after/pallas_call | solution.py:81
  72.0 8.1 %part_after.2 = bf16[224,512]{1,0:T(8,128)(2,1)} custom-call(bf16[448,512]{1,0:T(8,128)(2,1)} %copy-done.11, bf16[8,128]{1,0:T(8,128)(2,1)} %slice_bitcast_fusion.ready_ref), custom_call_target="tpu_custom_call" | custom-call | tf_op jit(solution)/shard_map/part_after/pallas_call | solution.py:81
  80.2 3.2 %collective-permute-start.11 = (bf16[224,512]{1,0:T(8,128)(2,1)}, bf16[224,512]{1,0:T(8,128)(2,1)}, u32[]{:S(2)}, u32[]{:S(2)}) collective-permute-start(bf16[224,512]{1,0:T(8,128)(2,1)} %part_after.3), channel_id=1, source_target_pairs={{0,224},{32,0},{64,32},{96,64},{128,96},{160,128},{192,160},{224,1... | collective-permute-start | bytes 688136 | tf_op jit(solution)/shard_map/ppermute | solution.py:412
  84.2 5.5 %collective-permute-done.9.refs_8_ = bf16[224,512]{1,0:T(8,128)(2,1)} collective-permute-done((bf16[224,512]{1,0:T(8,128)(2,1)}, bf16[224,512]{1,0:T(8,128)(2,1)}, u32[]{:S(2)}, u32[]{:S(2)}) %collective-permute-start.9) | collective-permute-done | bytes 229408 | tf_op jit(solution)/shard_map/ppermute | solution.py:412
  90.3 1.5 and_convert_fusion
  91.8 1.9 reshape.336
  97.0 8.2 %project.1 = (bf16[128,7168]{1,0:T(8,128)(2,1)}, bf16[32,7168]{1,0:T(8,128)(2,1)}, bf16[32,7168]{1,0:T(8,128)(2,1)}, bf16[32,7168]{1,0:T(8,128)(2,1)}, bf16[32,7168]{1,0:T(8,128)(2,1)}) custom-call(s32[2]{0:T(128)} %pad_add_fusion.place_ref, bf16[16,4,8,512]{3,2,1,0:T(8,128)(2,1)} %copy-done.9, bf16[4,512,128]{2,1,0:T(8,128)(2,1)} %uv_ref.1, ...), custom_call_target="tpu_custom_call" | custom-call | flops 1879048192 | bytes 11010048 | tf_op jit(solution)/shard_map/project/pallas_call | solution.py:185
  105.2 7.2 %all-to-all-start.2 = ((bf16[16,8,7168]{2,1,0:T(8,128)(2,1)}), bf16[16,8,7168]{2,1,0:T(8,128)(2,1)S(1)}, u32[]{:S(2)}, u32[]{:S(2)}) async-start(bf16[16,8,7168]{2,1,0:T(8,128)(2,1)} %bitcast.74), calls=%async_computation.2 | async-start | bytes 3670016 | tf_op jit(solution)/shard_map/all_to_all | solution.py:521
  112.4 27.0 %all-to-all-done.2.parts_ref = bf16[16,8,7168]{2,1,0:T(8,128)(2,1)S(1)} async-done(((bf16[16,8,7168]{2,1,0:T(8,128)(2,1)}), bf16[16,8,7168]{2,1,0:T(8,128)(2,1)S(1)}, u32[]{:S(2)}, u32[]{:S(2)}) %all-to-all-start.2) | async-done | bytes 1835040 | tf_op jit(solution)/shard_map/all_to_all | solution.py:521
  141.0 2.1 collective-permute-start.21
  143.1 27.2 %all_gather.3.x_ref = bf16[64,7168]{1,0:T(8,128)(2,1)S(1)} all-gather(bf16[8,7168]{1,0:T(8,128)(2,1)S(1)} %get-tuple-element.22), channel_id=1, replica_groups=mesh['z'=8,'core'=2,'y'=4,'x'=4] {'z'}, dimensions={0}, use_global_device_ids=true | all-gather | bytes 1032192 | tf_op jit(solution)/shard_map/all_gather | solution.py:528
  170.3 4.2 %gate_up.1 = bf16[8,64,256]{2,1,0:T(8,128)(2,1)S(1)} custom-call(s32[1]{0:T(128)} %bitcast.7.core_ref, bf16[64,7168]{1,0:T(8,128)(2,1)S(1)} %all_gather.3.x_ref, bf16[2,7168,128]{2,1,0:T(8,128)(2,1)S(1)} %bitcast.68, bf16[2,7168,128]{2,1,0:T(8,128)(2,1)} %collective-permute-done.17.other_ref), custom_call_target="tpu_custom_call" | custom-call | flops 469762048 | bytes 8257536 | tf_op jit(solution)/shard_map/gate_up/pallas_call | solution.py:298
  175.3 5.6 %all-to-all-start.3 = ((bf16[8,64,256]{2,1,0:T(8,128)(2,1)}), bf16[8,64,256]{2,1,0:T(8,128)(2,1)}, u32[]{:S(2)}, u32[]{:S(2)}) async-start(bf16[8,64,256]{2,1,0:T(8,128)(2,1)} %copy-done.3), calls=%async_computation.3 | async-start | bytes 524288 | tf_op jit(solution)/shard_map/all_to_all | solution.py:530
  180.9 1.3 iota_add_fusion.1
  182.2 1.2 add.191
  184.3 1.5 fusion.20
  185.8 5.7 %all-to-all-done.3.x_ref = bf16[8,64,256]{2,1,0:T(8,128)(2,1)} async-done(((bf16[8,64,256]{2,1,0:T(8,128)(2,1)}), bf16[8,64,256]{2,1,0:T(8,128)(2,1)}, u32[]{:S(2)}, u32[]{:S(2)}) %all-to-all-start.3) | async-done | bytes 262176 | tf_op jit(solution)/shard_map/all_to_all | solution.py:530
  191.5 2.8 %down_project.1 = bf16[8,8,896]{2,1,0:T(8,128)(2,1)S(1)} custom-call(s32[1]{0:T(128)} %bitcast.7.core_ref, bf16[8,64,256]{2,1,0:T(8,128)(2,1)} %all-to-all-done.3.x_ref, bf16[448,2048]{1,0:T(8,128)(2,1)S(1)} %bitcast.70, bf16[448,2048]{1,0:T(8,128)(2,1)} %collective-permute-done.18.other_ref, bf16[32,7168]{1,0:T(8,128)(2,1)S(1)} %collective-permute-done.19.refs_0_.refs_5_, ...), custom_call_target="tpu_custom_call" | custom-call | flops 234881024 | bytes 3670016 | tf_op jit(solution)/shard_map/down_project/pallas_call | solution.py:345
  195.0 3.4 %all-to-all-start.4 = ((bf16[8,8,896]{2,1,0:T(8,128)(2,1)}), bf16[8,8,896]{2,1,0:T(8,128)(2,1)S(1)}, u32[]{:S(2)}, u32[]{:S(2)}) async-start(bf16[8,8,896]{2,1,0:T(8,128)(2,1)} %copy-done.6), calls=%async_computation.4 | async-start | bytes 229376 | tf_op jit(solution)/shard_map/all_to_all | solution.py:532
  199.7 7.5 %all-to-all-done.4.refs_0_ = bf16[8,8,896]{2,1,0:T(8,128)(2,1)S(1)} async-done(((bf16[8,8,896]{2,1,0:T(8,128)(2,1)}), bf16[8,8,896]{2,1,0:T(8,128)(2,1)S(1)}, u32[]{:S(2)}, u32[]{:S(2)}) %all-to-all-start.4) | async-done | bytes 114720 | tf_op jit(solution)/shard_map/all_to_all | solution.py:532
  208.1 2.5 %collective-permute-start.23 = (bf16[8,8,896]{2,1,0:T(8,128)(2,1)S(1)}, bf16[8,8,896]{2,1,0:T(8,128)(2,1)S(1)}, u32[]{:S(2)}, u32[]{:S(2)}) collective-permute-start(bf16[8,8,896]{2,1,0:T(8,128)(2,1)S(1)} %all-to-all-done.4.refs_0_), channel_id=1, source_target_pairs={{0,2},{1,3},{2,0},{3,1},{4,6},{5,7},{6,4},{7,5},{8,10},{9,11},{10,... | collective-permute-start | bytes 344072 | tf_op jit(solution)/shard_map/ppermute | solution.py:412
  210.5 1.4 collective-permute-start.22
  212.3 2.1 collective-permute-done.23.refs_2_
  214.4 2.2 collective-permute-done.22.refs_1_
  219.0 1.9 collective-permute-start.25
  220.9 1.1 collective-permute-start.26
  222.0 2.4 %collective-permute-done.25 = bf16[8,7168]{1,0:T(8,128)(2,1)S(1)} collective-permute-done((bf16[8,7168]{1,0:T(8,128)(2,1)S(1)}, bf16[8,7168]{1,0:T(8,128)(2,1)S(1)}, u32[]{:S(2)}, u32[]{:S(2)}) %collective-permute-start.25) | collective-permute-done | bytes 114720 | tf_op jit(solution)/shard_map/ppermute | solution.py:412
  224.5 2.8 %collective-permute-done.26 = bf16[8,7168]{1,0:T(8,128)(2,1)S(1)} collective-permute-done((bf16[8,7168]{1,0:T(8,128)(2,1)S(1)}, bf16[8,7168]{1,0:T(8,128)(2,1)S(1)}, u32[]{:S(2)}, u32[]{:S(2)}) %collective-permute-start.26) | collective-permute-done | bytes 114720 | tf_op jit(solution)/shard_map/ppermute | solution.py:412
  227.2 1.2 collective-permute-done.27
  (154 shorter events, 30.9 us)
Async XLA Ops:
  0.0 7.9 %copy-start = (bf16[1,32,8,576]{3,2,1,0:T(8,128)(2,1)S(1)}, bf16[1,32,8,576]{3,2,1,0:T(8,128)(2,1)}, u32[]{:S(2)}) copy-start(bf16[1,32,8,576]{3,2,1,0:T(8,128)(2,1)} %param.20) | copy-start | bytes 884740
  0.0 18.6 %copy-start.19 = (bf16[2,4,7168]{2,1,0:T(4,128)(2,1)S(1)}, bf16[2,4,7168]{2,1,0:T(4,128)(2,1)}, u32[]{:S(2)}) copy-start(bf16[2,4,7168]{2,1,0:T(4,128)(2,1)} %param.15) | copy-start | bytes 344068
  1.3 50.2 %collective-permute-start.4 = (bf16[448,512]{1,0:T(8,128)(2,1)}, bf16[448,512]{1,0:T(8,128)(2,1)}, u32[]{:S(2)}, u32[]{:S(2)}) collective-permute-start(bf16[448,512]{1,0:T(8,128)(2,1)} %bitcast.78), channel_id=1, source_target_pairs={{0,16},{16,0},{1,17},{17,1},{2,18},{18,2},{3,19},{19,3},{4,20},{20... | collective-permute-start | bytes 1376264 | tf_op jit(solution)/shard_map/ppermute | solution.py:416
  1.3 20.7 %collective-permute-start.1 = (bf16[448,512]{1,0:T(8,128)(2,1)}, bf16[448,512]{1,0:T(8,128)(2,1)}, u32[]{:S(2)}, u32[]{:S(2)}) collective-permute-start(bf16[448,512]{1,0:T(8,128)(2,1)} %bitcast.79), channel_id=1, source_target_pairs={{0,224},{32,0},{64,32},{96,64},{128,96},{160,128},{192,160},{224,1... | collective-permute-start | bytes 1376264 | tf_op jit(solution)/shard_map/ppermute | solution.py:412
  7.1 17.5 %collective-permute-start = (bf16[448,512]{1,0:T(8,128)(2,1)}, bf16[448,512]{1,0:T(8,128)(2,1)}, u32[]{:S(2)}, u32[]{:S(2)}) collective-permute-start(bf16[448,512]{1,0:T(8,128)(2,1)} %bitcast.80), channel_id=1, source_target_pairs={{0,32},{32,64},{64,96},{96,128},{128,160},{160,192},{192,224},{224... | collective-permute-start | bytes 1376264 | tf_op jit(solution)/shard_map/ppermute | solution.py:412
  7.9 18.5 %copy-start.20 = (s32[2,64,8]{1,2,0:T(8,128)S(1)}, s32[2,64,8]{1,2,0:T(8,128)}, u32[]{:S(2)}) copy-start(s32[2,64,8]{1,2,0:T(8,128)} %param.26) | copy-start | bytes 12292
  9.3 19.7 %copy-start.8 = (bf16[2,1024,576]{1,2,0:T(8,128)(2,1)S(1)}, bf16[2,1024,576]{1,2,0:T(8,128)(2,1)}, u32[]{:S(2)}) copy-start(bf16[2,1024,576]{1,2,0:T(8,128)(2,1)} %param.18) | copy-start | bytes 7077892
  9.3 24.9 %all-to-all-start = ((bf16[16,2,8,576]{3,2,1,0:T(8,128)(2,1)}), bf16[16,2,8,576]{3,2,1,0:T(8,128)(2,1)}, u32[]{:S(2)}, u32[]{:S(2)}) async-start(bf16[16,2,8,576]{3,2,1,0:T(8,128)(2,1)} %bitcast.15), calls=%async_computation | async-start | bytes 655360 | tf_op jit(solution)/shard_map/all_to_all | solution.py:468
  14.2 156.1 %collective-permute-start.17 = (bf16[2,7168,128]{2,1,0:T(8,128)(2,1)}, bf16[2,7168,128]{2,1,0:T(8,128)(2,1)}, u32[]{:S(2)}, u32[]{:S(2)}) collective-permute-start(bf16[2,7168,128]{2,1,0:T(8,128)(2,1)} %bitcast.67), channel_id=1, source_target_pairs={{0,16},{16,0},{1,17},{17,1},{2,18},{18,2},{3,19},{19,3},{4,20},{20... | collective-permute-start | bytes 11010056 | tf_op jit(solution)/shard_map/ppermute | solution.py:416
  14.6 75.8 %copy-start.22 = (pred[2,2]{1,0:T(4,128)(4,1)}, pred[2,2]{1,0:T(4,128)(4,1)S(1)}, u32[]{:S(2)}) copy-start(pred[2,2]{1,0:T(4,128)(4,1)S(1)} %iota_compare_fusion.10) | copy-start | bytes 16
  27.2 2.9 %copy-start.21 = (pred[16,2,64]{2,0,1:T(8,128)(4,1)}, pred[16,2,64]{2,0,1:T(8,128)(4,1)S(1)}, u32[]{:S(2)}) copy-start(pred[16,2,64]{2,0,1:T(8,128)(4,1)S(1)} %copy.82) | copy-start | bytes 6148
  30.1 12.2 %collective-permute-start.3 = (bf16[448,512]{1,0:T(8,128)(2,1)}, bf16[448,512]{1,0:T(8,128)(2,1)}, u32[]{:S(2)}, u32[]{:S(2)}) collective-permute-start(bf16[448,512]{1,0:T(8,128)(2,1)} %collective-permute-done.1.refs_16_), channel_id=1, source_target_pairs={{0,224},{32,0},{64,32},{96,64},{128,96},{160,128},{192,160},{224,1... | collective-permute-start | bytes 1376264 | tf_op jit(solution)/shard_map/ppermute | solution.py:412
  32.5 13.1 %collective-permute-start.2 = (bf16[448,512]{1,0:T(8,128)(2,1)}, bf16[448,512]{1,0:T(8,128)(2,1)}, u32[]{:S(2)}, u32[]{:S(2)}) collective-permute-start(bf16[448,512]{1,0:T(8,128)(2,1)} %collective-permute-done.refs_2_), channel_id=1, source_target_pairs={{0,32},{32,64},{64,96},{96,128},{128,160},{160,192},{192,224},{224... | collective-permute-start | bytes 1376264 | tf_op jit(solution)/shard_map/ppermute | solution.py:412
  33.4 14.2 %copy-start.12 = (bf16[2,2,64,576]{3,2,1,0:T(8,128)(2,1)S(1)}, bf16[2,2,64,576]{3,2,1,0:T(8,128)(2,1)}, u32[]{:S(2)}) copy-start(bf16[2,2,64,576]{3,2,1,0:T(8,128)(2,1)} %copy.93) | copy-start | bytes 884740
  34.0 46.0 %collective-permute-start.16 = (bf16[448,512]{1,0:T(8,128)(2,1)}, bf16[448,512]{1,0:T(8,128)(2,1)}, u32[]{:S(2)}, u32[]{:S(2)}) collective-permute-start(bf16[448,512]{1,0:T(8,128)(2,1)} %collective-permute-done.1.refs_16_), channel_id=1, source_target_pairs={{0,16},{16,0},{1,17},{17,1},{2,18},{18,2},{3,19},{19,3},{4,20},{20... | collective-permute-start | bytes 1376264 | tf_op jit(solution)/shard_map/ppermute | solution.py:416
  49.0 12.0 %collective-permute-start.10 = (bf16[448,512]{1,0:T(8,128)(2,1)}, bf16[448,512]{1,0:T(8,128)(2,1)S(1)}, u32[]{:S(2)}, u32[]{:S(2)}) collective-permute-start(bf16[448,512]{1,0:T(8,128)(2,1)} %collective-permute-done.3.refs_14_), channel_id=1, source_target_pairs={{0,224},{32,0},{64,32},{96,64},{128,96},{160,128},{192,160},{224,1... | collective-permute-start | bytes 1376264 | tf_op jit(solution)/shard_map/ppermute | solution.py:412
  50.6 12.1 %collective-permute-start.7 = (bf16[448,512]{1,0:T(8,128)(2,1)}, bf16[448,512]{1,0:T(8,128)(2,1)S(1)}, u32[]{:S(2)}, u32[]{:S(2)}) collective-permute-start(bf16[448,512]{1,0:T(8,128)(2,1)} %collective-permute-done.2.refs_4_), channel_id=1, source_target_pairs={{0,32},{32,64},{64,96},{96,128},{128,160},{160,192},{192,224},{224... | collective-permute-start | bytes 1376264 | tf_op jit(solution)/shard_map/ppermute | solution.py:412
  51.5 28.7 %collective-permute-start.5 = (bf16[448,512]{1,0:T(8,128)(2,1)}, bf16[448,512]{1,0:T(8,128)(2,1)}, u32[]{:S(2)}, u32[]{:S(2)}) collective-permute-start(bf16[448,512]{1,0:T(8,128)(2,1)} %collective-permute-done.refs_2_), channel_id=1, source_target_pairs={{0,16},{16,0},{1,17},{17,1},{2,18},{18,2},{3,19},{19,3},{4,20},{20... | collective-permute-start | bytes 1376264 | tf_op jit(solution)/shard_map/ppermute | solution.py:416
  53.7 41.4 %all-to-all-start.1 = ((bf16[16,4,8,512]{3,2,1,0:T(8,128)(2,1)}), bf16[16,4,8,512]{3,2,1,0:T(8,128)(2,1)S(1)}, u32[]{:S(2)}, u32[]{:S(2)}) async-start(bf16[16,4,8,512]{3,2,1,0:T(8,128)(2,1)} %reshape.333), calls=%async_computation.1 | async-start | bytes 1048576 | tf_op jit(solution)/shard_map/all_to_all | solution.py:510
  61.1 22.5 %collective-permute-start.15 = (bf16[448,512]{1,0:T(8,128)(2,1)}, bf16[448,512]{1,0:T(8,128)(2,1)S(1)}, u32[]{:S(2)}, u32[]{:S(2)}) collective-permute-start(bf16[448,512]{1,0:T(8,128)(2,1)} %collective-permute-done.3.refs_14_), channel_id=1, source_target_pairs={{0,16},{16,0},{1,17},{17,1},{2,18},{18,2},{3,19},{19,3},{4,20},{20... | collective-permute-start | bytes 1376264 | tf_op jit(solution)/shard_map/ppermute | solution.py:416
  62.7 9.3 %copy-start.11 = (bf16[448,512]{1,0:T(8,128)(2,1)}, bf16[448,512]{1,0:T(8,128)(2,1)S(1)}, u32[]{:S(2)}) copy-start(bf16[448,512]{1,0:T(8,128)(2,1)S(1)} %collective-permute-done.7.block_ref.refs_6_) | copy-start | bytes 1376260
  62.7 21.0 %collective-permute-start.6 = (bf16[448,512]{1,0:T(8,128)(2,1)}, bf16[448,512]{1,0:T(8,128)(2,1)S(1)}, u32[]{:S(2)}, u32[]{:S(2)}) collective-permute-start(bf16[448,512]{1,0:T(8,128)(2,1)} %collective-permute-done.2.refs_4_), channel_id=1, source_target_pairs={{0,16},{16,0},{1,17},{17,1},{2,18},{18,2},{3,19},{19,3},{4,20},{20... | collective-permute-start | bytes 1376264 | tf_op jit(solution)/shard_map/ppermute | solution.py:416
  80.1 9.6 %collective-permute-start.9 = (bf16[224,512]{1,0:T(8,128)(2,1)}, bf16[224,512]{1,0:T(8,128)(2,1)}, u32[]{:S(2)}, u32[]{:S(2)}) collective-permute-start(bf16[224,512]{1,0:T(8,128)(2,1)} %part_after.2), channel_id=1, source_target_pairs={{0,32},{32,64},{64,96},{96,128},{128,160},{160,192},{192,224},{224... | collective-permute-start | bytes 688136 | tf_op jit(solution)/shard_map/ppermute | solution.py:412
  80.2 9.5 %collective-permute-start.11 = (bf16[224,512]{1,0:T(8,128)(2,1)}, bf16[224,512]{1,0:T(8,128)(2,1)}, u32[]{:S(2)}, u32[]{:S(2)}) collective-permute-start(bf16[224,512]{1,0:T(8,128)(2,1)} %part_after.3), channel_id=1, source_target_pairs={{0,224},{32,0},{64,32},{96,64},{128,96},{160,128},{192,160},{224,1... | collective-permute-start | bytes 688136 | tf_op jit(solution)/shard_map/ppermute | solution.py:412
  83.6 6.1 %copy-start.13 = (bf16[448,512]{1,0:T(8,128)(2,1)}, bf16[448,512]{1,0:T(8,128)(2,1)S(1)}, u32[]{:S(2)}) copy-start(bf16[448,512]{1,0:T(8,128)(2,1)S(1)} %collective-permute-done.15.refs_15_) | copy-start | bytes 1376260
  83.6 11.5 %collective-permute-start.14 = (bf16[448,512]{1,0:T(8,128)(2,1)}, bf16[448,512]{1,0:T(8,128)(2,1)S(1)}, u32[]{:S(2)}, u32[]{:S(2)}) collective-permute-start(bf16[448,512]{1,0:T(8,128)(2,1)} %copy-done.10), channel_id=1, source_target_pairs={{0,16},{16,0},{1,17},{17,1},{2,18},{18,2},{3,19},{19,3},{4,20},{20... | collective-permute-start | bytes 1376264 | tf_op jit(solution)/shard_map/ppermute | solution.py:416
  83.7 6.0 %copy-start.14 = (bf16[448,512]{1,0:T(8,128)(2,1)}, bf16[448,512]{1,0:T(8,128)(2,1)S(1)}, u32[]{:S(2)}) copy-start(bf16[448,512]{1,0:T(8,128)(2,1)S(1)} %collective-permute-done.6.refs_5_) | copy-start | bytes 1376260
  83.7 11.4 %collective-permute-start.8 = (bf16[448,512]{1,0:T(8,128)(2,1)}, bf16[448,512]{1,0:T(8,128)(2,1)S(1)}, u32[]{:S(2)}, u32[]{:S(2)}) collective-permute-start(bf16[448,512]{1,0:T(8,128)(2,1)} %copy-done.11), channel_id=1, source_target_pairs={{0,16},{16,0},{1,17},{17,1},{2,18},{18,2},{3,19},{19,3},{4,20},{20... | collective-permute-start | bytes 1376264 | tf_op jit(solution)/shard_map/ppermute | solution.py:416
  89.7 5.4 %collective-permute-start.12 = (bf16[224,512]{1,0:T(8,128)(2,1)}, bf16[224,512]{1,0:T(8,128)(2,1)S(1)}, u32[]{:S(2)}, u32[]{:S(2)}) collective-permute-start(bf16[224,512]{1,0:T(8,128)(2,1)} %collective-permute-done.9.refs_8_), channel_id=1, source_target_pairs={{0,16},{16,0},{1,17},{17,1},{2,18},{18,2},{3,19},{19,3},{4,20},{20... | collective-permute-start | bytes 688136 | tf_op jit(solution)/shard_map/ppermute | solution.py:416
  89.7 5.4 %collective-permute-start.13 = (bf16[224,512]{1,0:T(8,128)(2,1)}, bf16[224,512]{1,0:T(8,128)(2,1)S(1)}, u32[]{:S(2)}, u32[]{:S(2)}) collective-permute-start(bf16[224,512]{1,0:T(8,128)(2,1)} %collective-permute-done.11.refs_9_), channel_id=1, source_target_pairs={{0,16},{16,0},{1,17},{17,1},{2,18},{18,2},{3,19},{19,3},{4,20},{20... | collective-permute-start | bytes 688136 | tf_op jit(solution)/shard_map/ppermute | solution.py:416
  105.2 34.2 %copy-start.7 = (f32[7168]{0:T(1024)S(1)}, f32[7168]{0:T(1024)}, u32[]{:S(2)}) copy-start(f32[7168]{0:T(1024)} %param.25) | copy-start | bytes 86020
  105.2 34.2 %all-to-all-start.2 = ((bf16[16,8,7168]{2,1,0:T(8,128)(2,1)}), bf16[16,8,7168]{2,1,0:T(8,128)(2,1)S(1)}, u32[]{:S(2)}, u32[]{:S(2)}) async-start(bf16[16,8,7168]{2,1,0:T(8,128)(2,1)} %bitcast.74), calls=%async_computation.2 | async-start | bytes 3670016 | tf_op jit(solution)/shard_map/all_to_all | solution.py:521
  112.4 73.4 %collective-permute-start.18 = (bf16[448,2048]{1,0:T(8,128)(2,1)}, bf16[448,2048]{1,0:T(8,128)(2,1)}, u32[]{:S(2)}, u32[]{:S(2)}) collective-permute-start(bf16[448,2048]{1,0:T(8,128)(2,1)} %bitcast.69), channel_id=1, source_target_pairs={{0,16},{16,0},{1,17},{17,1},{2,18},{18,2},{3,19},{19,3},{4,20},{20... | collective-permute-start | bytes 5505032 | tf_op jit(solution)/shard_map/ppermute | solution.py:416
  139.4 30.9 %copy-start.1 = (bf16[1,2,7168,128]{3,2,1,0:T(8,128)(2,1)S(1)}, bf16[1,2,7168,128]{3,2,1,0:T(8,128)(2,1)}, u32[]{:S(2)}) copy-start(bf16[1,2,7168,128]{3,2,1,0:T(8,128)(2,1)} %param.28) | copy-start | bytes 11010052
  139.8 46.0 %collective-permute-start.19 = (bf16[32,7168]{1,0:T(8,128)(2,1)}, bf16[32,7168]{1,0:T(8,128)(2,1)S(1)}, u32[]{:S(2)}, u32[]{:S(2)}) collective-permute-start(bf16[32,7168]{1,0:T(8,128)(2,1)} %get-tuple-element.23), channel_id=1, source_target_pairs={{0,1},{1,2},{2,3},{3,0},{4,5},{5,6},{6,7},{7,4},{8,9},{9,10},{10,1... | collective-permute-start | bytes 1376264 | tf_op jit(solution)/shard_map/ppermute | solution.py:412
  139.9 45.9 %collective-permute-start.20 = (bf16[32,7168]{1,0:T(8,128)(2,1)}, bf16[32,7168]{1,0:T(8,128)(2,1)S(1)}, u32[]{:S(2)}, u32[]{:S(2)}) collective-permute-start(bf16[32,7168]{1,0:T(8,128)(2,1)} %get-tuple-element.24), channel_id=1, source_target_pairs={{0,2},{1,3},{2,0},{3,1},{4,6},{5,7},{6,4},{7,5},{8,10},{9,11},{10,... | collective-permute-start | bytes 1376264 | tf_op jit(solution)/shard_map/ppermute | solution.py:412
  141.0 44.8 %collective-permute-start.21 = (bf16[32,7168]{1,0:T(8,128)(2,1)}, bf16[32,7168]{1,0:T(8,128)(2,1)S(1)}, u32[]{:S(2)}, u32[]{:S(2)}) collective-permute-start(bf16[32,7168]{1,0:T(8,128)(2,1)} %get-tuple-element.25), channel_id=1, source_target_pairs={{0,3},{1,0},{2,1},{3,2},{4,7},{5,4},{6,5},{7,6},{8,11},{9,8},{10,9... | collective-permute-start | bytes 1376264 | tf_op jit(solution)/shard_map/ppermute | solution.py:412
  170.3 21.2 %copy-start.2 = (bf16[1,2048,448]{1,2,0:T(8,128)(2,1)S(1)}, bf16[1,2048,448]{1,2,0:T(8,128)(2,1)}, u32[]{:S(2)}) copy-start(bf16[1,2048,448]{1,2,0:T(8,128)(2,1)} %param.29) | copy-start | bytes 5505028
  175.3 16.2 %all-to-all-start.3 = ((bf16[8,64,256]{2,1,0:T(8,128)(2,1)}), bf16[8,64,256]{2,1,0:T(8,128)(2,1)}, u32[]{:S(2)}, u32[]{:S(2)}) async-start(bf16[8,64,256]{2,1,0:T(8,128)(2,1)} %copy-done.3), calls=%async_computation.3 | async-start | bytes 524288 | tf_op jit(solution)/shard_map/all_to_all | solution.py:530
  185.8 12.6 %copy-start.24 = (s32[16]{0:T(128)S(1)}, s32[16]{0:T(128)}, u32[]{:S(2)}) copy-start(s32[16]{0:T(128)} %add.191) | copy-start | bytes 196
  185.8 26.2 %copy-start.23 = (pred[2,2]{1,0:T(4,128)(4,1)S(1)}, pred[2,2]{1,0:T(4,128)(4,1)}, u32[]{:S(2)}) copy-start(pred[2,2]{1,0:T(4,128)(4,1)} %copy-done.22) | copy-start | bytes 16
  195.0 12.2 %all-to-all-start.4 = ((bf16[8,8,896]{2,1,0:T(8,128)(2,1)}), bf16[8,8,896]{2,1,0:T(8,128)(2,1)S(1)}, u32[]{:S(2)}, u32[]{:S(2)}) async-start(bf16[8,8,896]{2,1,0:T(8,128)(2,1)} %copy-done.6), calls=%async_computation.4 | async-start | bytes 229376 | tf_op jit(solution)/shard_map/all_to_all | solution.py:532
  207.2 5.1 %collective-permute-start.24 = (bf16[8,8,896]{2,1,0:T(8,128)(2,1)S(1)}, bf16[8,8,896]{2,1,0:T(8,128)(2,1)S(1)}, u32[]{:S(2)}, u32[]{:S(2)}) collective-permute-start(bf16[8,8,896]{2,1,0:T(8,128)(2,1)S(1)} %all-to-all-done.4.refs_0_), channel_id=1, source_target_pairs={{0,3},{1,0},{2,1},{3,2},{4,7},{5,4},{6,5},{7,6},{8,11},{9,8},{10,9... | collective-permute-start | bytes 344072 | tf_op jit(solution)/shard_map/ppermute | solution.py:412
  208.1 6.3 %collective-permute-start.23 = (bf16[8,8,896]{2,1,0:T(8,128)(2,1)S(1)}, bf16[8,8,896]{2,1,0:T(8,128)(2,1)S(1)}, u32[]{:S(2)}, u32[]{:S(2)}) collective-permute-start(bf16[8,8,896]{2,1,0:T(8,128)(2,1)S(1)} %all-to-all-done.4.refs_0_), channel_id=1, source_target_pairs={{0,2},{1,3},{2,0},{3,1},{4,6},{5,7},{6,4},{7,5},{8,10},{9,11},{10,... | collective-permute-start | bytes 344072 | tf_op jit(solution)/shard_map/ppermute | solution.py:412
  210.5 6.0 %collective-permute-start.22 = (bf16[8,8,896]{2,1,0:T(8,128)(2,1)S(1)}, bf16[8,8,896]{2,1,0:T(8,128)(2,1)S(1)}, u32[]{:S(2)}, u32[]{:S(2)}) collective-permute-start(bf16[8,8,896]{2,1,0:T(8,128)(2,1)S(1)} %all-to-all-done.4.refs_0_), channel_id=1, source_target_pairs={{0,1},{1,2},{2,3},{3,0},{4,5},{5,6},{6,7},{7,4},{8,9},{9,10},{10,1... | collective-permute-start | bytes 344072 | tf_op jit(solution)/shard_map/ppermute | solution.py:412
  219.0 5.5 %collective-permute-start.25 = (bf16[8,7168]{1,0:T(8,128)(2,1)S(1)}, bf16[8,7168]{1,0:T(8,128)(2,1)S(1)}, u32[]{:S(2)}, u32[]{:S(2)}) collective-permute-start(bf16[8,7168]{1,0:T(8,128)(2,1)S(1)} %get-tuple-element.28), channel_id=1, source_target_pairs={{0,4},{4,8},{8,12},{12,0},{1,5},{5,9},{9,13},{13,1},{2,6},{6,10},{... | collective-permute-start | bytes 344072 | tf_op jit(solution)/shard_map/ppermute | solution.py:412
  220.9 6.3 %collective-permute-start.26 = (bf16[8,7168]{1,0:T(8,128)(2,1)S(1)}, bf16[8,7168]{1,0:T(8,128)(2,1)S(1)}, u32[]{:S(2)}, u32[]{:S(2)}) collective-permute-start(bf16[8,7168]{1,0:T(8,128)(2,1)S(1)} %get-tuple-element.29), channel_id=1, source_target_pairs={{0,8},{4,12},{8,0},{12,4},{1,9},{5,13},{9,1},{13,5},{2,10},{6,14},... | collective-permute-start | bytes 344072 | tf_op jit(solution)/shard_map/ppermute | solution.py:412
  222.0 6.4 %collective-permute-start.27 = (bf16[8,7168]{1,0:T(8,128)(2,1)S(1)}, bf16[8,7168]{1,0:T(8,128)(2,1)S(1)}, u32[]{:S(2)}, u32[]{:S(2)}) collective-permute-start(bf16[8,7168]{1,0:T(8,128)(2,1)S(1)} %get-tuple-element.30), channel_id=1, source_target_pairs={{0,12},{4,0},{8,4},{12,8},{1,13},{5,1},{9,5},{13,9},{2,14},{6,2},{... | collective-permute-start | bytes 344072 | tf_op jit(solution)/shard_map/ppermute | solution.py:412
  (10 other events, 10.8 us)

commit v6 on v5

--- a/solution.py
+++ b/solution.py
@@ -15,113 +15,273 @@
 STEPS = 2
 
 
-def attend(query_rows, key_rows, lengths, recent):
-    rows, steps, heads, width = query_rows.shape
+NT = (((1,), (1,)), ((), ()))
+
+
+def context_of(query, scores, values, fresh, length):
     scaling = (VD + ROPE) ** (-0.5)
-    flat = query_rows.reshape(rows, steps * heads, width)
-    cache_scores = (
-        jnp.einsum("nqk,npk->nqp", flat, key_rows, preferred_element_type=jnp.float32) * scaling
-    )
-    places = lax.broadcasted_iota(jnp.int32, (1, 1, key_rows.shape[1]), 2)
-    cache_scores = jnp.where(places < lengths[:, None, None], cache_scores, -jnp.inf)
-    fresh_scores = (
-        jnp.einsum("nqk,nsk->nqs", flat, recent, preferred_element_type=jnp.float32) * scaling
-    )
-    step_of = jnp.arange(steps * heads, dtype=jnp.int32)[:, None] // heads
-    seen = jnp.arange(steps, dtype=jnp.int32)[None, :] <= step_of
-    fresh_scores = jnp.where(seen[None], fresh_scores, -jnp.inf)
-    highest = jnp.maximum(jnp.max(cache_scores, axis=2), jnp.max(fresh_scores, axis=2))[:, :, None]
-    cache_weights = jnp.exp(cache_scores - highest)
-    fresh_weights = jnp.exp(fresh_scores - highest)
-    totals = jnp.sum(cache_weights, axis=2, keepdims=True) + jnp.sum(
-        fresh_weights, axis=2, keepdims=True
-    )
-    cache_probs = (cache_weights / totals).astype(jnp.bfloat16)
-    fresh_probs = (fresh_weights / totals).astype(jnp.bfloat16)
-    context = jnp.einsum(
-        "nqp,npl->nql", cache_probs, key_rows[:, :, :LAT], preferred_element_type=jnp.float32
-    )
-    context = context + jnp.einsum(
-        "nqs,nsl->nql", fresh_probs, recent[:, :, :LAT], preferred_element_type=jnp.float32
-    )
-    return context.astype(jnp.bfloat16).reshape(rows, steps, heads, LAT)
-
-
-def routing(ids, weights, experts):
-    matched = ids[None] == experts[:, None, None, None]
-    present = jnp.any(matched, axis=3)
-    row_weight = jnp.sum(jnp.where(matched, weights[None], 0.0), axis=3)
-    rows = ids.shape[1]
-    before = (
-        jnp.arange(rows, dtype=jnp.int32)[:, None] < jnp.arange(rows, dtype=jnp.int32)[None, :]
-    )
-    slot_index = jnp.einsum(
-        "etr,rs->ets",
+    cached = scores(query) * scaling
+    places = lax.broadcasted_iota(jnp.int32, cached.shape, 1)
+    cached = jnp.where(places < length, cached, -jnp.inf)
+    recent = lax.dot_general(query, fresh, NT, preferred_element_type=jnp.float32) * scaling
+    step = lax.broadcasted_iota(jnp.int32, recent.shape, 0) // (query.shape[0] // STEPS)
+    recent = jnp.where(lax.broadcasted_iota(jnp.int32, recent.shape, 1) <= step, recent, -jnp.inf)
+    highest = jnp.maximum(
+        jnp.max(cached, axis=1, keepdims=True), jnp.max(recent, axis=1, keepdims=True)
+    )
+    cached, recent = jnp.exp(cached - highest), jnp.exp(recent - highest)
+    totals = jnp.sum(cached, axis=1, keepdims=True) + jnp.sum(recent, axis=1, keepdims=True)
+    cached, recent = (cached / totals).astype(jnp.bfloat16), (recent / totals).astype(jnp.bfloat16)
+    mixed = values(cached) + jnp.dot(
+        recent, fresh[:, :LAT], preferred_element_type=jnp.float32
+    )
+    return mixed.astype(jnp.bfloat16)
+
+
+def attend_resident_body(len_ref, q_ref, keys_ref, fresh_ref, out_ref):
+    keys = keys_ref[0]
+    query = jnp.concatenate([q_ref[t, 0] for t in range(STEPS)], axis=0)
+    out_ref[0] = context_of(
+        query,
+        lambda q: jnp.dot(q, keys, preferred_element_type=jnp.float32),
+        lambda p: lax.dot_general(p, keys[:LAT], NT, preferred_element_type=jnp.float32),
+        fresh_ref[0],
+        len_ref[pl.program_id(0)],
+    )
+
+
+def attend_resident(lengths, queries, keys, fresh):
+    rows, width, places = keys.shape
+    steps, _, heads, _ = queries.shape
+    return pl.pallas_call(
+        attend_resident_body,
+        grid=(rows,),
+        in_specs=[
+            pl.BlockSpec(memory_space=pltpu.SMEM),
+            pl.BlockSpec((steps, 1, heads, width), lambda i: (0, i, 0, 0)),
+            pl.BlockSpec((1, width, places), lambda i: (i, 0, 0)),
+            pl.BlockSpec((1, *fresh.shape[1:]), lambda i: (i, 0, 0)),
+        ],
+        out_specs=pl.BlockSpec((1, steps * heads, LAT), lambda i: (i, 0, 0)),
+        out_shape=jax.ShapeDtypeStruct((rows, steps * heads, LAT), jnp.bfloat16),
+        compiler_params=pltpu.CompilerParams(vmem_limit_bytes=24 * 1024 * 1024),
+        cost_estimate=pl.CostEstimate(
+            flops=4 * keys.size * steps * heads, bytes_accessed=20000000, transcendentals=0
+        ),
+        name="attend_resident",
+    )(lengths, queries, keys, fresh)
+
+
+def attend_new_body(len_ref, q_ref, taken_ref, fresh_ref, done_ref, *refs):
+    out_ref = refs[-1]
+    resident, queries, _ = done_ref.shape
+    fresh_rows = q_ref.shape[1]
+    contexts = [done_ref[n] for n in range(resident)]
+    for n in range(fresh_rows):
+        keys = taken_ref[:, n].astype(jnp.float32)
+        keys = keys.reshape(-1, keys.shape[2]).astype(jnp.bfloat16)
+        contexts.append(
+            context_of(
+                jnp.concatenate([q_ref[t, n] for t in range(STEPS)], axis=0),
+                lambda q: lax.dot_general(q, keys, NT, preferred_element_type=jnp.float32),
+                lambda p: jnp.dot(p, keys[:, :LAT], preferred_element_type=jnp.float32),
+                fresh_ref[n],
+                len_ref[n],
+            )
+        )
+    rows = resident + fresh_rows
+    context = jnp.concatenate(contexts, axis=0)
+    size = context.shape[0]
+    heads = queries // STEPS
+    to = lax.broadcasted_iota(jnp.int32, (size, size), 0)
+    source = to % rows * queries + to // rows % STEPS * heads + to // (rows * STEPS)
+    turn = (source == lax.broadcasted_iota(jnp.int32, (size, size), 1)).astype(jnp.float32)
+    turned = jnp.dot(turn.astype(jnp.bfloat16), context, preferred_element_type=jnp.float32)
+    out_ref[...] = turned.reshape(out_ref.shape).astype(jnp.bfloat16)
+
+
+def attend_new(lengths, queries, taken, fresh, done, columns, ready):
+    _, rows, _, width = taken.shape
+    steps, whole, heads, _ = queries.shape
+    out = (columns, heads // columns, steps * whole, LAT)
+    last = whole // rows - 1
+    return pl.pallas_call(
+        attend_new_body,
+        grid=(1,),
+        in_specs=[
+            pl.BlockSpec(memory_space=pltpu.SMEM),
+            pl.BlockSpec((steps, rows, heads, width), lambda i: (0, last, 0, 0)),
+            pl.BlockSpec(taken.shape, lambda i: (0, 0, 0, 0)),
+            pl.BlockSpec((rows, *fresh.shape[1:]), lambda i: (last, 0, 0)),
+            pl.BlockSpec(done.shape, lambda i: (0, 0, 0)),
+        ]
+        + [pl.BlockSpec(memory_space=pltpu.HBM)] * len(ready),
+        out_specs=pl.BlockSpec(out, lambda i: (0, 0, 0, 0)),
+        out_shape=jax.ShapeDtypeStruct(out, jnp.bfloat16),
+        compiler_params=pltpu.CompilerParams(vmem_limit_bytes=24 * 1024 * 1024),
+        cost_estimate=pl.CostEstimate(
+            flops=4 * taken.size * steps * heads, bytes_accessed=20000000, transcendentals=0
+        ),
+        name="attend_new",
+    )(lengths, queries, taken, fresh, done, *ready)
+
+
+def picked(one_hot, x, dims=(((1,), (0,)), ((), ()))):
+    one_hot = one_hot.astype(jnp.float32).astype(jnp.bfloat16)
+    total = None
+    for _ in range(3):
+        part = x.astype(jnp.bfloat16)
+        x = x - part.astype(jnp.float32)
+        term = lax.dot_general(one_hot, part, dims, preferred_element_type=jnp.float32)
+        total = term if total is None else total + term
+    return total
+
+
+def routing_body(sizes, place_ref, ids_ref, weights_ref, *refs):
+    long, short, rows_dev = sizes
+    select_ref, own_ref, spread_ref, present_ref, weight_ref = refs[-5:]
+    steps, _, rows = ids_ref.shape
+    columns = long * short
+    own_rows, slots = steps * rows_dev, steps * CAP
+    at_y, at_x = place_ref[2], place_ref[3]
+
+    def iota(shape, axis):
+        return lax.broadcasted_iota(jnp.int32, shape, axis)
+
+    for t in range(steps):
+        ids, weights = ids_ref[t], weights_ref[t]
+        for e in range(columns):
+            at = slice(e * steps + t, e * steps + t + 1)
+            matched = ids == e
+            present_ref[at] = jnp.max(matched.astype(jnp.float32), axis=0, keepdims=True)
+            weight_ref[at] = jnp.sum(jnp.where(matched, weights, 0.0), axis=0, keepdims=True)
+    present = present_ref[...]
+    before = iota((rows, rows), 0) < iota((rows, rows), 1)
+    place = jnp.dot(
         present.astype(jnp.bfloat16),
-        before.astype(jnp.bfloat16),
+        before.astype(jnp.float32).astype(jnp.bfloat16),
         preferred_element_type=jnp.float32,
-    ).astype(jnp.int32)
-    slots = jnp.arange(CAP, dtype=jnp.int32)[None, None, :, None]
-    chosen = (slot_index[:, :, None, :] == slots) & present[:, :, None, :]
-    return chosen, row_weight
-
-
-NT = (((1,), (1,)), ((), ()))
-
-
-def part_body(start, block_ref, ready_ref, out_ref, sem):
+    )
+    count = columns * slots
+    widen = iota((count, columns * steps), 0) // CAP == iota((count, columns * steps), 1)
+    slot = (iota((count, rows), 0) % CAP).astype(jnp.float32)
+    chosen = (picked(widen, place) == slot) & (picked(widen, present) > 0.5)
+    weighted = jnp.where(chosen, picked(widen, weight_ref[...]), 0.0)
+    total = columns * own_rows
+    to = iota((rows, total), 1)
+    spot = to // own_rows * rows_dev + to % rows_dev == iota((rows, total), 0)
+    same = (
+        iota((count, total), 0) // CAP % steps == iota((count, total), 1) // rows_dev % steps
+    )
+    spot = spot.astype(jnp.float32).astype(jnp.bfloat16)
+    chooser = jnp.dot(
+        chosen.astype(jnp.float32).astype(jnp.bfloat16), spot, preferred_element_type=jnp.float32
+    )
+    chooser = jnp.where(same, chooser, 0.0).astype(jnp.bfloat16)
+    select_ref[:count] = chooser
+    to = iota((total, total), 0)
+    from_x = (at_x + to // (long * own_rows)) % short
+    from_y = (at_y + to // own_rows % long) % long
+    source = (from_y * short + from_x) * own_rows + to % own_rows
+    turned = source == iota((total, total), 1)
+    select_ref[count:] = turned.astype(jnp.float32).astype(jnp.bfloat16)
+    head = at_y * short + at_x
+    mine = iota((total, own_rows), 0) == head * own_rows + iota((total, own_rows), 1)
+    own_ref[...] = jnp.dot(
+        chooser, mine.astype(jnp.float32).astype(jnp.bfloat16), preferred_element_type=jnp.float32
+    ).astype(jnp.bfloat16)
+    to = iota((short * slots, count), 0)
+    expert = at_y * short + (at_x + short - to // slots) % short
+    near = picked(expert * slots + to % slots == iota((short * slots, count), 1), weighted)
+    to = iota((long * own_rows, rows), 0)
+    row = ((at_y + to // own_rows) % long * short + at_x) * rows_dev + to % rows_dev
+    near = picked(row == iota((long * own_rows, rows), 1), near, NT)
+    shape = (long * own_rows, short * slots)
+    same = iota(shape, 0) // rows_dev % steps == iota(shape, 1) // CAP % steps
+    spread_ref[...] = jnp.where(same, near, 0.0)
+
+
+def routing(place, ids, weights, long, short, rows_dev, ready):
+    steps, _, rows = ids.shape
+    count, total = long * short * steps * CAP, rows * steps
+    vmem = pl.BlockSpec(memory_space=pltpu.VMEM)
+    return pl.pallas_call(
+        functools.partial(routing_body, (long, short, rows_dev)),
+        in_specs=[
+            pl.BlockSpec(memory_space=pltpu.SMEM),
+            vmem,
+            vmem,
+            *[pl.BlockSpec(memory_space=pltpu.HBM)] * len(ready),
+        ],
+        out_specs=[vmem] * 3,
+        out_shape=[
+            jax.ShapeDtypeStruct((count + total, total), jnp.bfloat16),
+            jax.ShapeDtypeStruct((count, steps * rows_dev), jnp.bfloat16),
+            jax.ShapeDtypeStruct((long * steps * rows_dev, short * steps * CAP), jnp.float32),
+        ],
+        scratch_shapes=[pltpu.VMEM((long * short * steps, rows), jnp.float32)] * 2,
+        compiler_params=pltpu.CompilerParams(vmem_limit_bytes=24 * 1024 * 1024),
+        cost_estimate=pl.CostEstimate(flops=0, bytes_accessed=10000000, transcendentals=0),
+        name="routing",
+    )(place, ids, weights, *ready)
+
+
+def after_body(up_ref, down_ref, ready_ref, out_up_ref, out_down_ref, pair_ref):
     del ready_ref
-    copy = pltpu.make_async_copy(block_ref.at[pl.ds(start, out_ref.shape[0])], out_ref, sem)
-    copy.start()
-    copy.wait()
-
-
-def part_after(block, start, size, ready):
-    anywhere = pl.BlockSpec(memory_space=pltpu.HBM)
-    return pl.pallas_call(
-        functools.partial(part_body, start),
-        in_specs=[anywhere, anywhere],
-        out_specs=anywhere,
-        out_shape=jax.ShapeDtypeStruct((size, block.shape[1]), block.dtype),
-        scratch_shapes=[pltpu.SemaphoreType.DMA(())],
-        name="part_after",
-    )(block, ready)
-
-
-def spread_blocks(block):
-    up = down = block
-    steps = []
-    for _ in range(1, lax.axis_size("z") // 2):
-        up, down = shifted(up, "z", 1), shifted(down, "z", -1)
-        steps.append((up, down))
-    return steps
-
-
-def all_blocks(block, steps, ready):
-    half = block.shape[0] // 2
-    (up, down), far = steps[-1], lax.axis_size("z") // 2
-    last = [
-        shifted(part_after(up, 0, half, ready), "z", 1),
-        shifted(part_after(down, half, half, ready), "z", -1),
-    ]
-    own = [[block]] + [[u] for u, _ in steps] + [last] + [[d] for _, d in steps[::-1]]
-    assert len(own) == 2 * far
-    return own, [[swap_cores(part) for part in parts] for parts in own]
+    for k, (ref, out_ref) in enumerate([(up_ref, out_up_ref), (down_ref, out_down_ref)]):
+        block = ref[...]
+        out_ref[...] = block
+        pair_ref[k] = block
+
+
+def after(up, down, ready, space):
+    vmem = pl.BlockSpec(memory_space=pltpu.VMEM)
+    one = jax.ShapeDtypeStruct(up.shape, up.dtype)
+    return pl.pallas_call(
+        after_body,
+        in_specs=[vmem, vmem, pl.BlockSpec(memory_space=space)],
+        out_specs=[vmem] * 3,
+        out_shape=[one, one, jax.ShapeDtypeStruct((2, *up.shape), up.dtype)],
+        compiler_params=pltpu.CompilerParams(vmem_limit_bytes=8 * 1024 * 1024),
+        name="after",
+    )(up, down, ready)
+
+
+def halves_body(up_ref, down_ref, ready_ref, first_ref, second_ref):
+    del ready_ref
+    half = first_ref.shape[0]
+    first_ref[...] = up_ref[:half]
+    second_ref[...] = down_ref[half:]
+
+
+def halves(up, down, ready):
+    vmem = pl.BlockSpec(memory_space=pltpu.VMEM)
+    half = jax.ShapeDtypeStruct((up.shape[0] // 2, up.shape[1]), up.dtype)
+    return pl.pallas_call(
+        halves_body,
+        in_specs=[vmem] * 3,
+        out_specs=[vmem] * 2,
+        out_shape=[half, half],
+        compiler_params=pltpu.CompilerParams(vmem_limit_bytes=8 * 1024 * 1024),
+        name="halves",
+    )(up, down, ready)
 
 
 def project_body(layout, place_ref, by_ref, uv_ref, select_ref, own_ref, hidden_ref, *refs):
-    total = sum(map(sum, layout))
+    total = 1 + max(i for pair in layout for parts in pair for i, _ in parts)
     blocks, outs = refs[:total], refs[total:-5]
     held, slots_ref, rows_ref, sems, out_sems = refs[-5:]
     chips = len(layout)
-    copies, at, start = [], 0, 0
-    for counts in layout:
-        for count in counts:
-            for r in blocks[at : at + count]:
-                size = r.shape[0]
-                copies.append(pltpu.make_async_copy(r, held.at[pl.ds(start, size)], sems.at[at]))
-                copies[-1].start()
-                at, start = at + 1, start + size
+    copies, start = [], 0
+    for pair in layout:
+        for i, j in pair[0] + pair[1]:
+            r = blocks[i] if j is None else blocks[i].at[j]
+            size = r.shape[0]
+            copies.append(
+                pltpu.make_async_copy(r, held.at[pl.ds(start, size)], sems.at[len(copies)])
+            )
+            copies[-1].start()
+            start += size
     values = []
     for k in range(uv_ref.shape[0]):
         context = by_ref[:, k].astype(jnp.float32).reshape(-1, by_ref.shape[3])
@@ -137,8 +297,8 @@
     width = held.shape[0] // chips
     core_width = width // 2
     leaving = []
-    for k, counts in enumerate(layout):
-        for _ in range(sum(counts)):
+    for k, (ours, theirs) in enumerate(layout):
+        for _ in ours + theirs:
             copies[at].wait()
             at += 1
         pair = [
@@ -173,12 +333,11 @@
         copy.wait()
 
 
-def project(place, by_head, w_uv, select, own, other, chooser, hidden, outer, inner):
-    layout = [(len(a), len(b)) for a, b in zip(own, other)]
-    blocks = [part for pair in zip(own, other) for parts in pair for part in parts]
+def project(place, by_head, w_uv, select, blocks, layout, chooser, hidden, outer, inner):
     rows, depth = select.shape[0], blocks[0].shape[1]
     half = rows // 2
-    width = sum(part.shape[0] for part in blocks)
+    width = sum(part.size for part in blocks) // depth
+    parts = sum(len(a) + len(b) for a, b in layout)
     each = half // inner
     vmem = pl.BlockSpec(memory_space=pltpu.VMEM)
     anywhere = pl.BlockSpec(memory_space=pltpu.HBM)
@@ -192,10 +351,10 @@
             pltpu.VMEM((width, depth), jnp.bfloat16),
             pltpu.VMEM((half, width), jnp.bfloat16),
             pltpu.VMEM((inner, each, width), jnp.bfloat16),
-            pltpu.SemaphoreType.DMA((len(blocks),)),
+            pltpu.SemaphoreType.DMA((parts,)),
             pltpu.SemaphoreType.DMA((1 + inner, len(layout))),
         ],
-        compiler_params=pltpu.CompilerParams(vmem_limit_bytes=58 * 1024 * 1024),
+        compiler_params=pltpu.CompilerParams(vmem_limit_bytes=63200000),
         cost_estimate=pl.CostEstimate(
             flops=2 * rows * depth * width,
             bytes_accessed=2 * depth * width + 2 * rows * width,
@@ -203,21 +362,6 @@
         ),
         name="project",
     )(place, by_head, w_uv, select, chooser, hidden, *blocks)
-
-
-def after_body(*refs):
-    del refs
-
-
-def after(x, *others):
-    return pl.pallas_call(
-        after_body,
-        in_specs=[pl.BlockSpec(memory_space=pltpu.HBM)] * (1 + len(others)),
-        out_specs=pl.BlockSpec(memory_space=pltpu.HBM),
-        out_shape=jax.ShapeDtypeStruct(x.shape, x.dtype),
-        input_output_aliases={0: 0},
-        name="after",
-    )(x, *others)
 
 
 def norm_body(parts_ref, gain_ref, *refs):
@@ -438,21 +582,14 @@
     groups, columns = chips * cores, long * short
     core, at_y, at_x = (lax.axis_index(a) for a in ("core", "y", "x"))
     group_index = lax.axis_index(group)
-    head_index = lax.axis_index(head)
     steps, rows_dev, width = hidden_in.shape
     resident = res_cache.shape[0]
     newcomers = rows_dev - resident
     requests = arrival.shape[1]
     own_rows = steps * rows_dev
-    rows_group = columns * own_rows
-    heads_dev = w_uv.shape[0]
     slots_dev = steps * CAP
 
-    place = jnp.stack([lax.axis_index("z"), core]).astype(jnp.int32)
-    ring = spread_blocks(w_o.T)
-    came = [[part[:8, :128] for part in parts] for parts in ring]
-    experts = after(jnp.arange(columns, dtype=jnp.int32), *came[0])
-    res_len = after(res_len, *came[0])
+    place = jnp.stack([lax.axis_index("z"), core, at_y, at_x]).astype(jnp.int32)
     gu_other = swap_cores(w_gu[0])
     down = w_down[0].T
     down_other = swap_cores(down)
@@ -463,7 +600,6 @@
     order = jnp.sum(jnp.where(claimed, places[None, :], 0), axis=1)
     len_sorted = jnp.sum(jnp.where(claimed, pre_len[0][None, :], 0), axis=1)
     new_len = lax.dynamic_slice(len_sorted, (group_index * newcomers,), (newcomers,))
-    new_len = after(new_len, *came[1])
     sorted_cache = jnp.take(pre_cache[0], order, axis=0, mode="clip")
     taken = lax.all_to_all(
         sorted_cache.reshape(groups, newcomers, *sorted_cache.shape[1:]),
@@ -472,51 +608,37 @@
         concat_axis=0,
         tiled=False,
     )
-    taken = jnp.swapaxes(taken, 0, 1).reshape(newcomers, -1, sorted_cache.shape[2])
-
-    chosen, row_weight = routing(expert_ids, route_weight, experts)
-    by_row = chosen.reshape(columns, steps, CAP, columns, rows_dev)
-    same = jnp.arange(steps)[:, None] == jnp.arange(steps)[None, :]
-    chooser = by_row[:, :, :, :, None, :] & same[None, :, None, None, :, None]
-    chooser = chooser.reshape(columns * slots_dev, rows_group).astype(jnp.bfloat16)
-    own_chooser = lax.dynamic_slice(
-        chooser, (0, head_index * own_rows), (columns * slots_dev, own_rows)
-    )
-    near = jnp.where(chosen, row_weight[:, :, None, :], 0.0)
-    expert_of = at_y * short + (at_x - jnp.arange(short, dtype=jnp.int32)) % short
-    row_of = ((at_y + jnp.arange(long, dtype=jnp.int32)) % long * short + at_x) * rows_dev
-    row_of = (row_of[:, None] + jnp.arange(rows_dev, dtype=jnp.int32)[None, :]).reshape(-1)
-    pick_expert = expert_of[:, None] == jnp.arange(columns, dtype=jnp.int32)[None, :]
-    pick_row = row_of[:, None] == jnp.arange(columns * rows_dev, dtype=jnp.int32)[None, :]
-    exact = dict(precision=lax.Precision.HIGHEST, preferred_element_type=jnp.float32)
-    near = jnp.einsum("je,etcr->jtcr", pick_expert.astype(jnp.float32), near, **exact)
-    near = jnp.einsum("jtcr,qr->jtcq", near, pick_row.astype(jnp.float32), **exact)
-    near = near.reshape(short, steps, CAP, long, rows_dev).transpose(3, 4, 0, 1, 2)
-    spread = jnp.where(same[None, :, None, None, :, None], near[:, None], 0.0)
-    spread = spread.reshape(long * own_rows, short * slots_dev)
-
-    by_row_queries = jnp.swapaxes(queries, 0, 1)
-    recent = jnp.swapaxes(fresh, 0, 1)
-    context = jnp.concatenate(
-        [
-            attend(by_row_queries[:resident], res_cache, res_len, recent[:resident]),
-            attend(by_row_queries[resident:], taken, new_len, recent[resident:]),
-        ],
-        axis=0,
-    )
-    context = context.reshape(rows_dev, steps, columns, heads_dev, LAT).transpose(2, 3, 1, 0, 4)
-    context = context.reshape(columns, heads_dev, own_rows, LAT)
-    w_own, w_other = all_blocks(w_o.T, ring, context[0, 0, :, :128])
+    recent = jnp.swapaxes(jnp.pad(fresh, ((0, 8 - steps), (0, 0), (0, 0))), 0, 1)
+    done = attend_resident(res_len, queries, jnp.swapaxes(res_cache, 1, 2), recent)
+    hidden_own = hidden_in.reshape(own_rows, width)
+    block = w_o.T
+    up, down_block, near = after(shifted(block, "z", 1), shifted(block, "z", -1), done, pltpu.VMEM)
+    context = attend_new(new_len, queries, taken, recent, done, columns, [gu_other, down_other])
+    select, own_chooser, spread = routing(
+        place,
+        jnp.swapaxes(expert_ids, 1, 2),
+        jnp.swapaxes(route_weight, 1, 2),
+        long,
+        short,
+        rows_dev,
+        [context, hidden_own],
+    )
+    up, down_block, mid = after(
+        shifted(up, "z", 1), shifted(down_block, "z", -1), context, pltpu.HBM
+    )
+    far = [shifted(up, "z", 1), shifted(down_block, "z", -1)]
+    first, second = halves(*far, select)
+    last = [shifted(first, "z", 1), shifted(second, "z", -1)]
+    blocks = [block, near, mid, *far, *last]
+    places = [[(0, None)], [(1, 0)], [(2, 0)], [(3, None)], [(5, None), (6, None)]]
+    places += [[(4, None)], [(2, 1)], [(1, 1)]]
+    assert len(places) == chips
+    count = len(blocks)
+    layout = [(parts, [(i + count, j) for i, j in parts]) for parts in places]
+    blocks = blocks + [swap_cores(part) for part in blocks]
     by_head = lax.all_to_all(context, head, split_axis=0, concat_axis=0, tiled=False)
-    hidden_own = hidden_in.reshape(own_rows, width)
-    from_x = (at_x + jnp.arange(short, dtype=jnp.int32)) % short
-    from_y = (at_y + jnp.arange(long, dtype=jnp.int32)) % long
-    row_from = (from_y[None, :, None] * short + from_x[:, None, None]) * own_rows
-    row_from = (row_from + jnp.arange(own_rows, dtype=jnp.int32)).reshape(-1)
-    turned = row_from[:, None] == jnp.arange(rows_group, dtype=jnp.int32)[None, :]
-    select = jnp.concatenate([chooser, turned.astype(jnp.bfloat16)], axis=0)
     part_slots, row_here, *row_away = project(
-        place, by_head, w_uv, select, w_own, w_other, own_chooser, hidden_own, long, short
+        place, by_head, w_uv, select, blocks, layout, own_chooser, hidden_own, long, short
     )
     slot_parts = lax.all_to_all(
         part_slots.reshape(columns, slots_dev, width), head, 0, 0, tiled=False

time: 230 us -> 191 us (0.83)
  blocking collectives: 27.2 us -> 68.9 us
  waiting for transfers between devices: 68.5 us -> 39.9 us
  local copies, waits for them, and re-layouts: 27.2 us -> 8.05 us
  starting transfers between devices: 55.1 us -> 45.1 us
  other arithmetic: 10.5 us -> 0.92 us
  matrix products: 7.68 us -> 0 us
  Pallas kernels: 32.3 us -> 27.3 us
    all_to_all x0 -> x2, blocking collectives: none -> 42 us  [the longest x1 30.8 us: per_device(): lax.all_to_all(part_slots.reshape(columns, slots_dev, width), head, 0, 0,...]
    all_to_all x2 -> x0, waiting for transfers between devices: 34.4 us -> none  [the longest x1 27 us: per_device(): lax.all_to_all(part_slots.reshape(columns, slots_dev, width), head, 0, 0,...]
    all_to_all x2 -> x0, starting transfers between devices: 10.5 us -> none  [the longest x1 7.16 us: per_device(): lax.all_to_all(part_slots.reshape(columns, slots_dev, width), head, 0, 0,...]
    dot_general x11 -> x0, matrix products: 7.68 us -> none  [the longest x2 1.94 us: attend(): jnp.einsum('nqk,npk->nqp', flat, key_rows, preferred_element_type=jnp.flo...]
    slice x7 -> x0, local copies, waits for them, and re-layouts: 6.93 us -> none  [the longest x4 5 us: per_device(): came = [[part[:8, :128] for part in parts] for parts in ring]]
    all_to_all x1, waiting for transfers between devices: 5.68 us -> 10.4 us  [per_device(): everywhere = lax.all_to_all(active, 'z', 0, 0, tiled=False)]
    pallas_call x5 -> x6, Pallas kernels: 16.1 us -> 11.9 us  [the longest x2 5.04 us: after(): pl.pallas_call(after_body, in_specs=[vmem, vmem, pl.BlockSpec(memory_spac...]
    unnamed x52 -> x41, local copies, waits for them, and re-layouts: 7.11 us -> 5.91 us
  transfers between devices with their start and end apart: 33 -> 29, of which waited for: 13 -> 13; matrix products, arithmetic and copies ran while one was open for 17% -> 2% of each run, Pallas kernels for 13% -> 8%
where the time goes in v6:
time: 191 us
  blocking collectives  68.9 us (36%)
  starting transfers between devices  45.1 us (24%)
  waiting for transfers between devices  39.9 us (21%)
  Pallas kernels  27.3 us (14%)
  local copies, waits for them, and re-layouts  8.05 us (4%)
    all_to_all x1, blocking collectives, per_device(): lax.all_to_all(part_slots.reshape(columns, slots_dev, width), head, 0, 0,...  30.8 us
    ppermute x17, waiting for transfers between devices, shifted(): return lax.ppermute(x, axis, [(i, (i + by) % size) for i in range(size)])  27.7 us
    ppermute x17, starting transfers between devices, shifted(): return lax.ppermute(x, axis, [(i, (i + by) % size) for i in range(size)])  27 us
    all_gather x1, blocking collectives, per_device(): portion = lax.all_gather(normed, 'z', axis=0, tiled=True)  26.8 us
    all_to_all x1, blocking collectives, per_device(): slot_values = lax.all_to_all(outcome, 'z', 0, 0, tiled=False)  11.3 us
    all_to_all x1, waiting for transfers between devices, per_device(): everywhere = lax.all_to_all(active, 'z', 0, 0, tiled=False)  10.4 us
    pallas_call x1, Pallas kernels, project(): pl.pallas_call(functools.partial(project_body, layout), in_specs=[pl.Bloc...  8.19 us
    all_to_all x1, starting transfers between devices, per_device(): lax.all_to_all(context, head, split_axis=0, concat_axis=0, tiled=False)  7.17 us
  transfers between devices with their start and end apart: 29, of which 13 were waited for; matrix products, arithmetic and copies ran while one was open for 2% of the time, Pallas kernels for 8%

profile of v6, /device:TPU:24, one launch (start us, length us, event | category | flops | bytes accessed | tf_op | source)
XLA Modules:
  0.0 190.5 jit_solution(4323874793856611076)
XLA Ops:
  0.5 5.9 %collective-permute-start.3 = (bf16[448,512]{1,0:T(8,128)(2,1)}, bf16[448,512]{1,0:T(8,128)(2,1)}, u32[]{:S(2)}, u32[]{:S(2)}) collective-permute-start(bf16[448,512]{1,0:T(8,128)(2,1)} %bitcast.15.refs_0_), channel_id=1, source_target_pairs={{0,224},{32,0},{64,32},{96,64},{128,96},{160,128},{192,160},{224,1... | collective-permute-start | bytes 1376264 | tf_op jit(solution)/shard_map/ppermute | solution.py:556
  6.4 0.8 select_reduce_fusion
  7.2 1.3 gather_fusion
  8.5 4.7 %all-to-all-start = ((bf16[16,2,8,576]{3,2,1,0:T(8,128)(2,1)}), bf16[16,2,8,576]{3,2,1,0:T(8,128)(2,1)S(1)}, u32[]{:S(2)}, u32[]{:S(2)}) async-start(bf16[16,2,8,576]{3,2,1,0:T(8,128)(2,1)} %bitcast.9), calls=%async_computation | async-start | bytes 655360 | tf_op jit(solution)/shard_map/all_to_all | solution.py:604
  13.2 0.7 copy.20
  14.0 1.7 copy-done.3
  16.3 2.9 %attend_resident.1.done_ref.ready_ref = bf16[2,128,512]{2,1,0:T(8,128)(2,1)S(1)} custom-call(s32[2]{0:T(128)S(1)} %copy-done.17, bf16[2,4,64,576]{3,2,1,0:T(8,128)(2,1)S(1)} %copy-done.2, bf16[2,576,1024]{2,1,0:T(8,128)(2,1)S(1)} %bitcast.23, bf16[4,8,576]{2,1,0:T(8,128)(2,1)S(1)} %pad_bitcast_fusion.fresh_ref), custom_call_target="tpu_custom_call" | custom-call | flops 603979776 | bytes 20000000 | tf_op jit(solution)/shard_map/attend_resident/pallas_call | solution.py:56
  19.2 1.9 %collective-permute-done.3.down_ref = bf16[448,512]{1,0:T(8,128)(2,1)} collective-permute-done((bf16[448,512]{1,0:T(8,128)(2,1)}, bf16[448,512]{1,0:T(8,128)(2,1)}, u32[]{:S(2)}, u32[]{:S(2)}) %collective-permute-start.3) | collective-permute-done | bytes 458784 | tf_op jit(solution)/shard_map/ppermute | solution.py:556
  21.1 3.4 %collective-permute-done.2.up_ref = bf16[448,512]{1,0:T(8,128)(2,1)} collective-permute-done((bf16[448,512]{1,0:T(8,128)(2,1)}, bf16[448,512]{1,0:T(8,128)(2,1)}, u32[]{:S(2)}, u32[]{:S(2)}) %collective-permute-start.2) | collective-permute-done | bytes 458784 | tf_op jit(solution)/shard_map/ppermute | solution.py:556
  24.5 2.5 %after.2 = (bf16[448,512]{1,0:T(8,128)(2,1)}, bf16[448,512]{1,0:T(8,128)(2,1)}, bf16[2,448,512]{2,1,0:T(8,128)(2,1)}) custom-call(bf16[448,512]{1,0:T(8,128)(2,1)} %collective-permute-done.2.up_ref, bf16[448,512]{1,0:T(8,128)(2,1)} %collective-permute-done.3.down_ref, bf16[2,128,512]{2,1,0:T(8,128)(2,1)S(1)} %attend_resident.1.done_ref.ready_ref), custom_call_target="tpu_custom_call" | custom-call | tf_op jit(solution)/shard_map/after/pallas_call | solution.py:240
  27.0 3.2 %collective-permute-start.5 = (bf16[448,512]{1,0:T(8,128)(2,1)}, bf16[448,512]{1,0:T(8,128)(2,1)}, u32[]{:S(2)}, u32[]{:S(2)}) collective-permute-start(bf16[448,512]{1,0:T(8,128)(2,1)} %get-tuple-element.34), channel_id=1, source_target_pairs={{0,224},{32,0},{64,32},{96,64},{128,96},{160,128},{192,160},{224,1... | collective-permute-start | bytes 1376264 | tf_op jit(solution)/shard_map/ppermute | solution.py:556
  30.3 2.7 %attend_new.1.refs_0_.ready_ref = bf16[16,4,8,512]{3,2,1,0:T(8,128)(2,1)} custom-call(s32[2]{0:T(128)S(1)} %dynamic_slice.3.len_ref, bf16[2,4,64,576]{3,2,1,0:T(8,128)(2,1)S(1)} %copy-done.2, bf16[16,2,8,576]{3,2,1,0:T(8,128)(2,1)S(1)} %all-to-all-done.taken_ref, bf16[4,8,576]{2,1,0:T(8,128)(2,1)S(1)} %pad_bitcast_fusion.fresh_ref, ...), custom_call_target="tpu_custom_call" | custom-call | flops 75497472 | bytes 20000000 | tf_op jit(solution)/shard_map/attend_new/pallas_call | solution.py:108
  33.0 4.0 %collective-permute-done.4.up_ref = bf16[448,512]{1,0:T(8,128)(2,1)} collective-permute-done((bf16[448,512]{1,0:T(8,128)(2,1)}, bf16[448,512]{1,0:T(8,128)(2,1)}, u32[]{:S(2)}, u32[]{:S(2)}) %collective-permute-start.4) | collective-permute-done | bytes 458784 | tf_op jit(solution)/shard_map/ppermute | solution.py:556
  37.0 2.6 %after.3 = (bf16[448,512]{1,0:T(8,128)(2,1)}, bf16[448,512]{1,0:T(8,128)(2,1)}, bf16[2,448,512]{2,1,0:T(8,128)(2,1)}) custom-call(bf16[448,512]{1,0:T(8,128)(2,1)} %collective-permute-done.4.up_ref, bf16[448,512]{1,0:T(8,128)(2,1)} %collective-permute-done.5.down_ref, bf16[16,4,8,512]{3,2,1,0:T(8,128)(2,1)} %attend_new.1.refs_0_.ready_ref), custom_call_target="tpu_custom_call" | custom-call | tf_op jit(solution)/shard_map/after/pallas_call | solution.py:240
  39.6 0.7 collective-permute-start.6
  40.2 2.6 %collective-permute-start.7 = (bf16[448,512]{1,0:T(8,128)(2,1)}, bf16[448,512]{1,0:T(8,128)(2,1)S(1)}, u32[]{:S(2)}, u32[]{:S(2)}) collective-permute-start(bf16[448,512]{1,0:T(8,128)(2,1)} %get-tuple-element.37), channel_id=1, source_target_pairs={{0,224},{32,0},{64,32},{96,64},{128,96},{160,128},{192,160},{224,1... | collective-permute-start | bytes 1376264 | tf_op jit(solution)/shard_map/ppermute | solution.py:556
  43.3 7.2 %all-to-all-start.1 = ((bf16[16,4,8,512]{3,2,1,0:T(8,128)(2,1)}), bf16[16,4,8,512]{3,2,1,0:T(8,128)(2,1)}, u32[]{:S(2)}, u32[]{:S(2)}) async-start(bf16[16,4,8,512]{3,2,1,0:T(8,128)(2,1)} %attend_new.1.refs_0_.ready_ref), calls=%async_computation.1 | async-start | bytes 1048576 | tf_op jit(solution)/shard_map/all_to_all | solution.py:639
  50.6 1.3 routing.1
  52.6 2.7 %collective-permute-start.8 = (bf16[224,512]{1,0:T(8,128)(2,1)S(1)}, bf16[224,512]{1,0:T(8,128)(2,1)S(1)}, u32[]{:S(2)}, u32[]{:S(2)}) collective-permute-start(bf16[224,512]{1,0:T(8,128)(2,1)S(1)} %get-tuple-element.38), channel_id=1, source_target_pairs={{0,32},{32,64},{64,96},{96,128},{128,160},{160,192},{192,224},{224... | collective-permute-start | bytes 688136 | tf_op jit(solution)/shard_map/ppermute | solution.py:556
  56.2 4.7 %collective-permute-done.8.refs_5_ = bf16[224,512]{1,0:T(8,128)(2,1)S(1)} collective-permute-done((bf16[224,512]{1,0:T(8,128)(2,1)S(1)}, bf16[224,512]{1,0:T(8,128)(2,1)S(1)}, u32[]{:S(2)}, u32[]{:S(2)}) %collective-permute-start.8) | collective-permute-done | bytes 229408 | tf_op jit(solution)/shard_map/ppermute | solution.py:556
  60.9 2.6 %collective-permute-done.9.refs_6_ = bf16[224,512]{1,0:T(8,128)(2,1)} collective-permute-done((bf16[224,512]{1,0:T(8,128)(2,1)S(1)}, bf16[224,512]{1,0:T(8,128)(2,1)}, u32[]{:S(2)}, u32[]{:S(2)}) %collective-permute-start.9) | collective-permute-done | bytes 229408 | tf_op jit(solution)/shard_map/ppermute | solution.py:556
  63.5 1.8 collective-permute-done.16.refs_13_
  65.3 8.2 %project.1 = (bf16[128,7168]{1,0:T(8,128)(2,1)}, bf16[32,7168]{1,0:T(8,128)(2,1)}, bf16[32,7168]{1,0:T(8,128)(2,1)}, bf16[32,7168]{1,0:T(8,128)(2,1)}, bf16[32,7168]{1,0:T(8,128)(2,1)}) custom-call(s32[4]{0:T(128)} %copy-done.16, bf16[16,4,8,512]{3,2,1,0:T(8,128)(2,1)} %all-to-all-done.1.by_ref, bf16[4,512,128]{2,1,0:T(8,128)(2,1)} %uv_ref.1, ...), custom_call_target="tpu_custom_call" | custom-call | flops 1879048192 | bytes 11010048 | tf_op jit(solution)/shard_map/project/pallas_call | solution.py:344
  73.5 30.8 %all_to_all.25.parts_ref = bf16[16,8,7168]{2,1,0:T(8,128)(2,1)S(1)} all-to-all(bf16[16,8,7168]{2,1,0:T(8,128)(2,1)} %bitcast.29), channel_id=1, replica_groups=mesh['z'=8,'core'=2,'y'=4,'x'=4] {'y','x'}, dimensions={0} | all-to-all | bytes 3670016 | tf_op jit(solution)/shard_map/all_to_all | solution.py:643
  105.3 1.9 collective-permute-start.18
  107.2 1.4 collective-permute-start.19
  108.6 26.8 %all_gather.3.x_ref = bf16[64,7168]{1,0:T(8,128)(2,1)S(1)} all-gather(bf16[8,7168]{1,0:T(8,128)(2,1)S(1)} %get-tuple-element.44), channel_id=1, replica_groups=mesh['z'=8,'core'=2,'y'=4,'x'=4] {'z'}, dimensions={0}, use_global_device_ids=true | all-gather | bytes 1032192 | tf_op jit(solution)/shard_map/all_gather | solution.py:650
  135.4 4.1 %gate_up.1 = bf16[8,64,256]{2,1,0:T(8,128)(2,1)S(1)} custom-call(s32[1]{0:T(128)} %bitcast.1.core_ref, bf16[64,7168]{1,0:T(8,128)(2,1)S(1)} %all_gather.3.x_ref, bf16[2,7168,128]{2,1,0:T(8,128)(2,1)S(1)} %bitcast.22, bf16[2,7168,128]{2,1,0:T(8,128)(2,1)} %collective-permute-done.refs_0_.other_ref), custom_call_target="tpu_custom_call" | custom-call | flops 469762048 | bytes 8257536 | tf_op jit(solution)/shard_map/gate_up/pallas_call | solution.py:442
  139.6 0.7 copy-done.9
  140.2 4.9 %all-to-all-start.3 = ((bf16[8,64,256]{2,1,0:T(8,128)(2,1)}), bf16[8,64,256]{2,1,0:T(8,128)(2,1)S(1)}, u32[]{:S(2)}, u32[]{:S(2)}) async-start(bf16[8,64,256]{2,1,0:T(8,128)(2,1)} %copy-done.9), calls=%async_computation.3 | async-start | bytes 524288 | tf_op jit(solution)/shard_map/all_to_all | solution.py:652
  145.2 10.4 %all-to-all-done.3.x_ref = bf16[8,64,256]{2,1,0:T(8,128)(2,1)S(1)} async-done(((bf16[8,64,256]{2,1,0:T(8,128)(2,1)}), bf16[8,64,256]{2,1,0:T(8,128)(2,1)S(1)}, u32[]{:S(2)}, u32[]{:S(2)}) %all-to-all-start.3) | async-done | bytes 262176 | tf_op jit(solution)/shard_map/all_to_all | solution.py:652
  155.7 1.5 copy-done.6
  157.2 1.2 down_project.1
  158.4 11.3 %all_to_all.26.refs_0_ = bf16[8,8,896]{2,1,0:T(8,128)(2,1)S(1)} all-to-all(bf16[8,8,896]{2,1,0:T(8,128)(2,1)S(1)} %down_project.1), channel_id=1, replica_groups=mesh['z'=8,'core'=2,'y'=4,'x'=4] {'z'}, dimensions={0} | all-to-all | bytes 229376 | tf_op jit(solution)/shard_map/all_to_all | solution.py:654
  169.7 0.9 collective-permute-start.22
  170.5 1.9 %collective-permute-start.21 = (bf16[8,8,896]{2,1,0:T(8,128)(2,1)S(1)}, bf16[8,8,896]{2,1,0:T(8,128)(2,1)S(1)}, u32[]{:S(2)}, u32[]{:S(2)}) collective-permute-start(bf16[8,8,896]{2,1,0:T(8,128)(2,1)S(1)} %all_to_all.26.refs_0_), channel_id=1, source_target_pairs={{0,2},{1,3},{2,0},{3,1},{4,6},{5,7},{6,4},{7,5},{8,10},{9,11},{10,... | collective-permute-start | bytes 344072 | tf_op jit(solution)/shard_map/ppermute | solution.py:556
  172.5 1.0 collective-permute-start.20
  173.5 1.0 collective-permute-done.22.refs_3_
  174.5 2.4 %collective-permute-done.21.refs_2_ = bf16[8,8,896]{2,1,0:T(8,128)(2,1)S(1)} collective-permute-done((bf16[8,8,896]{2,1,0:T(8,128)(2,1)S(1)}, bf16[8,8,896]{2,1,0:T(8,128)(2,1)S(1)}, u32[]{:S(2)}, u32[]{:S(2)}) %collective-permute-start.21) | collective-permute-done | bytes 114720 | tf_op jit(solution)/shard_map/ppermute | solution.py:556
  176.8 1.7 collective-permute-done.20.refs_1_
  178.5 1.5 combine.1
  180.0 2.2 %collective-permute-start.23 = (bf16[8,7168]{1,0:T(8,128)(2,1)S(1)}, bf16[8,7168]{1,0:T(8,128)(2,1)S(1)}, u32[]{:S(2)}, u32[]{:S(2)}) collective-permute-start(bf16[8,7168]{1,0:T(8,128)(2,1)S(1)} %get-tuple-element.50), channel_id=1, source_target_pairs={{0,4},{4,8},{8,12},{12,0},{1,5},{5,9},{9,13},{13,1},{2,6},{6,10},{... | collective-permute-start | bytes 344072 | tf_op jit(solution)/shard_map/ppermute | solution.py:556
  182.2 0.7 collective-permute-start.24
  182.9 0.7 collective-permute-start.25
  183.7 2.1 %collective-permute-done.23 = bf16[8,7168]{1,0:T(8,128)(2,1)S(1)} collective-permute-done((bf16[8,7168]{1,0:T(8,128)(2,1)S(1)}, bf16[8,7168]{1,0:T(8,128)(2,1)S(1)}, u32[]{:S(2)}, u32[]{:S(2)}) %collective-permute-start.23) | collective-permute-done | bytes 114720 | tf_op jit(solution)/shard_map/ppermute | solution.py:556
  185.8 2.8 %collective-permute-done.24 = bf16[8,7168]{1,0:T(8,128)(2,1)S(1)} collective-permute-done((bf16[8,7168]{1,0:T(8,128)(2,1)S(1)}, bf16[8,7168]{1,0:T(8,128)(2,1)S(1)}, u32[]{:S(2)}, u32[]{:S(2)}) %collective-permute-start.24) | collective-permute-done | bytes 114720 | tf_op jit(solution)/shard_map/ppermute | solution.py:556
  188.6 1.1 collective-permute-done.25
  189.8 0.7 reshape.16
  (74 shorter events, 4.6 us)
Async XLA Ops:
  0.0 7.2 %copy-start = (bf16[1,32,8,576]{3,2,1,0:T(8,128)(2,1)S(1)}, bf16[1,32,8,576]{3,2,1,0:T(8,128)(2,1)}, u32[]{:S(2)}) copy-start(bf16[1,32,8,576]{3,2,1,0:T(8,128)(2,1)} %param.20) | copy-start | bytes 884740
  0.0 14.0 %copy-start.2 = (bf16[2,4,64,576]{3,2,1,0:T(8,128)(2,1)S(1)}, bf16[2,4,64,576]{3,2,1,0:T(8,128)(2,1)}, u32[]{:S(2)}) copy-start(bf16[2,4,64,576]{3,2,1,0:T(8,128)(2,1)} %q_ref.3) | copy-start | bytes 1769476
  0.0 30.3 %collective-permute-start = (bf16[2,7168,128]{2,1,0:T(8,128)(2,1)}, bf16[2,7168,128]{2,1,0:T(8,128)(2,1)}, u32[]{:S(2)}, u32[]{:S(2)}) collective-permute-start(bf16[2,7168,128]{2,1,0:T(8,128)(2,1)} %bitcast.21), channel_id=1, source_target_pairs={{0,16},{16,0},{1,17},{17,1},{2,18},{18,2},{3,19},{19,3},{4,20},{20... | collective-permute-start | bytes 11010056 | tf_op jit(solution)/shard_map/ppermute | solution.py:560
  0.0 30.3 %collective-permute-start.1 = (bf16[448,2048]{1,0:T(8,128)(2,1)}, bf16[448,2048]{1,0:T(8,128)(2,1)S(1)}, u32[]{:S(2)}, u32[]{:S(2)}) collective-permute-start(bf16[448,2048]{1,0:T(8,128)(2,1)} %bitcast.24), channel_id=1, source_target_pairs={{0,16},{16,0},{1,17},{17,1},{2,18},{18,2},{3,19},{19,3},{4,20},{20... | collective-permute-start | bytes 5505032 | tf_op jit(solution)/shard_map/ppermute | solution.py:560
  0.5 20.6 %collective-permute-start.3 = (bf16[448,512]{1,0:T(8,128)(2,1)}, bf16[448,512]{1,0:T(8,128)(2,1)}, u32[]{:S(2)}, u32[]{:S(2)}) collective-permute-start(bf16[448,512]{1,0:T(8,128)(2,1)} %bitcast.15.refs_0_), channel_id=1, source_target_pairs={{0,224},{32,0},{64,32},{96,64},{128,96},{160,128},{192,160},{224,1... | collective-permute-start | bytes 1376264 | tf_op jit(solution)/shard_map/ppermute | solution.py:556
  6.4 18.1 %collective-permute-start.2 = (bf16[448,512]{1,0:T(8,128)(2,1)}, bf16[448,512]{1,0:T(8,128)(2,1)}, u32[]{:S(2)}, u32[]{:S(2)}) collective-permute-start(bf16[448,512]{1,0:T(8,128)(2,1)} %bitcast.15.refs_0_), channel_id=1, source_target_pairs={{0,32},{32,64},{64,96},{96,128},{128,160},{160,192},{192,224},{224... | collective-permute-start | bytes 1376264 | tf_op jit(solution)/shard_map/ppermute | solution.py:556
  8.5 21.8 %all-to-all-start = ((bf16[16,2,8,576]{3,2,1,0:T(8,128)(2,1)}), bf16[16,2,8,576]{3,2,1,0:T(8,128)(2,1)S(1)}, u32[]{:S(2)}, u32[]{:S(2)}) async-start(bf16[16,2,8,576]{3,2,1,0:T(8,128)(2,1)} %bitcast.9), calls=%async_computation | async-start | bytes 655360 | tf_op jit(solution)/shard_map/all_to_all | solution.py:604
  14.0 1.7 copy-start.3
  15.7 0.7 copy-start.17
  27.0 10.0 %collective-permute-start.4 = (bf16[448,512]{1,0:T(8,128)(2,1)}, bf16[448,512]{1,0:T(8,128)(2,1)}, u32[]{:S(2)}, u32[]{:S(2)}) collective-permute-start(bf16[448,512]{1,0:T(8,128)(2,1)} %get-tuple-element.33), channel_id=1, source_target_pairs={{0,32},{32,64},{64,96},{96,128},{128,160},{160,192},{192,224},{224... | collective-permute-start | bytes 1376264 | tf_op jit(solution)/shard_map/ppermute | solution.py:556
  27.0 10.0 %collective-permute-start.5 = (bf16[448,512]{1,0:T(8,128)(2,1)}, bf16[448,512]{1,0:T(8,128)(2,1)}, u32[]{:S(2)}, u32[]{:S(2)}) collective-permute-start(bf16[448,512]{1,0:T(8,128)(2,1)} %get-tuple-element.34), channel_id=1, source_target_pairs={{0,224},{32,0},{64,32},{96,64},{128,96},{160,128},{192,160},{224,1... | collective-permute-start | bytes 1376264 | tf_op jit(solution)/shard_map/ppermute | solution.py:556
  30.2 25.8 %collective-permute-start.11 = (bf16[2,448,512]{2,1,0:T(8,128)(2,1)}, bf16[2,448,512]{2,1,0:T(8,128)(2,1)}, u32[]{:S(2)}, u32[]{:S(2)}) collective-permute-start(bf16[2,448,512]{2,1,0:T(8,128)(2,1)} %get-tuple-element.32.refs_1_), channel_id=1, source_target_pairs={{0,16},{16,0},{1,17},{17,1},{2,18},{18,2},{3,19},{19,3},{4,20},{20... | collective-permute-start | bytes 2752520 | tf_op jit(solution)/shard_map/ppermute | solution.py:560
  33.0 17.6 %copy-start.19 = (bf16[2,4,7168]{2,1,0:T(4,128)(2,1)S(1)}, bf16[2,4,7168]{2,1,0:T(4,128)(2,1)}, u32[]{:S(2)}) copy-start(bf16[2,4,7168]{2,1,0:T(4,128)(2,1)} %param.15) | copy-start | bytes 344068
  33.0 17.6 %copy-start.14 = (s32[2,64,8]{1,2,0:T(8,128)S(1)}, s32[2,64,8]{1,2,0:T(8,128)}, u32[]{:S(2)}) copy-start(s32[2,64,8]{1,2,0:T(8,128)} %param.26) | copy-start | bytes 12292
  33.0 17.7 %copy-start.15 = (f32[2,64,8]{1,2,0:T(8,128)S(1)}, f32[2,64,8]{1,2,0:T(8,128)}, u32[]{:S(2)}) copy-start(f32[2,64,8]{1,2,0:T(8,128)} %param.27) | copy-start | bytes 12292
  39.6 13.0 %collective-permute-start.6 = (bf16[448,512]{1,0:T(8,128)(2,1)}, bf16[448,512]{1,0:T(8,128)(2,1)S(1)}, u32[]{:S(2)}, u32[]{:S(2)}) collective-permute-start(bf16[448,512]{1,0:T(8,128)(2,1)} %get-tuple-element.36), channel_id=1, source_target_pairs={{0,32},{32,64},{64,96},{96,128},{128,160},{160,192},{192,224},{224... | collective-permute-start | bytes 1376264 | tf_op jit(solution)/shard_map/ppermute | solution.py:556
  40.2 12.3 %collective-permute-start.7 = (bf16[448,512]{1,0:T(8,128)(2,1)}, bf16[448,512]{1,0:T(8,128)(2,1)S(1)}, u32[]{:S(2)}, u32[]{:S(2)}) collective-permute-start(bf16[448,512]{1,0:T(8,128)(2,1)} %get-tuple-element.37), channel_id=1, source_target_pairs={{0,224},{32,0},{64,32},{96,64},{128,96},{160,128},{192,160},{224,1... | collective-permute-start | bytes 1376264 | tf_op jit(solution)/shard_map/ppermute | solution.py:556
  42.8 12.5 %collective-permute-start.10 = (bf16[448,512]{1,0:T(8,128)(2,1)}, bf16[448,512]{1,0:T(8,128)(2,1)}, u32[]{:S(2)}, u32[]{:S(2)}) collective-permute-start(bf16[448,512]{1,0:T(8,128)(2,1)} %bitcast.15.refs_0_), channel_id=1, source_target_pairs={{0,16},{16,0},{1,17},{17,1},{2,18},{18,2},{3,19},{19,3},{4,20},{20... | collective-permute-start | bytes 1376264 | tf_op jit(solution)/shard_map/ppermute | solution.py:560
  42.8 20.7 %collective-permute-start.12 = (bf16[2,448,512]{2,1,0:T(8,128)(2,1)}, bf16[2,448,512]{2,1,0:T(8,128)(2,1)}, u32[]{:S(2)}, u32[]{:S(2)}) collective-permute-start(bf16[2,448,512]{2,1,0:T(8,128)(2,1)} %get-tuple-element.35.refs_2_), channel_id=1, source_target_pairs={{0,16},{16,0},{1,17},{17,1},{2,18},{18,2},{3,19},{19,3},{4,20},{20... | collective-permute-start | bytes 2752520 | tf_op jit(solution)/shard_map/ppermute | solution.py:560
  43.3 20.1 %all-to-all-start.1 = ((bf16[16,4,8,512]{3,2,1,0:T(8,128)(2,1)}), bf16[16,4,8,512]{3,2,1,0:T(8,128)(2,1)}, u32[]{:S(2)}, u32[]{:S(2)}) async-start(bf16[16,4,8,512]{3,2,1,0:T(8,128)(2,1)} %attend_new.1.refs_0_.ready_ref), calls=%async_computation.1 | async-start | bytes 1048576 | tf_op jit(solution)/shard_map/all_to_all | solution.py:639
  50.6 14.7 %copy-start.16 = (s32[4]{0:T(128)}, s32[4]{0:T(128)S(1)}, u32[]{:S(2)}) copy-start(s32[4]{0:T(128)S(1)} %pad_add_fusion.place_ref) | copy-start | bytes 52
  50.6 14.7 %copy-start.4 = (bf16[8,7168]{1,0:T(8,128)(2,1)}, bf16[8,7168]{1,0:T(8,128)(2,1)S(1)}, u32[]{:S(2)}) copy-start(bf16[8,7168]{1,0:T(8,128)(2,1)S(1)} %reshape.14.refs_1_.hidden_ref) | copy-start | bytes 344068
  52.6 12.7 %copy-start.11 = (bf16[256,128]{1,0:T(8,128)(2,1)}, bf16[256,128]{1,0:T(8,128)(2,1)S(1)}, u32[]{:S(2)}) copy-start(bf16[256,128]{1,0:T(8,128)(2,1)S(1)} %get-tuple-element.30.ready_ref.select_ref) | copy-start | bytes 196612
  52.6 12.7 %copy-start.7 = (bf16[448,512]{1,0:T(8,128)(2,1)}, bf16[448,512]{1,0:T(8,128)(2,1)S(1)}, u32[]{:S(2)}) copy-start(bf16[448,512]{1,0:T(8,128)(2,1)S(1)} %collective-permute-done.6.up_ref.refs_3_) | copy-start | bytes 1376260
  52.6 12.7 %copy-start.8 = (bf16[448,512]{1,0:T(8,128)(2,1)}, bf16[448,512]{1,0:T(8,128)(2,1)S(1)}, u32[]{:S(2)}) copy-start(bf16[448,512]{1,0:T(8,128)(2,1)S(1)} %collective-permute-done.7.down_ref.refs_4_) | copy-start | bytes 1376260
  52.6 8.2 %collective-permute-start.8 = (bf16[224,512]{1,0:T(8,128)(2,1)S(1)}, bf16[224,512]{1,0:T(8,128)(2,1)S(1)}, u32[]{:S(2)}, u32[]{:S(2)}) collective-permute-start(bf16[224,512]{1,0:T(8,128)(2,1)S(1)} %get-tuple-element.38), channel_id=1, source_target_pairs={{0,32},{32,64},{64,96},{96,128},{128,160},{160,192},{192,224},{224... | collective-permute-start | bytes 688136 | tf_op jit(solution)/shard_map/ppermute | solution.py:556
  55.3 8.1 %collective-permute-start.13 = (bf16[448,512]{1,0:T(8,128)(2,1)S(1)}, bf16[448,512]{1,0:T(8,128)(2,1)}, u32[]{:S(2)}, u32[]{:S(2)}) collective-permute-start(bf16[448,512]{1,0:T(8,128)(2,1)S(1)} %collective-permute-done.6.up_ref.refs_3_), channel_id=1, source_target_pairs={{0,16},{16,0},{1,17},{17,1},{2,18},{18,2},{3,19},{19,3},{4,20},{20... | collective-permute-start | bytes 1376264 | tf_op jit(solution)/shard_map/ppermute | solution.py:560
  55.3 8.1 %collective-permute-start.9 = (bf16[224,512]{1,0:T(8,128)(2,1)S(1)}, bf16[224,512]{1,0:T(8,128)(2,1)}, u32[]{:S(2)}, u32[]{:S(2)}) collective-permute-start(bf16[224,512]{1,0:T(8,128)(2,1)S(1)} %get-tuple-element.39), channel_id=1, source_target_pairs={{0,224},{32,0},{64,32},{96,64},{128,96},{160,128},{192,160},{224,1... | collective-permute-start | bytes 688136 | tf_op jit(solution)/shard_map/ppermute | solution.py:556
  56.0 9.3 %collective-permute-start.14 = (bf16[448,512]{1,0:T(8,128)(2,1)S(1)}, bf16[448,512]{1,0:T(8,128)(2,1)}, u32[]{:S(2)}, u32[]{:S(2)}) collective-permute-start(bf16[448,512]{1,0:T(8,128)(2,1)S(1)} %collective-permute-done.7.down_ref.refs_4_), channel_id=1, source_target_pairs={{0,16},{16,0},{1,17},{17,1},{2,18},{18,2},{3,19},{19,3},{4,20},{20... | collective-permute-start | bytes 1376264 | tf_op jit(solution)/shard_map/ppermute | solution.py:560
  60.9 4.4 %copy-start.18 = (bf16[224,512]{1,0:T(8,128)(2,1)}, bf16[224,512]{1,0:T(8,128)(2,1)S(1)}, u32[]{:S(2)}) copy-start(bf16[224,512]{1,0:T(8,128)(2,1)S(1)} %collective-permute-done.8.refs_5_) | copy-start | bytes 688132
  60.9 2.6 %collective-permute-start.15 = (bf16[224,512]{1,0:T(8,128)(2,1)S(1)}, bf16[224,512]{1,0:T(8,128)(2,1)}, u32[]{:S(2)}, u32[]{:S(2)}) collective-permute-start(bf16[224,512]{1,0:T(8,128)(2,1)S(1)} %collective-permute-done.8.refs_5_), channel_id=1, source_target_pairs={{0,16},{16,0},{1,17},{17,1},{2,18},{18,2},{3,19},{19,3},{4,20},{20... | collective-permute-start | bytes 688136 | tf_op jit(solution)/shard_map/ppermute | solution.py:560
  63.4 1.8 collective-permute-start.16
  73.5 30.8 %copy-start.13 = (f32[7168]{0:T(1024)S(1)}, f32[7168]{0:T(1024)}, u32[]{:S(2)}) copy-start(f32[7168]{0:T(1024)} %param.25) | copy-start | bytes 86020
  104.3 31.1 %copy-start.1 = (bf16[1,2,7168,128]{3,2,1,0:T(8,128)(2,1)S(1)}, bf16[1,2,7168,128]{3,2,1,0:T(8,128)(2,1)}, u32[]{:S(2)}) copy-start(bf16[1,2,7168,128]{3,2,1,0:T(8,128)(2,1)} %param.28) | copy-start | bytes 11010052
  104.7 40.5 %collective-permute-start.17 = (bf16[32,7168]{1,0:T(8,128)(2,1)}, bf16[32,7168]{1,0:T(8,128)(2,1)S(1)}, u32[]{:S(2)}, u32[]{:S(2)}) collective-permute-start(bf16[32,7168]{1,0:T(8,128)(2,1)} %get-tuple-element.45), channel_id=1, source_target_pairs={{0,1},{1,2},{2,3},{3,0},{4,5},{5,6},{6,7},{7,4},{8,9},{9,10},{10,1... | collective-permute-start | bytes 1376264 | tf_op jit(solution)/shard_map/ppermute | solution.py:556
  105.3 39.9 %collective-permute-start.18 = (bf16[32,7168]{1,0:T(8,128)(2,1)}, bf16[32,7168]{1,0:T(8,128)(2,1)S(1)}, u32[]{:S(2)}, u32[]{:S(2)}) collective-permute-start(bf16[32,7168]{1,0:T(8,128)(2,1)} %get-tuple-element.46), channel_id=1, source_target_pairs={{0,2},{1,3},{2,0},{3,1},{4,6},{5,7},{6,4},{7,5},{8,10},{9,11},{10,... | collective-permute-start | bytes 1376264 | tf_op jit(solution)/shard_map/ppermute | solution.py:556
  107.2 38.0 %collective-permute-start.19 = (bf16[32,7168]{1,0:T(8,128)(2,1)}, bf16[32,7168]{1,0:T(8,128)(2,1)}, u32[]{:S(2)}, u32[]{:S(2)}) collective-permute-start(bf16[32,7168]{1,0:T(8,128)(2,1)} %get-tuple-element.47), channel_id=1, source_target_pairs={{0,3},{1,0},{2,1},{3,2},{4,7},{5,4},{6,5},{7,6},{8,11},{9,8},{10,9... | collective-permute-start | bytes 1376264 | tf_op jit(solution)/shard_map/ppermute | solution.py:556
  139.5 0.7 copy-start.9
  140.2 15.4 %all-to-all-start.3 = ((bf16[8,64,256]{2,1,0:T(8,128)(2,1)}), bf16[8,64,256]{2,1,0:T(8,128)(2,1)S(1)}, u32[]{:S(2)}, u32[]{:S(2)}) async-start(bf16[8,64,256]{2,1,0:T(8,128)(2,1)} %copy-done.9), calls=%async_computation.3 | async-start | bytes 524288 | tf_op jit(solution)/shard_map/all_to_all | solution.py:652
  145.2 33.3 %copy-start.5 = (bf16[8,7168]{1,0:T(8,128)(2,1)S(1)}, bf16[8,7168]{1,0:T(8,128)(2,1)}, u32[]{:S(2)}) copy-start(bf16[8,7168]{1,0:T(8,128)(2,1)} %copy-done.4) | copy-start | bytes 344068
  155.7 1.5 copy-start.6
  157.2 21.3 %copy-start.10 = (bf16[32,7168]{1,0:T(8,128)(2,1)S(1)}, bf16[32,7168]{1,0:T(8,128)(2,1)}, u32[]{:S(2)}) copy-start(bf16[32,7168]{1,0:T(8,128)(2,1)} %get-tuple-element.48.refs_4_) | copy-start | bytes 1376260
  169.7 4.8 %collective-permute-start.22 = (bf16[8,8,896]{2,1,0:T(8,128)(2,1)S(1)}, bf16[8,8,896]{2,1,0:T(8,128)(2,1)S(1)}, u32[]{:S(2)}, u32[]{:S(2)}) collective-permute-start(bf16[8,8,896]{2,1,0:T(8,128)(2,1)S(1)} %all_to_all.26.refs_0_), channel_id=1, source_target_pairs={{0,3},{1,0},{2,1},{3,2},{4,7},{5,4},{6,5},{7,6},{8,11},{9,8},{10,9... | collective-permute-start | bytes 344072 | tf_op jit(solution)/shard_map/ppermute | solution.py:556
  170.5 6.3 %collective-permute-start.21 = (bf16[8,8,896]{2,1,0:T(8,128)(2,1)S(1)}, bf16[8,8,896]{2,1,0:T(8,128)(2,1)S(1)}, u32[]{:S(2)}, u32[]{:S(2)}) collective-permute-start(bf16[8,8,896]{2,1,0:T(8,128)(2,1)S(1)} %all_to_all.26.refs_0_), channel_id=1, source_target_pairs={{0,2},{1,3},{2,0},{3,1},{4,6},{5,7},{6,4},{7,5},{8,10},{9,11},{10,... | collective-permute-start | bytes 344072 | tf_op jit(solution)/shard_map/ppermute | solution.py:556
  172.5 6.0 %collective-permute-start.20 = (bf16[8,8,896]{2,1,0:T(8,128)(2,1)S(1)}, bf16[8,8,896]{2,1,0:T(8,128)(2,1)S(1)}, u32[]{:S(2)}, u32[]{:S(2)}) collective-permute-start(bf16[8,8,896]{2,1,0:T(8,128)(2,1)S(1)} %all_to_all.26.refs_0_), channel_id=1, source_target_pairs={{0,1},{1,2},{2,3},{3,0},{4,5},{5,6},{6,7},{7,4},{8,9},{9,10},{10,1... | collective-permute-start | bytes 344072 | tf_op jit(solution)/shard_map/ppermute | solution.py:556
  180.0 5.8 %collective-permute-start.23 = (bf16[8,7168]{1,0:T(8,128)(2,1)S(1)}, bf16[8,7168]{1,0:T(8,128)(2,1)S(1)}, u32[]{:S(2)}, u32[]{:S(2)}) collective-permute-start(bf16[8,7168]{1,0:T(8,128)(2,1)S(1)} %get-tuple-element.50), channel_id=1, source_target_pairs={{0,4},{4,8},{8,12},{12,0},{1,5},{5,9},{9,13},{13,1},{2,6},{6,10},{... | collective-permute-start | bytes 344072 | tf_op jit(solution)/shard_map/ppermute | solution.py:556
  182.2 6.4 %collective-permute-start.24 = (bf16[8,7168]{1,0:T(8,128)(2,1)S(1)}, bf16[8,7168]{1,0:T(8,128)(2,1)S(1)}, u32[]{:S(2)}, u32[]{:S(2)}) collective-permute-start(bf16[8,7168]{1,0:T(8,128)(2,1)S(1)} %get-tuple-element.51), channel_id=1, source_target_pairs={{0,8},{4,12},{8,0},{12,4},{1,9},{5,13},{9,1},{13,5},{2,10},{6,14},... | collective-permute-start | bytes 344072 | tf_op jit(solution)/shard_map/ppermute | solution.py:556
  182.9 6.8 %collective-permute-start.25 = (bf16[8,7168]{1,0:T(8,128)(2,1)S(1)}, bf16[8,7168]{1,0:T(8,128)(2,1)S(1)}, u32[]{:S(2)}, u32[]{:S(2)}) collective-permute-start(bf16[8,7168]{1,0:T(8,128)(2,1)S(1)} %get-tuple-element.52), channel_id=1, source_target_pairs={{0,12},{4,0},{8,4},{12,8},{1,13},{5,1},{9,5},{13,9},{2,14},{6,2},{... | collective-permute-start | bytes 344072 | tf_op jit(solution)/shard_map/ppermute | solution.py:556
  (1 other events, 0.6 us)

commit v7 on v6

--- a/solution.py
+++ b/solution.py
@@ -38,7 +38,7 @@
     return mixed.astype(jnp.bfloat16)
 
 
-def attend_resident_body(len_ref, q_ref, keys_ref, fresh_ref, out_ref):
+def attend_resident_body(row, len_ref, q_ref, keys_ref, fresh_ref, out_ref):
     keys = keys_ref[0]
     query = jnp.concatenate([q_ref[t, 0] for t in range(STEPS)], axis=0)
     out_ref[0] = context_of(
@@ -46,37 +46,37 @@
         lambda q: jnp.dot(q, keys, preferred_element_type=jnp.float32),
         lambda p: lax.dot_general(p, keys[:LAT], NT, preferred_element_type=jnp.float32),
         fresh_ref[0],
-        len_ref[pl.program_id(0)],
-    )
-
-
-def attend_resident(lengths, queries, keys, fresh):
-    rows, width, places = keys.shape
+        len_ref[row],
+    )
+
+
+def attend_resident(row, lengths, queries, keys, fresh):
+    _, width, places = keys.shape
     steps, _, heads, _ = queries.shape
     return pl.pallas_call(
-        attend_resident_body,
-        grid=(rows,),
+        functools.partial(attend_resident_body, row),
+        grid=(1,),
         in_specs=[
             pl.BlockSpec(memory_space=pltpu.SMEM),
-            pl.BlockSpec((steps, 1, heads, width), lambda i: (0, i, 0, 0)),
-            pl.BlockSpec((1, width, places), lambda i: (i, 0, 0)),
-            pl.BlockSpec((1, *fresh.shape[1:]), lambda i: (i, 0, 0)),
+            pl.BlockSpec((steps, 1, heads, width), lambda i: (0, row, 0, 0)),
+            pl.BlockSpec((1, width, places), lambda i: (row, 0, 0)),
+            pl.BlockSpec((1, *fresh.shape[1:]), lambda i: (row, 0, 0)),
         ],
-        out_specs=pl.BlockSpec((1, steps * heads, LAT), lambda i: (i, 0, 0)),
-        out_shape=jax.ShapeDtypeStruct((rows, steps * heads, LAT), jnp.bfloat16),
+        out_specs=pl.BlockSpec((1, steps * heads, LAT), lambda i: (0, 0, 0)),
+        out_shape=jax.ShapeDtypeStruct((1, steps * heads, LAT), jnp.bfloat16),
         compiler_params=pltpu.CompilerParams(vmem_limit_bytes=24 * 1024 * 1024),
         cost_estimate=pl.CostEstimate(
-            flops=4 * keys.size * steps * heads, bytes_accessed=20000000, transcendentals=0
+            flops=4 * width * places * steps * heads, bytes_accessed=10000000, transcendentals=0
         ),
         name="attend_resident",
     )(lengths, queries, keys, fresh)
 
 
-def attend_new_body(len_ref, q_ref, taken_ref, fresh_ref, done_ref, *refs):
+def attend_new_body(resident, len_ref, q_ref, taken_ref, fresh_ref, *refs):
     out_ref = refs[-1]
-    resident, queries, _ = done_ref.shape
+    queries = refs[0].shape[1]
     fresh_rows = q_ref.shape[1]
-    contexts = [done_ref[n] for n in range(resident)]
+    contexts = [refs[n][0] for n in range(resident)]
     for n in range(fresh_rows):
         keys = taken_ref[:, n].astype(jnp.float32)
         keys = keys.reshape(-1, keys.shape[2]).astype(jnp.bfloat16)
@@ -106,14 +106,14 @@
     out = (columns, heads // columns, steps * whole, LAT)
     last = whole // rows - 1
     return pl.pallas_call(
-        attend_new_body,
+        functools.partial(attend_new_body, len(done)),
         grid=(1,),
         in_specs=[
             pl.BlockSpec(memory_space=pltpu.SMEM),
             pl.BlockSpec((steps, rows, heads, width), lambda i: (0, last, 0, 0)),
             pl.BlockSpec(taken.shape, lambda i: (0, 0, 0, 0)),
             pl.BlockSpec((rows, *fresh.shape[1:]), lambda i: (last, 0, 0)),
-            pl.BlockSpec(done.shape, lambda i: (0, 0, 0)),
+            *[pl.BlockSpec(d.shape, lambda i: (0, 0, 0)) for d in done],
         ]
         + [pl.BlockSpec(memory_space=pltpu.HBM)] * len(ready),
         out_specs=pl.BlockSpec(out, lambda i: (0, 0, 0, 0)),
@@ -123,7 +123,7 @@
             flops=4 * taken.size * steps * heads, bytes_accessed=20000000, transcendentals=0
         ),
         name="attend_new",
-    )(lengths, queries, taken, fresh, done, *ready)
+    )(lengths, queries, taken, fresh, *done, *ready)
 
 
 def picked(one_hot, x, dims=(((1,), (0,)), ((), ()))):
@@ -221,7 +221,7 @@
         ],
         scratch_shapes=[pltpu.VMEM((long * short * steps, rows), jnp.float32)] * 2,
         compiler_params=pltpu.CompilerParams(vmem_limit_bytes=24 * 1024 * 1024),
-        cost_estimate=pl.CostEstimate(flops=0, bytes_accessed=10000000, transcendentals=0),
+        cost_estimate=pl.CostEstimate(flops=0, bytes_accessed=100000, transcendentals=0),
         name="routing",
     )(place, ids, weights, *ready)
 
@@ -243,6 +243,7 @@
         out_specs=[vmem] * 3,
         out_shape=[one, one, jax.ShapeDtypeStruct((2, *up.shape), up.dtype)],
         compiler_params=pltpu.CompilerParams(vmem_limit_bytes=8 * 1024 * 1024),
+        cost_estimate=pl.CostEstimate(flops=0, bytes_accessed=100000, transcendentals=0),
         name="after",
     )(up, down, ready)
 
@@ -263,6 +264,7 @@
         out_specs=[vmem] * 2,
         out_shape=[half, half],
         compiler_params=pltpu.CompilerParams(vmem_limit_bytes=8 * 1024 * 1024),
+        cost_estimate=pl.CostEstimate(flops=0, bytes_accessed=100000, transcendentals=0),
         name="halves",
     )(up, down, ready)
 
@@ -402,7 +404,8 @@
     )(parts, gain, *held)
 
 
-def gate_up_body(core_ref, x_ref, own_ref, other_ref, active_ref, gate, up):
+def gate_up_body(core_ref, x_ref, own_ref, other_ref, *refs):
+    active_ref, gate, up = refs[-3:]
     step = pl.program_id(0)
 
     @pl.when(step == 0)
@@ -435,7 +438,7 @@
                 active_ref[k, :, units:] = first
 
 
-def gate_up(core, x, own, other, copies):
+def gate_up(core, x, own, other, copies, ready):
     rows, depth = x.shape
     units = own.shape[2]
     tile = depth // 4
@@ -447,6 +450,7 @@
             pl.BlockSpec((rows, tile), lambda i: (0, i)),
             pl.BlockSpec((2, tile, units), lambda i: (0, i, 0)),
             pl.BlockSpec((2, tile, units), lambda i: (0, i, 0)),
+            *[pl.BlockSpec(memory_space=pltpu.HBM)] * len(ready),
         ],
         out_specs=pl.BlockSpec((copies, rows, 2 * units), lambda i: (0, 0, 0)),
         out_shape=jax.ShapeDtypeStruct((copies, rows, 2 * units), jnp.bfloat16),
@@ -458,11 +462,10 @@
             transcendentals=2 * rows * units,
         ),
         name="gate_up",
-    )(core, x, own, other)
-
-
-def down_body(core_ref, x_ref, own_ref, other_ref, *refs):
-    out_ref = refs[-1]
+    )(core, x, own, other, *ready)
+
+
+def down_body(core_ref, x_ref, own_ref, other_ref, out_ref):
     x = jnp.concatenate([x_ref[k] for k in range(x_ref.shape[0])], axis=1)
     half = own_ref.shape[0]
     parts, each = out_ref.shape[0], out_ref.shape[1]
@@ -482,7 +485,7 @@
         write(others, mine)
 
 
-def down_project(core, x, own, other, *ready):
+def down_project(core, x, own, other):
     parts, rows, _ = x.shape
     columns = 2 * own.shape[0]
     vmem = pl.BlockSpec(memory_space=pltpu.VMEM)
@@ -493,7 +496,6 @@
             vmem,
             vmem,
             vmem,
-            *[pl.BlockSpec(memory_space=pltpu.HBM)] * len(ready),
         ],
         out_specs=vmem,
         out_shape=jax.ShapeDtypeStruct((parts, rows // parts, columns), jnp.bfloat16),
@@ -504,7 +506,7 @@
             transcendentals=0,
         ),
         name="down_project",
-    )(core, x, own, other, *ready)
+    )(core, x, own, other)
 
 
 def combine_body(count, spread_ref, hidden_ref, *refs):
@@ -549,6 +551,29 @@
         ),
         name="combine",
     )(spread, hidden, *blocks, *sums)
+
+
+def finish_body(here_ref, *refs):
+    *parts, out_ref = refs
+    total = here_ref[...]
+    for r in parts:
+        total += r[...].astype(jnp.float32)
+    steps, rows, _ = out_ref.shape
+    for t in range(steps):
+        out_ref[t] = total[t * rows : (t + 1) * rows].astype(jnp.bfloat16)
+
+
+def finish(here, parts, steps):
+    rows, width = here.shape
+    vmem = pl.BlockSpec(memory_space=pltpu.VMEM)
+    return pl.pallas_call(
+        finish_body,
+        in_specs=[vmem] * (1 + len(parts)),
+        out_specs=vmem,
+        out_shape=jax.ShapeDtypeStruct((steps, rows // steps, width), jnp.bfloat16),
+        compiler_params=pltpu.CompilerParams(vmem_limit_bytes=8 * 1024 * 1024),
+        name="finish",
+    )(here, *parts)
 
 
 def shifted(x, axis, by):
@@ -609,10 +634,11 @@
         tiled=False,
     )
     recent = jnp.swapaxes(jnp.pad(fresh, ((0, 8 - steps), (0, 0), (0, 0))), 0, 1)
-    done = attend_resident(res_len, queries, jnp.swapaxes(res_cache, 1, 2), recent)
+    by_width = jnp.swapaxes(res_cache, 1, 2)
+    done = [attend_resident(k, res_len, queries, by_width, recent) for k in range(resident)]
     hidden_own = hidden_in.reshape(own_rows, width)
     block = w_o.T
-    up, down_block, near = after(shifted(block, "z", 1), shifted(block, "z", -1), done, pltpu.VMEM)
+    up, down_block, near = after(shifted(block, "z", 1), shifted(block, "z", -1), done[0], pltpu.VMEM)
     context = attend_new(new_len, queries, taken, recent, done, columns, [gu_other, down_other])
     select, own_chooser, spread = routing(
         place,
@@ -648,15 +674,13 @@
 
     core_now = jnp.reshape(core, (1,)).astype(jnp.int32)
     portion = lax.all_gather(normed, "z", axis=0, tiled=True)
-    active = gate_up(core_now, portion, w_gu[0], gu_other, chips)
+    active = gate_up(core_now, portion, w_gu[0], gu_other, chips, row_parts[1:])
     everywhere = lax.all_to_all(active, "z", 0, 0, tiled=False)
-    outcome = down_project(core_now, everywhere, down, down_other, *row_parts[1:])
+    outcome = down_project(core_now, everywhere, down, down_other)
     slot_values = lax.all_to_all(outcome, "z", 0, 0, tiled=False)
     beside = [slot_values] + [shifted(slot_values, "x", k) for k in range(1, short)]
     out, *mixed = combine(spread, hidden_own, beside, row_parts)
-    for k, part in enumerate(mixed):
-        out = out + shifted(part, "y", k + 1).astype(jnp.float32)
-    return out.astype(jnp.bfloat16).reshape(steps, rows_dev, width)
+    return finish(out, [shifted(part, "y", k + 1) for k, part in enumerate(mixed)], steps)
 
 
 def solution(mesh):

time: 191 us -> 188 us (0.984)
  blocking collectives: 68.9 us -> 83.7 us
  waiting for transfers between devices: 39.9 us -> 25.7 us
  starting transfers between devices: 45.1 us -> 40.4 us
    all_to_all x0 -> x1, blocking collectives: none -> 13.9 us  [per_device(): everywhere = lax.all_to_all(active, 'z', 0, 0, tiled=False)]
    all_to_all x1 -> x0, waiting for transfers between devices: 10.4 us -> none  [per_device(): everywhere = lax.all_to_all(active, 'z', 0, 0, tiled=False)]
    all_to_all x1 -> x0, starting transfers between devices: 4.93 us -> none  [per_device(): everywhere = lax.all_to_all(active, 'z', 0, 0, tiled=False)]
    ppermute x17, waiting for transfers between devices: 27.7 us -> 24 us  [shifted(): return lax.ppermute(x, axis, [(i, (i + by) % size) for i in range(size)])]
    pallas_call x2 -> x4, Pallas kernels: 5.55 us -> 7.17 us  [the longest x2 3.33 us: attend_resident(): pl.pallas_call(functools.partial(attend_resident_body, row), grid=(1,), i...]
    unnamed x41 -> x61, local copies, waits for them, and re-layouts: 5.91 us -> 5.9 us
  transfers between devices with their start and end apart: 29 -> 28, of which waited for: 13 -> 14; matrix products, arithmetic and copies ran while one was open for 2% -> 2% of each run, Pallas kernels for 8% -> 6%
where the time goes in v7:
time: 188 us; the launch traced here: 187 us
  blocking collectives  83.7 us (45%)
  starting transfers between devices  40.4 us (21%)
  Pallas kernels  28.4 us (15%)
  waiting for transfers between devices  25.7 us (14%)
  local copies, waits for them, and re-layouts  7.35 us (4%)
    all_to_all x1, blocking collectives, per_device(): lax.all_to_all(part_slots.reshape(columns, slots_dev, width), head, 0, 0,...  30.9 us
    all_gather x1, blocking collectives, per_device(): portion = lax.all_gather(normed, 'z', axis=0, tiled=True)  27.6 us
    ppermute x17, starting transfers between devices, shifted(): return lax.ppermute(x, axis, [(i, (i + by) % size) for i in range(size)])  27 us
    ppermute x17, waiting for transfers between devices, shifted(): return lax.ppermute(x, axis, [(i, (i + by) % size) for i in range(size)])  24 us
    all_to_all x1, blocking collectives, per_device(): everywhere = lax.all_to_all(active, 'z', 0, 0, tiled=False)  13.9 us
    all_to_all x1, blocking collectives, per_device(): slot_values = lax.all_to_all(outcome, 'z', 0, 0, tiled=False)  11.3 us
    pallas_call x1, Pallas kernels, project(): pl.pallas_call(functools.partial(project_body, layout), in_specs=[pl.Bloc...  8.19 us
    all_to_all x1, starting transfers between devices, per_device(): lax.all_to_all(context, head, split_axis=0, concat_axis=0, tiled=False)  7.16 us
  transfers between devices with their start and end apart: 28, of which 14 were waited for; matrix products, arithmetic and copies ran while one was open for 2% of the time, Pallas kernels for 6%

profile of v7, /device:TPU:24, one launch (start us, length us, event | category | flops | bytes accessed | tf_op | source)
XLA Modules:
  0.0 186.8 jit_solution(10222037846034507491)
XLA Ops:
  0.5 5.9 %collective-permute-start.3 = (bf16[448,512]{1,0:T(8,128)(2,1)}, bf16[448,512]{1,0:T(8,128)(2,1)}, u32[]{:S(2)}, u32[]{:S(2)}) collective-permute-start(bf16[448,512]{1,0:T(8,128)(2,1)} %bitcast.31), channel_id=1, source_target_pairs={{0,224},{32,0},{64,32},{96,64},{128,96},{160,128},{192,160},{224,1... | collective-permute-start | bytes 1376264 | tf_op jit(solution)/shard_map/ppermute | solution.py:581
  6.4 0.8 select_reduce_fusion
  7.2 1.3 gather_fusion
  8.5 4.8 %all-to-all-start = ((bf16[16,2,8,576]{3,2,1,0:T(8,128)(2,1)}), bf16[16,2,8,576]{3,2,1,0:T(8,128)(2,1)}, u32[]{:S(2)}, u32[]{:S(2)}) async-start(bf16[16,2,8,576]{3,2,1,0:T(8,128)(2,1)} %bitcast.9), calls=%async_computation | async-start | bytes 655360 | tf_op jit(solution)/shard_map/all_to_all | solution.py:629
  13.3 0.7 copy.20
  14.1 1.7 copy-done.1
  15.7 0.7 copy-done.23
  16.4 1.7 attend_resident.2.refs_0_.ready_ref
  18.0 3.1 %collective-permute-done.3.down_ref = bf16[448,512]{1,0:T(8,128)(2,1)} collective-permute-done((bf16[448,512]{1,0:T(8,128)(2,1)}, bf16[448,512]{1,0:T(8,128)(2,1)}, u32[]{:S(2)}, u32[]{:S(2)}) %collective-permute-start.3) | collective-permute-done | bytes 458784 | tf_op jit(solution)/shard_map/ppermute | solution.py:581
  21.1 3.3 %collective-permute-done.2.up_ref = bf16[448,512]{1,0:T(8,128)(2,1)} collective-permute-done((bf16[448,512]{1,0:T(8,128)(2,1)}, bf16[448,512]{1,0:T(8,128)(2,1)}, u32[]{:S(2)}, u32[]{:S(2)}) %collective-permute-start.2) | collective-permute-done | bytes 458784 | tf_op jit(solution)/shard_map/ppermute | solution.py:581
  24.5 2.5 %after.2 = (bf16[448,512]{1,0:T(8,128)(2,1)}, bf16[448,512]{1,0:T(8,128)(2,1)}, bf16[2,448,512]{2,1,0:T(8,128)(2,1)}) custom-call(bf16[448,512]{1,0:T(8,128)(2,1)} %collective-permute-done.2.up_ref, bf16[448,512]{1,0:T(8,128)(2,1)} %collective-permute-done.3.down_ref, bf16[1,128,512]{2,1,0:T(8,128)(2,1)S(1)} %attend_resident.2.refs_0_.ready_ref), custom_call_target="tpu_custom_call" | custom-call | bytes 100000 | tf_op jit(solution)/shard_map/after/pallas_call | solution.py:240
  27.0 3.2 %collective-permute-start.5 = (bf16[448,512]{1,0:T(8,128)(2,1)}, bf16[448,512]{1,0:T(8,128)(2,1)}, u32[]{:S(2)}, u32[]{:S(2)}) collective-permute-start(bf16[448,512]{1,0:T(8,128)(2,1)} %get-tuple-element.34), channel_id=1, source_target_pairs={{0,224},{32,0},{64,32},{96,64},{128,96},{160,128},{192,160},{224,1... | collective-permute-start | bytes 1376264 | tf_op jit(solution)/shard_map/ppermute | solution.py:581
  30.3 1.7 attend_resident.3.refs_1_
  32.7 0.9 copy-done.12
  33.5 3.1 %attend_new.1.refs_0_.ready_ref = bf16[16,4,8,512]{3,2,1,0:T(8,128)(2,1)} custom-call(s32[2]{0:T(128)S(1)} %dynamic_slice.3.len_ref, bf16[2,4,64,576]{3,2,1,0:T(8,128)(2,1)S(1)} %copy-done.3, bf16[16,2,8,576]{3,2,1,0:T(8,128)(2,1)} %all-to-all-done.taken_ref, bf16[4,8,576]{2,1,0:T(8,128)(2,1)S(1)} %pad_bitcast_fusion.fresh_ref, ...), custom_call_target="tpu_custom_call" | custom-call | flops 75497472 | bytes 20000000 | tf_op jit(solution)/shard_map/attend_new/pallas_call | solution.py:108
  37.0 1.3 after.3
  38.4 3.3 %collective-permute-start.7 = (bf16[448,512]{1,0:T(8,128)(2,1)S(1)}, bf16[448,512]{1,0:T(8,128)(2,1)S(1)}, u32[]{:S(2)}, u32[]{:S(2)}) collective-permute-start(bf16[448,512]{1,0:T(8,128)(2,1)S(1)} %get-tuple-element.37), channel_id=1, source_target_pairs={{0,224},{32,0},{64,32},{96,64},{128,96},{160,128},{192,160},{224,1... | collective-permute-start | bytes 1376264 | tf_op jit(solution)/shard_map/ppermute | solution.py:581
  42.2 7.2 %all-to-all-start.1 = ((bf16[16,4,8,512]{3,2,1,0:T(8,128)(2,1)}), bf16[16,4,8,512]{3,2,1,0:T(8,128)(2,1)}, u32[]{:S(2)}, u32[]{:S(2)}) async-start(bf16[16,4,8,512]{3,2,1,0:T(8,128)(2,1)} %attend_new.1.refs_0_.ready_ref), calls=%async_computation.1 | async-start | bytes 1048576 | tf_op jit(solution)/shard_map/all_to_all | solution.py:665
  49.5 1.3 routing.1
  50.8 0.6 copy-done.18
  51.5 0.8 collective-permute-done.6.up_ref.refs_3_
  52.7 3.0 %collective-permute-start.9 = (bf16[224,512]{1,0:T(8,128)(2,1)S(1)}, bf16[224,512]{1,0:T(8,128)(2,1)}, u32[]{:S(2)}, u32[]{:S(2)}) collective-permute-start(bf16[224,512]{1,0:T(8,128)(2,1)S(1)} %get-tuple-element.39), channel_id=1, source_target_pairs={{0,224},{32,0},{64,32},{96,64},{128,96},{160,128},{192,160},{224,1... | collective-permute-start | bytes 688136 | tf_op jit(solution)/shard_map/ppermute | solution.py:581
  55.9 4.8 %collective-permute-done.8.refs_5_ = bf16[224,512]{1,0:T(8,128)(2,1)S(1)} collective-permute-done((bf16[224,512]{1,0:T(8,128)(2,1)S(1)}, bf16[224,512]{1,0:T(8,128)(2,1)S(1)}, u32[]{:S(2)}, u32[]{:S(2)}) %collective-permute-start.8) | collective-permute-done | bytes 229408 | tf_op jit(solution)/shard_map/ppermute | solution.py:581
  61.2 0.9 collective-permute-done.15.refs_12_
  62.2 0.7 collective-permute-done.16.refs_13_
  63.6 8.2 %project.1 = (bf16[128,7168]{1,0:T(8,128)(2,1)}, bf16[32,7168]{1,0:T(8,128)(2,1)}, bf16[32,7168]{1,0:T(8,128)(2,1)}, bf16[32,7168]{1,0:T(8,128)(2,1)}, bf16[32,7168]{1,0:T(8,128)(2,1)}) custom-call(s32[4]{0:T(128)} %copy-done.22, bf16[16,4,8,512]{3,2,1,0:T(8,128)(2,1)} %all-to-all-done.1.by_ref, bf16[4,512,128]{2,1,0:T(8,128)(2,1)} %uv_ref.1, ...), custom_call_target="tpu_custom_call" | custom-call | flops 1879048192 | bytes 11010048 | tf_op jit(solution)/shard_map/project/pallas_call | solution.py:346
  71.8 30.9 %all_to_all.25.parts_ref = bf16[16,8,7168]{2,1,0:T(8,128)(2,1)S(1)} all-to-all(bf16[16,8,7168]{2,1,0:T(8,128)(2,1)} %bitcast.30), channel_id=1, replica_groups=mesh['z'=8,'core'=2,'y'=4,'x'=4] {'y','x'}, dimensions={0} | all-to-all | bytes 3670016 | tf_op jit(solution)/shard_map/all_to_all | solution.py:669
  103.1 0.6 collective-permute-start.17
  103.8 1.9 collective-permute-start.18
  105.6 1.5 collective-permute-start.19
  107.1 27.6 %all_gather.3.x_ref = bf16[64,7168]{1,0:T(8,128)(2,1)S(1)} all-gather(bf16[8,7168]{1,0:T(8,128)(2,1)S(1)} %get-tuple-element.44), channel_id=1, replica_groups=mesh['z'=8,'core'=2,'y'=4,'x'=4] {'z'}, dimensions={0}, use_global_device_ids=true | all-gather | bytes 1032192 | tf_op jit(solution)/shard_map/all_gather | solution.py:676
  134.7 4.2 %gate_up.1 = bf16[8,64,256]{2,1,0:T(8,128)(2,1)S(1)} custom-call(s32[1]{0:T(128)} %bitcast.1.core_ref, bf16[64,7168]{1,0:T(8,128)(2,1)S(1)} %all_gather.3.x_ref, bf16[2,7168,128]{2,1,0:T(8,128)(2,1)S(1)} %bitcast.24, bf16[2,7168,128]{2,1,0:T(8,128)(2,1)} %collective-permute-done.refs_2_.other_ref, ...), custom_call_target="tpu_custom_call" | custom-call | flops 469762048 | bytes 8257536 | tf_op jit(solution)/shard_map/gate_up/pallas_call | solution.py:445
  138.9 13.9 %all_to_all.26.x_ref = bf16[8,64,256]{2,1,0:T(8,128)(2,1)S(1)} all-to-all(bf16[8,64,256]{2,1,0:T(8,128)(2,1)S(1)} %gate_up.1), channel_id=1, replica_groups=mesh['z'=8,'core'=2,'y'=4,'x'=4] {'z'}, dimensions={0} | all-to-all | bytes 524288 | tf_op jit(solution)/shard_map/all_to_all | solution.py:678
  152.9 2.8 %down_project.1 = bf16[8,8,896]{2,1,0:T(8,128)(2,1)S(1)} custom-call(s32[1]{0:T(128)} %bitcast.1.core_ref, bf16[8,64,256]{2,1,0:T(8,128)(2,1)S(1)} %all_to_all.26.x_ref, bf16[448,2048]{1,0:T(8,128)(2,1)S(1)} %bitcast.26, bf16[448,2048]{1,0:T(8,128)(2,1)} %collective-permute-done.1.refs_3_.other_ref), custom_call_target="tpu_custom_call" | custom-call | flops 234881024 | bytes 3670016 | tf_op jit(solution)/shard_map/down_project/pallas_call | solution.py:492
  155.7 11.3 %all_to_all.27.refs_0_ = bf16[8,8,896]{2,1,0:T(8,128)(2,1)S(1)} all-to-all(bf16[8,8,896]{2,1,0:T(8,128)(2,1)S(1)} %down_project.1), channel_id=1, replica_groups=mesh['z'=8,'core'=2,'y'=4,'x'=4] {'z'}, dimensions={0} | all-to-all | bytes 229376 | tf_op jit(solution)/shard_map/all_to_all | solution.py:680
  167.0 1.1 collective-permute-start.22
  168.1 1.9 collective-permute-start.21
  169.9 1.0 collective-permute-start.20
  170.9 0.9 collective-permute-done.22.refs_3_
  171.8 2.6 %collective-permute-done.21.refs_2_ = bf16[8,8,896]{2,1,0:T(8,128)(2,1)S(1)} collective-permute-done((bf16[8,8,896]{2,1,0:T(8,128)(2,1)S(1)}, bf16[8,8,896]{2,1,0:T(8,128)(2,1)S(1)}, u32[]{:S(2)}, u32[]{:S(2)}) %collective-permute-start.21) | collective-permute-done | bytes 114720 | tf_op jit(solution)/shard_map/ppermute | solution.py:581
  174.4 1.6 collective-permute-done.20.refs_1_
  176.4 2.1 %collective-permute-start.23 = (bf16[8,7168]{1,0:T(8,128)(2,1)S(1)}, bf16[8,7168]{1,0:T(8,128)(2,1)S(1)}, u32[]{:S(2)}, u32[]{:S(2)}) collective-permute-start(bf16[8,7168]{1,0:T(8,128)(2,1)S(1)} %get-tuple-element.50), channel_id=1, source_target_pairs={{0,4},{4,8},{8,12},{12,0},{1,5},{5,9},{9,13},{13,1},{2,6},{6,10},{... | collective-permute-start | bytes 344072 | tf_op jit(solution)/shard_map/ppermute | solution.py:581
  178.6 0.7 collective-permute-start.24
  179.3 0.7 collective-permute-start.25
  180.0 2.1 %collective-permute-done.23.refs_0_ = bf16[8,7168]{1,0:T(8,128)(2,1)S(1)} collective-permute-done((bf16[8,7168]{1,0:T(8,128)(2,1)S(1)}, bf16[8,7168]{1,0:T(8,128)(2,1)S(1)}, u32[]{:S(2)}, u32[]{:S(2)}) %collective-permute-start.23) | collective-permute-done | bytes 114720 | tf_op jit(solution)/shard_map/ppermute | solution.py:581
  182.1 2.8 %collective-permute-done.24.refs_1_ = bf16[8,7168]{1,0:T(8,128)(2,1)S(1)} collective-permute-done((bf16[8,7168]{1,0:T(8,128)(2,1)S(1)}, bf16[8,7168]{1,0:T(8,128)(2,1)S(1)}, u32[]{:S(2)}, u32[]{:S(2)}) %collective-permute-start.24) | collective-permute-done | bytes 114720 | tf_op jit(solution)/shard_map/ppermute | solution.py:581
  184.9 1.1 collective-permute-done.25.refs_2_
  186.1 0.7 finish.1
  (93 shorter events, 4.9 us)
Async XLA Ops:
  0.0 14.0 %copy-start.3 = (bf16[2,4,64,576]{3,2,1,0:T(8,128)(2,1)S(1)}, bf16[2,4,64,576]{3,2,1,0:T(8,128)(2,1)}, u32[]{:S(2)}) copy-start(bf16[2,4,64,576]{3,2,1,0:T(8,128)(2,1)} %q_ref.5) | copy-start | bytes 1769476
  0.0 32.6 %collective-permute-start = (bf16[2,7168,128]{2,1,0:T(8,128)(2,1)}, bf16[2,7168,128]{2,1,0:T(8,128)(2,1)}, u32[]{:S(2)}, u32[]{:S(2)}) collective-permute-start(bf16[2,7168,128]{2,1,0:T(8,128)(2,1)} %bitcast.23), channel_id=1, source_target_pairs={{0,16},{16,0},{1,17},{17,1},{2,18},{18,2},{3,19},{19,3},{4,20},{20... | collective-permute-start | bytes 11010056 | tf_op jit(solution)/shard_map/ppermute | solution.py:585
  0.0 32.6 %collective-permute-start.1 = (bf16[448,2048]{1,0:T(8,128)(2,1)}, bf16[448,2048]{1,0:T(8,128)(2,1)}, u32[]{:S(2)}, u32[]{:S(2)}) collective-permute-start(bf16[448,2048]{1,0:T(8,128)(2,1)} %bitcast.25), channel_id=1, source_target_pairs={{0,16},{16,0},{1,17},{17,1},{2,18},{18,2},{3,19},{19,3},{4,20},{20... | collective-permute-start | bytes 5505032 | tf_op jit(solution)/shard_map/ppermute | solution.py:585
  0.5 20.6 %collective-permute-start.3 = (bf16[448,512]{1,0:T(8,128)(2,1)}, bf16[448,512]{1,0:T(8,128)(2,1)}, u32[]{:S(2)}, u32[]{:S(2)}) collective-permute-start(bf16[448,512]{1,0:T(8,128)(2,1)} %bitcast.31), channel_id=1, source_target_pairs={{0,224},{32,0},{64,32},{96,64},{128,96},{160,128},{192,160},{224,1... | collective-permute-start | bytes 1376264 | tf_op jit(solution)/shard_map/ppermute | solution.py:581
  6.4 18.1 %collective-permute-start.2 = (bf16[448,512]{1,0:T(8,128)(2,1)}, bf16[448,512]{1,0:T(8,128)(2,1)}, u32[]{:S(2)}, u32[]{:S(2)}) collective-permute-start(bf16[448,512]{1,0:T(8,128)(2,1)} %bitcast.32), channel_id=1, source_target_pairs={{0,32},{32,64},{64,96},{96,128},{128,160},{160,192},{192,224},{224... | collective-permute-start | bytes 1376264 | tf_op jit(solution)/shard_map/ppermute | solution.py:581
  8.5 24.1 %all-to-all-start = ((bf16[16,2,8,576]{3,2,1,0:T(8,128)(2,1)}), bf16[16,2,8,576]{3,2,1,0:T(8,128)(2,1)}, u32[]{:S(2)}, u32[]{:S(2)}) async-start(bf16[16,2,8,576]{3,2,1,0:T(8,128)(2,1)} %bitcast.9), calls=%async_computation | async-start | bytes 655360 | tf_op jit(solution)/shard_map/all_to_all | solution.py:629
  16.4 13.9 %copy-start.2 = (bf16[2,1024,576]{1,2,0:T(8,128)(2,1)S(1)}, bf16[2,1024,576]{1,2,0:T(8,128)(2,1)}, u32[]{:S(2)}) copy-start(bf16[2,1024,576]{1,2,0:T(8,128)(2,1)} %param.18) | copy-start | bytes 7077892
  16.4 13.9 %copy-start.24 = (s32[2]{0:T(128)S(1)}, s32[2]{0:T(128)}, u32[]{:S(2)}) copy-start(s32[2]{0:T(128)} %len_ref.3) | copy-start | bytes 28
  27.0 10.0 %collective-permute-start.4 = (bf16[448,512]{1,0:T(8,128)(2,1)}, bf16[448,512]{1,0:T(8,128)(2,1)}, u32[]{:S(2)}, u32[]{:S(2)}) collective-permute-start(bf16[448,512]{1,0:T(8,128)(2,1)} %get-tuple-element.33), channel_id=1, source_target_pairs={{0,32},{32,64},{64,96},{96,128},{128,160},{160,192},{192,224},{224... | collective-permute-start | bytes 1376264 | tf_op jit(solution)/shard_map/ppermute | solution.py:581
  27.0 10.0 %collective-permute-start.5 = (bf16[448,512]{1,0:T(8,128)(2,1)}, bf16[448,512]{1,0:T(8,128)(2,1)}, u32[]{:S(2)}, u32[]{:S(2)}) collective-permute-start(bf16[448,512]{1,0:T(8,128)(2,1)} %get-tuple-element.34), channel_id=1, source_target_pairs={{0,224},{32,0},{64,32},{96,64},{128,96},{160,128},{192,160},{224,1... | collective-permute-start | bytes 1376264 | tf_op jit(solution)/shard_map/ppermute | solution.py:581
  30.2 25.5 %collective-permute-start.11 = (bf16[2,448,512]{2,1,0:T(8,128)(2,1)}, bf16[2,448,512]{2,1,0:T(8,128)(2,1)}, u32[]{:S(2)}, u32[]{:S(2)}) collective-permute-start(bf16[2,448,512]{2,1,0:T(8,128)(2,1)} %get-tuple-element.32.refs_1_), channel_id=1, source_target_pairs={{0,16},{16,0},{1,17},{17,1},{2,18},{18,2},{3,19},{19,3},{4,20},{20... | collective-permute-start | bytes 2752520 | tf_op jit(solution)/shard_map/ppermute | solution.py:585
  36.7 12.8 %copy-start.29 = (bf16[2,4,7168]{2,1,0:T(4,128)(2,1)S(1)}, bf16[2,4,7168]{2,1,0:T(4,128)(2,1)}, u32[]{:S(2)}) copy-start(bf16[2,4,7168]{2,1,0:T(4,128)(2,1)} %param.15) | copy-start | bytes 344068
  36.7 12.8 %copy-start.20 = (s32[2,64,8]{1,2,0:T(8,128)S(1)}, s32[2,64,8]{1,2,0:T(8,128)}, u32[]{:S(2)}) copy-start(s32[2,64,8]{1,2,0:T(8,128)} %param.26) | copy-start | bytes 12292
  36.7 12.8 %copy-start.21 = (f32[2,64,8]{1,2,0:T(8,128)S(1)}, f32[2,64,8]{1,2,0:T(8,128)}, u32[]{:S(2)}) copy-start(f32[2,64,8]{1,2,0:T(8,128)} %param.27) | copy-start | bytes 12292
  38.3 24.6 %copy-start.10 = (bf16[2,448,512]{2,1,0:T(8,128)(2,1)}, bf16[2,448,512]{2,1,0:T(8,128)(2,1)S(1)}, u32[]{:S(2)}) copy-start(bf16[2,448,512]{2,1,0:T(8,128)(2,1)S(1)} %get-tuple-element.35.refs_2_) | copy-start | bytes 2752516
  38.3 14.0 %collective-permute-start.6 = (bf16[448,512]{1,0:T(8,128)(2,1)S(1)}, bf16[448,512]{1,0:T(8,128)(2,1)S(1)}, u32[]{:S(2)}, u32[]{:S(2)}) collective-permute-start(bf16[448,512]{1,0:T(8,128)(2,1)S(1)} %get-tuple-element.36), channel_id=1, source_target_pairs={{0,32},{32,64},{64,96},{96,128},{128,160},{160,192},{192,224},{224... | collective-permute-start | bytes 1376264 | tf_op jit(solution)/shard_map/ppermute | solution.py:581
  38.4 13.9 %collective-permute-start.7 = (bf16[448,512]{1,0:T(8,128)(2,1)S(1)}, bf16[448,512]{1,0:T(8,128)(2,1)S(1)}, u32[]{:S(2)}, u32[]{:S(2)}) collective-permute-start(bf16[448,512]{1,0:T(8,128)(2,1)S(1)} %get-tuple-element.37), channel_id=1, source_target_pairs={{0,224},{32,0},{64,32},{96,64},{128,96},{160,128},{192,160},{224,1... | collective-permute-start | bytes 1376264 | tf_op jit(solution)/shard_map/ppermute | solution.py:581
  41.7 11.0 %collective-permute-start.10 = (bf16[448,512]{1,0:T(8,128)(2,1)}, bf16[448,512]{1,0:T(8,128)(2,1)}, u32[]{:S(2)}, u32[]{:S(2)}) collective-permute-start(bf16[448,512]{1,0:T(8,128)(2,1)} %bitcast.33), channel_id=1, source_target_pairs={{0,16},{16,0},{1,17},{17,1},{2,18},{18,2},{3,19},{19,3},{4,20},{20... | collective-permute-start | bytes 1376264 | tf_op jit(solution)/shard_map/ppermute | solution.py:585
  41.7 19.5 %collective-permute-start.12 = (bf16[2,448,512]{2,1,0:T(8,128)(2,1)S(1)}, bf16[2,448,512]{2,1,0:T(8,128)(2,1)}, u32[]{:S(2)}, u32[]{:S(2)}) collective-permute-start(bf16[2,448,512]{2,1,0:T(8,128)(2,1)S(1)} %get-tuple-element.35.refs_2_), channel_id=1, source_target_pairs={{0,16},{16,0},{1,17},{17,1},{2,18},{18,2},{3,19},{19,3},{4,20},{20... | collective-permute-start | bytes 2752520 | tf_op jit(solution)/shard_map/ppermute | solution.py:585
  42.2 19.0 %all-to-all-start.1 = ((bf16[16,4,8,512]{3,2,1,0:T(8,128)(2,1)}), bf16[16,4,8,512]{3,2,1,0:T(8,128)(2,1)}, u32[]{:S(2)}, u32[]{:S(2)}) async-start(bf16[16,4,8,512]{3,2,1,0:T(8,128)(2,1)} %attend_new.1.refs_0_.ready_ref), calls=%async_computation.1 | async-start | bytes 1048576 | tf_op jit(solution)/shard_map/all_to_all | solution.py:665
  49.5 13.5 %copy-start.22 = (s32[4]{0:T(128)}, s32[4]{0:T(128)S(1)}, u32[]{:S(2)}) copy-start(s32[4]{0:T(128)S(1)} %pad_add_fusion.place_ref) | copy-start | bytes 52
  49.5 13.4 %copy-start.5 = (bf16[8,7168]{1,0:T(8,128)(2,1)}, bf16[8,7168]{1,0:T(8,128)(2,1)S(1)}, u32[]{:S(2)}) copy-start(bf16[8,7168]{1,0:T(8,128)(2,1)S(1)} %reshape.11.refs_1_.hidden_ref) | copy-start | bytes 344068
  51.5 11.5 %copy-start.17 = (bf16[256,128]{1,0:T(8,128)(2,1)}, bf16[256,128]{1,0:T(8,128)(2,1)S(1)}, u32[]{:S(2)}) copy-start(bf16[256,128]{1,0:T(8,128)(2,1)S(1)} %get-tuple-element.30.ready_ref.select_ref) | copy-start | bytes 196612
  52.3 10.7 %copy-start.8 = (bf16[448,512]{1,0:T(8,128)(2,1)}, bf16[448,512]{1,0:T(8,128)(2,1)S(1)}, u32[]{:S(2)}) copy-start(bf16[448,512]{1,0:T(8,128)(2,1)S(1)} %collective-permute-done.6.up_ref.refs_3_) | copy-start | bytes 1376260
  52.3 10.7 %copy-start.9 = (bf16[448,512]{1,0:T(8,128)(2,1)}, bf16[448,512]{1,0:T(8,128)(2,1)S(1)}, u32[]{:S(2)}) copy-start(bf16[448,512]{1,0:T(8,128)(2,1)S(1)} %collective-permute-done.7.down_ref.refs_4_) | copy-start | bytes 1376260
  52.3 8.4 %collective-permute-start.8 = (bf16[224,512]{1,0:T(8,128)(2,1)S(1)}, bf16[224,512]{1,0:T(8,128)(2,1)S(1)}, u32[]{:S(2)}, u32[]{:S(2)}) collective-permute-start(bf16[224,512]{1,0:T(8,128)(2,1)S(1)} %get-tuple-element.38), channel_id=1, source_target_pairs={{0,32},{32,64},{64,96},{96,128},{128,160},{160,192},{192,224},{224... | collective-permute-start | bytes 688136 | tf_op jit(solution)/shard_map/ppermute | solution.py:581
  52.4 8.8 %collective-permute-start.13 = (bf16[448,512]{1,0:T(8,128)(2,1)S(1)}, bf16[448,512]{1,0:T(8,128)(2,1)S(1)}, u32[]{:S(2)}, u32[]{:S(2)}) collective-permute-start(bf16[448,512]{1,0:T(8,128)(2,1)S(1)} %collective-permute-done.6.up_ref.refs_3_), channel_id=1, source_target_pairs={{0,16},{16,0},{1,17},{17,1},{2,18},{18,2},{3,19},{19,3},{4,20},{20... | collective-permute-start | bytes 1376264 | tf_op jit(solution)/shard_map/ppermute | solution.py:585
  52.7 8.5 %collective-permute-start.9 = (bf16[224,512]{1,0:T(8,128)(2,1)S(1)}, bf16[224,512]{1,0:T(8,128)(2,1)}, u32[]{:S(2)}, u32[]{:S(2)}) collective-permute-start(bf16[224,512]{1,0:T(8,128)(2,1)S(1)} %get-tuple-element.39), channel_id=1, source_target_pairs={{0,224},{32,0},{64,32},{96,64},{128,96},{160,128},{192,160},{224,1... | collective-permute-start | bytes 688136 | tf_op jit(solution)/shard_map/ppermute | solution.py:581
  55.7 7.2 %collective-permute-start.14 = (bf16[448,512]{1,0:T(8,128)(2,1)S(1)}, bf16[448,512]{1,0:T(8,128)(2,1)}, u32[]{:S(2)}, u32[]{:S(2)}) collective-permute-start(bf16[448,512]{1,0:T(8,128)(2,1)S(1)} %collective-permute-done.7.down_ref.refs_4_), channel_id=1, source_target_pairs={{0,16},{16,0},{1,17},{17,1},{2,18},{18,2},{3,19},{19,3},{4,20},{20... | collective-permute-start | bytes 1376264 | tf_op jit(solution)/shard_map/ppermute | solution.py:585
  60.7 1.5 collective-permute-start.15
  61.2 1.7 collective-permute-start.16
  71.8 30.9 %copy-start.14 = (bf16[32,7168]{1,0:T(8,128)(2,1)S(1)}, bf16[32,7168]{1,0:T(8,128)(2,1)}, u32[]{:S(2)}) copy-start(bf16[32,7168]{1,0:T(8,128)(2,1)} %get-tuple-element.41.refs_0_) | copy-start | bytes 1376260
  71.8 30.9 %copy-start.15 = (bf16[32,7168]{1,0:T(8,128)(2,1)S(1)}, bf16[32,7168]{1,0:T(8,128)(2,1)}, u32[]{:S(2)}) copy-start(bf16[32,7168]{1,0:T(8,128)(2,1)} %get-tuple-element.42.refs_1_) | copy-start | bytes 1376260
  71.8 30.9 %copy-start.16 = (bf16[32,7168]{1,0:T(8,128)(2,1)S(1)}, bf16[32,7168]{1,0:T(8,128)(2,1)}, u32[]{:S(2)}) copy-start(bf16[32,7168]{1,0:T(8,128)(2,1)} %get-tuple-element.43.refs_2_) | copy-start | bytes 1376260
  71.8 30.9 %copy-start.19 = (f32[7168]{0:T(1024)S(1)}, f32[7168]{0:T(1024)}, u32[]{:S(2)}) copy-start(f32[7168]{0:T(1024)} %param.25) | copy-start | bytes 86020
  102.7 32.0 %copy-start.4 = (bf16[1,2,7168,128]{3,2,1,0:T(8,128)(2,1)S(1)}, bf16[1,2,7168,128]{3,2,1,0:T(8,128)(2,1)}, u32[]{:S(2)}) copy-start(bf16[1,2,7168,128]{3,2,1,0:T(8,128)(2,1)} %param.28) | copy-start | bytes 11010052
  103.1 31.6 %collective-permute-start.17 = (bf16[32,7168]{1,0:T(8,128)(2,1)S(1)}, bf16[32,7168]{1,0:T(8,128)(2,1)S(1)}, u32[]{:S(2)}, u32[]{:S(2)}) collective-permute-start(bf16[32,7168]{1,0:T(8,128)(2,1)S(1)} %get-tuple-element.45), channel_id=1, source_target_pairs={{0,1},{1,2},{2,3},{3,0},{4,5},{5,6},{6,7},{7,4},{8,9},{9,10},{10,1... | collective-permute-start | bytes 1376264 | tf_op jit(solution)/shard_map/ppermute | solution.py:581
  103.8 30.9 %collective-permute-start.18 = (bf16[32,7168]{1,0:T(8,128)(2,1)S(1)}, bf16[32,7168]{1,0:T(8,128)(2,1)S(1)}, u32[]{:S(2)}, u32[]{:S(2)}) collective-permute-start(bf16[32,7168]{1,0:T(8,128)(2,1)S(1)} %get-tuple-element.46), channel_id=1, source_target_pairs={{0,2},{1,3},{2,0},{3,1},{4,6},{5,7},{6,4},{7,5},{8,10},{9,11},{10,... | collective-permute-start | bytes 1376264 | tf_op jit(solution)/shard_map/ppermute | solution.py:581
  105.6 29.1 %collective-permute-start.19 = (bf16[32,7168]{1,0:T(8,128)(2,1)S(1)}, bf16[32,7168]{1,0:T(8,128)(2,1)S(1)}, u32[]{:S(2)}, u32[]{:S(2)}) collective-permute-start(bf16[32,7168]{1,0:T(8,128)(2,1)S(1)} %get-tuple-element.47), channel_id=1, source_target_pairs={{0,3},{1,0},{2,1},{3,2},{4,7},{5,4},{6,5},{7,6},{8,11},{9,8},{10,9... | collective-permute-start | bytes 1376264 | tf_op jit(solution)/shard_map/ppermute | solution.py:581
  134.7 18.2 %copy-start.7 = (bf16[1,2048,448]{1,2,0:T(8,128)(2,1)S(1)}, bf16[1,2048,448]{1,2,0:T(8,128)(2,1)}, u32[]{:S(2)}) copy-start(bf16[1,2048,448]{1,2,0:T(8,128)(2,1)} %param.29) | copy-start | bytes 5505028
  152.9 23.0 %copy-start.6 = (bf16[8,7168]{1,0:T(8,128)(2,1)S(1)}, bf16[8,7168]{1,0:T(8,128)(2,1)}, u32[]{:S(2)}) copy-start(bf16[8,7168]{1,0:T(8,128)(2,1)} %copy-done.5) | copy-start | bytes 344068
  152.9 23.0 %copy-start.13 = (bf16[32,7168]{1,0:T(8,128)(2,1)S(1)}, bf16[32,7168]{1,0:T(8,128)(2,1)}, u32[]{:S(2)}) copy-start(bf16[32,7168]{1,0:T(8,128)(2,1)} %get-tuple-element.48.refs_4_) | copy-start | bytes 1376260
  167.0 4.8 %collective-permute-start.22 = (bf16[8,8,896]{2,1,0:T(8,128)(2,1)S(1)}, bf16[8,8,896]{2,1,0:T(8,128)(2,1)S(1)}, u32[]{:S(2)}, u32[]{:S(2)}) collective-permute-start(bf16[8,8,896]{2,1,0:T(8,128)(2,1)S(1)} %all_to_all.27.refs_0_), channel_id=1, source_target_pairs={{0,3},{1,0},{2,1},{3,2},{4,7},{5,4},{6,5},{7,6},{8,11},{9,8},{10,9... | collective-permute-start | bytes 344072 | tf_op jit(solution)/shard_map/ppermute | solution.py:581
  168.1 6.3 %collective-permute-start.21 = (bf16[8,8,896]{2,1,0:T(8,128)(2,1)S(1)}, bf16[8,8,896]{2,1,0:T(8,128)(2,1)S(1)}, u32[]{:S(2)}, u32[]{:S(2)}) collective-permute-start(bf16[8,8,896]{2,1,0:T(8,128)(2,1)S(1)} %all_to_all.27.refs_0_), channel_id=1, source_target_pairs={{0,2},{1,3},{2,0},{3,1},{4,6},{5,7},{6,4},{7,5},{8,10},{9,11},{10,... | collective-permute-start | bytes 344072 | tf_op jit(solution)/shard_map/ppermute | solution.py:581
  169.9 6.0 %collective-permute-start.20 = (bf16[8,8,896]{2,1,0:T(8,128)(2,1)S(1)}, bf16[8,8,896]{2,1,0:T(8,128)(2,1)S(1)}, u32[]{:S(2)}, u32[]{:S(2)}) collective-permute-start(bf16[8,8,896]{2,1,0:T(8,128)(2,1)S(1)} %all_to_all.27.refs_0_), channel_id=1, source_target_pairs={{0,1},{1,2},{2,3},{3,0},{4,5},{5,6},{6,7},{7,4},{8,9},{9,10},{10,1... | collective-permute-start | bytes 344072 | tf_op jit(solution)/shard_map/ppermute | solution.py:581
  176.4 5.7 %collective-permute-start.23 = (bf16[8,7168]{1,0:T(8,128)(2,1)S(1)}, bf16[8,7168]{1,0:T(8,128)(2,1)S(1)}, u32[]{:S(2)}, u32[]{:S(2)}) collective-permute-start(bf16[8,7168]{1,0:T(8,128)(2,1)S(1)} %get-tuple-element.50), channel_id=1, source_target_pairs={{0,4},{4,8},{8,12},{12,0},{1,5},{5,9},{9,13},{13,1},{2,6},{6,10},{... | collective-permute-start | bytes 344072 | tf_op jit(solution)/shard_map/ppermute | solution.py:581
  178.6 6.4 %collective-permute-start.24 = (bf16[8,7168]{1,0:T(8,128)(2,1)S(1)}, bf16[8,7168]{1,0:T(8,128)(2,1)S(1)}, u32[]{:S(2)}, u32[]{:S(2)}) collective-permute-start(bf16[8,7168]{1,0:T(8,128)(2,1)S(1)} %get-tuple-element.51), channel_id=1, source_target_pairs={{0,8},{4,12},{8,0},{12,4},{1,9},{5,13},{9,1},{13,5},{2,10},{6,14},... | collective-permute-start | bytes 344072 | tf_op jit(solution)/shard_map/ppermute | solution.py:581
  179.3 6.8 %collective-permute-start.25 = (bf16[8,7168]{1,0:T(8,128)(2,1)S(1)}, bf16[8,7168]{1,0:T(8,128)(2,1)S(1)}, u32[]{:S(2)}, u32[]{:S(2)}) collective-permute-start(bf16[8,7168]{1,0:T(8,128)(2,1)S(1)} %get-tuple-element.52), channel_id=1, source_target_pairs={{0,12},{4,0},{8,4},{12,8},{1,13},{5,1},{9,5},{13,9},{2,14},{6,2},{... | collective-permute-start | bytes 344072 | tf_op jit(solution)/shard_map/ppermute | solution.py:581
  (10 other events, 17.2 us)

commit v8 on v7

--- a/solution.py
+++ b/solution.py
@@ -441,7 +441,7 @@
 def gate_up(core, x, own, other, copies, ready):
     rows, depth = x.shape
     units = own.shape[2]
-    tile = depth // 4
+    tile = depth // 2
     return pl.pallas_call(
         gate_up_body,
         grid=(depth // tile,),
@@ -465,12 +465,19 @@
     )(core, x, own, other, *ready)
 
 
-def down_body(core_ref, x_ref, own_ref, other_ref, out_ref):
+def down_body(core_ref, x_ref, own_ref, other_ref, out_ref, held, sems):
+    copies = [
+        pltpu.make_async_copy(r, held.at[k], sems.at[k]) for k, r in enumerate((own_ref, other_ref))
+    ]
+    for copy in copies:
+        copy.start()
     x = jnp.concatenate([x_ref[k] for k in range(x_ref.shape[0])], axis=1)
     half = own_ref.shape[0]
     parts, each = out_ref.shape[0], out_ref.shape[1]
-    mine = lax.dot_general(x, own_ref[...], NT, preferred_element_type=jnp.float32)
-    others = lax.dot_general(x, other_ref[...], NT, preferred_element_type=jnp.float32)
+    copies[0].wait()
+    mine = lax.dot_general(x, held[0], NT, preferred_element_type=jnp.float32)
+    copies[1].wait()
+    others = lax.dot_general(x, held[1], NT, preferred_element_type=jnp.float32)
 
     def write(first, second):
         both = jnp.concatenate([first, second], axis=1).reshape(parts, each, 2 * half)
@@ -494,11 +501,14 @@
         in_specs=[
             pl.BlockSpec(memory_space=pltpu.SMEM),
             vmem,
-            vmem,
-            vmem,
+            *[pl.BlockSpec(memory_space=pltpu.HBM)] * 2,
         ],
         out_specs=vmem,
         out_shape=jax.ShapeDtypeStruct((parts, rows // parts, columns), jnp.bfloat16),
+        scratch_shapes=[
+            pltpu.VMEM((2, *own.shape), own.dtype),
+            pltpu.SemaphoreType.DMA((2,)),
+        ],
         compiler_params=pltpu.CompilerParams(vmem_limit_bytes=24 * 1024 * 1024),
         cost_estimate=pl.CostEstimate(
             flops=2 * rows * own.shape[1] * columns,

time: 188 us -> 186 us (0.989)
  no operation moved by 1% of the time
where the time goes in v8:
time: 186 us
  blocking collectives  83.9 us (45%)
  starting transfers between devices  40.3 us (22%)
  Pallas kernels  27.2 us (15%)
  waiting for transfers between devices  25.6 us (14%)
  local copies, waits for them, and re-layouts  7.35 us (4%)
    all_to_all x1, blocking collectives, per_device(): lax.all_to_all(part_slots.reshape(columns, slots_dev, width), head, 0, 0,...  30.9 us
    all_gather x1, blocking collectives, per_device(): portion = lax.all_gather(normed, 'z', axis=0, tiled=True)  27.6 us
    ppermute x17, starting transfers between devices, shifted(): return lax.ppermute(x, axis, [(i, (i + by) % size) for i in range(size)])  26.9 us
    ppermute x17, waiting for transfers between devices, shifted(): return lax.ppermute(x, axis, [(i, (i + by) % size) for i in range(size)])  23.9 us
    all_to_all x1, blocking collectives, per_device(): everywhere = lax.all_to_all(active, 'z', 0, 0, tiled=False)  14 us
    all_to_all x1, blocking collectives, per_device(): slot_values = lax.all_to_all(outcome, 'z', 0, 0, tiled=False)  11.3 us
    pallas_call x1, Pallas kernels, project(): pl.pallas_call(functools.partial(project_body, layout), in_specs=[pl.Bloc...  8.19 us
    all_to_all x1, starting transfers between devices, per_device(): lax.all_to_all(context, head, split_axis=0, concat_axis=0, tiled=False)  7.18 us
  transfers between devices with their start and end apart: 28, of which 14 were waited for; matrix products, arithmetic and copies ran while one was open for 2% of the time, Pallas kernels for 6%

profile of v8, /device:TPU:24, one launch (start us, length us, event | category | flops | bytes accessed | tf_op | source)
XLA Modules:
  0.0 185.6 jit_solution(14665190399973869439)
XLA Ops:
  0.5 5.9 %collective-permute-start.3 = (bf16[448,512]{1,0:T(8,128)(2,1)}, bf16[448,512]{1,0:T(8,128)(2,1)}, u32[]{:S(2)}, u32[]{:S(2)}) collective-permute-start(bf16[448,512]{1,0:T(8,128)(2,1)} %bitcast.31), channel_id=1, source_target_pairs={{0,224},{32,0},{64,32},{96,64},{128,96},{160,128},{192,160},{224,1... | collective-permute-start | bytes 1376264 | tf_op jit(solution)/shard_map/ppermute | solution.py:591
  6.4 0.8 select_reduce_fusion
  7.2 1.3 gather_fusion
  8.5 4.8 %all-to-all-start = ((bf16[16,2,8,576]{3,2,1,0:T(8,128)(2,1)}), bf16[16,2,8,576]{3,2,1,0:T(8,128)(2,1)}, u32[]{:S(2)}, u32[]{:S(2)}) async-start(bf16[16,2,8,576]{3,2,1,0:T(8,128)(2,1)} %bitcast.9), calls=%async_computation | async-start | bytes 655360 | tf_op jit(solution)/shard_map/all_to_all | solution.py:639
  13.3 0.7 copy.20
  14.1 1.7 copy-done.1
  15.7 0.7 copy-done.23
  16.4 1.7 attend_resident.2.refs_0_.ready_ref
  18.0 3.1 %collective-permute-done.3.down_ref = bf16[448,512]{1,0:T(8,128)(2,1)} collective-permute-done((bf16[448,512]{1,0:T(8,128)(2,1)}, bf16[448,512]{1,0:T(8,128)(2,1)}, u32[]{:S(2)}, u32[]{:S(2)}) %collective-permute-start.3) | collective-permute-done | bytes 458784 | tf_op jit(solution)/shard_map/ppermute | solution.py:591
  21.1 3.3 %collective-permute-done.2.up_ref = bf16[448,512]{1,0:T(8,128)(2,1)} collective-permute-done((bf16[448,512]{1,0:T(8,128)(2,1)}, bf16[448,512]{1,0:T(8,128)(2,1)}, u32[]{:S(2)}, u32[]{:S(2)}) %collective-permute-start.2) | collective-permute-done | bytes 458784 | tf_op jit(solution)/shard_map/ppermute | solution.py:591
  24.5 2.5 %after.2 = (bf16[448,512]{1,0:T(8,128)(2,1)}, bf16[448,512]{1,0:T(8,128)(2,1)}, bf16[2,448,512]{2,1,0:T(8,128)(2,1)}) custom-call(bf16[448,512]{1,0:T(8,128)(2,1)} %collective-permute-done.2.up_ref, bf16[448,512]{1,0:T(8,128)(2,1)} %collective-permute-done.3.down_ref, bf16[1,128,512]{2,1,0:T(8,128)(2,1)S(1)} %attend_resident.2.refs_0_.ready_ref), custom_call_target="tpu_custom_call" | custom-call | bytes 100000 | tf_op jit(solution)/shard_map/after/pallas_call | solution.py:240
  27.0 3.2 %collective-permute-start.5 = (bf16[448,512]{1,0:T(8,128)(2,1)}, bf16[448,512]{1,0:T(8,128)(2,1)}, u32[]{:S(2)}, u32[]{:S(2)}) collective-permute-start(bf16[448,512]{1,0:T(8,128)(2,1)} %get-tuple-element.34), channel_id=1, source_target_pairs={{0,224},{32,0},{64,32},{96,64},{128,96},{160,128},{192,160},{224,1... | collective-permute-start | bytes 1376264 | tf_op jit(solution)/shard_map/ppermute | solution.py:591
  30.3 1.7 attend_resident.3.refs_1_
  32.0 0.6 copy-done.11
  32.6 0.9 copy-done.12
  33.5 3.1 %attend_new.1.refs_0_.ready_ref = bf16[16,4,8,512]{3,2,1,0:T(8,128)(2,1)} custom-call(s32[2]{0:T(128)S(1)} %dynamic_slice.3.len_ref, bf16[2,4,64,576]{3,2,1,0:T(8,128)(2,1)S(1)} %copy-done.3, bf16[16,2,8,576]{3,2,1,0:T(8,128)(2,1)} %all-to-all-done.taken_ref, bf16[4,8,576]{2,1,0:T(8,128)(2,1)S(1)} %pad_bitcast_fusion.fresh_ref, ...), custom_call_target="tpu_custom_call" | custom-call | flops 75497472 | bytes 20000000 | tf_op jit(solution)/shard_map/attend_new/pallas_call | solution.py:108
  37.0 1.3 after.3
  38.4 3.3 %collective-permute-start.7 = (bf16[448,512]{1,0:T(8,128)(2,1)S(1)}, bf16[448,512]{1,0:T(8,128)(2,1)S(1)}, u32[]{:S(2)}, u32[]{:S(2)}) collective-permute-start(bf16[448,512]{1,0:T(8,128)(2,1)S(1)} %get-tuple-element.37), channel_id=1, source_target_pairs={{0,224},{32,0},{64,32},{96,64},{128,96},{160,128},{192,160},{224,1... | collective-permute-start | bytes 1376264 | tf_op jit(solution)/shard_map/ppermute | solution.py:591
  42.2 7.2 %all-to-all-start.1 = ((bf16[16,4,8,512]{3,2,1,0:T(8,128)(2,1)}), bf16[16,4,8,512]{3,2,1,0:T(8,128)(2,1)}, u32[]{:S(2)}, u32[]{:S(2)}) async-start(bf16[16,4,8,512]{3,2,1,0:T(8,128)(2,1)} %attend_new.1.refs_0_.ready_ref), calls=%async_computation.1 | async-start | bytes 1048576 | tf_op jit(solution)/shard_map/all_to_all | solution.py:675
  49.5 1.3 routing.1
  50.8 0.6 copy-done.18
  51.5 0.8 collective-permute-done.6.up_ref.refs_3_
  52.7 3.0 %collective-permute-start.9 = (bf16[224,512]{1,0:T(8,128)(2,1)S(1)}, bf16[224,512]{1,0:T(8,128)(2,1)}, u32[]{:S(2)}, u32[]{:S(2)}) collective-permute-start(bf16[224,512]{1,0:T(8,128)(2,1)S(1)} %get-tuple-element.39), channel_id=1, source_target_pairs={{0,224},{32,0},{64,32},{96,64},{128,96},{160,128},{192,160},{224,1... | collective-permute-start | bytes 688136 | tf_op jit(solution)/shard_map/ppermute | solution.py:591
  55.9 4.8 %collective-permute-done.8.refs_5_ = bf16[224,512]{1,0:T(8,128)(2,1)S(1)} collective-permute-done((bf16[224,512]{1,0:T(8,128)(2,1)S(1)}, bf16[224,512]{1,0:T(8,128)(2,1)S(1)}, u32[]{:S(2)}, u32[]{:S(2)}) %collective-permute-start.8) | collective-permute-done | bytes 229408 | tf_op jit(solution)/shard_map/ppermute | solution.py:591
  61.2 0.9 collective-permute-done.15.refs_12_
  62.2 0.7 collective-permute-done.16.refs_13_
  63.6 8.2 %project.1 = (bf16[128,7168]{1,0:T(8,128)(2,1)}, bf16[32,7168]{1,0:T(8,128)(2,1)}, bf16[32,7168]{1,0:T(8,128)(2,1)}, bf16[32,7168]{1,0:T(8,128)(2,1)}, bf16[32,7168]{1,0:T(8,128)(2,1)}) custom-call(s32[4]{0:T(128)} %copy-done.22, bf16[16,4,8,512]{3,2,1,0:T(8,128)(2,1)} %all-to-all-done.1.by_ref, bf16[4,512,128]{2,1,0:T(8,128)(2,1)} %uv_ref.1, ...), custom_call_target="tpu_custom_call" | custom-call | flops 1879048192 | bytes 11010048 | tf_op jit(solution)/shard_map/project/pallas_call | solution.py:346
  71.8 30.9 %all_to_all.25.parts_ref = bf16[16,8,7168]{2,1,0:T(8,128)(2,1)S(1)} all-to-all(bf16[16,8,7168]{2,1,0:T(8,128)(2,1)} %bitcast.30), channel_id=1, replica_groups=mesh['z'=8,'core'=2,'y'=4,'x'=4] {'y','x'}, dimensions={0} | all-to-all | bytes 3670016 | tf_op jit(solution)/shard_map/all_to_all | solution.py:679
  103.1 0.6 collective-permute-start.17
  103.8 1.8 collective-permute-start.18
  105.6 1.5 collective-permute-start.19
  107.1 27.6 %all_gather.3.x_ref = bf16[64,7168]{1,0:T(8,128)(2,1)S(1)} all-gather(bf16[8,7168]{1,0:T(8,128)(2,1)S(1)} %get-tuple-element.44), channel_id=1, replica_groups=mesh['z'=8,'core'=2,'y'=4,'x'=4] {'z'}, dimensions={0}, use_global_device_ids=true | all-gather | bytes 1032192 | tf_op jit(solution)/shard_map/all_gather | solution.py:686
  134.8 3.4 %gate_up.1 = bf16[8,64,256]{2,1,0:T(8,128)(2,1)S(1)} custom-call(s32[1]{0:T(128)} %bitcast.1.core_ref, bf16[64,7168]{1,0:T(8,128)(2,1)S(1)} %all_gather.3.x_ref, bf16[2,7168,128]{2,1,0:T(8,128)(2,1)S(1)} %bitcast.24, bf16[2,7168,128]{2,1,0:T(8,128)(2,1)} %collective-permute-done.refs_2_.other_ref, ...), custom_call_target="tpu_custom_call" | custom-call | flops 469762048 | bytes 8257536 | tf_op jit(solution)/shard_map/gate_up/pallas_call | solution.py:445
  138.1 14.0 %all_to_all.26.x_ref = bf16[8,64,256]{2,1,0:T(8,128)(2,1)S(1)} all-to-all(bf16[8,64,256]{2,1,0:T(8,128)(2,1)S(1)} %gate_up.1), channel_id=1, replica_groups=mesh['z'=8,'core'=2,'y'=4,'x'=4] {'z'}, dimensions={0} | all-to-all | bytes 524288 | tf_op jit(solution)/shard_map/all_to_all | solution.py:688
  152.2 2.5 %down_project.1 = bf16[8,8,896]{2,1,0:T(8,128)(2,1)S(1)} custom-call(s32[1]{0:T(128)} %bitcast.1.core_ref, bf16[8,64,256]{2,1,0:T(8,128)(2,1)S(1)} %all_to_all.26.x_ref, bf16[448,2048]{1,0:T(8,128)(2,1)S(1)} %bitcast.26, bf16[448,2048]{1,0:T(8,128)(2,1)} %collective-permute-done.1.refs_3_.other_ref), custom_call_target="tpu_custom_call" | custom-call | flops 234881024 | bytes 3670016 | tf_op jit(solution)/shard_map/down_project/pallas_call | solution.py:499
  154.7 11.3 %all_to_all.27.refs_0_ = bf16[8,8,896]{2,1,0:T(8,128)(2,1)S(1)} all-to-all(bf16[8,8,896]{2,1,0:T(8,128)(2,1)S(1)} %down_project.1), channel_id=1, replica_groups=mesh['z'=8,'core'=2,'y'=4,'x'=4] {'z'}, dimensions={0} | all-to-all | bytes 229376 | tf_op jit(solution)/shard_map/all_to_all | solution.py:690
  165.9 1.0 collective-permute-start.22
  166.9 1.9 %collective-permute-start.21 = (bf16[8,8,896]{2,1,0:T(8,128)(2,1)S(1)}, bf16[8,8,896]{2,1,0:T(8,128)(2,1)S(1)}, u32[]{:S(2)}, u32[]{:S(2)}) collective-permute-start(bf16[8,8,896]{2,1,0:T(8,128)(2,1)S(1)} %all_to_all.27.refs_0_), channel_id=1, source_target_pairs={{0,2},{1,3},{2,0},{3,1},{4,6},{5,7},{6,4},{7,5},{8,10},{9,11},{10,... | collective-permute-start | bytes 344072 | tf_op jit(solution)/shard_map/ppermute | solution.py:591
  168.8 0.9 collective-permute-start.20
  169.8 1.0 collective-permute-done.22.refs_3_
  170.7 2.5 %collective-permute-done.21.refs_2_ = bf16[8,8,896]{2,1,0:T(8,128)(2,1)S(1)} collective-permute-done((bf16[8,8,896]{2,1,0:T(8,128)(2,1)S(1)}, bf16[8,8,896]{2,1,0:T(8,128)(2,1)S(1)}, u32[]{:S(2)}, u32[]{:S(2)}) %collective-permute-start.21) | collective-permute-done | bytes 114720 | tf_op jit(solution)/shard_map/ppermute | solution.py:591
  173.2 1.6 collective-permute-done.20.refs_1_
  175.3 2.0 %collective-permute-start.23 = (bf16[8,7168]{1,0:T(8,128)(2,1)S(1)}, bf16[8,7168]{1,0:T(8,128)(2,1)S(1)}, u32[]{:S(2)}, u32[]{:S(2)}) collective-permute-start(bf16[8,7168]{1,0:T(8,128)(2,1)S(1)} %get-tuple-element.50), channel_id=1, source_target_pairs={{0,4},{4,8},{8,12},{12,0},{1,5},{5,9},{9,13},{13,1},{2,6},{6,10},{... | collective-permute-start | bytes 344072 | tf_op jit(solution)/shard_map/ppermute | solution.py:591
  177.3 0.9 collective-permute-start.24
  178.8 2.1 %collective-permute-done.23.refs_0_ = bf16[8,7168]{1,0:T(8,128)(2,1)S(1)} collective-permute-done((bf16[8,7168]{1,0:T(8,128)(2,1)S(1)}, bf16[8,7168]{1,0:T(8,128)(2,1)S(1)}, u32[]{:S(2)}, u32[]{:S(2)}) %collective-permute-start.23) | collective-permute-done | bytes 114720 | tf_op jit(solution)/shard_map/ppermute | solution.py:591
  180.9 2.8 %collective-permute-done.24.refs_1_ = bf16[8,7168]{1,0:T(8,128)(2,1)S(1)} collective-permute-done((bf16[8,7168]{1,0:T(8,128)(2,1)S(1)}, bf16[8,7168]{1,0:T(8,128)(2,1)S(1)}, u32[]{:S(2)}, u32[]{:S(2)}) %collective-permute-start.24) | collective-permute-done | bytes 114720 | tf_op jit(solution)/shard_map/ppermute | solution.py:591
  183.7 1.2 collective-permute-done.25.refs_2_
  184.9 0.7 finish.1
  (93 shorter events, 4.9 us)
Async XLA Ops:
  0.0 14.0 %copy-start.3 = (bf16[2,4,64,576]{3,2,1,0:T(8,128)(2,1)S(1)}, bf16[2,4,64,576]{3,2,1,0:T(8,128)(2,1)}, u32[]{:S(2)}) copy-start(bf16[2,4,64,576]{3,2,1,0:T(8,128)(2,1)} %q_ref.5) | copy-start | bytes 1769476
  0.0 32.6 %collective-permute-start = (bf16[2,7168,128]{2,1,0:T(8,128)(2,1)}, bf16[2,7168,128]{2,1,0:T(8,128)(2,1)}, u32[]{:S(2)}, u32[]{:S(2)}) collective-permute-start(bf16[2,7168,128]{2,1,0:T(8,128)(2,1)} %bitcast.23), channel_id=1, source_target_pairs={{0,16},{16,0},{1,17},{17,1},{2,18},{18,2},{3,19},{19,3},{4,20},{20... | collective-permute-start | bytes 11010056 | tf_op jit(solution)/shard_map/ppermute | solution.py:595
  0.0 32.6 %collective-permute-start.1 = (bf16[448,2048]{1,0:T(8,128)(2,1)}, bf16[448,2048]{1,0:T(8,128)(2,1)}, u32[]{:S(2)}, u32[]{:S(2)}) collective-permute-start(bf16[448,2048]{1,0:T(8,128)(2,1)} %bitcast.25), channel_id=1, source_target_pairs={{0,16},{16,0},{1,17},{17,1},{2,18},{18,2},{3,19},{19,3},{4,20},{20... | collective-permute-start | bytes 5505032 | tf_op jit(solution)/shard_map/ppermute | solution.py:595
  0.5 20.6 %collective-permute-start.3 = (bf16[448,512]{1,0:T(8,128)(2,1)}, bf16[448,512]{1,0:T(8,128)(2,1)}, u32[]{:S(2)}, u32[]{:S(2)}) collective-permute-start(bf16[448,512]{1,0:T(8,128)(2,1)} %bitcast.31), channel_id=1, source_target_pairs={{0,224},{32,0},{64,32},{96,64},{128,96},{160,128},{192,160},{224,1... | collective-permute-start | bytes 1376264 | tf_op jit(solution)/shard_map/ppermute | solution.py:591
  6.4 18.1 %collective-permute-start.2 = (bf16[448,512]{1,0:T(8,128)(2,1)}, bf16[448,512]{1,0:T(8,128)(2,1)}, u32[]{:S(2)}, u32[]{:S(2)}) collective-permute-start(bf16[448,512]{1,0:T(8,128)(2,1)} %bitcast.32), channel_id=1, source_target_pairs={{0,32},{32,64},{64,96},{96,128},{128,160},{160,192},{192,224},{224... | collective-permute-start | bytes 1376264 | tf_op jit(solution)/shard_map/ppermute | solution.py:591
  8.5 24.1 %all-to-all-start = ((bf16[16,2,8,576]{3,2,1,0:T(8,128)(2,1)}), bf16[16,2,8,576]{3,2,1,0:T(8,128)(2,1)}, u32[]{:S(2)}, u32[]{:S(2)}) async-start(bf16[16,2,8,576]{3,2,1,0:T(8,128)(2,1)} %bitcast.9), calls=%async_computation | async-start | bytes 655360 | tf_op jit(solution)/shard_map/all_to_all | solution.py:639
  16.4 13.9 %copy-start.2 = (bf16[2,1024,576]{1,2,0:T(8,128)(2,1)S(1)}, bf16[2,1024,576]{1,2,0:T(8,128)(2,1)}, u32[]{:S(2)}) copy-start(bf16[2,1024,576]{1,2,0:T(8,128)(2,1)} %param.18) | copy-start | bytes 7077892
  16.4 13.9 %copy-start.24 = (s32[2]{0:T(128)S(1)}, s32[2]{0:T(128)}, u32[]{:S(2)}) copy-start(s32[2]{0:T(128)} %len_ref.3) | copy-start | bytes 28
  27.0 10.0 %collective-permute-start.4 = (bf16[448,512]{1,0:T(8,128)(2,1)}, bf16[448,512]{1,0:T(8,128)(2,1)}, u32[]{:S(2)}, u32[]{:S(2)}) collective-permute-start(bf16[448,512]{1,0:T(8,128)(2,1)} %get-tuple-element.33), channel_id=1, source_target_pairs={{0,32},{32,64},{64,96},{96,128},{128,160},{160,192},{192,224},{224... | collective-permute-start | bytes 1376264 | tf_op jit(solution)/shard_map/ppermute | solution.py:591
  27.0 10.0 %collective-permute-start.5 = (bf16[448,512]{1,0:T(8,128)(2,1)}, bf16[448,512]{1,0:T(8,128)(2,1)}, u32[]{:S(2)}, u32[]{:S(2)}) collective-permute-start(bf16[448,512]{1,0:T(8,128)(2,1)} %get-tuple-element.34), channel_id=1, source_target_pairs={{0,224},{32,0},{64,32},{96,64},{128,96},{160,128},{192,160},{224,1... | collective-permute-start | bytes 1376264 | tf_op jit(solution)/shard_map/ppermute | solution.py:591
  30.2 25.5 %collective-permute-start.11 = (bf16[2,448,512]{2,1,0:T(8,128)(2,1)}, bf16[2,448,512]{2,1,0:T(8,128)(2,1)}, u32[]{:S(2)}, u32[]{:S(2)}) collective-permute-start(bf16[2,448,512]{2,1,0:T(8,128)(2,1)} %get-tuple-element.32.refs_1_), channel_id=1, source_target_pairs={{0,16},{16,0},{1,17},{17,1},{2,18},{18,2},{3,19},{19,3},{4,20},{20... | collective-permute-start | bytes 2752520 | tf_op jit(solution)/shard_map/ppermute | solution.py:595
  36.7 12.8 %copy-start.29 = (bf16[2,4,7168]{2,1,0:T(4,128)(2,1)S(1)}, bf16[2,4,7168]{2,1,0:T(4,128)(2,1)}, u32[]{:S(2)}) copy-start(bf16[2,4,7168]{2,1,0:T(4,128)(2,1)} %param.15) | copy-start | bytes 344068
  36.7 12.8 %copy-start.20 = (s32[2,64,8]{1,2,0:T(8,128)S(1)}, s32[2,64,8]{1,2,0:T(8,128)}, u32[]{:S(2)}) copy-start(s32[2,64,8]{1,2,0:T(8,128)} %param.26) | copy-start | bytes 12292
  36.7 12.8 %copy-start.21 = (f32[2,64,8]{1,2,0:T(8,128)S(1)}, f32[2,64,8]{1,2,0:T(8,128)}, u32[]{:S(2)}) copy-start(f32[2,64,8]{1,2,0:T(8,128)} %param.27) | copy-start | bytes 12292
  38.3 24.6 %copy-start.10 = (bf16[2,448,512]{2,1,0:T(8,128)(2,1)}, bf16[2,448,512]{2,1,0:T(8,128)(2,1)S(1)}, u32[]{:S(2)}) copy-start(bf16[2,448,512]{2,1,0:T(8,128)(2,1)S(1)} %get-tuple-element.35.refs_2_) | copy-start | bytes 2752516
  38.3 14.0 %collective-permute-start.6 = (bf16[448,512]{1,0:T(8,128)(2,1)S(1)}, bf16[448,512]{1,0:T(8,128)(2,1)S(1)}, u32[]{:S(2)}, u32[]{:S(2)}) collective-permute-start(bf16[448,512]{1,0:T(8,128)(2,1)S(1)} %get-tuple-element.36), channel_id=1, source_target_pairs={{0,32},{32,64},{64,96},{96,128},{128,160},{160,192},{192,224},{224... | collective-permute-start | bytes 1376264 | tf_op jit(solution)/shard_map/ppermute | solution.py:591
  38.4 13.9 %collective-permute-start.7 = (bf16[448,512]{1,0:T(8,128)(2,1)S(1)}, bf16[448,512]{1,0:T(8,128)(2,1)S(1)}, u32[]{:S(2)}, u32[]{:S(2)}) collective-permute-start(bf16[448,512]{1,0:T(8,128)(2,1)S(1)} %get-tuple-element.37), channel_id=1, source_target_pairs={{0,224},{32,0},{64,32},{96,64},{128,96},{160,128},{192,160},{224,1... | collective-permute-start | bytes 1376264 | tf_op jit(solution)/shard_map/ppermute | solution.py:591
  41.7 11.0 %collective-permute-start.10 = (bf16[448,512]{1,0:T(8,128)(2,1)}, bf16[448,512]{1,0:T(8,128)(2,1)}, u32[]{:S(2)}, u32[]{:S(2)}) collective-permute-start(bf16[448,512]{1,0:T(8,128)(2,1)} %bitcast.33), channel_id=1, source_target_pairs={{0,16},{16,0},{1,17},{17,1},{2,18},{18,2},{3,19},{19,3},{4,20},{20... | collective-permute-start | bytes 1376264 | tf_op jit(solution)/shard_map/ppermute | solution.py:595
  41.7 19.5 %collective-permute-start.12 = (bf16[2,448,512]{2,1,0:T(8,128)(2,1)S(1)}, bf16[2,448,512]{2,1,0:T(8,128)(2,1)}, u32[]{:S(2)}, u32[]{:S(2)}) collective-permute-start(bf16[2,448,512]{2,1,0:T(8,128)(2,1)S(1)} %get-tuple-element.35.refs_2_), channel_id=1, source_target_pairs={{0,16},{16,0},{1,17},{17,1},{2,18},{18,2},{3,19},{19,3},{4,20},{20... | collective-permute-start | bytes 2752520 | tf_op jit(solution)/shard_map/ppermute | solution.py:595
  42.2 19.0 %all-to-all-start.1 = ((bf16[16,4,8,512]{3,2,1,0:T(8,128)(2,1)}), bf16[16,4,8,512]{3,2,1,0:T(8,128)(2,1)}, u32[]{:S(2)}, u32[]{:S(2)}) async-start(bf16[16,4,8,512]{3,2,1,0:T(8,128)(2,1)} %attend_new.1.refs_0_.ready_ref), calls=%async_computation.1 | async-start | bytes 1048576 | tf_op jit(solution)/shard_map/all_to_all | solution.py:675
  49.5 13.4 %copy-start.22 = (s32[4]{0:T(128)}, s32[4]{0:T(128)S(1)}, u32[]{:S(2)}) copy-start(s32[4]{0:T(128)S(1)} %pad_add_fusion.place_ref) | copy-start | bytes 52
  49.5 13.4 %copy-start.5 = (bf16[8,7168]{1,0:T(8,128)(2,1)}, bf16[8,7168]{1,0:T(8,128)(2,1)S(1)}, u32[]{:S(2)}) copy-start(bf16[8,7168]{1,0:T(8,128)(2,1)S(1)} %reshape.11.refs_1_.hidden_ref) | copy-start | bytes 344068
  51.5 11.4 %copy-start.17 = (bf16[256,128]{1,0:T(8,128)(2,1)}, bf16[256,128]{1,0:T(8,128)(2,1)S(1)}, u32[]{:S(2)}) copy-start(bf16[256,128]{1,0:T(8,128)(2,1)S(1)} %get-tuple-element.30.ready_ref.select_ref) | copy-start | bytes 196612
  52.3 10.7 %copy-start.8 = (bf16[448,512]{1,0:T(8,128)(2,1)}, bf16[448,512]{1,0:T(8,128)(2,1)S(1)}, u32[]{:S(2)}) copy-start(bf16[448,512]{1,0:T(8,128)(2,1)S(1)} %collective-permute-done.6.up_ref.refs_3_) | copy-start | bytes 1376260
  52.3 10.7 %copy-start.9 = (bf16[448,512]{1,0:T(8,128)(2,1)}, bf16[448,512]{1,0:T(8,128)(2,1)S(1)}, u32[]{:S(2)}) copy-start(bf16[448,512]{1,0:T(8,128)(2,1)S(1)} %collective-permute-done.7.down_ref.refs_4_) | copy-start | bytes 1376260
  52.3 8.3 %collective-permute-start.8 = (bf16[224,512]{1,0:T(8,128)(2,1)S(1)}, bf16[224,512]{1,0:T(8,128)(2,1)S(1)}, u32[]{:S(2)}, u32[]{:S(2)}) collective-permute-start(bf16[224,512]{1,0:T(8,128)(2,1)S(1)} %get-tuple-element.38), channel_id=1, source_target_pairs={{0,32},{32,64},{64,96},{96,128},{128,160},{160,192},{192,224},{224... | collective-permute-start | bytes 688136 | tf_op jit(solution)/shard_map/ppermute | solution.py:591
  52.4 8.8 %collective-permute-start.13 = (bf16[448,512]{1,0:T(8,128)(2,1)S(1)}, bf16[448,512]{1,0:T(8,128)(2,1)S(1)}, u32[]{:S(2)}, u32[]{:S(2)}) collective-permute-start(bf16[448,512]{1,0:T(8,128)(2,1)S(1)} %collective-permute-done.6.up_ref.refs_3_), channel_id=1, source_target_pairs={{0,16},{16,0},{1,17},{17,1},{2,18},{18,2},{3,19},{19,3},{4,20},{20... | collective-permute-start | bytes 1376264 | tf_op jit(solution)/shard_map/ppermute | solution.py:595
  52.7 8.5 %collective-permute-start.9 = (bf16[224,512]{1,0:T(8,128)(2,1)S(1)}, bf16[224,512]{1,0:T(8,128)(2,1)}, u32[]{:S(2)}, u32[]{:S(2)}) collective-permute-start(bf16[224,512]{1,0:T(8,128)(2,1)S(1)} %get-tuple-element.39), channel_id=1, source_target_pairs={{0,224},{32,0},{64,32},{96,64},{128,96},{160,128},{192,160},{224,1... | collective-permute-start | bytes 688136 | tf_op jit(solution)/shard_map/ppermute | solution.py:591
  55.7 7.2 %collective-permute-start.14 = (bf16[448,512]{1,0:T(8,128)(2,1)S(1)}, bf16[448,512]{1,0:T(8,128)(2,1)}, u32[]{:S(2)}, u32[]{:S(2)}) collective-permute-start(bf16[448,512]{1,0:T(8,128)(2,1)S(1)} %collective-permute-done.7.down_ref.refs_4_), channel_id=1, source_target_pairs={{0,16},{16,0},{1,17},{17,1},{2,18},{18,2},{3,19},{19,3},{4,20},{20... | collective-permute-start | bytes 1376264 | tf_op jit(solution)/shard_map/ppermute | solution.py:595
  60.7 1.5 collective-permute-start.15
  61.2 1.7 collective-permute-start.16
  71.8 31.0 %copy-start.14 = (bf16[32,7168]{1,0:T(8,128)(2,1)S(1)}, bf16[32,7168]{1,0:T(8,128)(2,1)}, u32[]{:S(2)}) copy-start(bf16[32,7168]{1,0:T(8,128)(2,1)} %get-tuple-element.41.refs_0_) | copy-start | bytes 1376260
  71.8 31.0 %copy-start.15 = (bf16[32,7168]{1,0:T(8,128)(2,1)S(1)}, bf16[32,7168]{1,0:T(8,128)(2,1)}, u32[]{:S(2)}) copy-start(bf16[32,7168]{1,0:T(8,128)(2,1)} %get-tuple-element.42.refs_1_) | copy-start | bytes 1376260
  71.8 31.0 %copy-start.16 = (bf16[32,7168]{1,0:T(8,128)(2,1)S(1)}, bf16[32,7168]{1,0:T(8,128)(2,1)}, u32[]{:S(2)}) copy-start(bf16[32,7168]{1,0:T(8,128)(2,1)} %get-tuple-element.43.refs_2_) | copy-start | bytes 1376260
  71.8 31.0 %copy-start.19 = (f32[7168]{0:T(1024)S(1)}, f32[7168]{0:T(1024)}, u32[]{:S(2)}) copy-start(f32[7168]{0:T(1024)} %param.25) | copy-start | bytes 86020
  102.8 32.0 %copy-start.4 = (bf16[1,2,7168,128]{3,2,1,0:T(8,128)(2,1)S(1)}, bf16[1,2,7168,128]{3,2,1,0:T(8,128)(2,1)}, u32[]{:S(2)}) copy-start(bf16[1,2,7168,128]{3,2,1,0:T(8,128)(2,1)} %param.28) | copy-start | bytes 11010052
  103.1 31.6 %collective-permute-start.17 = (bf16[32,7168]{1,0:T(8,128)(2,1)S(1)}, bf16[32,7168]{1,0:T(8,128)(2,1)S(1)}, u32[]{:S(2)}, u32[]{:S(2)}) collective-permute-start(bf16[32,7168]{1,0:T(8,128)(2,1)S(1)} %get-tuple-element.45), channel_id=1, source_target_pairs={{0,1},{1,2},{2,3},{3,0},{4,5},{5,6},{6,7},{7,4},{8,9},{9,10},{10,1... | collective-permute-start | bytes 1376264 | tf_op jit(solution)/shard_map/ppermute | solution.py:591
  103.8 30.9 %collective-permute-start.18 = (bf16[32,7168]{1,0:T(8,128)(2,1)S(1)}, bf16[32,7168]{1,0:T(8,128)(2,1)S(1)}, u32[]{:S(2)}, u32[]{:S(2)}) collective-permute-start(bf16[32,7168]{1,0:T(8,128)(2,1)S(1)} %get-tuple-element.46), channel_id=1, source_target_pairs={{0,2},{1,3},{2,0},{3,1},{4,6},{5,7},{6,4},{7,5},{8,10},{9,11},{10,... | collective-permute-start | bytes 1376264 | tf_op jit(solution)/shard_map/ppermute | solution.py:591
  105.6 29.1 %collective-permute-start.19 = (bf16[32,7168]{1,0:T(8,128)(2,1)S(1)}, bf16[32,7168]{1,0:T(8,128)(2,1)S(1)}, u32[]{:S(2)}, u32[]{:S(2)}) collective-permute-start(bf16[32,7168]{1,0:T(8,128)(2,1)S(1)} %get-tuple-element.47), channel_id=1, source_target_pairs={{0,3},{1,0},{2,1},{3,2},{4,7},{5,4},{6,5},{7,6},{8,11},{9,8},{10,9... | collective-permute-start | bytes 1376264 | tf_op jit(solution)/shard_map/ppermute | solution.py:591
  134.7 17.4 %copy-start.7 = (bf16[1,2048,448]{1,2,0:T(8,128)(2,1)S(1)}, bf16[1,2048,448]{1,2,0:T(8,128)(2,1)}, u32[]{:S(2)}) copy-start(bf16[1,2048,448]{1,2,0:T(8,128)(2,1)} %param.29) | copy-start | bytes 5505028
  152.2 22.7 %copy-start.6 = (bf16[8,7168]{1,0:T(8,128)(2,1)S(1)}, bf16[8,7168]{1,0:T(8,128)(2,1)}, u32[]{:S(2)}) copy-start(bf16[8,7168]{1,0:T(8,128)(2,1)} %copy-done.5) | copy-start | bytes 344068
  152.2 22.7 %copy-start.13 = (bf16[32,7168]{1,0:T(8,128)(2,1)S(1)}, bf16[32,7168]{1,0:T(8,128)(2,1)}, u32[]{:S(2)}) copy-start(bf16[32,7168]{1,0:T(8,128)(2,1)} %get-tuple-element.48.refs_4_) | copy-start | bytes 1376260
  165.9 4.8 %collective-permute-start.22 = (bf16[8,8,896]{2,1,0:T(8,128)(2,1)S(1)}, bf16[8,8,896]{2,1,0:T(8,128)(2,1)S(1)}, u32[]{:S(2)}, u32[]{:S(2)}) collective-permute-start(bf16[8,8,896]{2,1,0:T(8,128)(2,1)S(1)} %all_to_all.27.refs_0_), channel_id=1, source_target_pairs={{0,3},{1,0},{2,1},{3,2},{4,7},{5,4},{6,5},{7,6},{8,11},{9,8},{10,9... | collective-permute-start | bytes 344072 | tf_op jit(solution)/shard_map/ppermute | solution.py:591
  166.9 6.3 %collective-permute-start.21 = (bf16[8,8,896]{2,1,0:T(8,128)(2,1)S(1)}, bf16[8,8,896]{2,1,0:T(8,128)(2,1)S(1)}, u32[]{:S(2)}, u32[]{:S(2)}) collective-permute-start(bf16[8,8,896]{2,1,0:T(8,128)(2,1)S(1)} %all_to_all.27.refs_0_), channel_id=1, source_target_pairs={{0,2},{1,3},{2,0},{3,1},{4,6},{5,7},{6,4},{7,5},{8,10},{9,11},{10,... | collective-permute-start | bytes 344072 | tf_op jit(solution)/shard_map/ppermute | solution.py:591
  168.8 6.0 %collective-permute-start.20 = (bf16[8,8,896]{2,1,0:T(8,128)(2,1)S(1)}, bf16[8,8,896]{2,1,0:T(8,128)(2,1)S(1)}, u32[]{:S(2)}, u32[]{:S(2)}) collective-permute-start(bf16[8,8,896]{2,1,0:T(8,128)(2,1)S(1)} %all_to_all.27.refs_0_), channel_id=1, source_target_pairs={{0,1},{1,2},{2,3},{3,0},{4,5},{5,6},{6,7},{7,4},{8,9},{9,10},{10,1... | collective-permute-start | bytes 344072 | tf_op jit(solution)/shard_map/ppermute | solution.py:591
  175.3 5.6 %collective-permute-start.23 = (bf16[8,7168]{1,0:T(8,128)(2,1)S(1)}, bf16[8,7168]{1,0:T(8,128)(2,1)S(1)}, u32[]{:S(2)}, u32[]{:S(2)}) collective-permute-start(bf16[8,7168]{1,0:T(8,128)(2,1)S(1)} %get-tuple-element.50), channel_id=1, source_target_pairs={{0,4},{4,8},{8,12},{12,0},{1,5},{5,9},{9,13},{13,1},{2,6},{6,10},{... | collective-permute-start | bytes 344072 | tf_op jit(solution)/shard_map/ppermute | solution.py:591
  177.3 6.4 %collective-permute-start.24 = (bf16[8,7168]{1,0:T(8,128)(2,1)S(1)}, bf16[8,7168]{1,0:T(8,128)(2,1)S(1)}, u32[]{:S(2)}, u32[]{:S(2)}) collective-permute-start(bf16[8,7168]{1,0:T(8,128)(2,1)S(1)} %get-tuple-element.51), channel_id=1, source_target_pairs={{0,8},{4,12},{8,0},{12,4},{1,9},{5,13},{9,1},{13,5},{2,10},{6,14},... | collective-permute-start | bytes 344072 | tf_op jit(solution)/shard_map/ppermute | solution.py:591
  178.2 6.6 %collective-permute-start.25 = (bf16[8,7168]{1,0:T(8,128)(2,1)S(1)}, bf16[8,7168]{1,0:T(8,128)(2,1)S(1)}, u32[]{:S(2)}, u32[]{:S(2)}) collective-permute-start(bf16[8,7168]{1,0:T(8,128)(2,1)S(1)} %get-tuple-element.52), channel_id=1, source_target_pairs={{0,12},{4,0},{8,4},{12,8},{1,13},{5,1},{9,5},{13,9},{2,14},{6,2},{... | collective-permute-start | bytes 344072 | tf_op jit(solution)/shard_map/ppermute | solution.py:591
  (10 other events, 17.2 us)
